TPU v7x, 256 devices: a whole 4x4x8 slice. The times are simulated.
256 devices in a mesh: row: 8 (over y, core), col: 32 (over x, z).
Axes of the slice: x: 4, y: 4, z: 8, core: 2. Of those that a mesh axis runs over, the one named last changes fastest.
Arguments:
- src_embed: bfloat16 [32768, 256], P(('row', 'col'))
- tgt_embed: bfloat16 [32768, 256], P(('col', 'row')), may hold values from -0.375 to 0.375
- tiles: int32 [8, 32, 2, 128], P('row', 'col'), may hold values from 0 to 31, as said below
- counts: int32 [8, 32], P('row', 'col'), may hold values from 1 to 128, as said below
Outputs:
- source_potential: float32 [32768], P('row')
- target_potential: float32 [32768], P('col')
Inputs may be any that keep to these rules, and one draw needn't show every extreme that they name: tiles[r, c, 0, k] is a source block among the 32 of row index r and tiles[r, c, 1, k] a target block among the 8 of col index c; the first counts[r, c] slots of a device hold distinct pairs, the other slots hold pairs that are not part of the support; every source block and every target block appears in some counted slot of some device. `counts`: some device uses all 128 slots in every draw.
All inputs are finite; a program needn't handle non-finite values.
Results may differ from a plain program's by a relative error of at most 0.00035.
Values may be sent and summed in bfloat16 or wider, within the bound.
No kernel may reach another device: no remote copies, remote signals or barrier semaphores. Data moves between devices by JAX's collectives and lax.ppermute only.
A program may use at most 128 MiB of HBM per device.

v0:
```python
import functools
import math

import jax
import jax.numpy as jnp
from jax import lax
from jax.experimental import pallas as pl
from jax.experimental.pallas import tpu as pltpu
from jax.sharding import Mesh
from jax.sharding import PartitionSpec as P

TILE = 128
ITERS = 2
ENTROPY = 0.05
KAPPA = math.log2(math.e) / ENTROPY
EMPTY = -1e30
UNROLL = 16
ROW = ("y", "core")
COL = ("x", "s", "p")
SRC_PEERS = ("x", "s")
TGT_PEERS = ("p", "y", "core")
F32 = jnp.float32
NT = (((1,), (1,)), ((), ()))
VMEM = pl.BlockSpec(memory_space=pltpu.VMEM)
SMEM = pl.BlockSpec(memory_space=pltpu.SMEM)
PARAMS = pltpu.CompilerParams(vmem_limit_bytes=24 * 2**20)


def square_rows(cells):
    wide = cells.astype(F32)
    square = wide * wide
    high = square.astype(jnp.bfloat16)
    low = (square - high.astype(F32)).astype(jnp.bfloat16)
    ones = jnp.ones((8, cells.shape[1]), jnp.bfloat16)
    total = lax.dot_general(ones, high, NT, preferred_element_type=F32)
    total += lax.dot_general(ones, low, NT, preferred_element_type=F32)
    return total[0:1]


def log_sum(parts):
    highest = jnp.max(parts, axis=0)
    return highest + jnp.log2(jnp.sum(jnp.exp2(parts - highest[None]), axis=0))


def expand(weights, wide):
    blocks = weights.shape[0]
    columns = jnp.concatenate([weights, jnp.zeros((TILE - blocks, TILE), F32)], axis=0).T
    for n in range(blocks):
        wide[n] = jnp.broadcast_to(columns[:, n : n + 1], (TILE, TILE))


def tile_sums(tile, count, near, far, wide, peaks, totals):
    near_blocks, far_blocks = near.shape[0], far.shape[0]
    spare = near_blocks * far_blocks
    peaks[...] = jnp.full(peaks.shape, EMPTY, F32)
    totals[...] = jnp.zeros(totals.shape, F32)

    @pl.loop(0, (count + UNROLL - 1) // UNROLL)
    def _(step):
        for u in range(UNROLL):
            k = step * UNROLL + u
            n, f = tile(jnp.where(k < count, k, 0))
            inner = lax.dot_general(near[n], far[f], NT, preferred_element_type=F32)
            score = (inner * (2.0 * KAPPA) + wide[n]).reshape(TILE // 8, 8, TILE)
            peak = jnp.max(score, axis=0)
            slot = jnp.where(k < count, f * near_blocks + n, spare)
            peaks[slot] = peak
            totals[slot] = jnp.sum(jnp.exp2(score - peak[None]), axis=0)

    rows = []
    for f in range(far_blocks):
        at = pl.ds(f * near_blocks, near_blocks)
        peak = peaks[at]
        highest = jnp.max(jnp.max(peak, axis=0), axis=0, keepdims=True)
        whole = jnp.sum(totals[at] * jnp.exp2(peak - highest[None]), axis=0)
        whole = jnp.sum(whole, axis=0, keepdims=True)
        rows.append(jnp.where(whole > 0.0, highest + jnp.log2(whole), EMPTY))
    return jnp.concatenate(rows, axis=0)


def pick_kernel(mine, other, parity, picked, total):
    p = parity[0]
    targets = 8

    def scan(lists, col, start):
        def step(k, at):
            a, b = lists[0, k], lists[1, k]
            picked[at] = (a // 2) * (2 * targets) + col * targets + b
            return at + jnp.where((k < lists[2, 0]) & (a % 2 == p), 1, 0)

        return lax.fori_loop(0, TILE, step, start, unroll=8)

    total[0] = scan(other, 1 - p, scan(mine, p, 0))


def source_tiles(tiles, tgt_blocks):
    def tile(k):
        code = tiles[k]
        return lax.rem(code, tgt_blocks), lax.div(code, tgt_blocks)

    return tile


def target_tiles(tiles, tgt_blocks):
    def tile(k):
        code = tiles[k]
        return lax.div(code, tgt_blocks), lax.rem(code, tgt_blocks)

    return tile


def first_kernel(tiles, count, src, tgt, out, sq_src, sq_tgt, wide, peaks, totals):
    for b in range(tgt.shape[0]):
        sq_tgt[b : b + 1, :] = square_rows(tgt[b])
    for a in range(src.shape[0]):
        sq_src[a : a + 1, :] = square_rows(src[a])
    expand(sq_tgt[...] * -KAPPA, wide)
    sums = tile_sums(source_tiles(tiles, tgt.shape[0]), count[0], tgt, src, wide, peaks, totals)
    out[...] = jnp.broadcast_to(sums[None], out.shape)


def source_kernel(log_cells, tiles, count, src, tgt, parts, out, wide, peaks, totals):
    expand(-log_cells - log_sum(parts[...]), wide)
    sums = tile_sums(source_tiles(tiles, tgt.shape[0]), count[0], tgt, src, wide, peaks, totals)
    out[...] = jnp.broadcast_to(sums[None], out.shape)


def target_kernel(log_cells, tiles, count, src, tgt, parts, sq_src, out, pot, wide, peaks, totals):
    weights = -log_cells - log_sum(parts[...])
    pot[...] = weights * (1.0 / KAPPA) + sq_src[...]
    expand(weights, wide)
    sums = tile_sums(target_tiles(tiles, tgt.shape[0]), count[0], src, tgt, wide, peaks, totals)
    copies, blocks = out.shape[0], out.shape[1]
    if blocks == sums.shape[0]:
        out[...] = jnp.broadcast_to(sums[None], out.shape)
    else:
        cols = sums.shape[0] // blocks
        each = copies // cols
        for col in range(cols):
            piece = sums[col * blocks : (col + 1) * blocks]
            out[col * each : (col + 1) * each] = jnp.broadcast_to(piece[None], (each,) + piece.shape)


def last_kernel(log_cells, parity, parts, sq_tgt, mine, other, tgt_pot, src_pot):
    p = parity[0]
    blocks = tgt_pot.shape[0]
    squares = jnp.where(p == 0, sq_tgt[0:blocks], sq_tgt[blocks : 2 * blocks])
    tgt_pot[...] = (-log_cells - log_sum(parts[...])) * (1.0 / KAPPA) + squares
    src_pot[:, 0, :] = jnp.where(p == 0, mine[...], other[...])
    src_pot[:, 1, :] = jnp.where(p == 0, other[...], mine[...])


def half_step(kernel, outs, near_blocks, slots, tiles, count, *args):
    return pl.pallas_call(
        kernel,
        out_shape=[jax.ShapeDtypeStruct(s, F32) for s in outs],
        in_specs=[SMEM] * 2 + [VMEM] * len(args),
        out_specs=[VMEM] * len(outs),
        scratch_shapes=[
            pltpu.VMEM((near_blocks, TILE, TILE), F32),
            pltpu.VMEM((slots + 1, 8, TILE), F32),
            pltpu.VMEM((slots + 1, 8, TILE), F32),
        ],
        compiler_params=PARAMS,
    )(tiles, count, *args)


def exchange(copies, peers):
    return lax.all_to_all(copies, peers, 0, 0, tiled=True)


def gather(block, peers):
    return exchange(jnp.broadcast_to(block[None], (lax.axis_size(peers),) + block.shape), peers)


def local(src_embed, tgt_embed, tiles, counts):
    rows, cols = lax.axis_size(ROW), lax.axis_size(COL)
    log_cells = math.log2(rows * cols * TILE)
    parity = lax.axis_index("p").astype(jnp.int32).reshape(1)
    partner = lambda v: lax.ppermute(v, "p", [(0, 1), (1, 0)])

    lists = jnp.concatenate([tiles[0, 0], jnp.broadcast_to(counts[0, 0], (1, TILE))], axis=0)
    other_lists = partner(lists)
    tgt = gather(tgt_embed, TGT_PEERS)
    src = gather(src_embed, SRC_PEERS)
    picked, count = pl.pallas_call(
        pick_kernel,
        out_shape=[jax.ShapeDtypeStruct((2 * TILE + UNROLL,), jnp.int32), jax.ShapeDtypeStruct((1,), jnp.int32)],
        in_specs=[SMEM] * 3,
        out_specs=[SMEM] * 2,
        compiler_params=PARAMS,
    )(lists, other_lists, parity)

    srcs, tgts = src.shape[0], tgt.shape[0]
    slots = srcs * tgts
    src_out, tgt_out = (srcs, srcs, TILE), (tgts, tgts, TILE)
    for sweep in range(ITERS):
        if sweep == 0:
            parts, sq_src, sq_tgt = half_step(
                first_kernel, [src_out, (srcs, TILE), (tgts, TILE)], tgts, slots, picked, count, src, tgt
            )
        else:
            (parts,) = half_step(
                functools.partial(source_kernel, log_cells), [src_out], tgts, slots, picked, count, src, tgt, parts
            )
        parts = exchange(parts, SRC_PEERS)
        last = sweep == ITERS - 1
        parts, src_pot = half_step(
            functools.partial(target_kernel, log_cells),
            [(tgts, rows, TILE) if last else tgt_out, (srcs, TILE)],
            srcs,
            slots,
            picked,
            count,
            src,
            tgt,
            parts,
            sq_src,
        )
        if last:
            other_pot = partner(src_pot)
        parts = exchange(parts, TGT_PEERS)
    tgt_pot, both = pl.pallas_call(
        functools.partial(last_kernel, log_cells),
        out_shape=[jax.ShapeDtypeStruct((rows, TILE), F32), jax.ShapeDtypeStruct((srcs, 2, TILE), F32)],
        in_specs=[SMEM] + [VMEM] * 4,
        out_specs=[VMEM] * 2,
        compiler_params=PARAMS,
    )(parity, parts, sq_tgt, src_pot, other_pot)
    return (both.reshape(-1), tgt_pot.reshape(-1))


def solution(mesh):
    fine = Mesh(mesh.devices.reshape(4, 2, 4, 4, 2), ROW + COL)
    in_specs = (P(ROW + COL, None), P(COL + ROW, None), P(ROW, COL, None, None), P(ROW, COL))
    return jax.shard_map(local, mesh=fine, in_specs=in_specs, out_specs=(P(ROW), P(COL)), check_vma=False)
```

profile of v0, /device:TPU:1, one launch (start us, length us, event | category | flops | bytes accessed | tf_op | source)
XLA Modules:
  0.0 137.9 jit_solution(13244337149540887848)
XLA Ops:
  0.6 0.9 broadcast_in_dim.4
  1.6 0.0 copy-start
  1.6 38.9 %all_to_all.30.src = bf16[16,128,256]{2,1,0:T(8,128)(2,1)S(1)} all-to-all(bf16[16,128,256]{2,1,0:T(8,128)(2,1)S(1)} %broadcast_in_dim.4), channel_id=1, replica_groups=mesh['y'=4,'core'=2,'x'=4,'s'=4,'p'=2] {'x','s'}, dimensions={0} | all-to-all | bytes 2097152 | tf_op jit(solution)/shard_map/all_to_all | solution.py:169
  40.5 0.0 copy-done
  40.5 1.1 broadcast_in_dim.5
  41.6 8.4 %all-to-all-start.1 = ((bf16[16,128,256]{2,1,0:T(8,128)(2,1)}), bf16[16,128,256]{2,1,0:T(8,128)(2,1)S(1)}, u32[]{:S(2)}, u32[]{:S(2)}) async-start(bf16[16,128,256]{2,1,0:T(8,128)(2,1)} %broadcast_in_dim.5), calls=%async_computation.1 | async-start | bytes 2097152 | tf_op jit(solution)/shard_map/all_to_all | solution.py:169
  50.7 0.0 copy-start.1
  50.7 0.7 copy-done.1
  51.3 1.4 %collective-permute-start = (s32[3,128]{1,0:T(4,128)S(1)}, s32[3,128]{1,0:T(4,128)S(1)}, u32[]{:S(2)}, u32[]{:S(2)}) collective-permute-start(s32[3,128]{1,0:T(4,128)S(1)} %concatenate.3.mine), channel_id=1, source_target_pairs={{0,1},{1,0},{2,3},{3,2},{4,5},{5,4},{6,7},{7,6},{8,9},{9,8},{10,11... | collective-permute-start | bytes 4616 | tf_op jit(solution)/shard_map/ppermute | solution.py:180
  52.7 10.8 %collective-permute-done.other = s32[3,128]{1,0:T(4,128)S(1)} collective-permute-done((s32[3,128]{1,0:T(4,128)S(1)}, s32[3,128]{1,0:T(4,128)S(1)}, u32[]{:S(2)}, u32[]{:S(2)}) %collective-permute-start) | collective-permute-done | bytes 1568 | tf_op jit(solution)/shard_map/ppermute | solution.py:180
  63.5 3.9 %shard_map.59 = (s32[272]{0:T(512)S(1)}, s32[1]{0:T(128)}) custom-call(s32[3,128]{1,0:T(4,128)S(1)} %concatenate.3.mine, s32[3,128]{1,0:T(4,128)S(1)} %collective-permute-done.other, s32[1]{0:T(128)} %bitcast.parity), custom_call_target="tpu_custom_call" | custom-call | tf_op jit(solution)/shard_map/pallas_call | solution.py:186
  67.5 0.0 all-to-all-done.1.tgt
  67.5 4.1 %shard_map.60 = (f32[16,16,128]{2,1,0:T(8,128)S(1)}, f32[16,128]{1,0:T(8,128)S(1)}, f32[16,128]{1,0:T(8,128)S(1)}) custom-call(s32[272]{0:T(512)S(1)} %get-tuple-element.12.tiles, s32[1]{0:T(128)} %get-tuple-element.13.count, bf16[16,128,256]{2,1,0:T(8,128)(2,1)S(1)} %all_to_all.30.src, bf16[16,128,256]{2,1,0:T(8,128)(2,1)S(1)} %all-to-all-done.1.tgt), custom_call_target="tpu_custom_call" | custom-call | tf_op jit(solution)/shard_map/pallas_call | solution.py:154
  71.6 14.0 %all_to_all.31.parts = f32[16,16,128]{2,1,0:T(8,128)S(1)} all-to-all(f32[16,16,128]{2,1,0:T(8,128)S(1)} %get-tuple-element.14), channel_id=1, replica_groups=mesh['y'=4,'core'=2,'x'=4,'s'=4,'p'=2] {'x','s'}, dimensions={0} | all-to-all | bytes 262144 | tf_op jit(solution)/shard_map/all_to_all | solution.py:169
  85.7 3.8 %shard_map.61 = (f32[16,16,128]{2,1,0:T(8,128)S(1)}, f32[16,128]{1,0:T(8,128)}) custom-call(s32[272]{0:T(512)S(1)} %get-tuple-element.12.tiles, s32[1]{0:T(128)} %get-tuple-element.13.count, bf16[16,128,256]{2,1,0:T(8,128)(2,1)S(1)} %all_to_all.30.src, bf16[16,128,256]{2,1,0:T(8,128)(2,1)S(1)} %all-to-all-done.1.tgt, f32[16,16,128]{2,1,0:T(8,128)S(1)} %all_to_all.31.parts, ...), custom_call_target="tpu_custom_call" | custom-call | tf_op jit(solution)/shard_map/pallas_call | solution.py:154
  89.5 14.2 %all_to_all.32.parts = f32[16,16,128]{2,1,0:T(8,128)S(1)} all-to-all(f32[16,16,128]{2,1,0:T(8,128)S(1)} %get-tuple-element.16), channel_id=1, replica_groups=mesh['y'=4,'core'=2,'x'=4,'s'=4,'p'=2] {'p','y','core'}, dimensions={0} | all-to-all | bytes 262144 | tf_op jit(solution)/shard_map/all_to_all | solution.py:169
  103.7 3.5 %shard_map.62 = f32[16,16,128]{2,1,0:T(8,128)S(1)} custom-call(s32[272]{0:T(512)S(1)} %get-tuple-element.12.tiles, s32[1]{0:T(128)} %get-tuple-element.13.count, bf16[16,128,256]{2,1,0:T(8,128)(2,1)S(1)} %all_to_all.30.src, bf16[16,128,256]{2,1,0:T(8,128)(2,1)S(1)} %all-to-all-done.1.tgt, f32[16,16,128]{2,1,0:T(8,128)S(1)} %all_to_all.32.parts), custom_call_target="tpu_custom_call" | custom-call | tf_op jit(solution)/shard_map/pallas_call | solution.py:154
  107.2 12.7 %all_to_all.33.parts = f32[16,16,128]{2,1,0:T(8,128)S(1)} all-to-all(f32[16,16,128]{2,1,0:T(8,128)S(1)} %shard_map.62), channel_id=1, replica_groups=mesh['y'=4,'core'=2,'x'=4,'s'=4,'p'=2] {'x','s'}, dimensions={0} | all-to-all | bytes 262144 | tf_op jit(solution)/shard_map/all_to_all | solution.py:169
  119.8 4.1 %shard_map.63 = (f32[16,8,128]{2,1,0:T(8,128)}, f32[16,128]{1,0:T(8,128)S(1)}) custom-call(s32[272]{0:T(512)S(1)} %get-tuple-element.12.tiles, s32[1]{0:T(128)} %get-tuple-element.13.count, bf16[16,128,256]{2,1,0:T(8,128)(2,1)S(1)} %all_to_all.30.src, bf16[16,128,256]{2,1,0:T(8,128)(2,1)S(1)} %all-to-all-done.1.tgt, f32[16,16,128]{2,1,0:T(8,128)S(1)} %all_to_all.33.parts, ...), custom_call_target="tpu_custom_call" | custom-call | tf_op jit(solution)/shard_map/pallas_call | solution.py:154
  123.9 7.5 %all-to-all-start.5 = ((f32[16,8,128]{2,1,0:T(8,128)}), f32[16,8,128]{2,1,0:T(8,128)S(1)}, u32[]{:S(2)}, u32[]{:S(2)}) async-start(f32[16,8,128]{2,1,0:T(8,128)} %get-tuple-element.17), calls=%async_computation.5 | async-start | bytes 131072 | tf_op jit(solution)/shard_map/all_to_all | solution.py:169
  131.4 1.4 %collective-permute-start.1 = (f32[16,128]{1,0:T(8,128)S(1)}, f32[16,128]{1,0:T(8,128)S(1)}, u32[]{:S(2)}, u32[]{:S(2)}) collective-permute-start(f32[16,128]{1,0:T(8,128)S(1)} %get-tuple-element.19.mine), channel_id=1, source_target_pairs={{0,1},{1,0},{2,3},{3,2},{4,5},{5,4},{6,7},{7,6},{8,9},{9,8},{10,11... | collective-permute-start | bytes 24584 | tf_op jit(solution)/shard_map/ppermute | solution.py:180
  132.8 1.7 %collective-permute-done.1.other = f32[16,128]{1,0:T(8,128)S(1)} collective-permute-done((f32[16,128]{1,0:T(8,128)S(1)}, f32[16,128]{1,0:T(8,128)S(1)}, u32[]{:S(2)}, u32[]{:S(2)}) %collective-permute-start.1) | collective-permute-done | bytes 8224 | tf_op jit(solution)/shard_map/ppermute | solution.py:180
  134.5 2.8 %all-to-all-done.5.parts = f32[16,8,128]{2,1,0:T(8,128)S(1)} async-done(((f32[16,8,128]{2,1,0:T(8,128)}), f32[16,8,128]{2,1,0:T(8,128)S(1)}, u32[]{:S(2)}, u32[]{:S(2)}) %all-to-all-start.5) | async-done | bytes 65568 | tf_op jit(solution)/shard_map/all_to_all | solution.py:169
  137.2 0.6 shard_map.64
  (1 shorter events, 0.0 us)
Async XLA Ops:
  1.6 38.9 %copy-start = (bf16[128,256]{1,0:T(8,128)(2,1)S(1)}, bf16[128,256]{1,0:T(8,128)(2,1)}, u32[]{:S(2)}) copy-start(bf16[128,256]{1,0:T(8,128)(2,1)} %param.5) | copy-start | bytes 196612
  41.6 25.9 %all-to-all-start.1 = ((bf16[16,128,256]{2,1,0:T(8,128)(2,1)}), bf16[16,128,256]{2,1,0:T(8,128)(2,1)S(1)}, u32[]{:S(2)}, u32[]{:S(2)}) async-start(bf16[16,128,256]{2,1,0:T(8,128)(2,1)} %broadcast_in_dim.5), calls=%async_computation.1 | async-start | bytes 2097152 | tf_op jit(solution)/shard_map/all_to_all | solution.py:169
  50.7 0.7 copy-start.1
  51.3 12.2 %collective-permute-start = (s32[3,128]{1,0:T(4,128)S(1)}, s32[3,128]{1,0:T(4,128)S(1)}, u32[]{:S(2)}, u32[]{:S(2)}) collective-permute-start(s32[3,128]{1,0:T(4,128)S(1)} %concatenate.3.mine), channel_id=1, source_target_pairs={{0,1},{1,0},{2,3},{3,2},{4,5},{5,4},{6,7},{7,6},{8,9},{9,8},{10,11... | collective-permute-start | bytes 4616 | tf_op jit(solution)/shard_map/ppermute | solution.py:180
  123.9 13.3 %all-to-all-start.5 = ((f32[16,8,128]{2,1,0:T(8,128)}), f32[16,8,128]{2,1,0:T(8,128)S(1)}, u32[]{:S(2)}, u32[]{:S(2)}) async-start(f32[16,8,128]{2,1,0:T(8,128)} %get-tuple-element.17), calls=%async_computation.5 | async-start | bytes 131072 | tf_op jit(solution)/shard_map/all_to_all | solution.py:169
  131.4 3.1 %collective-permute-start.1 = (f32[16,128]{1,0:T(8,128)S(1)}, f32[16,128]{1,0:T(8,128)S(1)}, u32[]{:S(2)}, u32[]{:S(2)}) collective-permute-start(f32[16,128]{1,0:T(8,128)S(1)} %get-tuple-element.19.mine), channel_id=1, source_target_pairs={{0,1},{1,0},{2,3},{3,2},{4,5},{5,4},{6,7},{7,6},{8,9},{9,8},{10,11... | collective-permute-start | bytes 24584 | tf_op jit(solution)/shard_map/ppermute | solution.py:180
where the time goes:
time: 140 us; the launch traced here: 138 us
  blocking collectives  79.8 us (57%)
  Pallas kernels  20.1 us (14%)
  starting transfers between devices  18.7 us (13%)
  waiting for transfers between devices  15.3 us (11%)
  local copies, waits for them, and re-layouts  2.69 us (2%)
    all_to_all x4, blocking collectives, exchange(): return lax.all_to_all(copies, peers, 0, 0, tiled=True)  79.8 us
    all_to_all x2, starting transfers between devices, exchange(): return lax.all_to_all(copies, peers, 0, 0, tiled=True)  15.9 us
    pallas_call x4, Pallas kernels, half_step(): pl.pallas_call(kernel, out_shape=[jax.ShapeDtypeStruct(s, F32) for s in o...  15.5 us
    ppermute x2, waiting for transfers between devices, local(): partner = lambda v: lax.ppermute(v, 'p', [(0, 1), (1, 0)])  12.5 us
    pallas_call x1, Pallas kernels, local(): pl.pallas_call(pick_kernel, out_shape=[jax.ShapeDtypeStruct((2 * TILE + U...  3.9 us
  transfers between devices with their start and end apart: 4, of which 3 were waited for; matrix products, arithmetic and copies ran while one was open for 0% of the time, Pallas kernels for 3%

commit v1 on v0

--- a/solution.py
+++ b/solution.py
@@ -109,7 +109,15 @@
     return tile
 
 
-def first_kernel(tiles, count, src, tgt, out, sq_src, sq_tgt, wide, peaks, totals):
+def first_kernel(tiles, count, place, tgt, *rest):
+    sides = len(rest) - 7
+    pieces, (out, src, sq_src, sq_tgt, wide, peaks, totals) = rest[:sides], rest[sides:]
+    deep = pieces[0].shape[0]
+    for dx, piece in enumerate(pieces):
+        x = lax.rem(place[0] + (sides - dx), sides)
+        for ds in range(deep):
+            s = lax.rem(place[1] + (deep - ds), deep)
+            src[x * deep + s] = piece[ds]
     for b in range(tgt.shape[0]):
         sq_tgt[b : b + 1, :] = square_rows(tgt[b])
     for a in range(src.shape[0]):
@@ -150,11 +158,11 @@
     src_pot[:, 1, :] = jnp.where(p == 0, other[...], mine[...])
 
 
-def half_step(kernel, outs, near_blocks, slots, tiles, count, *args):
+def half_step(kernel, outs, near_blocks, slots, scalars, *args):
     return pl.pallas_call(
         kernel,
-        out_shape=[jax.ShapeDtypeStruct(s, F32) for s in outs],
-        in_specs=[SMEM] * 2 + [VMEM] * len(args),
+        out_shape=[s if isinstance(s, jax.ShapeDtypeStruct) else jax.ShapeDtypeStruct(s, F32) for s in outs],
+        in_specs=[SMEM] * len(scalars) + [VMEM] * len(args),
         out_specs=[VMEM] * len(outs),
         scratch_shapes=[
             pltpu.VMEM((near_blocks, TILE, TILE), F32),
@@ -162,7 +170,7 @@
             pltpu.VMEM((slots + 1, 8, TILE), F32),
         ],
         compiler_params=PARAMS,
-    )(tiles, count, *args)
+    )(*scalars, *args)
 
 
 def exchange(copies, peers):
@@ -171,6 +179,12 @@
 
 def gather(block, peers):
     return exchange(jnp.broadcast_to(block[None], (lax.axis_size(peers),) + block.shape), peers)
+
+
+def shifts(block, axis):
+    n = lax.axis_size(axis)
+    turn = lambda d: lax.ppermute(block, axis, [(i, (i + d) % n) for i in range(n)])
+    return [block] + [turn(d) for d in range(1, n)]
 
 
 def local(src_embed, tgt_embed, tiles, counts):
@@ -182,7 +196,7 @@
     lists = jnp.concatenate([tiles[0, 0], jnp.broadcast_to(counts[0, 0], (1, TILE))], axis=0)
     other_lists = partner(lists)
     tgt = gather(tgt_embed, TGT_PEERS)
-    src = gather(src_embed, SRC_PEERS)
+    src_pieces = shifts(jnp.concatenate([v[None] for v in shifts(src_embed, "s")]), "x")
     picked, count = pl.pallas_call(
         pick_kernel,
         out_shape=[jax.ShapeDtypeStruct((2 * TILE + UNROLL,), jnp.int32), jax.ShapeDtypeStruct((1,), jnp.int32)],
@@ -191,17 +205,26 @@
         compiler_params=PARAMS,
     )(lists, other_lists, parity)
 
-    srcs, tgts = src.shape[0], tgt.shape[0]
+    srcs, tgts = len(src_pieces) * src_pieces[0].shape[0], tgt.shape[0]
+    src_shape = jax.ShapeDtypeStruct((srcs,) + src_embed.shape, src_embed.dtype)
+    scalars = (picked, count)
+    place = jnp.stack([lax.axis_index("x"), lax.axis_index("s")]).astype(jnp.int32)
     slots = srcs * tgts
     src_out, tgt_out = (srcs, srcs, TILE), (tgts, tgts, TILE)
     for sweep in range(ITERS):
         if sweep == 0:
-            parts, sq_src, sq_tgt = half_step(
-                first_kernel, [src_out, (srcs, TILE), (tgts, TILE)], tgts, slots, picked, count, src, tgt
+            parts, src, sq_src, sq_tgt = half_step(
+                first_kernel,
+                [src_out, src_shape, (srcs, TILE), (tgts, TILE)],
+                tgts,
+                slots,
+                scalars + (place,),
+                tgt,
+                *src_pieces,
             )
         else:
             (parts,) = half_step(
-                functools.partial(source_kernel, log_cells), [src_out], tgts, slots, picked, count, src, tgt, parts
+                functools.partial(source_kernel, log_cells), [src_out], tgts, slots, scalars, src, tgt, parts
             )
         parts = exchange(parts, SRC_PEERS)
         last = sweep == ITERS - 1
@@ -210,8 +233,7 @@
             [(tgts, rows, TILE) if last else tgt_out, (srcs, TILE)],
             srcs,
             slots,
-            picked,
-            count,
+            scalars,
             src,
             tgt,
             parts,

time: 140 us -> 121 us (0.86); the launches traced: 138 us -> 121 us
  blocking collectives: 79.8 us -> 39.1 us
  waiting for transfers between devices: 15.3 us -> 25.8 us
  starting transfers between devices: 18.7 us -> 28.3 us
  Pallas kernels: 20.1 us -> 24.1 us
    all_to_all x4 -> x3, blocking collectives: 79.8 us -> 39.1 us  [exchange(): return lax.all_to_all(copies, peers, 0, 0, tiled=True)]
    ppermute x0 -> x6, waiting for transfers between devices: none -> 19.5 us  [shifts(): lax.ppermute(block, axis, [(i, (i + d) % n) for i in range(n)])]
    ppermute x0 -> x6, starting transfers between devices: none -> 13.4 us  [shifts(): lax.ppermute(block, axis, [(i, (i + d) % n) for i in range(n)])]
    ppermute x2, waiting for transfers between devices: 12.5 us -> 3.46 us  [local(): partner = lambda v: lax.ppermute(v, 'p', [(0, 1), (1, 0)])]
    pallas_call x4, Pallas kernels: 15.5 us -> 19.6 us  [half_step(): pl.pallas_call(kernel, out_shape=[s if isinstance(s, jax.ShapeDtypeStruct...]
    all_to_all x2, starting transfers between devices: 15.9 us -> 12.7 us  [exchange(): return lax.all_to_all(copies, peers, 0, 0, tiled=True)]
  transfers between devices with their start and end apart: 4 -> 10, of which waited for: 3 -> 6; matrix products, arithmetic and copies ran while one was open for 0% -> 0% of each run, Pallas kernels for 3% -> 3%
where the time goes in v1:
time: 121 us
  blocking collectives  39.1 us (32%)
  starting transfers between devices  28.3 us (23%)
  waiting for transfers between devices  25.8 us (21%)
  Pallas kernels  24.1 us (20%)
  local copies, waits for them, and re-layouts  2.6 us (2%)
  between operations  1.35 us (1%)
    all_to_all x3, blocking collectives, exchange(): return lax.all_to_all(copies, peers, 0, 0, tiled=True)  39.1 us
    pallas_call x4, Pallas kernels, half_step(): pl.pallas_call(kernel, out_shape=[s if isinstance(s, jax.ShapeDtypeStruct...  19.6 us
    ppermute x6, waiting for transfers between devices, shifts(): lax.ppermute(block, axis, [(i, (i + d) % n) for i in range(n)])  19.5 us
    ppermute x6, starting transfers between devices, shifts(): lax.ppermute(block, axis, [(i, (i + d) % n) for i in range(n)])  13.4 us
    all_to_all x2, starting transfers between devices, exchange(): return lax.all_to_all(copies, peers, 0, 0, tiled=True)  12.7 us
    pallas_call x1, Pallas kernels, local(): pl.pallas_call(pick_kernel, out_shape=[jax.ShapeDtypeStruct((2 * TILE + U...  3.9 us
    ppermute x2, waiting for transfers between devices, local(): partner = lambda v: lax.ppermute(v, 'p', [(0, 1), (1, 0)])  3.46 us
    all_to_all x2, waiting for transfers between devices, exchange(): return lax.all_to_all(copies, peers, 0, 0, tiled=True)  2.77 us
  transfers between devices with their start and end apart: 10, of which 6 were waited for; matrix products, arithmetic and copies ran while one was open for 0% of the time, Pallas kernels for 3%

profile of v1, /device:TPU:1, one launch (start us, length us, event | category | flops | bytes accessed | tf_op | source)
XLA Modules:
  0.0 121.4 jit_solution(18270404155130744427)
XLA Ops:
  0.6 1.9 %broadcast_in_dim.19 = bf16[16,128,256]{2,1,0:T(8,128)(2,1)} broadcast(bf16[128,256]{1,0:T(8,128)(2,1)} %param.5), dimensions={1,2} | broadcast | bytes 1114112 | tf_op jit(solution)/shard_map/broadcast_in_dim | solution.py:181
  2.6 0.0 copy-start
  2.6 7.5 %all-to-all-start = ((bf16[16,128,256]{2,1,0:T(8,128)(2,1)}), bf16[16,128,256]{2,1,0:T(8,128)(2,1)S(1)}, u32[]{:S(2)}, u32[]{:S(2)}) async-start(bf16[16,128,256]{2,1,0:T(8,128)(2,1)} %broadcast_in_dim.19), calls=%async_computation | async-start | bytes 2097152 | tf_op jit(solution)/shard_map/all_to_all | solution.py:177
  10.0 0.0 copy-done
  10.0 3.1 %collective-permute-start.1 = (bf16[128,256]{1,0:T(8,128)(2,1)S(1)}, bf16[128,256]{1,0:T(8,128)(2,1)S(1)}, u32[]{:S(2)}, u32[]{:S(2)}) collective-permute-start(bf16[128,256]{1,0:T(8,128)(2,1)S(1)} %copy-done), channel_id=1, source_target_pairs={{0,2},{2,4},{4,6},{6,0},{1,3},{3,5},{5,7},{7,1},{8,10},{10,12},{12... | collective-permute-start | bytes 196616 | tf_op jit(solution)/shard_map/ppermute | solution.py:186
  13.1 2.2 %collective-permute-start.3 = (bf16[128,256]{1,0:T(8,128)(2,1)S(1)}, bf16[128,256]{1,0:T(8,128)(2,1)S(1)}, u32[]{:S(2)}, u32[]{:S(2)}) collective-permute-start(bf16[128,256]{1,0:T(8,128)(2,1)S(1)} %copy-done), channel_id=1, source_target_pairs={{0,6},{2,0},{4,2},{6,4},{1,7},{3,1},{5,3},{7,5},{8,14},{10,8},{12,... | collective-permute-start | bytes 196616 | tf_op jit(solution)/shard_map/ppermute | solution.py:186
  15.3 4.4 %collective-permute-start.2 = (bf16[128,256]{1,0:T(8,128)(2,1)S(1)}, bf16[128,256]{1,0:T(8,128)(2,1)S(1)}, u32[]{:S(2)}, u32[]{:S(2)}) collective-permute-start(bf16[128,256]{1,0:T(8,128)(2,1)S(1)} %copy-done), channel_id=1, source_target_pairs={{0,4},{2,6},{4,0},{6,2},{1,5},{3,7},{5,1},{7,3},{8,12},{10,14},{12... | collective-permute-start | bytes 196616 | tf_op jit(solution)/shard_map/ppermute | solution.py:186
  19.7 11.0 %collective-permute-done.1 = bf16[128,256]{1,0:T(8,128)(2,1)S(1)} collective-permute-done((bf16[128,256]{1,0:T(8,128)(2,1)S(1)}, bf16[128,256]{1,0:T(8,128)(2,1)S(1)}, u32[]{:S(2)}, u32[]{:S(2)}) %collective-permute-start.1) | collective-permute-done | bytes 65568 | tf_op jit(solution)/shard_map/ppermute | solution.py:186
  30.7 0.0 collective-permute-done.3
  30.7 2.3 %collective-permute-done.2 = bf16[128,256]{1,0:T(8,128)(2,1)S(1)} collective-permute-done((bf16[128,256]{1,0:T(8,128)(2,1)S(1)}, bf16[128,256]{1,0:T(8,128)(2,1)S(1)}, u32[]{:S(2)}, u32[]{:S(2)}) %collective-permute-start.2) | collective-permute-done | bytes 65568 | tf_op jit(solution)/shard_map/ppermute | solution.py:186
  33.1 2.6 %collective-permute-start.6 = (bf16[4,128,256]{2,1,0:T(8,128)(2,1)S(1)}, bf16[4,128,256]{2,1,0:T(8,128)(2,1)S(1)}, u32[]{:S(2)}, u32[]{:S(2)}) collective-permute-start(bf16[4,128,256]{2,1,0:T(8,128)(2,1)S(1)} %pad_maximum_fusion.rest_0_), channel_id=1, source_target_pairs={{0,24},{8,0},{16,8},{24,16},{1,25},{9,1},{17,9},{25,17},{2,26},{10... | collective-permute-start | bytes 786440 | tf_op jit(solution)/shard_map/ppermute | solution.py:186
  35.6 0.5 collective-permute-start.5
  36.1 0.6 collective-permute-start.4
  37.4 0.0 copy-start.1
  37.4 0.7 copy-done.1
  38.1 0.9 collective-permute-start
  39.0 0.1 pad_add_fusion.place
  39.0 1.8 %collective-permute-done.other = s32[3,128]{1,0:T(4,128)S(1)} collective-permute-done((s32[3,128]{1,0:T(4,128)S(1)}, s32[3,128]{1,0:T(4,128)S(1)}, u32[]{:S(2)}, u32[]{:S(2)}) %collective-permute-start) | collective-permute-done | bytes 1568 | tf_op jit(solution)/shard_map/ppermute | solution.py:194
  40.8 3.9 %shard_map.59 = (s32[272]{0:T(512)S(1)}, s32[1]{0:T(128)}) custom-call(s32[3,128]{1,0:T(4,128)S(1)} %concatenate.6.mine, s32[3,128]{1,0:T(4,128)S(1)} %collective-permute-done.other, s32[1]{0:T(128)} %bitcast.parity), custom_call_target="tpu_custom_call" | custom-call | tf_op jit(solution)/shard_map/pallas_call | solution.py:200
  44.7 0.0 collective-permute-done.6.rest_3_
  44.7 0.0 collective-permute-done.5.rest_2_
  44.7 6.2 %collective-permute-done.4.rest_1_ = bf16[4,128,256]{2,1,0:T(8,128)(2,1)S(1)} collective-permute-done((bf16[4,128,256]{2,1,0:T(8,128)(2,1)S(1)}, bf16[4,128,256]{2,1,0:T(8,128)(2,1)S(1)}, u32[]{:S(2)}, u32[]{:S(2)}) %collective-permute-start.4) | collective-permute-done | bytes 262176 | tf_op jit(solution)/shard_map/ppermute | solution.py:186
  51.0 0.0 all-to-all-done.tgt
  51.0 5.2 %shard_map.60 = (f32[16,16,128]{2,1,0:T(8,128)S(1)}, bf16[16,128,256]{2,1,0:T(8,128)(2,1)S(1)}, f32[16,128]{1,0:T(8,128)S(1)}, f32[16,128]{1,0:T(8,128)S(1)}) custom-call(s32[272]{0:T(512)S(1)} %get-tuple-element.13.tiles, s32[1]{0:T(128)} %get-tuple-element.14.count, s32[2]{0:T(128)S(1)} %pad_add_fusion.place, bf16[16,128,256]{2,1,0:T(8,128)(2,1)S(1)} %all-to-all-done.tgt, ...), custom_call_target="tpu_custom_call" | custom-call | tf_op jit(solution)/shard_map/pallas_call | solution.py:162
  56.2 13.7 %all_to_all.25.parts = f32[16,16,128]{2,1,0:T(8,128)S(1)} all-to-all(f32[16,16,128]{2,1,0:T(8,128)S(1)} %get-tuple-element.16), channel_id=1, replica_groups=mesh['y'=4,'core'=2,'x'=4,'s'=4,'p'=2] {'x','s'}, dimensions={0} | all-to-all | bytes 262144 | tf_op jit(solution)/shard_map/all_to_all | solution.py:177
  69.9 4.8 %shard_map.61 = (f32[16,16,128]{2,1,0:T(8,128)S(1)}, f32[16,128]{1,0:T(8,128)}) custom-call(s32[272]{0:T(512)S(1)} %get-tuple-element.13.tiles, s32[1]{0:T(128)} %get-tuple-element.14.count, bf16[16,128,256]{2,1,0:T(8,128)(2,1)S(1)} %get-tuple-element.15.src, bf16[16,128,256]{2,1,0:T(8,128)(2,1)S(1)} %all-to-all-done.tgt, ...), custom_call_target="tpu_custom_call" | custom-call | tf_op jit(solution)/shard_map/pallas_call | solution.py:162
  74.7 12.3 %all_to_all.26.parts = f32[16,16,128]{2,1,0:T(8,128)S(1)} all-to-all(f32[16,16,128]{2,1,0:T(8,128)S(1)} %get-tuple-element.18), channel_id=1, replica_groups=mesh['y'=4,'core'=2,'x'=4,'s'=4,'p'=2] {'p','y','core'}, dimensions={0} | all-to-all | bytes 262144 | tf_op jit(solution)/shard_map/all_to_all | solution.py:177
  87.0 4.5 %shard_map.62 = f32[16,16,128]{2,1,0:T(8,128)S(1)} custom-call(s32[272]{0:T(512)S(1)} %get-tuple-element.13.tiles, s32[1]{0:T(128)} %get-tuple-element.14.count, bf16[16,128,256]{2,1,0:T(8,128)(2,1)S(1)} %get-tuple-element.15.src, bf16[16,128,256]{2,1,0:T(8,128)(2,1)S(1)} %all-to-all-done.tgt, f32[16,16,128]{2,1,0:T(8,128)S(1)} %all_to_all.26.parts), custom_call_target="tpu_custom_call" | custom-call | tf_op jit(solution)/shard_map/pallas_call | solution.py:162
  91.5 13.1 %all_to_all.27.parts = f32[16,16,128]{2,1,0:T(8,128)S(1)} all-to-all(f32[16,16,128]{2,1,0:T(8,128)S(1)} %shard_map.62), channel_id=1, replica_groups=mesh['y'=4,'core'=2,'x'=4,'s'=4,'p'=2] {'x','s'}, dimensions={0} | all-to-all | bytes 262144 | tf_op jit(solution)/shard_map/all_to_all | solution.py:177
  104.6 5.1 %shard_map.63 = (f32[16,8,128]{2,1,0:T(8,128)}, f32[16,128]{1,0:T(8,128)S(1)}) custom-call(s32[272]{0:T(512)S(1)} %get-tuple-element.13.tiles, s32[1]{0:T(128)} %get-tuple-element.14.count, bf16[16,128,256]{2,1,0:T(8,128)(2,1)S(1)} %get-tuple-element.15.src, bf16[16,128,256]{2,1,0:T(8,128)(2,1)S(1)} %all-to-all-done.tgt, ...), custom_call_target="tpu_custom_call" | custom-call | tf_op jit(solution)/shard_map/pallas_call | solution.py:162
  109.7 5.2 %all-to-all-start.4 = ((f32[16,8,128]{2,1,0:T(8,128)}), f32[16,8,128]{2,1,0:T(8,128)S(1)}, u32[]{:S(2)}, u32[]{:S(2)}) async-start(f32[16,8,128]{2,1,0:T(8,128)} %get-tuple-element.19), calls=%async_computation.4 | async-start | bytes 131072 | tf_op jit(solution)/shard_map/all_to_all | solution.py:177
  114.9 1.4 %collective-permute-start.7 = (f32[16,128]{1,0:T(8,128)S(1)}, f32[16,128]{1,0:T(8,128)S(1)}, u32[]{:S(2)}, u32[]{:S(2)}) collective-permute-start(f32[16,128]{1,0:T(8,128)S(1)} %get-tuple-element.21.mine), channel_id=1, source_target_pairs={{0,1},{1,0},{2,3},{3,2},{4,5},{5,4},{6,7},{7,6},{8,9},{9,8},{10,11... | collective-permute-start | bytes 24584 | tf_op jit(solution)/shard_map/ppermute | solution.py:194
  116.3 1.7 %collective-permute-done.7.other = f32[16,128]{1,0:T(8,128)S(1)} collective-permute-done((f32[16,128]{1,0:T(8,128)S(1)}, f32[16,128]{1,0:T(8,128)S(1)}, u32[]{:S(2)}, u32[]{:S(2)}) %collective-permute-start.7) | collective-permute-done | bytes 8224 | tf_op jit(solution)/shard_map/ppermute | solution.py:194
  118.0 2.8 %all-to-all-done.4.parts = f32[16,8,128]{2,1,0:T(8,128)S(1)} async-done(((f32[16,8,128]{2,1,0:T(8,128)}), f32[16,8,128]{2,1,0:T(8,128)S(1)}, u32[]{:S(2)}, u32[]{:S(2)}) %all-to-all-start.4) | async-done | bytes 65568 | tf_op jit(solution)/shard_map/all_to_all | solution.py:177
  120.7 0.6 shard_map.64
  (2 shorter events, 0.0 us)
Async XLA Ops:
  2.6 7.5 %copy-start = (bf16[128,256]{1,0:T(8,128)(2,1)S(1)}, bf16[128,256]{1,0:T(8,128)(2,1)}, u32[]{:S(2)}) copy-start(bf16[128,256]{1,0:T(8,128)(2,1)} %param.4) | copy-start | bytes 196612
  2.6 48.4 %all-to-all-start = ((bf16[16,128,256]{2,1,0:T(8,128)(2,1)}), bf16[16,128,256]{2,1,0:T(8,128)(2,1)S(1)}, u32[]{:S(2)}, u32[]{:S(2)}) async-start(bf16[16,128,256]{2,1,0:T(8,128)(2,1)} %broadcast_in_dim.19), calls=%async_computation | async-start | bytes 2097152 | tf_op jit(solution)/shard_map/all_to_all | solution.py:177
  10.0 20.7 %collective-permute-start.1 = (bf16[128,256]{1,0:T(8,128)(2,1)S(1)}, bf16[128,256]{1,0:T(8,128)(2,1)S(1)}, u32[]{:S(2)}, u32[]{:S(2)}) collective-permute-start(bf16[128,256]{1,0:T(8,128)(2,1)S(1)} %copy-done), channel_id=1, source_target_pairs={{0,2},{2,4},{4,6},{6,0},{1,3},{3,5},{5,7},{7,1},{8,10},{10,12},{12... | collective-permute-start | bytes 196616 | tf_op jit(solution)/shard_map/ppermute | solution.py:186
  13.1 17.6 %collective-permute-start.3 = (bf16[128,256]{1,0:T(8,128)(2,1)S(1)}, bf16[128,256]{1,0:T(8,128)(2,1)S(1)}, u32[]{:S(2)}, u32[]{:S(2)}) collective-permute-start(bf16[128,256]{1,0:T(8,128)(2,1)S(1)} %copy-done), channel_id=1, source_target_pairs={{0,6},{2,0},{4,2},{6,4},{1,7},{3,1},{5,3},{7,5},{8,14},{10,8},{12,... | collective-permute-start | bytes 196616 | tf_op jit(solution)/shard_map/ppermute | solution.py:186
  15.3 17.7 %collective-permute-start.2 = (bf16[128,256]{1,0:T(8,128)(2,1)S(1)}, bf16[128,256]{1,0:T(8,128)(2,1)S(1)}, u32[]{:S(2)}, u32[]{:S(2)}) collective-permute-start(bf16[128,256]{1,0:T(8,128)(2,1)S(1)} %copy-done), channel_id=1, source_target_pairs={{0,4},{2,6},{4,0},{6,2},{1,5},{3,7},{5,1},{7,3},{8,12},{10,14},{12... | collective-permute-start | bytes 196616 | tf_op jit(solution)/shard_map/ppermute | solution.py:186
  33.1 11.7 %collective-permute-start.6 = (bf16[4,128,256]{2,1,0:T(8,128)(2,1)S(1)}, bf16[4,128,256]{2,1,0:T(8,128)(2,1)S(1)}, u32[]{:S(2)}, u32[]{:S(2)}) collective-permute-start(bf16[4,128,256]{2,1,0:T(8,128)(2,1)S(1)} %pad_maximum_fusion.rest_0_), channel_id=1, source_target_pairs={{0,24},{8,0},{16,8},{24,16},{1,25},{9,1},{17,9},{25,17},{2,26},{10... | collective-permute-start | bytes 786440 | tf_op jit(solution)/shard_map/ppermute | solution.py:186
  35.6 9.1 %collective-permute-start.5 = (bf16[4,128,256]{2,1,0:T(8,128)(2,1)S(1)}, bf16[4,128,256]{2,1,0:T(8,128)(2,1)S(1)}, u32[]{:S(2)}, u32[]{:S(2)}) collective-permute-start(bf16[4,128,256]{2,1,0:T(8,128)(2,1)S(1)} %pad_maximum_fusion.rest_0_), channel_id=1, source_target_pairs={{0,16},{8,24},{16,0},{24,8},{1,17},{9,25},{17,1},{25,9},{2,18},{10... | collective-permute-start | bytes 786440 | tf_op jit(solution)/shard_map/ppermute | solution.py:186
  36.1 14.8 %collective-permute-start.4 = (bf16[4,128,256]{2,1,0:T(8,128)(2,1)S(1)}, bf16[4,128,256]{2,1,0:T(8,128)(2,1)S(1)}, u32[]{:S(2)}, u32[]{:S(2)}) collective-permute-start(bf16[4,128,256]{2,1,0:T(8,128)(2,1)S(1)} %pad_maximum_fusion.rest_0_), channel_id=1, source_target_pairs={{0,8},{8,16},{16,24},{24,0},{1,9},{9,17},{17,25},{25,1},{2,10},{10... | collective-permute-start | bytes 786440 | tf_op jit(solution)/shard_map/ppermute | solution.py:186
  37.4 0.7 copy-start.1
  38.1 2.7 %collective-permute-start = (s32[3,128]{1,0:T(4,128)S(1)}, s32[3,128]{1,0:T(4,128)S(1)}, u32[]{:S(2)}, u32[]{:S(2)}) collective-permute-start(s32[3,128]{1,0:T(4,128)S(1)} %concatenate.6.mine), channel_id=1, source_target_pairs={{0,1},{1,0},{2,3},{3,2},{4,5},{5,4},{6,7},{7,6},{8,9},{9,8},{10,11... | collective-permute-start | bytes 4616 | tf_op jit(solution)/shard_map/ppermute | solution.py:194
  109.7 11.0 %all-to-all-start.4 = ((f32[16,8,128]{2,1,0:T(8,128)}), f32[16,8,128]{2,1,0:T(8,128)S(1)}, u32[]{:S(2)}, u32[]{:S(2)}) async-start(f32[16,8,128]{2,1,0:T(8,128)} %get-tuple-element.19), calls=%async_computation.4 | async-start | bytes 131072 | tf_op jit(solution)/shard_map/all_to_all | solution.py:177
  114.9 3.1 %collective-permute-start.7 = (f32[16,128]{1,0:T(8,128)S(1)}, f32[16,128]{1,0:T(8,128)S(1)}, u32[]{:S(2)}, u32[]{:S(2)}) collective-permute-start(f32[16,128]{1,0:T(8,128)S(1)} %get-tuple-element.21.mine), channel_id=1, source_target_pairs={{0,1},{1,0},{2,3},{3,2},{4,5},{5,4},{6,7},{7,6},{8,9},{9,8},{10,11... | collective-permute-start | bytes 24584 | tf_op jit(solution)/shard_map/ppermute | solution.py:194

commit v2 on v1

--- a/solution.py
+++ b/solution.py
@@ -109,15 +109,23 @@
     return tile
 
 
-def first_kernel(tiles, count, place, tgt, *rest):
-    sides = len(rest) - 7
-    pieces, (out, src, sq_src, sq_tgt, wide, peaks, totals) = rest[:sides], rest[sides:]
+def pack_kernel(*refs):
+    for n, block in enumerate(refs[:-1]):
+        refs[-1][n] = block[...]
+
+
+def first_kernel(tiles, count, place, tgt_mine, tgt_other, *rest):
+    sides = len(rest) - 8
+    pieces, (out, src, tgt, sq_src, sq_tgt, wide, peaks, totals) = rest[:sides], rest[sides:]
     deep = pieces[0].shape[0]
     for dx, piece in enumerate(pieces):
         x = lax.rem(place[0] + (sides - dx), sides)
         for ds in range(deep):
             s = lax.rem(place[1] + (deep - ds), deep)
             src[x * deep + s] = piece[ds]
+    for n in range(tgt_mine.shape[0]):
+        tgt[2 * n + place[2]] = tgt_mine[n]
+        tgt[2 * n + 1 - place[2]] = tgt_other[n]
     for b in range(tgt.shape[0]):
         sq_tgt[b : b + 1, :] = square_rows(tgt[b])
     for a in range(src.shape[0]):
@@ -177,14 +185,26 @@
     return lax.all_to_all(copies, peers, 0, 0, tiled=True)
 
 
-def gather(block, peers):
-    return exchange(jnp.broadcast_to(block[None], (lax.axis_size(peers),) + block.shape), peers)
-
-
 def shifts(block, axis):
     n = lax.axis_size(axis)
     turn = lambda d: lax.ppermute(block, axis, [(i, (i + d) % n) for i in range(n)])
     return [block] + [turn(d) for d in range(1, n)]
+
+
+def bands(src_embed, tgt_embed):
+    receivers = lax.axis_size(("p", "y"))
+    tgt = exchange(jnp.broadcast_to(tgt_embed[None], (receivers,) + tgt_embed.shape), ("p", "y"))
+    blocks = shifts(src_embed, "s")
+    together = pl.pallas_call(
+        pack_kernel,
+        out_shape=jax.ShapeDtypeStruct((len(blocks),) + src_embed.shape, src_embed.dtype),
+        in_specs=[VMEM] * len(blocks),
+        out_specs=VMEM,
+        compiler_params=PARAMS,
+    )(*blocks)
+    src_pieces = shifts(together, "x")
+    tgt_pieces = shifts(tgt, "core")
+    return src_pieces, tgt_pieces
 
 
 def local(src_embed, tgt_embed, tiles, counts):
@@ -195,8 +215,7 @@
 
     lists = jnp.concatenate([tiles[0, 0], jnp.broadcast_to(counts[0, 0], (1, TILE))], axis=0)
     other_lists = partner(lists)
-    tgt = gather(tgt_embed, TGT_PEERS)
-    src_pieces = shifts(jnp.concatenate([v[None] for v in shifts(src_embed, "s")]), "x")
+    src_pieces, tgt_pieces = bands(src_embed, tgt_embed)
     picked, count = pl.pallas_call(
         pick_kernel,
         out_shape=[jax.ShapeDtypeStruct((2 * TILE + UNROLL,), jnp.int32), jax.ShapeDtypeStruct((1,), jnp.int32)],
@@ -205,21 +224,22 @@
         compiler_params=PARAMS,
     )(lists, other_lists, parity)
 
-    srcs, tgts = len(src_pieces) * src_pieces[0].shape[0], tgt.shape[0]
+    srcs, tgts = (len(pieces) * pieces[0].shape[0] for pieces in (src_pieces, tgt_pieces))
     src_shape = jax.ShapeDtypeStruct((srcs,) + src_embed.shape, src_embed.dtype)
+    tgt_shape = jax.ShapeDtypeStruct((tgts,) + tgt_embed.shape, tgt_embed.dtype)
     scalars = (picked, count)
-    place = jnp.stack([lax.axis_index("x"), lax.axis_index("s")]).astype(jnp.int32)
+    place = jnp.stack([lax.axis_index(a) for a in ("x", "s", "core")]).astype(jnp.int32)
     slots = srcs * tgts
     src_out, tgt_out = (srcs, srcs, TILE), (tgts, tgts, TILE)
     for sweep in range(ITERS):
         if sweep == 0:
-            parts, src, sq_src, sq_tgt = half_step(
+            parts, src, tgt, sq_src, sq_tgt = half_step(
                 first_kernel,
-                [src_out, src_shape, (srcs, TILE), (tgts, TILE)],
+                [src_out, src_shape, tgt_shape, (srcs, TILE), (tgts, TILE)],
                 tgts,
                 slots,
                 scalars + (place,),
-                tgt,
+                *tgt_pieces,
                 *src_pieces,
             )
         else:

time: 121 us -> 122 us (level)
  blocking collectives: 39.1 us -> 57 us
  waiting for transfers between devices: 25.8 us -> 15.4 us
  Pallas kernels: 24.1 us -> 18.5 us
    all_to_all x3 -> x4, blocking collectives: 39.1 us -> 57 us  [exchange(): return lax.all_to_all(copies, peers, 0, 0, tiled=True)]
    ppermute x6 -> x7, waiting for transfers between devices: 19.5 us -> 9.79 us  [shifts(): lax.ppermute(block, axis, [(i, (i + d) % n) for i in range(n)])]
    pallas_call x4, Pallas kernels: 19.6 us -> 13.9 us  [half_step(): pl.pallas_call(kernel, out_shape=[s if isinstance(s, jax.ShapeDtypeStruct...]
    all_to_all x2 -> x1, starting transfers between devices: 12.7 us -> 9.74 us  [exchange(): return lax.all_to_all(copies, peers, 0, 0, tiled=True)]
    ppermute x6 -> x7, starting transfers between devices: 13.4 us -> 15.7 us  [shifts(): lax.ppermute(block, axis, [(i, (i + d) % n) for i in range(n)])]
    all_to_all x2 -> x1, waiting for transfers between devices: 2.77 us -> 2.79 us  [exchange(): return lax.all_to_all(copies, peers, 0, 0, tiled=True)]
where the time goes in v2:
time: 122 us
  blocking collectives  57 us (47%)
  starting transfers between devices  28.5 us (23%)
  Pallas kernels  18.5 us (15%)
  waiting for transfers between devices  15.4 us (13%)
  local copies, waits for them, and re-layouts  1.56 us (1%)
  between operations  1.35 us (1%)
    all_to_all x4, blocking collectives, exchange(): return lax.all_to_all(copies, peers, 0, 0, tiled=True)  57 us
    ppermute x7, starting transfers between devices, shifts(): lax.ppermute(block, axis, [(i, (i + d) % n) for i in range(n)])  15.7 us
    pallas_call x4, Pallas kernels, half_step(): pl.pallas_call(kernel, out_shape=[s if isinstance(s, jax.ShapeDtypeStruct...  13.9 us
    ppermute x7, waiting for transfers between devices, shifts(): lax.ppermute(block, axis, [(i, (i + d) % n) for i in range(n)])  9.79 us
    all_to_all x1, starting transfers between devices, exchange(): return lax.all_to_all(copies, peers, 0, 0, tiled=True)  9.74 us
    pallas_call x1, Pallas kernels, local(): pl.pallas_call(pick_kernel, out_shape=[jax.ShapeDtypeStruct((2 * TILE + U...  3.9 us
    ppermute x2, starting transfers between devices, local(): partner = lambda v: lax.ppermute(v, 'p', [(0, 1), (1, 0)])  3.05 us
    ppermute x2, waiting for transfers between devices, local(): partner = lambda v: lax.ppermute(v, 'p', [(0, 1), (1, 0)])  2.86 us
  transfers between devices with their start and end apart: 10, of which 6 were waited for; matrix products, arithmetic and copies ran while one was open for 0% of the time, Pallas kernels for 3%

profile of v2, /device:TPU:1, one launch (start us, length us, event | category | flops | bytes accessed | tf_op | source)
XLA Modules:
  0.0 122.4 jit_solution(17823769201636563660)
XLA Ops:
  0.6 0.9 broadcast_in_dim.2
  1.5 0.0 copy-start
  1.5 14.9 %all_to_all.25.tgt_mine = bf16[8,128,256]{2,1,0:T(8,128)(2,1)S(1)} all-to-all(bf16[8,128,256]{2,1,0:T(8,128)(2,1)S(1)} %broadcast_in_dim.2), channel_id=1, replica_groups=mesh['y'=4,'core'=2,'x'=4,'s'=4,'p'=2] {'p','y'}, dimensions={0} | all-to-all | bytes 1048576 | tf_op jit(solution)/shard_map/all_to_all | solution.py:185
  16.4 2.4 %collective-permute-start.1 = (bf16[8,128,256]{2,1,0:T(8,128)(2,1)S(1)}, bf16[8,128,256]{2,1,0:T(8,128)(2,1)S(1)}, u32[]{:S(2)}, u32[]{:S(2)}) collective-permute-start(bf16[8,128,256]{2,1,0:T(8,128)(2,1)S(1)} %all_to_all.25.tgt_mine), channel_id=1, source_target_pairs={{0,32},{32,0},{1,33},{33,1},{2,34},{34,2},{3,35},{35,3},{4,36},{36... | collective-permute-start | bytes 1572872 | tf_op jit(solution)/shard_map/ppermute | solution.py:190
  18.8 0.0 copy-done
  18.9 6.0 %collective-permute-start.3 = (bf16[128,256]{1,0:T(8,128)(2,1)S(1)}, bf16[128,256]{1,0:T(8,128)(2,1)S(1)}, u32[]{:S(2)}, u32[]{:S(2)}) collective-permute-start(bf16[128,256]{1,0:T(8,128)(2,1)S(1)} %copy-done), channel_id=1, source_target_pairs={{0,4},{2,6},{4,0},{6,2},{1,5},{3,7},{5,1},{7,3},{8,12},{10,14},{12... | collective-permute-start | bytes 196616 | tf_op jit(solution)/shard_map/ppermute | solution.py:190
  24.9 1.2 collective-permute-start.2
  26.1 2.4 %collective-permute-start.4 = (bf16[128,256]{1,0:T(8,128)(2,1)S(1)}, bf16[128,256]{1,0:T(8,128)(2,1)S(1)}, u32[]{:S(2)}, u32[]{:S(2)}) collective-permute-start(bf16[128,256]{1,0:T(8,128)(2,1)S(1)} %copy-done), channel_id=1, source_target_pairs={{0,6},{2,0},{4,2},{6,4},{1,7},{3,1},{5,3},{7,5},{8,14},{10,8},{12,... | collective-permute-start | bytes 196616 | tf_op jit(solution)/shard_map/ppermute | solution.py:190
  28.4 0.0 collective-permute-done.3.refs_2_
  28.4 3.1 %collective-permute-done.2.refs_1_ = bf16[128,256]{1,0:T(8,128)(2,1)S(1)} collective-permute-done((bf16[128,256]{1,0:T(8,128)(2,1)S(1)}, bf16[128,256]{1,0:T(8,128)(2,1)S(1)}, u32[]{:S(2)}, u32[]{:S(2)}) %collective-permute-start.2) | collective-permute-done | bytes 65568 | tf_op jit(solution)/shard_map/ppermute | solution.py:190
  31.6 0.6 collective-permute-done.4.refs_3_
  32.2 2.6 %collective-permute-start.7 = (bf16[4,128,256]{2,1,0:T(8,128)(2,1)S(1)}, bf16[4,128,256]{2,1,0:T(8,128)(2,1)S(1)}, u32[]{:S(2)}, u32[]{:S(2)}) collective-permute-start(bf16[4,128,256]{2,1,0:T(8,128)(2,1)S(1)} %shard_map.60.rest_0_), channel_id=1, source_target_pairs={{0,24},{8,0},{16,8},{24,16},{1,25},{9,1},{17,9},{25,17},{2,26},{10... | collective-permute-start | bytes 786440 | tf_op jit(solution)/shard_map/ppermute | solution.py:190
  34.7 0.5 collective-permute-start.6
  35.2 0.6 collective-permute-start.5
  36.5 0.0 copy-start.1
  36.5 0.7 copy-done.1
  37.2 1.6 %collective-permute-start = (s32[3,128]{1,0:T(4,128)S(1)}, s32[3,128]{1,0:T(4,128)S(1)}, u32[]{:S(2)}, u32[]{:S(2)}) collective-permute-start(s32[3,128]{1,0:T(4,128)S(1)} %concatenate.3.mine), channel_id=1, source_target_pairs={{0,1},{1,0},{2,3},{3,2},{4,5},{5,4},{6,7},{7,6},{8,9},{9,8},{10,11... | collective-permute-start | bytes 4616 | tf_op jit(solution)/shard_map/ppermute | solution.py:214
  38.8 0.1 pad_add_fusion.place
  38.9 1.2 collective-permute-done.other
  40.1 3.9 %shard_map.59 = (s32[272]{0:T(512)S(1)}, s32[1]{0:T(128)}) custom-call(s32[3,128]{1,0:T(4,128)S(1)} %concatenate.3.mine, s32[3,128]{1,0:T(4,128)S(1)} %collective-permute-done.other, s32[1]{0:T(128)} %bitcast.parity), custom_call_target="tpu_custom_call" | custom-call | tf_op jit(solution)/shard_map/pallas_call | solution.py:219
  44.0 0.0 collective-permute-done.7.rest_3_
  44.0 0.0 collective-permute-done.6.rest_2_
  44.0 6.1 %collective-permute-done.5.rest_1_ = bf16[4,128,256]{2,1,0:T(8,128)(2,1)S(1)} collective-permute-done((bf16[4,128,256]{2,1,0:T(8,128)(2,1)S(1)}, bf16[4,128,256]{2,1,0:T(8,128)(2,1)S(1)}, u32[]{:S(2)}, u32[]{:S(2)}) %collective-permute-start.5) | collective-permute-done | bytes 262176 | tf_op jit(solution)/shard_map/ppermute | solution.py:190
  50.1 0.0 collective-permute-done.1.tgt_other
  50.1 3.8 %shard_map.61 = (f32[16,16,128]{2,1,0:T(8,128)S(1)}, bf16[16,128,256]{2,1,0:T(8,128)(2,1)S(1)}, bf16[16,128,256]{2,1,0:T(8,128)(2,1)S(1)}, f32[16,128]{1,0:T(8,128)S(1)}, f32[16,128]{1,0:T(8,128)S(1)}) custom-call(s32[272]{0:T(512)S(1)} %get-tuple-element.14.tiles, s32[1]{0:T(128)} %get-tuple-element.15.count, s32[3]{0:T(128)S(1)} %pad_add_fusion.place, ...), custom_call_target="tpu_custom_call" | custom-call | tf_op jit(solution)/shard_map/pallas_call | solution.py:170
  53.9 15.6 %all_to_all.26.parts = f32[16,16,128]{2,1,0:T(8,128)S(1)} all-to-all(f32[16,16,128]{2,1,0:T(8,128)S(1)} %get-tuple-element.18), channel_id=1, replica_groups=mesh['y'=4,'core'=2,'x'=4,'s'=4,'p'=2] {'x','s'}, dimensions={0} | all-to-all | bytes 262144 | tf_op jit(solution)/shard_map/all_to_all | solution.py:185
  69.5 3.4 %shard_map.62 = (f32[16,16,128]{2,1,0:T(8,128)S(1)}, f32[16,128]{1,0:T(8,128)}) custom-call(s32[272]{0:T(512)S(1)} %get-tuple-element.14.tiles, s32[1]{0:T(128)} %get-tuple-element.15.count, bf16[16,128,256]{2,1,0:T(8,128)(2,1)S(1)} %get-tuple-element.16.src, bf16[16,128,256]{2,1,0:T(8,128)(2,1)S(1)} %get-tuple-element.17.tgt, ...), custom_call_target="tpu_custom_call" | custom-call | tf_op jit(solution)/shard_map/pallas_call | solution.py:170
  72.9 14.0 %all_to_all.27.parts = f32[16,16,128]{2,1,0:T(8,128)S(1)} all-to-all(f32[16,16,128]{2,1,0:T(8,128)S(1)} %get-tuple-element.20), channel_id=1, replica_groups=mesh['y'=4,'core'=2,'x'=4,'s'=4,'p'=2] {'p','y','core'}, dimensions={0} | all-to-all | bytes 262144 | tf_op jit(solution)/shard_map/all_to_all | solution.py:185
  86.9 3.0 %shard_map.63 = f32[16,16,128]{2,1,0:T(8,128)S(1)} custom-call(s32[272]{0:T(512)S(1)} %get-tuple-element.14.tiles, s32[1]{0:T(128)} %get-tuple-element.15.count, bf16[16,128,256]{2,1,0:T(8,128)(2,1)S(1)} %get-tuple-element.16.src, bf16[16,128,256]{2,1,0:T(8,128)(2,1)S(1)} %get-tuple-element.17.tgt, f32[16,16,128]{2,1,0:T(8,128)S(1)} %all_to_all.27.parts), custom_call_target="tpu_custom_call" | custom-call | tf_op jit(solution)/shard_map/pallas_call | solution.py:170
  89.9 12.5 %all_to_all.28.parts = f32[16,16,128]{2,1,0:T(8,128)S(1)} all-to-all(f32[16,16,128]{2,1,0:T(8,128)S(1)} %shard_map.63), channel_id=1, replica_groups=mesh['y'=4,'core'=2,'x'=4,'s'=4,'p'=2] {'x','s'}, dimensions={0} | all-to-all | bytes 262144 | tf_op jit(solution)/shard_map/all_to_all | solution.py:185
  102.4 3.7 %shard_map.64 = (f32[16,8,128]{2,1,0:T(8,128)}, f32[16,128]{1,0:T(8,128)S(1)}) custom-call(s32[272]{0:T(512)S(1)} %get-tuple-element.14.tiles, s32[1]{0:T(128)} %get-tuple-element.15.count, bf16[16,128,256]{2,1,0:T(8,128)(2,1)S(1)} %get-tuple-element.16.src, bf16[16,128,256]{2,1,0:T(8,128)(2,1)S(1)} %get-tuple-element.17.tgt, ...), custom_call_target="tpu_custom_call" | custom-call | tf_op jit(solution)/shard_map/pallas_call | solution.py:170
  106.1 9.7 %all-to-all-start.4 = ((f32[16,8,128]{2,1,0:T(8,128)}), f32[16,8,128]{2,1,0:T(8,128)S(1)}, u32[]{:S(2)}, u32[]{:S(2)}) async-start(f32[16,8,128]{2,1,0:T(8,128)} %get-tuple-element.21), calls=%async_computation.4 | async-start | bytes 131072 | tf_op jit(solution)/shard_map/all_to_all | solution.py:185
  115.8 1.4 %collective-permute-start.8 = (f32[16,128]{1,0:T(8,128)S(1)}, f32[16,128]{1,0:T(8,128)S(1)}, u32[]{:S(2)}, u32[]{:S(2)}) collective-permute-start(f32[16,128]{1,0:T(8,128)S(1)} %get-tuple-element.23.mine), channel_id=1, source_target_pairs={{0,1},{1,0},{2,3},{3,2},{4,5},{5,4},{6,7},{7,6},{8,9},{9,8},{10,11... | collective-permute-start | bytes 24584 | tf_op jit(solution)/shard_map/ppermute | solution.py:214
  117.3 1.7 %collective-permute-done.8.other = f32[16,128]{1,0:T(8,128)S(1)} collective-permute-done((f32[16,128]{1,0:T(8,128)S(1)}, f32[16,128]{1,0:T(8,128)S(1)}, u32[]{:S(2)}, u32[]{:S(2)}) %collective-permute-start.8) | collective-permute-done | bytes 8224 | tf_op jit(solution)/shard_map/ppermute | solution.py:214
  118.9 2.8 %all-to-all-done.4.parts = f32[16,8,128]{2,1,0:T(8,128)S(1)} async-done(((f32[16,8,128]{2,1,0:T(8,128)}), f32[16,8,128]{2,1,0:T(8,128)S(1)}, u32[]{:S(2)}, u32[]{:S(2)}) %all-to-all-start.4) | async-done | bytes 65568 | tf_op jit(solution)/shard_map/all_to_all | solution.py:185
  121.7 0.6 shard_map.65
  (2 shorter events, 0.0 us)
Async XLA Ops:
  1.5 17.3 %copy-start = (bf16[128,256]{1,0:T(8,128)(2,1)S(1)}, bf16[128,256]{1,0:T(8,128)(2,1)}, u32[]{:S(2)}) copy-start(bf16[128,256]{1,0:T(8,128)(2,1)} %refs_0_.1) | copy-start | bytes 196612
  16.4 33.6 %collective-permute-start.1 = (bf16[8,128,256]{2,1,0:T(8,128)(2,1)S(1)}, bf16[8,128,256]{2,1,0:T(8,128)(2,1)S(1)}, u32[]{:S(2)}, u32[]{:S(2)}) collective-permute-start(bf16[8,128,256]{2,1,0:T(8,128)(2,1)S(1)} %all_to_all.25.tgt_mine), channel_id=1, source_target_pairs={{0,32},{32,0},{1,33},{33,1},{2,34},{34,2},{3,35},{35,3},{4,36},{36... | collective-permute-start | bytes 1572872 | tf_op jit(solution)/shard_map/ppermute | solution.py:190
  18.9 9.6 %collective-permute-start.3 = (bf16[128,256]{1,0:T(8,128)(2,1)S(1)}, bf16[128,256]{1,0:T(8,128)(2,1)S(1)}, u32[]{:S(2)}, u32[]{:S(2)}) collective-permute-start(bf16[128,256]{1,0:T(8,128)(2,1)S(1)} %copy-done), channel_id=1, source_target_pairs={{0,4},{2,6},{4,0},{6,2},{1,5},{3,7},{5,1},{7,3},{8,12},{10,14},{12... | collective-permute-start | bytes 196616 | tf_op jit(solution)/shard_map/ppermute | solution.py:190
  24.9 6.7 %collective-permute-start.2 = (bf16[128,256]{1,0:T(8,128)(2,1)S(1)}, bf16[128,256]{1,0:T(8,128)(2,1)S(1)}, u32[]{:S(2)}, u32[]{:S(2)}) collective-permute-start(bf16[128,256]{1,0:T(8,128)(2,1)S(1)} %copy-done), channel_id=1, source_target_pairs={{0,2},{2,4},{4,6},{6,0},{1,3},{3,5},{5,7},{7,1},{8,10},{10,12},{12... | collective-permute-start | bytes 196616 | tf_op jit(solution)/shard_map/ppermute | solution.py:190
  26.1 6.1 %collective-permute-start.4 = (bf16[128,256]{1,0:T(8,128)(2,1)S(1)}, bf16[128,256]{1,0:T(8,128)(2,1)S(1)}, u32[]{:S(2)}, u32[]{:S(2)}) collective-permute-start(bf16[128,256]{1,0:T(8,128)(2,1)S(1)} %copy-done), channel_id=1, source_target_pairs={{0,6},{2,0},{4,2},{6,4},{1,7},{3,1},{5,3},{7,5},{8,14},{10,8},{12,... | collective-permute-start | bytes 196616 | tf_op jit(solution)/shard_map/ppermute | solution.py:190
  32.2 11.8 %collective-permute-start.7 = (bf16[4,128,256]{2,1,0:T(8,128)(2,1)S(1)}, bf16[4,128,256]{2,1,0:T(8,128)(2,1)S(1)}, u32[]{:S(2)}, u32[]{:S(2)}) collective-permute-start(bf16[4,128,256]{2,1,0:T(8,128)(2,1)S(1)} %shard_map.60.rest_0_), channel_id=1, source_target_pairs={{0,24},{8,0},{16,8},{24,16},{1,25},{9,1},{17,9},{25,17},{2,26},{10... | collective-permute-start | bytes 786440 | tf_op jit(solution)/shard_map/ppermute | solution.py:190
  34.7 9.3 %collective-permute-start.6 = (bf16[4,128,256]{2,1,0:T(8,128)(2,1)S(1)}, bf16[4,128,256]{2,1,0:T(8,128)(2,1)S(1)}, u32[]{:S(2)}, u32[]{:S(2)}) collective-permute-start(bf16[4,128,256]{2,1,0:T(8,128)(2,1)S(1)} %shard_map.60.rest_0_), channel_id=1, source_target_pairs={{0,16},{8,24},{16,0},{24,8},{1,17},{9,25},{17,1},{25,9},{2,18},{10... | collective-permute-start | bytes 786440 | tf_op jit(solution)/shard_map/ppermute | solution.py:190
  35.2 14.8 %collective-permute-start.5 = (bf16[4,128,256]{2,1,0:T(8,128)(2,1)S(1)}, bf16[4,128,256]{2,1,0:T(8,128)(2,1)S(1)}, u32[]{:S(2)}, u32[]{:S(2)}) collective-permute-start(bf16[4,128,256]{2,1,0:T(8,128)(2,1)S(1)} %shard_map.60.rest_0_), channel_id=1, source_target_pairs={{0,8},{8,16},{16,24},{24,0},{1,9},{9,17},{17,25},{25,1},{2,10},{10... | collective-permute-start | bytes 786440 | tf_op jit(solution)/shard_map/ppermute | solution.py:190
  36.5 0.7 copy-start.1
  37.2 2.9 %collective-permute-start = (s32[3,128]{1,0:T(4,128)S(1)}, s32[3,128]{1,0:T(4,128)S(1)}, u32[]{:S(2)}, u32[]{:S(2)}) collective-permute-start(s32[3,128]{1,0:T(4,128)S(1)} %concatenate.3.mine), channel_id=1, source_target_pairs={{0,1},{1,0},{2,3},{3,2},{4,5},{5,4},{6,7},{7,6},{8,9},{9,8},{10,11... | collective-permute-start | bytes 4616 | tf_op jit(solution)/shard_map/ppermute | solution.py:214
  106.1 15.6 %all-to-all-start.4 = ((f32[16,8,128]{2,1,0:T(8,128)}), f32[16,8,128]{2,1,0:T(8,128)S(1)}, u32[]{:S(2)}, u32[]{:S(2)}) async-start(f32[16,8,128]{2,1,0:T(8,128)} %get-tuple-element.21), calls=%async_computation.4 | async-start | bytes 131072 | tf_op jit(solution)/shard_map/all_to_all | solution.py:185
  115.8 3.1 %collective-permute-start.8 = (f32[16,128]{1,0:T(8,128)S(1)}, f32[16,128]{1,0:T(8,128)S(1)}, u32[]{:S(2)}, u32[]{:S(2)}) collective-permute-start(f32[16,128]{1,0:T(8,128)S(1)} %get-tuple-element.23.mine), channel_id=1, source_target_pairs={{0,1},{1,0},{2,3},{3,2},{4,5},{5,4},{6,7},{7,6},{8,9},{9,8},{10,11... | collective-permute-start | bytes 24584 | tf_op jit(solution)/shard_map/ppermute | solution.py:214

commit v3 on v2

--- a/solution.py
+++ b/solution.py
@@ -110,8 +110,9 @@
 
 
 def pack_kernel(*refs):
-    for n, block in enumerate(refs[:-1]):
-        refs[-1][n] = block[...]
+    blocks = refs[0].shape[0]
+    for n, piece in enumerate(refs[:-1]):
+        refs[-1][n * blocks : (n + 1) * blocks] = piece[...]
 
 
 def first_kernel(tiles, count, place, tgt_mine, tgt_other, *rest):
@@ -123,9 +124,13 @@
         for ds in range(deep):
             s = lax.rem(place[1] + (deep - ds), deep)
             src[x * deep + s] = piece[ds]
+    far = 4
     for n in range(tgt_mine.shape[0]):
-        tgt[2 * n + place[2]] = tgt_mine[n]
-        tgt[2 * n + 1 - place[2]] = tgt_other[n]
+        y = lax.rem(place[2] + (far - n // 2), far)
+        p = lax.rem(place[3] + n % 2, 2)
+        at = p * (2 * far) + 2 * y
+        tgt[at + place[4]] = tgt_mine[n]
+        tgt[at + 1 - place[4]] = tgt_other[n]
     for b in range(tgt.shape[0]):
         sq_tgt[b : b + 1, :] = square_rows(tgt[b])
     for a in range(src.shape[0]):
@@ -191,19 +196,20 @@
     return [block] + [turn(d) for d in range(1, n)]
 
 
+def pack(pieces):
+    blocks, rows, width = pieces[0].shape
+    return pl.pallas_call(
+        pack_kernel,
+        out_shape=jax.ShapeDtypeStruct((len(pieces) * blocks, rows, width), pieces[0].dtype),
+        in_specs=[VMEM] * len(pieces),
+        out_specs=VMEM,
+        compiler_params=PARAMS,
+    )(*pieces)
+
+
 def bands(src_embed, tgt_embed):
-    receivers = lax.axis_size(("p", "y"))
-    tgt = exchange(jnp.broadcast_to(tgt_embed[None], (receivers,) + tgt_embed.shape), ("p", "y"))
-    blocks = shifts(src_embed, "s")
-    together = pl.pallas_call(
-        pack_kernel,
-        out_shape=jax.ShapeDtypeStruct((len(blocks),) + src_embed.shape, src_embed.dtype),
-        in_specs=[VMEM] * len(blocks),
-        out_specs=VMEM,
-        compiler_params=PARAMS,
-    )(*blocks)
-    src_pieces = shifts(together, "x")
-    tgt_pieces = shifts(tgt, "core")
+    src_pieces = shifts(pack(shifts(src_embed[None], "s")), "x")
+    tgt_pieces = shifts(pack(shifts(pack(shifts(tgt_embed[None], "p")), "y")), "core")
     return src_pieces, tgt_pieces
 
 
@@ -228,7 +234,7 @@
     src_shape = jax.ShapeDtypeStruct((srcs,) + src_embed.shape, src_embed.dtype)
     tgt_shape = jax.ShapeDtypeStruct((tgts,) + tgt_embed.shape, tgt_embed.dtype)
     scalars = (picked, count)
-    place = jnp.stack([lax.axis_index(a) for a in ("x", "s", "core")]).astype(jnp.int32)
+    place = jnp.stack([lax.axis_index(a) for a in ("x", "s", "y", "p", "core")]).astype(jnp.int32)
     slots = srcs * tgts
     src_out, tgt_out = (srcs, srcs, TILE), (tgts, tgts, TILE)
     for sweep in range(ITERS):

time: 122 us -> 122 us (level); the launches traced: 122 us -> 121 us
  blocking collectives: 57 us -> 43.5 us
  waiting for transfers between devices: 15.4 us -> 24.6 us
  starting transfers between devices: 28.5 us -> 31.1 us
    all_to_all x4 -> x3, blocking collectives: 57 us -> 43.5 us  [exchange(): return lax.all_to_all(copies, peers, 0, 0, tiled=True)]
    ppermute x7 -> x11, waiting for transfers between devices: 9.79 us -> 19 us  [shifts(): lax.ppermute(block, axis, [(i, (i + d) % n) for i in range(n)])]
    ppermute x7 -> x11, starting transfers between devices: 15.7 us -> 20.9 us  [shifts(): lax.ppermute(block, axis, [(i, (i + d) % n) for i in range(n)])]
    all_to_all x1, starting transfers between devices: 9.74 us -> 6.87 us  [exchange(): return lax.all_to_all(copies, peers, 0, 0, tiled=True)]
  transfers between devices with their start and end apart: 10 -> 14, of which waited for: 6 -> 10; matrix products, arithmetic and copies ran while one was open for 0% -> 0% of each run, Pallas kernels for 3% -> 3%
where the time goes in v3:
time: 122 us; the launch traced here: 121 us
  blocking collectives  43.5 us (36%)
  starting transfers between devices  31.1 us (25%)
  waiting for transfers between devices  24.6 us (20%)
  Pallas kernels  18.5 us (15%)
  local copies, waits for them, and re-layouts  1.61 us (1%)
  between operations  1.36 us (1%)
    all_to_all x3, blocking collectives, exchange(): return lax.all_to_all(copies, peers, 0, 0, tiled=True)  43.5 us
    ppermute x11, starting transfers between devices, shifts(): lax.ppermute(block, axis, [(i, (i + d) % n) for i in range(n)])  20.9 us
    ppermute x11, waiting for transfers between devices, shifts(): lax.ppermute(block, axis, [(i, (i + d) % n) for i in range(n)])  19 us
    pallas_call x4, Pallas kernels, half_step(): pl.pallas_call(kernel, out_shape=[s if isinstance(s, jax.ShapeDtypeStruct...  13.9 us
    all_to_all x1, starting transfers between devices, exchange(): return lax.all_to_all(copies, peers, 0, 0, tiled=True)  6.87 us
    pallas_call x1, Pallas kernels, local(): pl.pallas_call(pick_kernel, out_shape=[jax.ShapeDtypeStruct((2 * TILE + U...  3.9 us
    ppermute x2, starting transfers between devices, local(): partner = lambda v: lax.ppermute(v, 'p', [(0, 1), (1, 0)])  3.33 us
    ppermute x2, waiting for transfers between devices, local(): partner = lambda v: lax.ppermute(v, 'p', [(0, 1), (1, 0)])  2.85 us
  transfers between devices with their start and end apart: 14, of which 10 were waited for; matrix products, arithmetic and copies ran while one was open for 0% of the time, Pallas kernels for 3%

profile of v3, /device:TPU:1, one launch (start us, length us, event | category | flops | bytes accessed | tf_op | source)
XLA Modules:
  0.0 120.8 jit_solution(2978962129731585233)
XLA Ops:
  0.6 2.6 %collective-permute-start.1 = (bf16[1,128,256]{2,1,0:T(8,128)(2,1)}, bf16[1,128,256]{2,1,0:T(8,128)(2,1)S(1)}, u32[]{:S(2)}, u32[]{:S(2)}) collective-permute-start(bf16[1,128,256]{2,1,0:T(8,128)(2,1)} %bitcast.12), channel_id=1, source_target_pairs={{0,1},{1,0},{2,3},{3,2},{4,5},{5,4},{6,7},{7,6},{8,9},{9,8},{10,11... | collective-permute-start | bytes 196616 | tf_op jit(solution)/shard_map/ppermute | solution.py:195
  3.2 1.9 %collective-permute-done.1.refs_1_ = bf16[1,128,256]{2,1,0:T(8,128)(2,1)S(1)} collective-permute-done((bf16[1,128,256]{2,1,0:T(8,128)(2,1)}, bf16[1,128,256]{2,1,0:T(8,128)(2,1)S(1)}, u32[]{:S(2)}, u32[]{:S(2)}) %collective-permute-start.1) | collective-permute-done | bytes 65568 | tf_op jit(solution)/shard_map/ppermute | solution.py:195
  5.0 0.0 copy-start
  5.1 0.8 copy-done
  5.9 0.0 copy-start.1
  5.9 2.8 %collective-permute-start.4 = (bf16[2,128,256]{2,1,0:T(8,128)(2,1)S(1)}, bf16[2,128,256]{2,1,0:T(8,128)(2,1)S(1)}, u32[]{:S(2)}, u32[]{:S(2)}) collective-permute-start(bf16[2,128,256]{2,1,0:T(8,128)(2,1)S(1)} %shard_map.60.refs_0_), channel_id=1, source_target_pairs={{0,192},{64,0},{128,64},{192,128},{1,193},{65,1},{129,65},{193,129... | collective-permute-start | bytes 393224 | tf_op jit(solution)/shard_map/ppermute | solution.py:195
  8.7 0.3 collective-permute-start.3
  9.1 0.7 collective-permute-start.2
  9.8 2.6 %collective-permute-done.4.refs_3_ = bf16[2,128,256]{2,1,0:T(8,128)(2,1)S(1)} collective-permute-done((bf16[2,128,256]{2,1,0:T(8,128)(2,1)S(1)}, bf16[2,128,256]{2,1,0:T(8,128)(2,1)S(1)}, u32[]{:S(2)}, u32[]{:S(2)}) %collective-permute-start.4) | collective-permute-done | bytes 131104 | tf_op jit(solution)/shard_map/ppermute | solution.py:195
  12.4 1.8 %collective-permute-done.3.refs_2_ = bf16[2,128,256]{2,1,0:T(8,128)(2,1)S(1)} collective-permute-done((bf16[2,128,256]{2,1,0:T(8,128)(2,1)S(1)}, bf16[2,128,256]{2,1,0:T(8,128)(2,1)S(1)}, u32[]{:S(2)}, u32[]{:S(2)}) %collective-permute-start.3) | collective-permute-done | bytes 131104 | tf_op jit(solution)/shard_map/ppermute | solution.py:195
  14.2 3.2 %collective-permute-done.2.refs_1_ = bf16[2,128,256]{2,1,0:T(8,128)(2,1)S(1)} collective-permute-done((bf16[2,128,256]{2,1,0:T(8,128)(2,1)S(1)}, bf16[2,128,256]{2,1,0:T(8,128)(2,1)S(1)}, u32[]{:S(2)}, u32[]{:S(2)}) %collective-permute-start.2) | collective-permute-done | bytes 131104 | tf_op jit(solution)/shard_map/ppermute | solution.py:195
  17.3 1.7 %collective-permute-start.5 = (bf16[8,128,256]{2,1,0:T(8,128)(2,1)S(1)}, bf16[8,128,256]{2,1,0:T(8,128)(2,1)S(1)}, u32[]{:S(2)}, u32[]{:S(2)}) collective-permute-start(bf16[8,128,256]{2,1,0:T(8,128)(2,1)S(1)} %shard_map.61.tgt_mine), channel_id=1, source_target_pairs={{0,32},{32,0},{1,33},{33,1},{2,34},{34,2},{3,35},{35,3},{4,36},{36... | collective-permute-start | bytes 1572872 | tf_op jit(solution)/shard_map/ppermute | solution.py:195
  19.1 0.0 copy-done.1
  19.1 5.9 %collective-permute-start.8 = (bf16[1,128,256]{2,1,0:T(8,128)(2,1)S(1)}, bf16[1,128,256]{2,1,0:T(8,128)(2,1)S(1)}, u32[]{:S(2)}, u32[]{:S(2)}) collective-permute-start(bf16[1,128,256]{2,1,0:T(8,128)(2,1)S(1)} %bitcast.14), channel_id=1, source_target_pairs={{0,6},{2,0},{4,2},{6,4},{1,7},{3,1},{5,3},{7,5},{8,14},{10,8},{12,... | collective-permute-start | bytes 196616 | tf_op jit(solution)/shard_map/ppermute | solution.py:195
  24.9 0.9 collective-permute-start.7
  25.8 2.4 %collective-permute-start.6 = (bf16[1,128,256]{2,1,0:T(8,128)(2,1)S(1)}, bf16[1,128,256]{2,1,0:T(8,128)(2,1)S(1)}, u32[]{:S(2)}, u32[]{:S(2)}) collective-permute-start(bf16[1,128,256]{2,1,0:T(8,128)(2,1)S(1)} %bitcast.16), channel_id=1, source_target_pairs={{0,2},{2,4},{4,6},{6,0},{1,3},{3,5},{5,7},{7,1},{8,10},{10,12},{12... | collective-permute-start | bytes 196616 | tf_op jit(solution)/shard_map/ppermute | solution.py:195
  28.2 0.0 collective-permute-done.8.refs_3_
  28.2 4.0 %collective-permute-done.7.refs_2_ = bf16[1,128,256]{2,1,0:T(8,128)(2,1)S(1)} collective-permute-done((bf16[1,128,256]{2,1,0:T(8,128)(2,1)S(1)}, bf16[1,128,256]{2,1,0:T(8,128)(2,1)S(1)}, u32[]{:S(2)}, u32[]{:S(2)}) %collective-permute-start.7) | collective-permute-done | bytes 65568 | tf_op jit(solution)/shard_map/ppermute | solution.py:195
  32.2 0.6 collective-permute-done.6.refs_1_
  32.8 2.6 %collective-permute-start.11 = (bf16[4,128,256]{2,1,0:T(8,128)(2,1)S(1)}, bf16[4,128,256]{2,1,0:T(8,128)(2,1)S(1)}, u32[]{:S(2)}, u32[]{:S(2)}) collective-permute-start(bf16[4,128,256]{2,1,0:T(8,128)(2,1)S(1)} %shard_map.62.rest_0_), channel_id=1, source_target_pairs={{0,24},{8,0},{16,8},{24,16},{1,25},{9,1},{17,9},{25,17},{2,26},{10... | collective-permute-start | bytes 786440 | tf_op jit(solution)/shard_map/ppermute | solution.py:195
  35.4 0.5 collective-permute-start.10
  35.9 0.6 collective-permute-start.9
  37.2 0.0 copy-start.2
  37.2 0.7 copy-done.2
  37.9 1.9 %collective-permute-start = (s32[3,128]{1,0:T(4,128)S(1)}, s32[3,128]{1,0:T(4,128)S(1)}, u32[]{:S(2)}, u32[]{:S(2)}) collective-permute-start(s32[3,128]{1,0:T(4,128)S(1)} %concatenate.3.mine), channel_id=1, source_target_pairs={{0,1},{1,0},{2,3},{3,2},{4,5},{5,4},{6,7},{7,6},{8,9},{9,8},{10,11... | collective-permute-start | bytes 4616 | tf_op jit(solution)/shard_map/ppermute | solution.py:220
  39.8 0.1 stack.20.place
  39.9 1.2 collective-permute-done.other
  41.1 3.9 %shard_map.59 = (s32[272]{0:T(512)S(1)}, s32[1]{0:T(128)}) custom-call(s32[3,128]{1,0:T(4,128)S(1)} %concatenate.3.mine, s32[3,128]{1,0:T(4,128)S(1)} %collective-permute-done.other, s32[1]{0:T(128)} %bitcast.parity), custom_call_target="tpu_custom_call" | custom-call | tf_op jit(solution)/shard_map/pallas_call | solution.py:225
  45.0 0.0 collective-permute-done.11.rest_3_
  45.0 0.0 collective-permute-done.10.rest_2_
  45.0 5.0 %collective-permute-done.9.rest_1_ = bf16[4,128,256]{2,1,0:T(8,128)(2,1)S(1)} collective-permute-done((bf16[4,128,256]{2,1,0:T(8,128)(2,1)S(1)}, bf16[4,128,256]{2,1,0:T(8,128)(2,1)S(1)}, u32[]{:S(2)}, u32[]{:S(2)}) %collective-permute-start.9) | collective-permute-done | bytes 262176 | tf_op jit(solution)/shard_map/ppermute | solution.py:195
  50.0 0.0 collective-permute-done.5.tgt_other
  50.0 3.8 %shard_map.63 = (f32[16,16,128]{2,1,0:T(8,128)S(1)}, bf16[16,128,256]{2,1,0:T(8,128)(2,1)S(1)}, bf16[16,128,256]{2,1,0:T(8,128)(2,1)S(1)}, f32[16,128]{1,0:T(8,128)S(1)}, f32[16,128]{1,0:T(8,128)S(1)}) custom-call(s32[272]{0:T(512)S(1)} %get-tuple-element.14.tiles, s32[1]{0:T(128)} %get-tuple-element.15.count, s32[5]{0:T(128)S(1)} %stack.20.place, ...), custom_call_target="tpu_custom_call" | custom-call | tf_op jit(solution)/shard_map/pallas_call | solution.py:175
  53.8 15.9 %all_to_all.20.parts = f32[16,16,128]{2,1,0:T(8,128)S(1)} all-to-all(f32[16,16,128]{2,1,0:T(8,128)S(1)} %get-tuple-element.18), channel_id=1, replica_groups=mesh['y'=4,'core'=2,'x'=4,'s'=4,'p'=2] {'x','s'}, dimensions={0} | all-to-all | bytes 262144 | tf_op jit(solution)/shard_map/all_to_all | solution.py:190
  69.7 3.4 %shard_map.64 = (f32[16,16,128]{2,1,0:T(8,128)S(1)}, f32[16,128]{1,0:T(8,128)}) custom-call(s32[272]{0:T(512)S(1)} %get-tuple-element.14.tiles, s32[1]{0:T(128)} %get-tuple-element.15.count, bf16[16,128,256]{2,1,0:T(8,128)(2,1)S(1)} %get-tuple-element.16.src, bf16[16,128,256]{2,1,0:T(8,128)(2,1)S(1)} %get-tuple-element.17.tgt, ...), custom_call_target="tpu_custom_call" | custom-call | tf_op jit(solution)/shard_map/pallas_call | solution.py:175
  73.1 13.7 %all_to_all.21.parts = f32[16,16,128]{2,1,0:T(8,128)S(1)} all-to-all(f32[16,16,128]{2,1,0:T(8,128)S(1)} %get-tuple-element.20), channel_id=1, replica_groups=mesh['y'=4,'core'=2,'x'=4,'s'=4,'p'=2] {'p','y','core'}, dimensions={0} | all-to-all | bytes 262144 | tf_op jit(solution)/shard_map/all_to_all | solution.py:190
  86.8 3.0 %shard_map.65 = f32[16,16,128]{2,1,0:T(8,128)S(1)} custom-call(s32[272]{0:T(512)S(1)} %get-tuple-element.14.tiles, s32[1]{0:T(128)} %get-tuple-element.15.count, bf16[16,128,256]{2,1,0:T(8,128)(2,1)S(1)} %get-tuple-element.16.src, bf16[16,128,256]{2,1,0:T(8,128)(2,1)S(1)} %get-tuple-element.17.tgt, f32[16,16,128]{2,1,0:T(8,128)S(1)} %all_to_all.21.parts), custom_call_target="tpu_custom_call" | custom-call | tf_op jit(solution)/shard_map/pallas_call | solution.py:175
  89.9 13.9 %all_to_all.22.parts = f32[16,16,128]{2,1,0:T(8,128)S(1)} all-to-all(f32[16,16,128]{2,1,0:T(8,128)S(1)} %shard_map.65), channel_id=1, replica_groups=mesh['y'=4,'core'=2,'x'=4,'s'=4,'p'=2] {'x','s'}, dimensions={0} | all-to-all | bytes 262144 | tf_op jit(solution)/shard_map/all_to_all | solution.py:190
  103.8 3.7 %shard_map.66 = (f32[16,8,128]{2,1,0:T(8,128)}, f32[16,128]{1,0:T(8,128)S(1)}) custom-call(s32[272]{0:T(512)S(1)} %get-tuple-element.14.tiles, s32[1]{0:T(128)} %get-tuple-element.15.count, bf16[16,128,256]{2,1,0:T(8,128)(2,1)S(1)} %get-tuple-element.16.src, bf16[16,128,256]{2,1,0:T(8,128)(2,1)S(1)} %get-tuple-element.17.tgt, ...), custom_call_target="tpu_custom_call" | custom-call | tf_op jit(solution)/shard_map/pallas_call | solution.py:175
  107.4 6.9 %all-to-all-start.3 = ((f32[16,8,128]{2,1,0:T(8,128)}), f32[16,8,128]{2,1,0:T(8,128)S(1)}, u32[]{:S(2)}, u32[]{:S(2)}) async-start(f32[16,8,128]{2,1,0:T(8,128)} %get-tuple-element.21), calls=%async_computation.3 | async-start | bytes 131072 | tf_op jit(solution)/shard_map/all_to_all | solution.py:190
  114.3 1.4 %collective-permute-start.12 = (f32[16,128]{1,0:T(8,128)S(1)}, f32[16,128]{1,0:T(8,128)S(1)}, u32[]{:S(2)}, u32[]{:S(2)}) collective-permute-start(f32[16,128]{1,0:T(8,128)S(1)} %get-tuple-element.23.mine), channel_id=1, source_target_pairs={{0,1},{1,0},{2,3},{3,2},{4,5},{5,4},{6,7},{7,6},{8,9},{9,8},{10,11... | collective-permute-start | bytes 24584 | tf_op jit(solution)/shard_map/ppermute | solution.py:220
  115.7 1.7 %collective-permute-done.12.other = f32[16,128]{1,0:T(8,128)S(1)} collective-permute-done((f32[16,128]{1,0:T(8,128)S(1)}, f32[16,128]{1,0:T(8,128)S(1)}, u32[]{:S(2)}, u32[]{:S(2)}) %collective-permute-start.12) | collective-permute-done | bytes 8224 | tf_op jit(solution)/shard_map/ppermute | solution.py:220
  117.4 2.8 %all-to-all-done.3.parts = f32[16,8,128]{2,1,0:T(8,128)S(1)} async-done(((f32[16,8,128]{2,1,0:T(8,128)}), f32[16,8,128]{2,1,0:T(8,128)S(1)}, u32[]{:S(2)}, u32[]{:S(2)}) %all-to-all-start.3) | async-done | bytes 65568 | tf_op jit(solution)/shard_map/all_to_all | solution.py:190
  120.1 0.6 shard_map.67
  (4 shorter events, 0.1 us)
Async XLA Ops:
  0.6 4.4 %collective-permute-start.1 = (bf16[1,128,256]{2,1,0:T(8,128)(2,1)}, bf16[1,128,256]{2,1,0:T(8,128)(2,1)S(1)}, u32[]{:S(2)}, u32[]{:S(2)}) collective-permute-start(bf16[1,128,256]{2,1,0:T(8,128)(2,1)} %bitcast.12), channel_id=1, source_target_pairs={{0,1},{1,0},{2,3},{3,2},{4,5},{5,4},{6,7},{7,6},{8,9},{9,8},{10,11... | collective-permute-start | bytes 196616 | tf_op jit(solution)/shard_map/ppermute | solution.py:195
  5.0 0.8 copy-start
  5.9 13.2 %copy-start.1 = (bf16[128,256]{1,0:T(8,128)(2,1)S(1)}, bf16[128,256]{1,0:T(8,128)(2,1)}, u32[]{:S(2)}) copy-start(bf16[128,256]{1,0:T(8,128)(2,1)} %param.4) | copy-start | bytes 196612
  5.9 6.5 %collective-permute-start.4 = (bf16[2,128,256]{2,1,0:T(8,128)(2,1)S(1)}, bf16[2,128,256]{2,1,0:T(8,128)(2,1)S(1)}, u32[]{:S(2)}, u32[]{:S(2)}) collective-permute-start(bf16[2,128,256]{2,1,0:T(8,128)(2,1)S(1)} %shard_map.60.refs_0_), channel_id=1, source_target_pairs={{0,192},{64,0},{128,64},{192,128},{1,193},{65,1},{129,65},{193,129... | collective-permute-start | bytes 393224 | tf_op jit(solution)/shard_map/ppermute | solution.py:195
  8.7 5.4 %collective-permute-start.3 = (bf16[2,128,256]{2,1,0:T(8,128)(2,1)S(1)}, bf16[2,128,256]{2,1,0:T(8,128)(2,1)S(1)}, u32[]{:S(2)}, u32[]{:S(2)}) collective-permute-start(bf16[2,128,256]{2,1,0:T(8,128)(2,1)S(1)} %shard_map.60.refs_0_), channel_id=1, source_target_pairs={{0,128},{64,192},{128,0},{192,64},{1,129},{65,193},{129,1},{193,65... | collective-permute-start | bytes 393224 | tf_op jit(solution)/shard_map/ppermute | solution.py:195
  9.1 8.2 %collective-permute-start.2 = (bf16[2,128,256]{2,1,0:T(8,128)(2,1)S(1)}, bf16[2,128,256]{2,1,0:T(8,128)(2,1)S(1)}, u32[]{:S(2)}, u32[]{:S(2)}) collective-permute-start(bf16[2,128,256]{2,1,0:T(8,128)(2,1)S(1)} %shard_map.60.refs_0_), channel_id=1, source_target_pairs={{0,64},{64,128},{128,192},{192,0},{1,65},{65,129},{129,193},{193,1... | collective-permute-start | bytes 393224 | tf_op jit(solution)/shard_map/ppermute | solution.py:195
  17.3 32.6 %collective-permute-start.5 = (bf16[8,128,256]{2,1,0:T(8,128)(2,1)S(1)}, bf16[8,128,256]{2,1,0:T(8,128)(2,1)S(1)}, u32[]{:S(2)}, u32[]{:S(2)}) collective-permute-start(bf16[8,128,256]{2,1,0:T(8,128)(2,1)S(1)} %shard_map.61.tgt_mine), channel_id=1, source_target_pairs={{0,32},{32,0},{1,33},{33,1},{2,34},{34,2},{3,35},{35,3},{4,36},{36... | collective-permute-start | bytes 1572872 | tf_op jit(solution)/shard_map/ppermute | solution.py:195
  19.1 9.1 %collective-permute-start.8 = (bf16[1,128,256]{2,1,0:T(8,128)(2,1)S(1)}, bf16[1,128,256]{2,1,0:T(8,128)(2,1)S(1)}, u32[]{:S(2)}, u32[]{:S(2)}) collective-permute-start(bf16[1,128,256]{2,1,0:T(8,128)(2,1)S(1)} %bitcast.14), channel_id=1, source_target_pairs={{0,6},{2,0},{4,2},{6,4},{1,7},{3,1},{5,3},{7,5},{8,14},{10,8},{12,... | collective-permute-start | bytes 196616 | tf_op jit(solution)/shard_map/ppermute | solution.py:195
  24.9 7.2 %collective-permute-start.7 = (bf16[1,128,256]{2,1,0:T(8,128)(2,1)S(1)}, bf16[1,128,256]{2,1,0:T(8,128)(2,1)S(1)}, u32[]{:S(2)}, u32[]{:S(2)}) collective-permute-start(bf16[1,128,256]{2,1,0:T(8,128)(2,1)S(1)} %bitcast.15), channel_id=1, source_target_pairs={{0,4},{2,6},{4,0},{6,2},{1,5},{3,7},{5,1},{7,3},{8,12},{10,14},{12... | collective-permute-start | bytes 196616 | tf_op jit(solution)/shard_map/ppermute | solution.py:195
  25.8 7.0 %collective-permute-start.6 = (bf16[1,128,256]{2,1,0:T(8,128)(2,1)S(1)}, bf16[1,128,256]{2,1,0:T(8,128)(2,1)S(1)}, u32[]{:S(2)}, u32[]{:S(2)}) collective-permute-start(bf16[1,128,256]{2,1,0:T(8,128)(2,1)S(1)} %bitcast.16), channel_id=1, source_target_pairs={{0,2},{2,4},{4,6},{6,0},{1,3},{3,5},{5,7},{7,1},{8,10},{10,12},{12... | collective-permute-start | bytes 196616 | tf_op jit(solution)/shard_map/ppermute | solution.py:195
  32.8 12.1 %collective-permute-start.11 = (bf16[4,128,256]{2,1,0:T(8,128)(2,1)S(1)}, bf16[4,128,256]{2,1,0:T(8,128)(2,1)S(1)}, u32[]{:S(2)}, u32[]{:S(2)}) collective-permute-start(bf16[4,128,256]{2,1,0:T(8,128)(2,1)S(1)} %shard_map.62.rest_0_), channel_id=1, source_target_pairs={{0,24},{8,0},{16,8},{24,16},{1,25},{9,1},{17,9},{25,17},{2,26},{10... | collective-permute-start | bytes 786440 | tf_op jit(solution)/shard_map/ppermute | solution.py:195
  35.4 9.6 %collective-permute-start.10 = (bf16[4,128,256]{2,1,0:T(8,128)(2,1)S(1)}, bf16[4,128,256]{2,1,0:T(8,128)(2,1)S(1)}, u32[]{:S(2)}, u32[]{:S(2)}) collective-permute-start(bf16[4,128,256]{2,1,0:T(8,128)(2,1)S(1)} %shard_map.62.rest_0_), channel_id=1, source_target_pairs={{0,16},{8,24},{16,0},{24,8},{1,17},{9,25},{17,1},{25,9},{2,18},{10... | collective-permute-start | bytes 786440 | tf_op jit(solution)/shard_map/ppermute | solution.py:195
  35.9 14.0 %collective-permute-start.9 = (bf16[4,128,256]{2,1,0:T(8,128)(2,1)S(1)}, bf16[4,128,256]{2,1,0:T(8,128)(2,1)S(1)}, u32[]{:S(2)}, u32[]{:S(2)}) collective-permute-start(bf16[4,128,256]{2,1,0:T(8,128)(2,1)S(1)} %shard_map.62.rest_0_), channel_id=1, source_target_pairs={{0,8},{8,16},{16,24},{24,0},{1,9},{9,17},{17,25},{25,1},{2,10},{10... | collective-permute-start | bytes 786440 | tf_op jit(solution)/shard_map/ppermute | solution.py:195
  37.2 0.7 copy-start.2
  37.9 3.2 %collective-permute-start = (s32[3,128]{1,0:T(4,128)S(1)}, s32[3,128]{1,0:T(4,128)S(1)}, u32[]{:S(2)}, u32[]{:S(2)}) collective-permute-start(s32[3,128]{1,0:T(4,128)S(1)} %concatenate.3.mine), channel_id=1, source_target_pairs={{0,1},{1,0},{2,3},{3,2},{4,5},{5,4},{6,7},{7,6},{8,9},{9,8},{10,11... | collective-permute-start | bytes 4616 | tf_op jit(solution)/shard_map/ppermute | solution.py:220
  107.4 12.7 %all-to-all-start.3 = ((f32[16,8,128]{2,1,0:T(8,128)}), f32[16,8,128]{2,1,0:T(8,128)S(1)}, u32[]{:S(2)}, u32[]{:S(2)}) async-start(f32[16,8,128]{2,1,0:T(8,128)} %get-tuple-element.21), calls=%async_computation.3 | async-start | bytes 131072 | tf_op jit(solution)/shard_map/all_to_all | solution.py:190
  114.3 3.1 %collective-permute-start.12 = (f32[16,128]{1,0:T(8,128)S(1)}, f32[16,128]{1,0:T(8,128)S(1)}, u32[]{:S(2)}, u32[]{:S(2)}) collective-permute-start(f32[16,128]{1,0:T(8,128)S(1)} %get-tuple-element.23.mine), channel_id=1, source_target_pairs={{0,1},{1,0},{2,3},{3,2},{4,5},{5,4},{6,7},{7,6},{8,9},{9,8},{10,11... | collective-permute-start | bytes 24584 | tf_op jit(solution)/shard_map/ppermute | solution.py:220

commit v4 on v2

--- a/solution.py
+++ b/solution.py
@@ -109,23 +109,25 @@
     return tile
 
 
-def pack_kernel(*refs):
-    for n, block in enumerate(refs[:-1]):
-        refs[-1][n] = block[...]
-
-
-def first_kernel(tiles, count, place, tgt_mine, tgt_other, *rest):
-    sides = len(rest) - 8
-    pieces, (out, src, tgt, sq_src, sq_tgt, wide, peaks, totals) = rest[:sides], rest[sides:]
-    deep = pieces[0].shape[0]
-    for dx, piece in enumerate(pieces):
-        x = lax.rem(place[0] + (sides - dx), sides)
-        for ds in range(deep):
-            s = lax.rem(place[1] + (deep - ds), deep)
-            src[x * deep + s] = piece[ds]
-    for n in range(tgt_mine.shape[0]):
-        tgt[2 * n + place[2]] = tgt_mine[n]
-        tgt[2 * n + 1 - place[2]] = tgt_other[n]
+def pack_kernel(srcs, *refs):
+    src, tgt = refs[-2:]
+    for n in range(srcs):
+        src[n] = refs[n][...]
+    for n in range(len(refs) - 2 - srcs):
+        tgt[n] = refs[srcs + n][...]
+
+
+def first_kernel(tiles, count, place, *refs):
+    pieces, (out, src, tgt, sq_src, sq_tgt, wide, peaks, totals) = refs[:-8], refs[-8:]
+    sides = len(pieces) // 2
+    for d in range(sides):
+        x, y = (lax.rem(place[axis] + (sides - d), sides) for axis in (0, 2))
+        for n in range(pieces[d].shape[0]):
+            s = lax.rem(place[1] + (sides - n), sides)
+            src[x * sides + s] = pieces[d][n]
+        for n in range(pieces[sides + d].shape[0]):
+            p, core = place[3] ^ (n % 2), place[4] ^ (n // 2)
+            tgt[p * (2 * sides) + 2 * y + core] = pieces[sides + d][n]
     for b in range(tgt.shape[0]):
         sq_tgt[b : b + 1, :] = square_rows(tgt[b])
     for a in range(src.shape[0]):
@@ -191,20 +193,24 @@
     return [block] + [turn(d) for d in range(1, n)]
 
 
+def swaps(block, axes):
+    n = lax.axis_size(axes)
+    return [block] + [lax.ppermute(block, axes, [(i, i ^ d) for i in range(n)]) for d in range(1, n)]
+
+
 def bands(src_embed, tgt_embed):
-    receivers = lax.axis_size(("p", "y"))
-    tgt = exchange(jnp.broadcast_to(tgt_embed[None], (receivers,) + tgt_embed.shape), ("p", "y"))
-    blocks = shifts(src_embed, "s")
-    together = pl.pallas_call(
-        pack_kernel,
-        out_shape=jax.ShapeDtypeStruct((len(blocks),) + src_embed.shape, src_embed.dtype),
+    src_blocks, tgt_blocks = shifts(src_embed, "s"), swaps(tgt_embed, ("core", "p"))
+    blocks = src_blocks + tgt_blocks
+    src, tgt = pl.pallas_call(
+        functools.partial(pack_kernel, len(src_blocks)),
+        out_shape=[
+            jax.ShapeDtypeStruct((len(group),) + group[0].shape, group[0].dtype) for group in (src_blocks, tgt_blocks)
+        ],
         in_specs=[VMEM] * len(blocks),
-        out_specs=VMEM,
+        out_specs=[VMEM] * 2,
         compiler_params=PARAMS,
     )(*blocks)
-    src_pieces = shifts(together, "x")
-    tgt_pieces = shifts(tgt, "core")
-    return src_pieces, tgt_pieces
+    return shifts(src, "x"), shifts(tgt, "y")
 
 
 def local(src_embed, tgt_embed, tiles, counts):
@@ -228,7 +234,7 @@
     src_shape = jax.ShapeDtypeStruct((srcs,) + src_embed.shape, src_embed.dtype)
     tgt_shape = jax.ShapeDtypeStruct((tgts,) + tgt_embed.shape, tgt_embed.dtype)
     scalars = (picked, count)
-    place = jnp.stack([lax.axis_index(a) for a in ("x", "s", "core")]).astype(jnp.int32)
+    place = jnp.stack([lax.axis_index(a) for a in ("x", "s", "y", "p", "core")]).astype(jnp.int32)
     slots = srcs * tgts
     src_out, tgt_out = (srcs, srcs, TILE), (tgts, tgts, TILE)
     for sweep in range(ITERS):
@@ -239,8 +245,8 @@
                 tgts,
                 slots,
                 scalars + (place,),
+                *src_pieces,
                 *tgt_pieces,
-                *src_pieces,
             )
         else:
             (parts,) = half_step(

time: 122 us -> 119 us (0.975)
  blocking collectives: 57 us -> 41.9 us
  Pallas kernels: 18.5 us -> 24.7 us
  starting transfers between devices: 28.5 us -> 31.3 us
  waiting for transfers between devices: 15.4 us -> 16.7 us
    all_to_all x4 -> x3, blocking collectives: 57 us -> 41.9 us  [exchange(): return lax.all_to_all(copies, peers, 0, 0, tiled=True)]
    pallas_call x4, Pallas kernels: 13.9 us -> 20.2 us  [half_step(): pl.pallas_call(kernel, out_shape=[s if isinstance(s, jax.ShapeDtypeStruct...]
    ppermute x7 -> x9, starting transfers between devices: 15.7 us -> 20.2 us  [shifts(): lax.ppermute(block, axis, [(i, (i + d) % n) for i in range(n)])]
    ppermute x0 -> x3, waiting for transfers between devices: none -> 4.04 us  [swaps(): lax.ppermute(block, axes, [(i, i ^ d) for i in range(n)])]
    all_to_all x1, starting transfers between devices: 9.74 us -> 5.84 us  [exchange(): return lax.all_to_all(copies, peers, 0, 0, tiled=True)]
    ppermute x0 -> x3, starting transfers between devices: none -> 3.15 us  [swaps(): lax.ppermute(block, axes, [(i, i ^ d) for i in range(n)])]
    unnamed x4 -> x6, local copies, waits for them, and re-layouts: 0.68 us -> 2.35 us
    ppermute x7 -> x9, waiting for transfers between devices: 9.79 us -> 8.21 us  [shifts(): lax.ppermute(block, axis, [(i, (i + d) % n) for i in range(n)])]
  transfers between devices with their start and end apart: 10 -> 15, of which waited for: 6 -> 7; matrix products, arithmetic and copies ran while one was open for 0% -> 0% of each run, Pallas kernels for 3% -> 3%
where the time goes in v4:
time: 119 us; the launch traced here: 118 us
  blocking collectives  41.9 us (35%)
  starting transfers between devices  31.3 us (26%)
  Pallas kernels  24.7 us (21%)
  waiting for transfers between devices  16.7 us (14%)
  local copies, waits for them, and re-layouts  2.44 us (2%)
  between operations  1.34 us (1%)
    all_to_all x3, blocking collectives, exchange(): return lax.all_to_all(copies, peers, 0, 0, tiled=True)  41.9 us
    ppermute x9, starting transfers between devices, shifts(): lax.ppermute(block, axis, [(i, (i + d) % n) for i in range(n)])  20.2 us
    pallas_call x4, Pallas kernels, half_step(): pl.pallas_call(kernel, out_shape=[s if isinstance(s, jax.ShapeDtypeStruct...  20.2 us
    ppermute x9, waiting for transfers between devices, shifts(): lax.ppermute(block, axis, [(i, (i + d) % n) for i in range(n)])  8.21 us
    all_to_all x1, starting transfers between devices, exchange(): return lax.all_to_all(copies, peers, 0, 0, tiled=True)  5.84 us
    ppermute x3, waiting for transfers between devices, swaps(): lax.ppermute(block, axes, [(i, i ^ d) for i in range(n)])  4.04 us
    pallas_call x1, Pallas kernels, local(): pl.pallas_call(pick_kernel, out_shape=[jax.ShapeDtypeStruct((2 * TILE + U...  3.9 us
    ppermute x3, starting transfers between devices, swaps(): lax.ppermute(block, axes, [(i, i ^ d) for i in range(n)])  3.15 us
  transfers between devices with their start and end apart: 15, of which 7 were waited for; matrix products, arithmetic and copies ran while one was open for 0% of the time, Pallas kernels for 3%

profile of v4, /device:TPU:1, one launch (start us, length us, event | category | flops | bytes accessed | tf_op | source)
XLA Modules:
  0.0 118.4 jit_solution(2664277953793196644)
XLA Ops:
  0.6 7.8 %collective-permute-start.2 = (bf16[128,256]{1,0:T(8,128)(2,1)}, bf16[128,256]{1,0:T(8,128)(2,1)S(1)}, u32[]{:S(2)}, u32[]{:S(2)}) collective-permute-start(bf16[128,256]{1,0:T(8,128)(2,1)} %refs_0_.1), channel_id=1, source_target_pairs={{0,4},{2,6},{4,0},{6,2},{1,5},{3,7},{5,1},{7,3},{8,12},{10,14},{12... | collective-permute-start | bytes 196616 | tf_op jit(solution)/shard_map/ppermute | solution.py:192
  8.5 1.2 %collective-permute-start.1 = (bf16[128,256]{1,0:T(8,128)(2,1)}, bf16[128,256]{1,0:T(8,128)(2,1)S(1)}, u32[]{:S(2)}, u32[]{:S(2)}) collective-permute-start(bf16[128,256]{1,0:T(8,128)(2,1)} %refs_0_.1), channel_id=1, source_target_pairs={{0,2},{2,4},{4,6},{6,0},{1,3},{3,5},{5,7},{7,1},{8,10},{10,12},{12... | collective-permute-start | bytes 196616 | tf_op jit(solution)/shard_map/ppermute | solution.py:192
  9.6 2.4 %collective-permute-start.3 = (bf16[128,256]{1,0:T(8,128)(2,1)}, bf16[128,256]{1,0:T(8,128)(2,1)S(1)}, u32[]{:S(2)}, u32[]{:S(2)}) collective-permute-start(bf16[128,256]{1,0:T(8,128)(2,1)} %refs_0_.1), channel_id=1, source_target_pairs={{0,6},{2,0},{4,2},{6,4},{1,7},{3,1},{5,3},{7,5},{8,14},{10,8},{12,... | collective-permute-start | bytes 196616 | tf_op jit(solution)/shard_map/ppermute | solution.py:192
  12.0 1.5 %collective-permute-start.5 = (bf16[128,256]{1,0:T(8,128)(2,1)}, bf16[128,256]{1,0:T(8,128)(2,1)S(1)}, u32[]{:S(2)}, u32[]{:S(2)}) collective-permute-start(bf16[128,256]{1,0:T(8,128)(2,1)} %refs_4_.1), channel_id=1, source_target_pairs={{0,32},{1,33},{32,0},{33,1},{2,34},{3,35},{34,2},{35,3},{4,36},{5,... | collective-permute-start | bytes 196616 | tf_op jit(solution)/shard_map/ppermute | solution.py:198
  13.5 0.7 collective-permute-start.4
  14.3 0.0 collective-permute-done.2.refs_2_
  14.3 0.9 collective-permute-start.6
  15.2 0.0 collective-permute-done.1.refs_1_
  15.2 0.0 collective-permute-done.3.refs_3_
  15.2 0.0 collective-permute-done.5.refs_6_
  15.2 2.6 %collective-permute-done.4.refs_5_ = bf16[128,256]{1,0:T(8,128)(2,1)S(1)} collective-permute-done((bf16[128,256]{1,0:T(8,128)(2,1)}, bf16[128,256]{1,0:T(8,128)(2,1)S(1)}, u32[]{:S(2)}, u32[]{:S(2)}) %collective-permute-start.4) | collective-permute-done | bytes 65568 | tf_op jit(solution)/shard_map/ppermute | solution.py:198
  17.8 1.4 %collective-permute-done.6.refs_7_ = bf16[128,256]{1,0:T(8,128)(2,1)S(1)} collective-permute-done((bf16[128,256]{1,0:T(8,128)(2,1)}, bf16[128,256]{1,0:T(8,128)(2,1)S(1)}, u32[]{:S(2)}, u32[]{:S(2)}) %collective-permute-start.6) | collective-permute-done | bytes 65568 | tf_op jit(solution)/shard_map/ppermute | solution.py:198
  19.2 0.0 copy-start
  19.2 0.8 copy-done
  20.1 0.0 copy-start.1
  20.1 0.8 copy-done.1
  21.0 2.6 %collective-permute-start.9 = (bf16[4,128,256]{2,1,0:T(8,128)(2,1)S(1)}, bf16[4,128,256]{2,1,0:T(8,128)(2,1)S(1)}, u32[]{:S(2)}, u32[]{:S(2)}) collective-permute-start(bf16[4,128,256]{2,1,0:T(8,128)(2,1)S(1)} %get-tuple-element.18.refs_0_), channel_id=1, source_target_pairs={{0,24},{8,0},{16,8},{24,16},{1,25},{9,1},{17,9},{25,17},{2,26},{10... | collective-permute-start | bytes 786440 | tf_op jit(solution)/shard_map/ppermute | solution.py:192
  24.2 0.0 copy-start.2
  24.2 0.7 copy-done.2
  24.9 0.7 collective-permute-start
  25.6 0.5 collective-permute-start.8
  26.1 0.6 collective-permute-start.7
  26.7 2.7 %collective-permute-start.12 = (bf16[4,128,256]{2,1,0:T(8,128)(2,1)S(1)}, bf16[4,128,256]{2,1,0:T(8,128)(2,1)S(1)}, u32[]{:S(2)}, u32[]{:S(2)}) collective-permute-start(bf16[4,128,256]{2,1,0:T(8,128)(2,1)S(1)} %get-tuple-element.19.refs_4_), channel_id=1, source_target_pairs={{0,192},{64,0},{128,64},{192,128},{1,193},{65,1},{129,65},{193,129... | collective-permute-start | bytes 786440 | tf_op jit(solution)/shard_map/ppermute | solution.py:192
  29.4 0.0 collective-permute-done.other
  29.4 1.1 collective-permute-start.11
  30.5 3.8 %collective-permute-done.9.refs_3_ = bf16[4,128,256]{2,1,0:T(8,128)(2,1)S(1)} collective-permute-done((bf16[4,128,256]{2,1,0:T(8,128)(2,1)S(1)}, bf16[4,128,256]{2,1,0:T(8,128)(2,1)S(1)}, u32[]{:S(2)}, u32[]{:S(2)}) %collective-permute-start.9) | collective-permute-done | bytes 262176 | tf_op jit(solution)/shard_map/ppermute | solution.py:192
  34.3 1.3 %collective-permute-start.10 = (bf16[4,128,256]{2,1,0:T(8,128)(2,1)S(1)}, bf16[4,128,256]{2,1,0:T(8,128)(2,1)S(1)}, u32[]{:S(2)}, u32[]{:S(2)}) collective-permute-start(bf16[4,128,256]{2,1,0:T(8,128)(2,1)S(1)} %get-tuple-element.19.refs_4_), channel_id=1, source_target_pairs={{0,64},{64,128},{128,192},{192,0},{1,65},{65,129},{129,193},{193,1... | collective-permute-start | bytes 786440 | tf_op jit(solution)/shard_map/ppermute | solution.py:192
  35.6 0.1 stack.20.place
  35.7 3.9 %shard_map.59 = (s32[272]{0:T(512)S(1)}, s32[1]{0:T(128)}) custom-call(s32[3,128]{1,0:T(4,128)S(1)} %concatenate.3.mine, s32[3,128]{1,0:T(4,128)S(1)} %collective-permute-done.other, s32[1]{0:T(128)} %bitcast.parity), custom_call_target="tpu_custom_call" | custom-call | tf_op jit(solution)/shard_map/pallas_call | solution.py:225
  39.6 0.0 collective-permute-done.8.refs_2_
  39.6 1.3 %collective-permute-done.7.refs_1_ = bf16[4,128,256]{2,1,0:T(8,128)(2,1)S(1)} collective-permute-done((bf16[4,128,256]{2,1,0:T(8,128)(2,1)S(1)}, bf16[4,128,256]{2,1,0:T(8,128)(2,1)S(1)}, u32[]{:S(2)}, u32[]{:S(2)}) %collective-permute-start.7) | collective-permute-done | bytes 262176 | tf_op jit(solution)/shard_map/ppermute | solution.py:192
  40.9 0.0 collective-permute-done.12.refs_7_
  40.9 0.0 collective-permute-done.11.refs_6_
  40.9 3.1 %collective-permute-done.10.refs_5_ = bf16[4,128,256]{2,1,0:T(8,128)(2,1)S(1)} collective-permute-done((bf16[4,128,256]{2,1,0:T(8,128)(2,1)S(1)}, bf16[4,128,256]{2,1,0:T(8,128)(2,1)S(1)}, u32[]{:S(2)}, u32[]{:S(2)}) %collective-permute-start.10) | collective-permute-done | bytes 262176 | tf_op jit(solution)/shard_map/ppermute | solution.py:192
  44.0 5.3 %shard_map.61 = (f32[16,16,128]{2,1,0:T(8,128)S(1)}, bf16[16,128,256]{2,1,0:T(8,128)(2,1)S(1)}, bf16[16,128,256]{2,1,0:T(8,128)(2,1)S(1)}, f32[16,128]{1,0:T(8,128)S(1)}, f32[16,128]{1,0:T(8,128)S(1)}) custom-call(s32[272]{0:T(512)S(1)} %get-tuple-element.16.tiles, s32[1]{0:T(128)} %get-tuple-element.17.count, s32[5]{0:T(128)S(1)} %stack.20.place, ...), custom_call_target="tpu_custom_call" | custom-call | tf_op jit(solution)/shard_map/pallas_call | solution.py:172
  49.3 16.5 %all_to_all.20.parts = f32[16,16,128]{2,1,0:T(8,128)S(1)} all-to-all(f32[16,16,128]{2,1,0:T(8,128)S(1)} %get-tuple-element.22), channel_id=1, replica_groups=mesh['y'=4,'core'=2,'x'=4,'s'=4,'p'=2] {'x','s'}, dimensions={0} | all-to-all | bytes 262144 | tf_op jit(solution)/shard_map/all_to_all | solution.py:187
  65.9 5.1 %shard_map.62 = (f32[16,16,128]{2,1,0:T(8,128)S(1)}, f32[16,128]{1,0:T(8,128)}) custom-call(s32[272]{0:T(512)S(1)} %get-tuple-element.16.tiles, s32[1]{0:T(128)} %get-tuple-element.17.count, bf16[16,128,256]{2,1,0:T(8,128)(2,1)S(1)} %get-tuple-element.20.src, bf16[16,128,256]{2,1,0:T(8,128)(2,1)S(1)} %get-tuple-element.21.tgt, ...), custom_call_target="tpu_custom_call" | custom-call | tf_op jit(solution)/shard_map/pallas_call | solution.py:172
  71.0 12.7 %all_to_all.21.parts = f32[16,16,128]{2,1,0:T(8,128)S(1)} all-to-all(f32[16,16,128]{2,1,0:T(8,128)S(1)} %get-tuple-element.24), channel_id=1, replica_groups=mesh['y'=4,'core'=2,'x'=4,'s'=4,'p'=2] {'p','y','core'}, dimensions={0} | all-to-all | bytes 262144 | tf_op jit(solution)/shard_map/all_to_all | solution.py:187
  83.7 4.6 %shard_map.63 = f32[16,16,128]{2,1,0:T(8,128)S(1)} custom-call(s32[272]{0:T(512)S(1)} %get-tuple-element.16.tiles, s32[1]{0:T(128)} %get-tuple-element.17.count, bf16[16,128,256]{2,1,0:T(8,128)(2,1)S(1)} %get-tuple-element.20.src, bf16[16,128,256]{2,1,0:T(8,128)(2,1)S(1)} %get-tuple-element.21.tgt, f32[16,16,128]{2,1,0:T(8,128)S(1)} %all_to_all.21.parts), custom_call_target="tpu_custom_call" | custom-call | tf_op jit(solution)/shard_map/pallas_call | solution.py:172
  88.3 12.7 %all_to_all.22.parts = f32[16,16,128]{2,1,0:T(8,128)S(1)} all-to-all(f32[16,16,128]{2,1,0:T(8,128)S(1)} %shard_map.63), channel_id=1, replica_groups=mesh['y'=4,'core'=2,'x'=4,'s'=4,'p'=2] {'x','s'}, dimensions={0} | all-to-all | bytes 262144 | tf_op jit(solution)/shard_map/all_to_all | solution.py:187
  100.9 5.2 %shard_map.64 = (f32[16,8,128]{2,1,0:T(8,128)}, f32[16,128]{1,0:T(8,128)S(1)}) custom-call(s32[272]{0:T(512)S(1)} %get-tuple-element.16.tiles, s32[1]{0:T(128)} %get-tuple-element.17.count, bf16[16,128,256]{2,1,0:T(8,128)(2,1)S(1)} %get-tuple-element.20.src, bf16[16,128,256]{2,1,0:T(8,128)(2,1)S(1)} %get-tuple-element.21.tgt, ...), custom_call_target="tpu_custom_call" | custom-call | tf_op jit(solution)/shard_map/pallas_call | solution.py:172
  106.1 5.8 %all-to-all-start.3 = ((f32[16,8,128]{2,1,0:T(8,128)}), f32[16,8,128]{2,1,0:T(8,128)S(1)}, u32[]{:S(2)}, u32[]{:S(2)}) async-start(f32[16,8,128]{2,1,0:T(8,128)} %get-tuple-element.25), calls=%async_computation.3 | async-start | bytes 131072 | tf_op jit(solution)/shard_map/all_to_all | solution.py:187
  111.9 1.4 %collective-permute-start.13 = (f32[16,128]{1,0:T(8,128)S(1)}, f32[16,128]{1,0:T(8,128)S(1)}, u32[]{:S(2)}, u32[]{:S(2)}) collective-permute-start(f32[16,128]{1,0:T(8,128)S(1)} %get-tuple-element.27.mine), channel_id=1, source_target_pairs={{0,1},{1,0},{2,3},{3,2},{4,5},{5,4},{6,7},{7,6},{8,9},{9,8},{10,11... | collective-permute-start | bytes 24584 | tf_op jit(solution)/shard_map/ppermute | solution.py:220
  113.3 1.7 %collective-permute-done.13.other = f32[16,128]{1,0:T(8,128)S(1)} collective-permute-done((f32[16,128]{1,0:T(8,128)S(1)}, f32[16,128]{1,0:T(8,128)S(1)}, u32[]{:S(2)}, u32[]{:S(2)}) %collective-permute-start.13) | collective-permute-done | bytes 8224 | tf_op jit(solution)/shard_map/ppermute | solution.py:220
  115.0 2.8 %all-to-all-done.3.parts = f32[16,8,128]{2,1,0:T(8,128)S(1)} async-done(((f32[16,8,128]{2,1,0:T(8,128)}), f32[16,8,128]{2,1,0:T(8,128)S(1)}, u32[]{:S(2)}, u32[]{:S(2)}) %all-to-all-start.3) | async-done | bytes 65568 | tf_op jit(solution)/shard_map/all_to_all | solution.py:187
  117.8 0.6 shard_map.65
  (2 shorter events, 0.0 us)
Async XLA Ops:
  0.6 13.7 %collective-permute-start.2 = (bf16[128,256]{1,0:T(8,128)(2,1)}, bf16[128,256]{1,0:T(8,128)(2,1)S(1)}, u32[]{:S(2)}, u32[]{:S(2)}) collective-permute-start(bf16[128,256]{1,0:T(8,128)(2,1)} %refs_0_.1), channel_id=1, source_target_pairs={{0,4},{2,6},{4,0},{6,2},{1,5},{3,7},{5,1},{7,3},{8,12},{10,14},{12... | collective-permute-start | bytes 196616 | tf_op jit(solution)/shard_map/ppermute | solution.py:192
  8.5 6.7 %collective-permute-start.1 = (bf16[128,256]{1,0:T(8,128)(2,1)}, bf16[128,256]{1,0:T(8,128)(2,1)S(1)}, u32[]{:S(2)}, u32[]{:S(2)}) collective-permute-start(bf16[128,256]{1,0:T(8,128)(2,1)} %refs_0_.1), channel_id=1, source_target_pairs={{0,2},{2,4},{4,6},{6,0},{1,3},{3,5},{5,7},{7,1},{8,10},{10,12},{12... | collective-permute-start | bytes 196616 | tf_op jit(solution)/shard_map/ppermute | solution.py:192
  9.6 5.5 %collective-permute-start.3 = (bf16[128,256]{1,0:T(8,128)(2,1)}, bf16[128,256]{1,0:T(8,128)(2,1)S(1)}, u32[]{:S(2)}, u32[]{:S(2)}) collective-permute-start(bf16[128,256]{1,0:T(8,128)(2,1)} %refs_0_.1), channel_id=1, source_target_pairs={{0,6},{2,0},{4,2},{6,4},{1,7},{3,1},{5,3},{7,5},{8,14},{10,8},{12,... | collective-permute-start | bytes 196616 | tf_op jit(solution)/shard_map/ppermute | solution.py:192
  12.0 3.2 %collective-permute-start.5 = (bf16[128,256]{1,0:T(8,128)(2,1)}, bf16[128,256]{1,0:T(8,128)(2,1)S(1)}, u32[]{:S(2)}, u32[]{:S(2)}) collective-permute-start(bf16[128,256]{1,0:T(8,128)(2,1)} %refs_4_.1), channel_id=1, source_target_pairs={{0,32},{1,33},{32,0},{33,1},{2,34},{3,35},{34,2},{35,3},{4,36},{5,... | collective-permute-start | bytes 196616 | tf_op jit(solution)/shard_map/ppermute | solution.py:198
  13.5 4.3 %collective-permute-start.4 = (bf16[128,256]{1,0:T(8,128)(2,1)}, bf16[128,256]{1,0:T(8,128)(2,1)S(1)}, u32[]{:S(2)}, u32[]{:S(2)}) collective-permute-start(bf16[128,256]{1,0:T(8,128)(2,1)} %refs_4_.1), channel_id=1, source_target_pairs={{0,1},{1,0},{32,33},{33,32},{2,3},{3,2},{34,35},{35,34},{4,5},{5,4... | collective-permute-start | bytes 196616 | tf_op jit(solution)/shard_map/ppermute | solution.py:198
  14.3 4.9 %collective-permute-start.6 = (bf16[128,256]{1,0:T(8,128)(2,1)}, bf16[128,256]{1,0:T(8,128)(2,1)S(1)}, u32[]{:S(2)}, u32[]{:S(2)}) collective-permute-start(bf16[128,256]{1,0:T(8,128)(2,1)} %refs_4_.1), channel_id=1, source_target_pairs={{0,33},{1,32},{32,1},{33,0},{2,35},{3,34},{34,3},{35,2},{4,37},{5,... | collective-permute-start | bytes 196616 | tf_op jit(solution)/shard_map/ppermute | solution.py:198
  19.2 0.8 copy-start
  20.1 0.8 copy-start.1
  21.0 13.4 %collective-permute-start.9 = (bf16[4,128,256]{2,1,0:T(8,128)(2,1)S(1)}, bf16[4,128,256]{2,1,0:T(8,128)(2,1)S(1)}, u32[]{:S(2)}, u32[]{:S(2)}) collective-permute-start(bf16[4,128,256]{2,1,0:T(8,128)(2,1)S(1)} %get-tuple-element.18.refs_0_), channel_id=1, source_target_pairs={{0,24},{8,0},{16,8},{24,16},{1,25},{9,1},{17,9},{25,17},{2,26},{10... | collective-permute-start | bytes 786440 | tf_op jit(solution)/shard_map/ppermute | solution.py:192
  24.2 0.7 copy-start.2
  24.9 4.6 %collective-permute-start = (s32[3,128]{1,0:T(4,128)S(1)}, s32[3,128]{1,0:T(4,128)S(1)}, u32[]{:S(2)}, u32[]{:S(2)}) collective-permute-start(s32[3,128]{1,0:T(4,128)S(1)} %concatenate.3.mine), channel_id=1, source_target_pairs={{0,1},{1,0},{2,3},{3,2},{4,5},{5,4},{6,7},{7,6},{8,9},{9,8},{10,11... | collective-permute-start | bytes 4616 | tf_op jit(solution)/shard_map/ppermute | solution.py:220
  25.6 14.1 %collective-permute-start.8 = (bf16[4,128,256]{2,1,0:T(8,128)(2,1)S(1)}, bf16[4,128,256]{2,1,0:T(8,128)(2,1)S(1)}, u32[]{:S(2)}, u32[]{:S(2)}) collective-permute-start(bf16[4,128,256]{2,1,0:T(8,128)(2,1)S(1)} %get-tuple-element.18.refs_0_), channel_id=1, source_target_pairs={{0,16},{8,24},{16,0},{24,8},{1,17},{9,25},{17,1},{25,9},{2,18},{10... | collective-permute-start | bytes 786440 | tf_op jit(solution)/shard_map/ppermute | solution.py:192
  26.1 14.8 %collective-permute-start.7 = (bf16[4,128,256]{2,1,0:T(8,128)(2,1)S(1)}, bf16[4,128,256]{2,1,0:T(8,128)(2,1)S(1)}, u32[]{:S(2)}, u32[]{:S(2)}) collective-permute-start(bf16[4,128,256]{2,1,0:T(8,128)(2,1)S(1)} %get-tuple-element.18.refs_0_), channel_id=1, source_target_pairs={{0,8},{8,16},{16,24},{24,0},{1,9},{9,17},{17,25},{25,1},{2,10},{10... | collective-permute-start | bytes 786440 | tf_op jit(solution)/shard_map/ppermute | solution.py:192
  26.7 14.2 %collective-permute-start.12 = (bf16[4,128,256]{2,1,0:T(8,128)(2,1)S(1)}, bf16[4,128,256]{2,1,0:T(8,128)(2,1)S(1)}, u32[]{:S(2)}, u32[]{:S(2)}) collective-permute-start(bf16[4,128,256]{2,1,0:T(8,128)(2,1)S(1)} %get-tuple-element.19.refs_4_), channel_id=1, source_target_pairs={{0,192},{64,0},{128,64},{192,128},{1,193},{65,1},{129,65},{193,129... | collective-permute-start | bytes 786440 | tf_op jit(solution)/shard_map/ppermute | solution.py:192
  29.4 11.5 %collective-permute-start.11 = (bf16[4,128,256]{2,1,0:T(8,128)(2,1)S(1)}, bf16[4,128,256]{2,1,0:T(8,128)(2,1)S(1)}, u32[]{:S(2)}, u32[]{:S(2)}) collective-permute-start(bf16[4,128,256]{2,1,0:T(8,128)(2,1)S(1)} %get-tuple-element.19.refs_4_), channel_id=1, source_target_pairs={{0,128},{64,192},{128,0},{192,64},{1,129},{65,193},{129,1},{193,65... | collective-permute-start | bytes 786440 | tf_op jit(solution)/shard_map/ppermute | solution.py:192
  34.3 9.7 %collective-permute-start.10 = (bf16[4,128,256]{2,1,0:T(8,128)(2,1)S(1)}, bf16[4,128,256]{2,1,0:T(8,128)(2,1)S(1)}, u32[]{:S(2)}, u32[]{:S(2)}) collective-permute-start(bf16[4,128,256]{2,1,0:T(8,128)(2,1)S(1)} %get-tuple-element.19.refs_4_), channel_id=1, source_target_pairs={{0,64},{64,128},{128,192},{192,0},{1,65},{65,129},{129,193},{193,1... | collective-permute-start | bytes 786440 | tf_op jit(solution)/shard_map/ppermute | solution.py:192
  106.1 11.7 %all-to-all-start.3 = ((f32[16,8,128]{2,1,0:T(8,128)}), f32[16,8,128]{2,1,0:T(8,128)S(1)}, u32[]{:S(2)}, u32[]{:S(2)}) async-start(f32[16,8,128]{2,1,0:T(8,128)} %get-tuple-element.25), calls=%async_computation.3 | async-start | bytes 131072 | tf_op jit(solution)/shard_map/all_to_all | solution.py:187
  111.9 3.1 %collective-permute-start.13 = (f32[16,128]{1,0:T(8,128)S(1)}, f32[16,128]{1,0:T(8,128)S(1)}, u32[]{:S(2)}, u32[]{:S(2)}) collective-permute-start(f32[16,128]{1,0:T(8,128)S(1)} %get-tuple-element.27.mine), channel_id=1, source_target_pairs={{0,1},{1,0},{2,3},{3,2},{4,5},{5,4},{6,7},{7,6},{8,9},{9,8},{10,11... | collective-permute-start | bytes 24584 | tf_op jit(solution)/shard_map/ppermute | solution.py:220

commit v5 on v4

--- a/solution.py
+++ b/solution.py
@@ -109,24 +109,32 @@
     return tile
 
 
-def pack_kernel(srcs, *refs):
-    src, tgt = refs[-2:]
-    for n in range(srcs):
-        src[n] = refs[n][...]
-    for n in range(len(refs) - 2 - srcs):
-        tgt[n] = refs[srcs + n][...]
+def pack_kernel(src_mine, tgt_mine, lists, *refs):
+    src, tgt, sems = refs[-3:]
+    sides = src.shape[0] - 1
+    copies = [
+        pltpu.make_async_copy(src_mine, src.at[0], sems.at[0]),
+        pltpu.make_async_copy(tgt_mine, tgt.at[0], sems.at[1]),
+    ]
+    for copy in copies:
+        copy.start()
+    for n in range(sides):
+        src[n + 1] = refs[n][...]
+    for n in range(tgt.shape[0] - 1):
+        tgt[n + 1] = refs[sides + n][...]
+    for copy in copies:
+        copy.wait()
 
 
 def first_kernel(tiles, count, place, *refs):
     pieces, (out, src, tgt, sq_src, sq_tgt, wide, peaks, totals) = refs[:-8], refs[-8:]
     sides = len(pieces) // 2
     for d in range(sides):
-        x, y = (lax.rem(place[axis] + (sides - d), sides) for axis in (0, 2))
-        for n in range(pieces[d].shape[0]):
-            s = lax.rem(place[1] + (sides - n), sides)
+        x = lax.rem(place[0] + (sides - d), sides)
+        core, p = place[4] ^ (d // 2), place[3] ^ (d % 2)
+        for n in range(sides):
+            s, y = (lax.rem(place[axis] + (sides - n), sides) for axis in (1, 2))
             src[x * sides + s] = pieces[d][n]
-        for n in range(pieces[sides + d].shape[0]):
-            p, core = place[3] ^ (n % 2), place[4] ^ (n // 2)
             tgt[p * (2 * sides) + 2 * y + core] = pieces[sides + d][n]
     for b in range(tgt.shape[0]):
         sq_tgt[b : b + 1, :] = square_rows(tgt[b])
@@ -198,19 +206,20 @@
     return [block] + [lax.ppermute(block, axes, [(i, i ^ d) for i in range(n)]) for d in range(1, n)]
 
 
-def bands(src_embed, tgt_embed):
-    src_blocks, tgt_blocks = shifts(src_embed, "s"), swaps(tgt_embed, ("core", "p"))
-    blocks = src_blocks + tgt_blocks
+def bands(src_embed, tgt_embed, lists):
+    src_blocks, tgt_blocks = shifts(src_embed, "s"), shifts(tgt_embed, "y")
+    far = src_blocks[1:] + tgt_blocks[1:]
     src, tgt = pl.pallas_call(
-        functools.partial(pack_kernel, len(src_blocks)),
+        pack_kernel,
         out_shape=[
             jax.ShapeDtypeStruct((len(group),) + group[0].shape, group[0].dtype) for group in (src_blocks, tgt_blocks)
         ],
-        in_specs=[VMEM] * len(blocks),
+        in_specs=[pl.BlockSpec(memory_space=pl.ANY)] * 3 + [VMEM] * len(far),
         out_specs=[VMEM] * 2,
-        compiler_params=PARAMS,
-    )(*blocks)
-    return shifts(src, "x"), shifts(tgt, "y")
+        scratch_shapes=[pltpu.SemaphoreType.DMA((2,))],
+        compiler_params=PARAMS,
+    )(src_embed, tgt_embed, lists, *far)
+    return shifts(src, "x"), swaps(tgt, ("core", "p"))
 
 
 def local(src_embed, tgt_embed, tiles, counts):
@@ -221,7 +230,7 @@
 
     lists = jnp.concatenate([tiles[0, 0], jnp.broadcast_to(counts[0, 0], (1, TILE))], axis=0)
     other_lists = partner(lists)
-    src_pieces, tgt_pieces = bands(src_embed, tgt_embed)
+    src_pieces, tgt_pieces = bands(src_embed, tgt_embed, other_lists)
     picked, count = pl.pallas_call(
         pick_kernel,
         out_shape=[jax.ShapeDtypeStruct((2 * TILE + UNROLL,), jnp.int32), jax.ShapeDtypeStruct((1,), jnp.int32)],

time: 119 us -> 117 us (0.983)
  Pallas kernels: 24.7 us -> 18.8 us
  blocking collectives: 41.9 us -> 46.9 us
  waiting for transfers between devices: 16.7 us -> 12 us
  starting transfers between devices: 31.3 us -> 34.7 us
    pallas_call x4, Pallas kernels: 20.2 us -> 14.1 us  [half_step(): pl.pallas_call(kernel, out_shape=[s if isinstance(s, jax.ShapeDtypeStruct...]
    all_to_all x3, blocking collectives: 41.9 us -> 46.9 us  [exchange(): return lax.all_to_all(copies, peers, 0, 0, tiled=True)]
    ppermute x3, waiting for transfers between devices: 4.04 us -> 0.89 us  [swaps(): lax.ppermute(block, axes, [(i, i ^ d) for i in range(n)])]
    ppermute x3, starting transfers between devices: 3.15 us -> 4.94 us  [swaps(): lax.ppermute(block, axes, [(i, i ^ d) for i in range(n)])]
    ppermute x9, waiting for transfers between devices: 8.21 us -> 6.68 us  [shifts(): lax.ppermute(block, axis, [(i, (i + d) % n) for i in range(n)])]
  transfers between devices with their start and end apart: 15 -> 15, of which waited for: 7 -> 6; matrix products, arithmetic and copies ran while one was open for 0% -> 0% of each run, Pallas kernels for 3% -> 3%
where the time goes in v5:
time: 117 us; the launch traced here: 116 us
  blocking collectives  46.9 us (40%)
  starting transfers between devices  34.7 us (30%)
  Pallas kernels  18.8 us (16%)
  waiting for transfers between devices  12 us (10%)
  local copies, waits for them, and re-layouts  2.44 us (2%)
  between operations  1.35 us (1%)
    all_to_all x3, blocking collectives, exchange(): return lax.all_to_all(copies, peers, 0, 0, tiled=True)  46.9 us
    ppermute x9, starting transfers between devices, shifts(): lax.ppermute(block, axis, [(i, (i + d) % n) for i in range(n)])  20.7 us
    pallas_call x4, Pallas kernels, half_step(): pl.pallas_call(kernel, out_shape=[s if isinstance(s, jax.ShapeDtypeStruct...  14.1 us
    all_to_all x1, starting transfers between devices, exchange(): return lax.all_to_all(copies, peers, 0, 0, tiled=True)  6.95 us
    ppermute x9, waiting for transfers between devices, shifts(): lax.ppermute(block, axis, [(i, (i + d) % n) for i in range(n)])  6.68 us
    ppermute x3, starting transfers between devices, swaps(): lax.ppermute(block, axes, [(i, i ^ d) for i in range(n)])  4.94 us
    pallas_call x1, Pallas kernels, local(): pl.pallas_call(pick_kernel, out_shape=[jax.ShapeDtypeStruct((2 * TILE + U...  3.9 us
    all_to_all x1, waiting for transfers between devices, exchange(): return lax.all_to_all(copies, peers, 0, 0, tiled=True)  2.77 us
  transfers between devices with their start and end apart: 15, of which 6 were waited for; matrix products, arithmetic and copies ran while one was open for 0% of the time, Pallas kernels for 3%

profile of v5, /device:TPU:1, one launch (start us, length us, event | category | flops | bytes accessed | tf_op | source)
XLA Modules:
  0.0 116.2 jit_solution(5451320495258023637)
XLA Ops:
  0.6 7.8 %collective-permute-start.2 = (bf16[128,256]{1,0:T(8,128)(2,1)}, bf16[128,256]{1,0:T(8,128)(2,1)S(1)}, u32[]{:S(2)}, u32[]{:S(2)}) collective-permute-start(bf16[128,256]{1,0:T(8,128)(2,1)} %src_mine.1), channel_id=1, source_target_pairs={{0,4},{2,6},{4,0},{6,2},{1,5},{3,7},{5,1},{7,3},{8,12},{10,14},{12... | collective-permute-start | bytes 196616 | tf_op jit(solution)/shard_map/ppermute | solution.py:200
  9.1 0.0 copy-start.2
  9.1 0.7 copy-done.2
  9.8 0.7 collective-permute-start
  10.5 1.2 %collective-permute-start.1 = (bf16[128,256]{1,0:T(8,128)(2,1)}, bf16[128,256]{1,0:T(8,128)(2,1)S(1)}, u32[]{:S(2)}, u32[]{:S(2)}) collective-permute-start(bf16[128,256]{1,0:T(8,128)(2,1)} %src_mine.1), channel_id=1, source_target_pairs={{0,2},{2,4},{4,6},{6,0},{1,3},{3,5},{5,7},{7,1},{8,10},{10,12},{12... | collective-permute-start | bytes 196616 | tf_op jit(solution)/shard_map/ppermute | solution.py:200
  11.7 2.4 %collective-permute-start.3 = (bf16[128,256]{1,0:T(8,128)(2,1)}, bf16[128,256]{1,0:T(8,128)(2,1)S(1)}, u32[]{:S(2)}, u32[]{:S(2)}) collective-permute-start(bf16[128,256]{1,0:T(8,128)(2,1)} %src_mine.1), channel_id=1, source_target_pairs={{0,6},{2,0},{4,2},{6,4},{1,7},{3,1},{5,3},{7,5},{8,14},{10,8},{12,... | collective-permute-start | bytes 196616 | tf_op jit(solution)/shard_map/ppermute | solution.py:200
  14.1 2.9 %collective-permute-start.5 = (bf16[128,256]{1,0:T(8,128)(2,1)}, bf16[128,256]{1,0:T(8,128)(2,1)S(1)}, u32[]{:S(2)}, u32[]{:S(2)}) collective-permute-start(bf16[128,256]{1,0:T(8,128)(2,1)} %tgt_mine.1), channel_id=1, source_target_pairs={{0,128},{64,192},{128,0},{192,64},{1,129},{65,193},{129,1},{193,65... | collective-permute-start | bytes 196616 | tf_op jit(solution)/shard_map/ppermute | solution.py:200
  17.0 0.0 collective-permute-done.other.lists
  17.0 0.4 collective-permute-start.4
  17.4 0.0 collective-permute-done.2.refs_1_
  17.4 2.3 %collective-permute-start.6 = (bf16[128,256]{1,0:T(8,128)(2,1)}, bf16[128,256]{1,0:T(8,128)(2,1)S(1)}, u32[]{:S(2)}, u32[]{:S(2)}) collective-permute-start(bf16[128,256]{1,0:T(8,128)(2,1)} %tgt_mine.1), channel_id=1, source_target_pairs={{0,192},{64,0},{128,64},{192,128},{1,193},{65,1},{129,65},{193,129... | collective-permute-start | bytes 196616 | tf_op jit(solution)/shard_map/ppermute | solution.py:200
  19.7 0.0 collective-permute-done.1.refs_0_
  19.7 0.0 collective-permute-done.3.refs_2_
  19.7 0.0 collective-permute-done.5.refs_4_
  19.7 2.3 %collective-permute-done.4.refs_3_ = bf16[128,256]{1,0:T(8,128)(2,1)S(1)} collective-permute-done((bf16[128,256]{1,0:T(8,128)(2,1)}, bf16[128,256]{1,0:T(8,128)(2,1)S(1)}, u32[]{:S(2)}, u32[]{:S(2)}) %collective-permute-start.4) | collective-permute-done | bytes 65568 | tf_op jit(solution)/shard_map/ppermute | solution.py:200
  22.0 0.0 collective-permute-done.6.refs_5_
  22.0 0.0 copy-start
  22.0 0.8 copy-done
  22.9 0.0 copy-start.1
  22.9 0.8 copy-done.1
  23.7 0.2 shard_map.60
  23.9 2.6 %collective-permute-start.9 = (bf16[4,128,256]{2,1,0:T(8,128)(2,1)S(1)}, bf16[4,128,256]{2,1,0:T(8,128)(2,1)S(1)}, u32[]{:S(2)}, u32[]{:S(2)}) collective-permute-start(bf16[4,128,256]{2,1,0:T(8,128)(2,1)S(1)} %get-tuple-element.18.refs_0_), channel_id=1, source_target_pairs={{0,24},{8,0},{16,8},{24,16},{1,25},{9,1},{17,9},{25,17},{2,26},{10... | collective-permute-start | bytes 786440 | tf_op jit(solution)/shard_map/ppermute | solution.py:200
  26.5 0.5 collective-permute-start.8
  27.0 0.6 collective-permute-start.7
  27.6 4.2 %collective-permute-start.12 = (bf16[4,128,256]{2,1,0:T(8,128)(2,1)S(1)}, bf16[4,128,256]{2,1,0:T(8,128)(2,1)S(1)}, u32[]{:S(2)}, u32[]{:S(2)}) collective-permute-start(bf16[4,128,256]{2,1,0:T(8,128)(2,1)S(1)} %get-tuple-element.19.refs_4_), channel_id=1, source_target_pairs={{0,33},{1,32},{32,1},{33,0},{2,35},{3,34},{34,3},{35,2},{4,37},{5,... | collective-permute-start | bytes 786440 | tf_op jit(solution)/shard_map/ppermute | solution.py:206
  31.8 0.0 collective-permute-start.11
  31.8 0.5 collective-permute-done.9.refs_3_
  32.3 0.7 collective-permute-start.10
  33.0 0.1 stack.20.place
  33.1 3.9 %shard_map.59 = (s32[272]{0:T(512)S(1)}, s32[1]{0:T(128)}) custom-call(s32[3,128]{1,0:T(4,128)S(1)} %concatenate.3.mine, s32[3,128]{1,0:T(4,128)S(1)} %collective-permute-done.other.lists, s32[1]{0:T(128)} %bitcast.parity), custom_call_target="tpu_custom_call" | custom-call | tf_op jit(solution)/shard_map/pallas_call | solution.py:234
  37.0 0.0 collective-permute-done.8.refs_2_
  37.0 3.9 %collective-permute-done.7.refs_1_ = bf16[4,128,256]{2,1,0:T(8,128)(2,1)S(1)} collective-permute-done((bf16[4,128,256]{2,1,0:T(8,128)(2,1)S(1)}, bf16[4,128,256]{2,1,0:T(8,128)(2,1)S(1)}, u32[]{:S(2)}, u32[]{:S(2)}) %collective-permute-start.7) | collective-permute-done | bytes 262176 | tf_op jit(solution)/shard_map/ppermute | solution.py:200
  40.9 0.0 collective-permute-done.12.refs_7_
  40.9 0.0 collective-permute-done.11.refs_6_
  40.9 0.9 collective-permute-done.10.refs_5_
  41.8 3.8 %shard_map.61 = (f32[16,16,128]{2,1,0:T(8,128)S(1)}, bf16[16,128,256]{2,1,0:T(8,128)(2,1)S(1)}, bf16[16,128,256]{2,1,0:T(8,128)(2,1)S(1)}, f32[16,128]{1,0:T(8,128)S(1)}, f32[16,128]{1,0:T(8,128)S(1)}) custom-call(s32[272]{0:T(512)S(1)} %get-tuple-element.16.tiles, s32[1]{0:T(128)} %get-tuple-element.17.count, s32[5]{0:T(128)S(1)} %stack.20.place, ...), custom_call_target="tpu_custom_call" | custom-call | tf_op jit(solution)/shard_map/pallas_call | solution.py:180
  45.6 16.1 %all_to_all.20.parts = f32[16,16,128]{2,1,0:T(8,128)S(1)} all-to-all(f32[16,16,128]{2,1,0:T(8,128)S(1)} %get-tuple-element.22), channel_id=1, replica_groups=mesh['y'=4,'core'=2,'x'=4,'s'=4,'p'=2] {'x','s'}, dimensions={0} | all-to-all | bytes 262144 | tf_op jit(solution)/shard_map/all_to_all | solution.py:195
  61.7 3.6 %shard_map.62 = (f32[16,16,128]{2,1,0:T(8,128)S(1)}, f32[16,128]{1,0:T(8,128)}) custom-call(s32[272]{0:T(512)S(1)} %get-tuple-element.16.tiles, s32[1]{0:T(128)} %get-tuple-element.17.count, bf16[16,128,256]{2,1,0:T(8,128)(2,1)S(1)} %get-tuple-element.20.src, bf16[16,128,256]{2,1,0:T(8,128)(2,1)S(1)} %get-tuple-element.21.tgt, ...), custom_call_target="tpu_custom_call" | custom-call | tf_op jit(solution)/shard_map/pallas_call | solution.py:180
  65.3 16.8 %all_to_all.21.parts = f32[16,16,128]{2,1,0:T(8,128)S(1)} all-to-all(f32[16,16,128]{2,1,0:T(8,128)S(1)} %get-tuple-element.24), channel_id=1, replica_groups=mesh['y'=4,'core'=2,'x'=4,'s'=4,'p'=2] {'p','y','core'}, dimensions={0} | all-to-all | bytes 262144 | tf_op jit(solution)/shard_map/all_to_all | solution.py:195
  82.1 3.0 %shard_map.63 = f32[16,16,128]{2,1,0:T(8,128)S(1)} custom-call(s32[272]{0:T(512)S(1)} %get-tuple-element.16.tiles, s32[1]{0:T(128)} %get-tuple-element.17.count, bf16[16,128,256]{2,1,0:T(8,128)(2,1)S(1)} %get-tuple-element.20.src, bf16[16,128,256]{2,1,0:T(8,128)(2,1)S(1)} %get-tuple-element.21.tgt, f32[16,16,128]{2,1,0:T(8,128)S(1)} %all_to_all.21.parts), custom_call_target="tpu_custom_call" | custom-call | tf_op jit(solution)/shard_map/pallas_call | solution.py:180
  85.1 14.0 %all_to_all.22.parts = f32[16,16,128]{2,1,0:T(8,128)S(1)} all-to-all(f32[16,16,128]{2,1,0:T(8,128)S(1)} %shard_map.63), channel_id=1, replica_groups=mesh['y'=4,'core'=2,'x'=4,'s'=4,'p'=2] {'x','s'}, dimensions={0} | all-to-all | bytes 262144 | tf_op jit(solution)/shard_map/all_to_all | solution.py:195
  99.2 3.7 %shard_map.64 = (f32[16,8,128]{2,1,0:T(8,128)}, f32[16,128]{1,0:T(8,128)S(1)}) custom-call(s32[272]{0:T(512)S(1)} %get-tuple-element.16.tiles, s32[1]{0:T(128)} %get-tuple-element.17.count, bf16[16,128,256]{2,1,0:T(8,128)(2,1)S(1)} %get-tuple-element.20.src, bf16[16,128,256]{2,1,0:T(8,128)(2,1)S(1)} %get-tuple-element.21.tgt, ...), custom_call_target="tpu_custom_call" | custom-call | tf_op jit(solution)/shard_map/pallas_call | solution.py:180
  102.8 6.9 %all-to-all-start.3 = ((f32[16,8,128]{2,1,0:T(8,128)}), f32[16,8,128]{2,1,0:T(8,128)S(1)}, u32[]{:S(2)}, u32[]{:S(2)}) async-start(f32[16,8,128]{2,1,0:T(8,128)} %get-tuple-element.25), calls=%async_computation.3 | async-start | bytes 131072 | tf_op jit(solution)/shard_map/all_to_all | solution.py:195
  109.8 1.4 %collective-permute-start.13 = (f32[16,128]{1,0:T(8,128)S(1)}, f32[16,128]{1,0:T(8,128)S(1)}, u32[]{:S(2)}, u32[]{:S(2)}) collective-permute-start(f32[16,128]{1,0:T(8,128)S(1)} %get-tuple-element.27.mine), channel_id=1, source_target_pairs={{0,1},{1,0},{2,3},{3,2},{4,5},{5,4},{6,7},{7,6},{8,9},{9,8},{10,11... | collective-permute-start | bytes 24584 | tf_op jit(solution)/shard_map/ppermute | solution.py:229
  111.2 1.7 %collective-permute-done.13.other = f32[16,128]{1,0:T(8,128)S(1)} collective-permute-done((f32[16,128]{1,0:T(8,128)S(1)}, f32[16,128]{1,0:T(8,128)S(1)}, u32[]{:S(2)}, u32[]{:S(2)}) %collective-permute-start.13) | collective-permute-done | bytes 8224 | tf_op jit(solution)/shard_map/ppermute | solution.py:229
  112.8 2.8 %all-to-all-done.3.parts = f32[16,8,128]{2,1,0:T(8,128)S(1)} async-done(((f32[16,8,128]{2,1,0:T(8,128)}), f32[16,8,128]{2,1,0:T(8,128)S(1)}, u32[]{:S(2)}, u32[]{:S(2)}) %all-to-all-start.3) | async-done | bytes 65568 | tf_op jit(solution)/shard_map/all_to_all | solution.py:195
  115.6 0.6 shard_map.65
  (1 shorter events, 0.0 us)
Async XLA Ops:
  0.6 16.8 %collective-permute-start.2 = (bf16[128,256]{1,0:T(8,128)(2,1)}, bf16[128,256]{1,0:T(8,128)(2,1)S(1)}, u32[]{:S(2)}, u32[]{:S(2)}) collective-permute-start(bf16[128,256]{1,0:T(8,128)(2,1)} %src_mine.1), channel_id=1, source_target_pairs={{0,4},{2,6},{4,0},{6,2},{1,5},{3,7},{5,1},{7,3},{8,12},{10,14},{12... | collective-permute-start | bytes 196616 | tf_op jit(solution)/shard_map/ppermute | solution.py:200
  9.1 0.7 copy-start.2
  9.8 7.2 %collective-permute-start = (s32[3,128]{1,0:T(4,128)S(1)}, s32[3,128]{1,0:T(4,128)S(1)}, u32[]{:S(2)}, u32[]{:S(2)}) collective-permute-start(s32[3,128]{1,0:T(4,128)S(1)} %concatenate.3.mine), channel_id=1, source_target_pairs={{0,1},{1,0},{2,3},{3,2},{4,5},{5,4},{6,7},{7,6},{8,9},{9,8},{10,11... | collective-permute-start | bytes 4616 | tf_op jit(solution)/shard_map/ppermute | solution.py:229
  10.5 9.2 %collective-permute-start.1 = (bf16[128,256]{1,0:T(8,128)(2,1)}, bf16[128,256]{1,0:T(8,128)(2,1)S(1)}, u32[]{:S(2)}, u32[]{:S(2)}) collective-permute-start(bf16[128,256]{1,0:T(8,128)(2,1)} %src_mine.1), channel_id=1, source_target_pairs={{0,2},{2,4},{4,6},{6,0},{1,3},{3,5},{5,7},{7,1},{8,10},{10,12},{12... | collective-permute-start | bytes 196616 | tf_op jit(solution)/shard_map/ppermute | solution.py:200
  11.7 8.0 %collective-permute-start.3 = (bf16[128,256]{1,0:T(8,128)(2,1)}, bf16[128,256]{1,0:T(8,128)(2,1)S(1)}, u32[]{:S(2)}, u32[]{:S(2)}) collective-permute-start(bf16[128,256]{1,0:T(8,128)(2,1)} %src_mine.1), channel_id=1, source_target_pairs={{0,6},{2,0},{4,2},{6,4},{1,7},{3,1},{5,3},{7,5},{8,14},{10,8},{12,... | collective-permute-start | bytes 196616 | tf_op jit(solution)/shard_map/ppermute | solution.py:200
  14.1 5.6 %collective-permute-start.5 = (bf16[128,256]{1,0:T(8,128)(2,1)}, bf16[128,256]{1,0:T(8,128)(2,1)S(1)}, u32[]{:S(2)}, u32[]{:S(2)}) collective-permute-start(bf16[128,256]{1,0:T(8,128)(2,1)} %tgt_mine.1), channel_id=1, source_target_pairs={{0,128},{64,192},{128,0},{192,64},{1,129},{65,193},{129,1},{193,65... | collective-permute-start | bytes 196616 | tf_op jit(solution)/shard_map/ppermute | solution.py:200
  17.0 5.0 %collective-permute-start.4 = (bf16[128,256]{1,0:T(8,128)(2,1)}, bf16[128,256]{1,0:T(8,128)(2,1)S(1)}, u32[]{:S(2)}, u32[]{:S(2)}) collective-permute-start(bf16[128,256]{1,0:T(8,128)(2,1)} %tgt_mine.1), channel_id=1, source_target_pairs={{0,64},{64,128},{128,192},{192,0},{1,65},{65,129},{129,193},{193,1... | collective-permute-start | bytes 196616 | tf_op jit(solution)/shard_map/ppermute | solution.py:200
  17.4 4.6 %collective-permute-start.6 = (bf16[128,256]{1,0:T(8,128)(2,1)}, bf16[128,256]{1,0:T(8,128)(2,1)S(1)}, u32[]{:S(2)}, u32[]{:S(2)}) collective-permute-start(bf16[128,256]{1,0:T(8,128)(2,1)} %tgt_mine.1), channel_id=1, source_target_pairs={{0,192},{64,0},{128,64},{192,128},{1,193},{65,1},{129,65},{193,129... | collective-permute-start | bytes 196616 | tf_op jit(solution)/shard_map/ppermute | solution.py:200
  22.0 0.8 copy-start
  22.9 0.8 copy-start.1
  23.9 8.4 %collective-permute-start.9 = (bf16[4,128,256]{2,1,0:T(8,128)(2,1)S(1)}, bf16[4,128,256]{2,1,0:T(8,128)(2,1)S(1)}, u32[]{:S(2)}, u32[]{:S(2)}) collective-permute-start(bf16[4,128,256]{2,1,0:T(8,128)(2,1)S(1)} %get-tuple-element.18.refs_0_), channel_id=1, source_target_pairs={{0,24},{8,0},{16,8},{24,16},{1,25},{9,1},{17,9},{25,17},{2,26},{10... | collective-permute-start | bytes 786440 | tf_op jit(solution)/shard_map/ppermute | solution.py:200
  26.5 10.5 %collective-permute-start.8 = (bf16[4,128,256]{2,1,0:T(8,128)(2,1)S(1)}, bf16[4,128,256]{2,1,0:T(8,128)(2,1)S(1)}, u32[]{:S(2)}, u32[]{:S(2)}) collective-permute-start(bf16[4,128,256]{2,1,0:T(8,128)(2,1)S(1)} %get-tuple-element.18.refs_0_), channel_id=1, source_target_pairs={{0,16},{8,24},{16,0},{24,8},{1,17},{9,25},{17,1},{25,9},{2,18},{10... | collective-permute-start | bytes 786440 | tf_op jit(solution)/shard_map/ppermute | solution.py:200
  27.0 13.9 %collective-permute-start.7 = (bf16[4,128,256]{2,1,0:T(8,128)(2,1)S(1)}, bf16[4,128,256]{2,1,0:T(8,128)(2,1)S(1)}, u32[]{:S(2)}, u32[]{:S(2)}) collective-permute-start(bf16[4,128,256]{2,1,0:T(8,128)(2,1)S(1)} %get-tuple-element.18.refs_0_), channel_id=1, source_target_pairs={{0,8},{8,16},{16,24},{24,0},{1,9},{9,17},{17,25},{25,1},{2,10},{10... | collective-permute-start | bytes 786440 | tf_op jit(solution)/shard_map/ppermute | solution.py:200
  27.6 13.3 %collective-permute-start.12 = (bf16[4,128,256]{2,1,0:T(8,128)(2,1)S(1)}, bf16[4,128,256]{2,1,0:T(8,128)(2,1)S(1)}, u32[]{:S(2)}, u32[]{:S(2)}) collective-permute-start(bf16[4,128,256]{2,1,0:T(8,128)(2,1)S(1)} %get-tuple-element.19.refs_4_), channel_id=1, source_target_pairs={{0,33},{1,32},{32,1},{33,0},{2,35},{3,34},{34,3},{35,2},{4,37},{5,... | collective-permute-start | bytes 786440 | tf_op jit(solution)/shard_map/ppermute | solution.py:206
  31.8 9.1 %collective-permute-start.11 = (bf16[4,128,256]{2,1,0:T(8,128)(2,1)S(1)}, bf16[4,128,256]{2,1,0:T(8,128)(2,1)S(1)}, u32[]{:S(2)}, u32[]{:S(2)}) collective-permute-start(bf16[4,128,256]{2,1,0:T(8,128)(2,1)S(1)} %get-tuple-element.19.refs_4_), channel_id=1, source_target_pairs={{0,32},{1,33},{32,0},{33,1},{2,34},{3,35},{34,2},{35,3},{4,36},{5,... | collective-permute-start | bytes 786440 | tf_op jit(solution)/shard_map/ppermute | solution.py:206
  32.3 9.5 %collective-permute-start.10 = (bf16[4,128,256]{2,1,0:T(8,128)(2,1)S(1)}, bf16[4,128,256]{2,1,0:T(8,128)(2,1)S(1)}, u32[]{:S(2)}, u32[]{:S(2)}) collective-permute-start(bf16[4,128,256]{2,1,0:T(8,128)(2,1)S(1)} %get-tuple-element.19.refs_4_), channel_id=1, source_target_pairs={{0,1},{1,0},{32,33},{33,32},{2,3},{3,2},{34,35},{35,34},{4,5},{5,4... | collective-permute-start | bytes 786440 | tf_op jit(solution)/shard_map/ppermute | solution.py:206
  102.8 12.8 %all-to-all-start.3 = ((f32[16,8,128]{2,1,0:T(8,128)}), f32[16,8,128]{2,1,0:T(8,128)S(1)}, u32[]{:S(2)}, u32[]{:S(2)}) async-start(f32[16,8,128]{2,1,0:T(8,128)} %get-tuple-element.25), calls=%async_computation.3 | async-start | bytes 131072 | tf_op jit(solution)/shard_map/all_to_all | solution.py:195
  109.8 3.1 %collective-permute-start.13 = (f32[16,128]{1,0:T(8,128)S(1)}, f32[16,128]{1,0:T(8,128)S(1)}, u32[]{:S(2)}, u32[]{:S(2)}) collective-permute-start(f32[16,128]{1,0:T(8,128)S(1)} %get-tuple-element.27.mine), channel_id=1, source_target_pairs={{0,1},{1,0},{2,3},{3,2},{4,5},{5,4},{6,7},{7,6},{8,9},{9,8},{10,11... | collective-permute-start | bytes 24584 | tf_op jit(solution)/shard_map/ppermute | solution.py:229

commit v6 on v5

--- a/solution.py
+++ b/solution.py
@@ -109,21 +109,18 @@
     return tile
 
 
-def pack_kernel(src_mine, tgt_mine, lists, *refs):
-    src, tgt, sems = refs[-3:]
-    sides = src.shape[0] - 1
-    copies = [
-        pltpu.make_async_copy(src_mine, src.at[0], sems.at[0]),
-        pltpu.make_async_copy(tgt_mine, tgt.at[0], sems.at[1]),
-    ]
-    for copy in copies:
-        copy.start()
+def own_kernel(src_mine, tgt_mine, src, tgt):
+    src[...] = src_mine[...]
+    tgt[...] = tgt_mine[...]
+
+
+def pack_kernel(lists, *refs):
+    src, tgt = refs[-2:]
+    sides = src.shape[0]
     for n in range(sides):
-        src[n + 1] = refs[n][...]
-    for n in range(tgt.shape[0] - 1):
-        tgt[n + 1] = refs[sides + n][...]
-    for copy in copies:
-        copy.wait()
+        src[n] = refs[n][...]
+    for n in range(tgt.shape[0]):
+        tgt[n] = refs[sides + n][...]
 
 
 def first_kernel(tiles, count, place, *refs):
@@ -131,7 +128,7 @@
     sides = len(pieces) // 2
     for d in range(sides):
         x = lax.rem(place[0] + (sides - d), sides)
-        core, p = place[4] ^ (d // 2), place[3] ^ (d % 2)
+        p, core = place[3] ^ (d // 2), place[4] ^ (d % 2)
         for n in range(sides):
             s, y = (lax.rem(place[axis] + (sides - n), sides) for axis in (1, 2))
             src[x * sides + s] = pieces[d][n]
@@ -201,25 +198,23 @@
     return [block] + [turn(d) for d in range(1, n)]
 
 
-def swaps(block, axes):
-    n = lax.axis_size(axes)
-    return [block] + [lax.ppermute(block, axes, [(i, i ^ d) for i in range(n)]) for d in range(1, n)]
-
-
 def bands(src_embed, tgt_embed, lists):
-    src_blocks, tgt_blocks = shifts(src_embed, "s"), shifts(tgt_embed, "y")
-    far = src_blocks[1:] + tgt_blocks[1:]
+    block = jax.ShapeDtypeStruct(src_embed.shape, src_embed.dtype)
+    own = pl.pallas_call(
+        own_kernel, out_shape=[block] * 2, in_specs=[VMEM] * 2, out_specs=[VMEM] * 2, compiler_params=PARAMS
+    )(src_embed, tgt_embed)
+    src_blocks, tgt_blocks = shifts(src_embed, "s")[1:], shifts(tgt_embed, "y")[1:]
+    blocks = [own[0]] + src_blocks + [own[1]] + tgt_blocks
+    group = jax.ShapeDtypeStruct((1 + len(src_blocks),) + src_embed.shape, src_embed.dtype)
     src, tgt = pl.pallas_call(
         pack_kernel,
-        out_shape=[
-            jax.ShapeDtypeStruct((len(group),) + group[0].shape, group[0].dtype) for group in (src_blocks, tgt_blocks)
-        ],
-        in_specs=[pl.BlockSpec(memory_space=pl.ANY)] * 3 + [VMEM] * len(far),
+        out_shape=[group] * 2,
+        in_specs=[pl.BlockSpec(memory_space=pl.ANY)] + [VMEM] * len(blocks),
         out_specs=[VMEM] * 2,
-        scratch_shapes=[pltpu.SemaphoreType.DMA((2,))],
-        compiler_params=PARAMS,
-    )(src_embed, tgt_embed, lists, *far)
-    return shifts(src, "x"), swaps(tgt, ("core", "p"))
+        compiler_params=PARAMS,
+    )(lists, *blocks)
+    tgt_pieces = [piece for side in shifts(tgt, "p") for piece in shifts(side, "core")]
+    return shifts(src, "x"), tgt_pieces
 
 
 def local(src_embed, tgt_embed, tiles, counts):

time: 117 us -> 115 us (0.983); the launches traced: 116 us -> 117 us
  blocking collectives: 46.9 us -> 39.7 us
  starting transfers between devices: 34.7 us -> 37.6 us
  waiting for transfers between devices: 12 us -> 14.7 us
  Pallas kernels: 18.8 us -> 20.7 us
    all_to_all x3, blocking collectives: 46.9 us -> 39.7 us  [exchange(): return lax.all_to_all(copies, peers, 0, 0, tiled=True)]
    ppermute x3 -> x0, starting transfers between devices: 4.94 us -> none  [swaps(): lax.ppermute(block, axes, [(i, i ^ d) for i in range(n)])]
    ppermute x9 -> x12, starting transfers between devices: 20.7 us -> 24.5 us  [shifts(): lax.ppermute(block, axis, [(i, (i + d) % n) for i in range(n)])]
    ppermute x9 -> x12, waiting for transfers between devices: 6.68 us -> 10.3 us  [shifts(): lax.ppermute(block, axis, [(i, (i + d) % n) for i in range(n)])]
    all_to_all x1, starting transfers between devices: 6.95 us -> 10.1 us  [exchange(): return lax.all_to_all(copies, peers, 0, 0, tiled=True)]
    pallas_call x4, Pallas kernels: 14.1 us -> 16.1 us  [half_step(): pl.pallas_call(kernel, out_shape=[s if isinstance(s, jax.ShapeDtypeStruct...]
  transfers between devices with their start and end apart: 15 -> 15, of which waited for: 6 -> 5; matrix products, arithmetic and copies ran while one was open for 0% -> 0% of each run, Pallas kernels for 3% -> 3%
where the time goes in v6:
time: 115 us; the launch traced here: 117 us
  blocking collectives  39.7 us (35%)
  starting transfers between devices  37.6 us (33%)
  Pallas kernels  20.7 us (18%)
  waiting for transfers between devices  14.7 us (13%)
  local copies, waits for them, and re-layouts  2.44 us (2%)
  between operations  1.37 us (1%)
    all_to_all x3, blocking collectives, exchange(): return lax.all_to_all(copies, peers, 0, 0, tiled=True)  39.7 us
    ppermute x12, starting transfers between devices, shifts(): lax.ppermute(block, axis, [(i, (i + d) % n) for i in range(n)])  24.5 us
    pallas_call x4, Pallas kernels, half_step(): pl.pallas_call(kernel, out_shape=[s if isinstance(s, jax.ShapeDtypeStruct...  16.1 us
    ppermute x12, waiting for transfers between devices, shifts(): lax.ppermute(block, axis, [(i, (i + d) % n) for i in range(n)])  10.3 us
    all_to_all x1, starting transfers between devices, exchange(): return lax.all_to_all(copies, peers, 0, 0, tiled=True)  10.1 us
    pallas_call x1, Pallas kernels, local(): pl.pallas_call(pick_kernel, out_shape=[jax.ShapeDtypeStruct((2 * TILE + U...  3.9 us
    ppermute x2, starting transfers between devices, local(): partner = lambda v: lax.ppermute(v, 'p', [(0, 1), (1, 0)])  3.07 us
    all_to_all x1, waiting for transfers between devices, exchange(): return lax.all_to_all(copies, peers, 0, 0, tiled=True)  2.79 us
  transfers between devices with their start and end apart: 15, of which 5 were waited for; matrix products, arithmetic and copies ran while one was open for 0% of the time, Pallas kernels for 3%

profile of v6, /device:TPU:1, one launch (start us, length us, event | category | flops | bytes accessed | tf_op | source)
XLA Modules:
  0.0 116.5 jit_solution(6184729459795587177)
XLA Ops:
  0.6 3.9 %collective-permute-start.1 = (bf16[128,256]{1,0:T(8,128)(2,1)}, bf16[128,256]{1,0:T(8,128)(2,1)S(1)}, u32[]{:S(2)}, u32[]{:S(2)}) collective-permute-start(bf16[128,256]{1,0:T(8,128)(2,1)} %src_mine.1), channel_id=1, source_target_pairs={{0,2},{2,4},{4,6},{6,0},{1,3},{3,5},{5,7},{7,1},{8,10},{10,12},{12... | collective-permute-start | bytes 196616 | tf_op jit(solution)/shard_map/ppermute | solution.py:197
  5.2 0.0 copy-start.2
  5.2 0.7 copy-done.2
  5.9 1.6 %collective-permute-start = (s32[3,128]{1,0:T(4,128)S(1)}, s32[3,128]{1,0:T(4,128)S(1)}, u32[]{:S(2)}, u32[]{:S(2)}) collective-permute-start(s32[3,128]{1,0:T(4,128)S(1)} %concatenate.3.mine), channel_id=1, source_target_pairs={{0,1},{1,0},{2,3},{3,2},{4,5},{5,4},{6,7},{7,6},{8,9},{9,8},{10,11... | collective-permute-start | bytes 4616 | tf_op jit(solution)/shard_map/ppermute | solution.py:224
  7.5 2.1 %collective-permute-start.3 = (bf16[128,256]{1,0:T(8,128)(2,1)}, bf16[128,256]{1,0:T(8,128)(2,1)S(1)}, u32[]{:S(2)}, u32[]{:S(2)}) collective-permute-start(bf16[128,256]{1,0:T(8,128)(2,1)} %src_mine.1), channel_id=1, source_target_pairs={{0,6},{2,0},{4,2},{6,4},{1,7},{3,1},{5,3},{7,5},{8,14},{10,8},{12,... | collective-permute-start | bytes 196616 | tf_op jit(solution)/shard_map/ppermute | solution.py:197
  9.6 4.5 %collective-permute-start.2 = (bf16[128,256]{1,0:T(8,128)(2,1)}, bf16[128,256]{1,0:T(8,128)(2,1)S(1)}, u32[]{:S(2)}, u32[]{:S(2)}) collective-permute-start(bf16[128,256]{1,0:T(8,128)(2,1)} %src_mine.1), channel_id=1, source_target_pairs={{0,4},{2,6},{4,0},{6,2},{1,5},{3,7},{5,1},{7,3},{8,12},{10,14},{12... | collective-permute-start | bytes 196616 | tf_op jit(solution)/shard_map/ppermute | solution.py:197
  14.1 1.3 %collective-permute-start.4 = (bf16[128,256]{1,0:T(8,128)(2,1)}, bf16[128,256]{1,0:T(8,128)(2,1)S(1)}, u32[]{:S(2)}, u32[]{:S(2)}) collective-permute-start(bf16[128,256]{1,0:T(8,128)(2,1)} %tgt_mine.1), channel_id=1, source_target_pairs={{0,64},{64,128},{128,192},{192,0},{1,65},{65,129},{129,193},{193,1... | collective-permute-start | bytes 196616 | tf_op jit(solution)/shard_map/ppermute | solution.py:197
  15.4 0.0 collective-permute-done.other.lists
  15.4 1.4 %collective-permute-start.6 = (bf16[128,256]{1,0:T(8,128)(2,1)}, bf16[128,256]{1,0:T(8,128)(2,1)S(1)}, u32[]{:S(2)}, u32[]{:S(2)}) collective-permute-start(bf16[128,256]{1,0:T(8,128)(2,1)} %tgt_mine.1), channel_id=1, source_target_pairs={{0,192},{64,0},{128,64},{192,128},{1,193},{65,1},{129,65},{193,129... | collective-permute-start | bytes 196616 | tf_op jit(solution)/shard_map/ppermute | solution.py:197
  16.8 0.0 collective-permute-done.1.refs_1_
  16.8 1.6 %collective-permute-start.5 = (bf16[128,256]{1,0:T(8,128)(2,1)}, bf16[128,256]{1,0:T(8,128)(2,1)S(1)}, u32[]{:S(2)}, u32[]{:S(2)}) collective-permute-start(bf16[128,256]{1,0:T(8,128)(2,1)} %tgt_mine.1), channel_id=1, source_target_pairs={{0,128},{64,192},{128,0},{192,64},{1,129},{65,193},{129,1},{193,65... | collective-permute-start | bytes 196616 | tf_op jit(solution)/shard_map/ppermute | solution.py:197
  18.5 0.0 copy-start
  18.5 0.8 copy-done
  19.3 0.0 copy-start.1
  19.3 0.8 copy-done.1
  20.2 0.0 collective-permute-done.3.refs_3_
  20.2 0.0 collective-permute-done.2.refs_2_
  20.2 0.0 collective-permute-done.4.refs_5_
  20.2 0.0 collective-permute-done.6.refs_7_
  20.2 1.8 %collective-permute-done.5.refs_6_ = bf16[128,256]{1,0:T(8,128)(2,1)S(1)} collective-permute-done((bf16[128,256]{1,0:T(8,128)(2,1)}, bf16[128,256]{1,0:T(8,128)(2,1)S(1)}, u32[]{:S(2)}, u32[]{:S(2)}) %collective-permute-start.5) | collective-permute-done | bytes 65568 | tf_op jit(solution)/shard_map/ppermute | solution.py:197
  22.0 0.8 collective-permute-start.11
  22.8 3.4 %collective-permute-start.10 = (bf16[4,128,256]{2,1,0:T(8,128)(2,1)S(1)}, bf16[4,128,256]{2,1,0:T(8,128)(2,1)S(1)}, u32[]{:S(2)}, u32[]{:S(2)}) collective-permute-start(bf16[4,128,256]{2,1,0:T(8,128)(2,1)S(1)} %get-tuple-element.23.refs_4_), channel_id=1, source_target_pairs={{0,32},{32,0},{1,33},{33,1},{2,34},{34,2},{3,35},{35,3},{4,36},{36... | collective-permute-start | bytes 786440 | tf_op jit(solution)/shard_map/ppermute | solution.py:197
  26.3 2.5 %collective-permute-start.9 = (bf16[4,128,256]{2,1,0:T(8,128)(2,1)S(1)}, bf16[4,128,256]{2,1,0:T(8,128)(2,1)S(1)}, u32[]{:S(2)}, u32[]{:S(2)}) collective-permute-start(bf16[4,128,256]{2,1,0:T(8,128)(2,1)S(1)} %get-tuple-element.22.refs_0_), channel_id=1, source_target_pairs={{0,24},{8,0},{16,8},{24,16},{1,25},{9,1},{17,9},{25,17},{2,26},{10... | collective-permute-start | bytes 786440 | tf_op jit(solution)/shard_map/ppermute | solution.py:197
  28.7 0.5 collective-permute-start.8
  29.3 0.6 collective-permute-start.7
  29.9 0.0 collective-permute-done.11.refs_6_
  29.9 1.8 %collective-permute-start.12 = (bf16[4,128,256]{2,1,0:T(8,128)(2,1)S(1)}, bf16[4,128,256]{2,1,0:T(8,128)(2,1)S(1)}, u32[]{:S(2)}, u32[]{:S(2)}) collective-permute-start(bf16[4,128,256]{2,1,0:T(8,128)(2,1)S(1)} %collective-permute-done.11.refs_6_), channel_id=1, source_target_pairs={{0,32},{32,0},{1,33},{33,1},{2,34},{34,2},{3,35},{35,3},{4,36},{36... | collective-permute-start | bytes 786440 | tf_op jit(solution)/shard_map/ppermute | solution.py:197
  31.6 0.1 stack.20.place
  31.7 3.9 %shard_map.59 = (s32[272]{0:T(512)S(1)}, s32[1]{0:T(128)}) custom-call(s32[3,128]{1,0:T(4,128)S(1)} %concatenate.3.mine, s32[3,128]{1,0:T(4,128)S(1)} %collective-permute-done.other.lists, s32[1]{0:T(128)} %bitcast.parity), custom_call_target="tpu_custom_call" | custom-call | tf_op jit(solution)/shard_map/pallas_call | solution.py:229
  35.6 0.0 collective-permute-done.10.refs_5_
  35.6 4.3 %collective-permute-done.9.refs_3_ = bf16[4,128,256]{2,1,0:T(8,128)(2,1)S(1)} collective-permute-done((bf16[4,128,256]{2,1,0:T(8,128)(2,1)S(1)}, bf16[4,128,256]{2,1,0:T(8,128)(2,1)S(1)}, u32[]{:S(2)}, u32[]{:S(2)}) %collective-permute-start.9) | collective-permute-done | bytes 262176 | tf_op jit(solution)/shard_map/ppermute | solution.py:197
  39.9 0.0 collective-permute-done.8.refs_2_
  39.9 4.1 %collective-permute-done.7.refs_1_ = bf16[4,128,256]{2,1,0:T(8,128)(2,1)S(1)} collective-permute-done((bf16[4,128,256]{2,1,0:T(8,128)(2,1)S(1)}, bf16[4,128,256]{2,1,0:T(8,128)(2,1)S(1)}, u32[]{:S(2)}, u32[]{:S(2)}) %collective-permute-start.7) | collective-permute-done | bytes 262176 | tf_op jit(solution)/shard_map/ppermute | solution.py:197
  44.1 0.0 collective-permute-done.12.refs_7_
  44.1 4.3 %shard_map.62 = (f32[16,16,128]{2,1,0:T(8,128)S(1)}, bf16[16,128,256]{2,1,0:T(8,128)(2,1)S(1)}, bf16[16,128,256]{2,1,0:T(8,128)(2,1)S(1)}, f32[16,128]{1,0:T(8,128)S(1)}, f32[16,128]{1,0:T(8,128)S(1)}) custom-call(s32[272]{0:T(512)S(1)} %get-tuple-element.18.tiles, s32[1]{0:T(128)} %get-tuple-element.19.count, s32[5]{0:T(128)S(1)} %stack.20.place, ...), custom_call_target="tpu_custom_call" | custom-call | tf_op jit(solution)/shard_map/pallas_call | solution.py:177
  48.4 13.2 %all_to_all.20.parts = f32[16,16,128]{2,1,0:T(8,128)S(1)} all-to-all(f32[16,16,128]{2,1,0:T(8,128)S(1)} %get-tuple-element.26), channel_id=1, replica_groups=mesh['y'=4,'core'=2,'x'=4,'s'=4,'p'=2] {'x','s'}, dimensions={0} | all-to-all | bytes 262144 | tf_op jit(solution)/shard_map/all_to_all | solution.py:192
  61.6 4.1 %shard_map.63 = (f32[16,16,128]{2,1,0:T(8,128)S(1)}, f32[16,128]{1,0:T(8,128)}) custom-call(s32[272]{0:T(512)S(1)} %get-tuple-element.18.tiles, s32[1]{0:T(128)} %get-tuple-element.19.count, bf16[16,128,256]{2,1,0:T(8,128)(2,1)S(1)} %get-tuple-element.24.src, bf16[16,128,256]{2,1,0:T(8,128)(2,1)S(1)} %get-tuple-element.25.tgt, ...), custom_call_target="tpu_custom_call" | custom-call | tf_op jit(solution)/shard_map/pallas_call | solution.py:177
  65.7 14.3 %all_to_all.21.parts = f32[16,16,128]{2,1,0:T(8,128)S(1)} all-to-all(f32[16,16,128]{2,1,0:T(8,128)S(1)} %get-tuple-element.28), channel_id=1, replica_groups=mesh['y'=4,'core'=2,'x'=4,'s'=4,'p'=2] {'p','y','core'}, dimensions={0} | all-to-all | bytes 262144 | tf_op jit(solution)/shard_map/all_to_all | solution.py:192
  80.0 3.5 %shard_map.64 = f32[16,16,128]{2,1,0:T(8,128)S(1)} custom-call(s32[272]{0:T(512)S(1)} %get-tuple-element.18.tiles, s32[1]{0:T(128)} %get-tuple-element.19.count, bf16[16,128,256]{2,1,0:T(8,128)(2,1)S(1)} %get-tuple-element.24.src, bf16[16,128,256]{2,1,0:T(8,128)(2,1)S(1)} %get-tuple-element.25.tgt, f32[16,16,128]{2,1,0:T(8,128)S(1)} %all_to_all.21.parts), custom_call_target="tpu_custom_call" | custom-call | tf_op jit(solution)/shard_map/pallas_call | solution.py:177
  83.6 12.2 %all_to_all.22.parts = f32[16,16,128]{2,1,0:T(8,128)S(1)} all-to-all(f32[16,16,128]{2,1,0:T(8,128)S(1)} %shard_map.64), channel_id=1, replica_groups=mesh['y'=4,'core'=2,'x'=4,'s'=4,'p'=2] {'x','s'}, dimensions={0} | all-to-all | bytes 262144 | tf_op jit(solution)/shard_map/all_to_all | solution.py:192
  95.8 4.2 %shard_map.65 = (f32[16,8,128]{2,1,0:T(8,128)}, f32[16,128]{1,0:T(8,128)S(1)}) custom-call(s32[272]{0:T(512)S(1)} %get-tuple-element.18.tiles, s32[1]{0:T(128)} %get-tuple-element.19.count, bf16[16,128,256]{2,1,0:T(8,128)(2,1)S(1)} %get-tuple-element.24.src, bf16[16,128,256]{2,1,0:T(8,128)(2,1)S(1)} %get-tuple-element.25.tgt, ...), custom_call_target="tpu_custom_call" | custom-call | tf_op jit(solution)/shard_map/pallas_call | solution.py:177
  99.9 10.1 %all-to-all-start.3 = ((f32[16,8,128]{2,1,0:T(8,128)}), f32[16,8,128]{2,1,0:T(8,128)S(1)}, u32[]{:S(2)}, u32[]{:S(2)}) async-start(f32[16,8,128]{2,1,0:T(8,128)} %get-tuple-element.29), calls=%async_computation.3 | async-start | bytes 131072 | tf_op jit(solution)/shard_map/all_to_all | solution.py:192
  110.0 1.4 %collective-permute-start.13 = (f32[16,128]{1,0:T(8,128)S(1)}, f32[16,128]{1,0:T(8,128)S(1)}, u32[]{:S(2)}, u32[]{:S(2)}) collective-permute-start(f32[16,128]{1,0:T(8,128)S(1)} %get-tuple-element.31.mine), channel_id=1, source_target_pairs={{0,1},{1,0},{2,3},{3,2},{4,5},{5,4},{6,7},{7,6},{8,9},{9,8},{10,11... | collective-permute-start | bytes 24584 | tf_op jit(solution)/shard_map/ppermute | solution.py:224
  111.4 1.7 %collective-permute-done.13.other = f32[16,128]{1,0:T(8,128)S(1)} collective-permute-done((f32[16,128]{1,0:T(8,128)S(1)}, f32[16,128]{1,0:T(8,128)S(1)}, u32[]{:S(2)}, u32[]{:S(2)}) %collective-permute-start.13) | collective-permute-done | bytes 8224 | tf_op jit(solution)/shard_map/ppermute | solution.py:224
  113.1 2.8 %all-to-all-done.3.parts = f32[16,8,128]{2,1,0:T(8,128)S(1)} async-done(((f32[16,8,128]{2,1,0:T(8,128)}), f32[16,8,128]{2,1,0:T(8,128)S(1)}, u32[]{:S(2)}, u32[]{:S(2)}) %all-to-all-start.3) | async-done | bytes 65568 | tf_op jit(solution)/shard_map/all_to_all | solution.py:192
  115.9 0.6 shard_map.66
  (3 shorter events, 0.0 us)
Async XLA Ops:
  0.6 16.2 %collective-permute-start.1 = (bf16[128,256]{1,0:T(8,128)(2,1)}, bf16[128,256]{1,0:T(8,128)(2,1)S(1)}, u32[]{:S(2)}, u32[]{:S(2)}) collective-permute-start(bf16[128,256]{1,0:T(8,128)(2,1)} %src_mine.1), channel_id=1, source_target_pairs={{0,2},{2,4},{4,6},{6,0},{1,3},{3,5},{5,7},{7,1},{8,10},{10,12},{12... | collective-permute-start | bytes 196616 | tf_op jit(solution)/shard_map/ppermute | solution.py:197
  5.2 0.7 copy-start.2
  5.9 9.5 %collective-permute-start = (s32[3,128]{1,0:T(4,128)S(1)}, s32[3,128]{1,0:T(4,128)S(1)}, u32[]{:S(2)}, u32[]{:S(2)}) collective-permute-start(s32[3,128]{1,0:T(4,128)S(1)} %concatenate.3.mine), channel_id=1, source_target_pairs={{0,1},{1,0},{2,3},{3,2},{4,5},{5,4},{6,7},{7,6},{8,9},{9,8},{10,11... | collective-permute-start | bytes 4616 | tf_op jit(solution)/shard_map/ppermute | solution.py:224
  7.5 12.7 %collective-permute-start.3 = (bf16[128,256]{1,0:T(8,128)(2,1)}, bf16[128,256]{1,0:T(8,128)(2,1)S(1)}, u32[]{:S(2)}, u32[]{:S(2)}) collective-permute-start(bf16[128,256]{1,0:T(8,128)(2,1)} %src_mine.1), channel_id=1, source_target_pairs={{0,6},{2,0},{4,2},{6,4},{1,7},{3,1},{5,3},{7,5},{8,14},{10,8},{12,... | collective-permute-start | bytes 196616 | tf_op jit(solution)/shard_map/ppermute | solution.py:197
  9.6 10.6 %collective-permute-start.2 = (bf16[128,256]{1,0:T(8,128)(2,1)}, bf16[128,256]{1,0:T(8,128)(2,1)S(1)}, u32[]{:S(2)}, u32[]{:S(2)}) collective-permute-start(bf16[128,256]{1,0:T(8,128)(2,1)} %src_mine.1), channel_id=1, source_target_pairs={{0,4},{2,6},{4,0},{6,2},{1,5},{3,7},{5,1},{7,3},{8,12},{10,14},{12... | collective-permute-start | bytes 196616 | tf_op jit(solution)/shard_map/ppermute | solution.py:197
  14.1 6.1 %collective-permute-start.4 = (bf16[128,256]{1,0:T(8,128)(2,1)}, bf16[128,256]{1,0:T(8,128)(2,1)S(1)}, u32[]{:S(2)}, u32[]{:S(2)}) collective-permute-start(bf16[128,256]{1,0:T(8,128)(2,1)} %tgt_mine.1), channel_id=1, source_target_pairs={{0,64},{64,128},{128,192},{192,0},{1,65},{65,129},{129,193},{193,1... | collective-permute-start | bytes 196616 | tf_op jit(solution)/shard_map/ppermute | solution.py:197
  15.4 4.8 %collective-permute-start.6 = (bf16[128,256]{1,0:T(8,128)(2,1)}, bf16[128,256]{1,0:T(8,128)(2,1)S(1)}, u32[]{:S(2)}, u32[]{:S(2)}) collective-permute-start(bf16[128,256]{1,0:T(8,128)(2,1)} %tgt_mine.1), channel_id=1, source_target_pairs={{0,192},{64,0},{128,64},{192,128},{1,193},{65,1},{129,65},{193,129... | collective-permute-start | bytes 196616 | tf_op jit(solution)/shard_map/ppermute | solution.py:197
  16.8 5.1 %collective-permute-start.5 = (bf16[128,256]{1,0:T(8,128)(2,1)}, bf16[128,256]{1,0:T(8,128)(2,1)S(1)}, u32[]{:S(2)}, u32[]{:S(2)}) collective-permute-start(bf16[128,256]{1,0:T(8,128)(2,1)} %tgt_mine.1), channel_id=1, source_target_pairs={{0,128},{64,192},{128,0},{192,64},{1,129},{65,193},{129,1},{193,65... | collective-permute-start | bytes 196616 | tf_op jit(solution)/shard_map/ppermute | solution.py:197
  18.5 0.8 copy-start
  19.3 0.8 copy-start.1
  22.0 7.8 %collective-permute-start.11 = (bf16[4,128,256]{2,1,0:T(8,128)(2,1)S(1)}, bf16[4,128,256]{2,1,0:T(8,128)(2,1)S(1)}, u32[]{:S(2)}, u32[]{:S(2)}) collective-permute-start(bf16[4,128,256]{2,1,0:T(8,128)(2,1)S(1)} %get-tuple-element.23.refs_4_), channel_id=1, source_target_pairs={{0,1},{1,0},{2,3},{3,2},{4,5},{5,4},{6,7},{7,6},{8,9},{9,8},{10,11... | collective-permute-start | bytes 786440 | tf_op jit(solution)/shard_map/ppermute | solution.py:197
  22.8 12.8 %collective-permute-start.10 = (bf16[4,128,256]{2,1,0:T(8,128)(2,1)S(1)}, bf16[4,128,256]{2,1,0:T(8,128)(2,1)S(1)}, u32[]{:S(2)}, u32[]{:S(2)}) collective-permute-start(bf16[4,128,256]{2,1,0:T(8,128)(2,1)S(1)} %get-tuple-element.23.refs_4_), channel_id=1, source_target_pairs={{0,32},{32,0},{1,33},{33,1},{2,34},{34,2},{3,35},{35,3},{4,36},{36... | collective-permute-start | bytes 786440 | tf_op jit(solution)/shard_map/ppermute | solution.py:197
  26.3 13.7 %collective-permute-start.9 = (bf16[4,128,256]{2,1,0:T(8,128)(2,1)S(1)}, bf16[4,128,256]{2,1,0:T(8,128)(2,1)S(1)}, u32[]{:S(2)}, u32[]{:S(2)}) collective-permute-start(bf16[4,128,256]{2,1,0:T(8,128)(2,1)S(1)} %get-tuple-element.22.refs_0_), channel_id=1, source_target_pairs={{0,24},{8,0},{16,8},{24,16},{1,25},{9,1},{17,9},{25,17},{2,26},{10... | collective-permute-start | bytes 786440 | tf_op jit(solution)/shard_map/ppermute | solution.py:197
  28.7 11.2 %collective-permute-start.8 = (bf16[4,128,256]{2,1,0:T(8,128)(2,1)S(1)}, bf16[4,128,256]{2,1,0:T(8,128)(2,1)S(1)}, u32[]{:S(2)}, u32[]{:S(2)}) collective-permute-start(bf16[4,128,256]{2,1,0:T(8,128)(2,1)S(1)} %get-tuple-element.22.refs_0_), channel_id=1, source_target_pairs={{0,16},{8,24},{16,0},{24,8},{1,17},{9,25},{17,1},{25,9},{2,18},{10... | collective-permute-start | bytes 786440 | tf_op jit(solution)/shard_map/ppermute | solution.py:197
  29.3 14.8 %collective-permute-start.7 = (bf16[4,128,256]{2,1,0:T(8,128)(2,1)S(1)}, bf16[4,128,256]{2,1,0:T(8,128)(2,1)S(1)}, u32[]{:S(2)}, u32[]{:S(2)}) collective-permute-start(bf16[4,128,256]{2,1,0:T(8,128)(2,1)S(1)} %get-tuple-element.22.refs_0_), channel_id=1, source_target_pairs={{0,8},{8,16},{16,24},{24,0},{1,9},{9,17},{17,25},{25,1},{2,10},{10... | collective-permute-start | bytes 786440 | tf_op jit(solution)/shard_map/ppermute | solution.py:197
  29.9 14.2 %collective-permute-start.12 = (bf16[4,128,256]{2,1,0:T(8,128)(2,1)S(1)}, bf16[4,128,256]{2,1,0:T(8,128)(2,1)S(1)}, u32[]{:S(2)}, u32[]{:S(2)}) collective-permute-start(bf16[4,128,256]{2,1,0:T(8,128)(2,1)S(1)} %collective-permute-done.11.refs_6_), channel_id=1, source_target_pairs={{0,32},{32,0},{1,33},{33,1},{2,34},{34,2},{3,35},{35,3},{4,36},{36... | collective-permute-start | bytes 786440 | tf_op jit(solution)/shard_map/ppermute | solution.py:197
  99.9 16.0 %all-to-all-start.3 = ((f32[16,8,128]{2,1,0:T(8,128)}), f32[16,8,128]{2,1,0:T(8,128)S(1)}, u32[]{:S(2)}, u32[]{:S(2)}) async-start(f32[16,8,128]{2,1,0:T(8,128)} %get-tuple-element.29), calls=%async_computation.3 | async-start | bytes 131072 | tf_op jit(solution)/shard_map/all_to_all | solution.py:192
  110.0 3.1 %collective-permute-start.13 = (f32[16,128]{1,0:T(8,128)S(1)}, f32[16,128]{1,0:T(8,128)S(1)}, u32[]{:S(2)}, u32[]{:S(2)}) collective-permute-start(f32[16,128]{1,0:T(8,128)S(1)} %get-tuple-element.31.mine), channel_id=1, source_target_pairs={{0,1},{1,0},{2,3},{3,2},{4,5},{5,4},{6,7},{7,6},{8,9},{9,8},{10,11... | collective-permute-start | bytes 24584 | tf_op jit(solution)/shard_map/ppermute | solution.py:224

commit v7 on v6

--- a/solution.py
+++ b/solution.py
@@ -23,6 +23,7 @@
 NT = (((1,), (1,)), ((), ()))
 VMEM = pl.BlockSpec(memory_space=pltpu.VMEM)
 SMEM = pl.BlockSpec(memory_space=pltpu.SMEM)
+ANY = pl.BlockSpec(memory_space=pl.ANY)
 PARAMS = pltpu.CompilerParams(vmem_limit_bytes=24 * 2**20)
 
 
@@ -78,33 +79,39 @@
     return jnp.concatenate(rows, axis=0)
 
 
-def pick_kernel(mine, other, parity, picked, total):
-    p = parity[0]
+def pick_kernel(mine, other, place, picked):
+    p = place[3]
     targets = 8
 
     def scan(lists, col, start):
         def step(k, at):
             a, b = lists[0, k], lists[1, k]
-            picked[at] = (a // 2) * (2 * targets) + col * targets + b
+            picked[1 + at // TILE, at % TILE] = (a // 2) * (2 * targets) + col * targets + b
             return at + jnp.where((k < lists[2, 0]) & (a % 2 == p), 1, 0)
 
         return lax.fori_loop(0, TILE, step, start, unroll=8)
 
-    total[0] = scan(other, 1 - p, scan(mine, p, 0))
+    picked[0, 0] = scan(other, 1 - p, scan(mine, p, 0))
+    for n in range(place.shape[0]):
+        picked[0, 1 + n] = place[n]
+
+
+def tile_code(tiles, k):
+    return tiles[1 + k // TILE, k % TILE]
 
 
 def source_tiles(tiles, tgt_blocks):
     def tile(k):
-        code = tiles[k]
-        return lax.rem(code, tgt_blocks), lax.div(code, tgt_blocks)
+        code = tile_code(tiles, k)
+        return code % tgt_blocks, code // tgt_blocks
 
     return tile
 
 
 def target_tiles(tiles, tgt_blocks):
     def tile(k):
-        code = tiles[k]
-        return lax.div(code, tgt_blocks), lax.rem(code, tgt_blocks)
+        code = tile_code(tiles, k)
+        return code // tgt_blocks, code % tgt_blocks
 
     return tile
 
@@ -123,36 +130,56 @@
         tgt[n] = refs[sides + n][...]
 
 
-def first_kernel(tiles, count, place, *refs):
-    pieces, (out, src, tgt, sq_src, sq_tgt, wide, peaks, totals) = refs[:-8], refs[-8:]
-    sides = len(pieces) // 2
+def join_kernel(*refs):
+    blocks = refs[0].shape[0]
+    for n, piece in enumerate(refs[:-1]):
+        refs[-1][n * blocks : (n + 1) * blocks] = piece[...]
+
+
+def first_kernel(picked, *refs):
+    pieces, (out, src, tgt, sq_src, sq_tgt, wide, peaks, totals, tiles, sem) = refs[:-10], refs[-10:]
+    fetch = pltpu.make_async_copy(picked, tiles, sem)
+    fetch.start()
+    tgt_pieces = pieces[4:]
+    sides, cores = len(pieces) - len(tgt_pieces), len(tgt_pieces)
+    fetch.wait()
+    place = [tiles[0, 1 + n] for n in range(5)]
     for d in range(sides):
         x = lax.rem(place[0] + (sides - d), sides)
-        p, core = place[3] ^ (d // 2), place[4] ^ (d % 2)
-        for n in range(sides):
-            s, y = (lax.rem(place[axis] + (sides - n), sides) for axis in (1, 2))
+        for n in range(pieces[d].shape[0]):
+            s = lax.rem(place[1] + (sides - n), sides)
             src[x * sides + s] = pieces[d][n]
-            tgt[p * (2 * sides) + 2 * y + core] = pieces[sides + d][n]
+    for d, piece in enumerate(tgt_pieces):
+        core = place[4] ^ d
+        for n in range(piece.shape[0]):
+            p, y = place[3] ^ (n // sides), lax.rem(place[2] + (sides - n % sides), sides)
+            tgt[p * (cores * sides) + cores * y + core] = piece[n]
     for b in range(tgt.shape[0]):
         sq_tgt[b : b + 1, :] = square_rows(tgt[b])
     for a in range(src.shape[0]):
         sq_src[a : a + 1, :] = square_rows(src[a])
     expand(sq_tgt[...] * -KAPPA, wide)
-    sums = tile_sums(source_tiles(tiles, tgt.shape[0]), count[0], tgt, src, wide, peaks, totals)
+    sums = tile_sums(source_tiles(tiles, tgt.shape[0]), tiles[0, 0], tgt, src, wide, peaks, totals)
     out[...] = jnp.broadcast_to(sums[None], out.shape)
 
 
-def source_kernel(log_cells, tiles, count, src, tgt, parts, out, wide, peaks, totals):
+def source_kernel(log_cells, picked, src, tgt, parts, out, wide, peaks, totals, tiles, sem):
+    fetch = pltpu.make_async_copy(picked, tiles, sem)
+    fetch.start()
     expand(-log_cells - log_sum(parts[...]), wide)
-    sums = tile_sums(source_tiles(tiles, tgt.shape[0]), count[0], tgt, src, wide, peaks, totals)
+    fetch.wait()
+    sums = tile_sums(source_tiles(tiles, tgt.shape[0]), tiles[0, 0], tgt, src, wide, peaks, totals)
     out[...] = jnp.broadcast_to(sums[None], out.shape)
 
 
-def target_kernel(log_cells, tiles, count, src, tgt, parts, sq_src, out, pot, wide, peaks, totals):
+def target_kernel(log_cells, picked, src, tgt, parts, sq_src, out, pot, wide, peaks, totals, tiles, sem):
+    fetch = pltpu.make_async_copy(picked, tiles, sem)
+    fetch.start()
     weights = -log_cells - log_sum(parts[...])
     pot[...] = weights * (1.0 / KAPPA) + sq_src[...]
     expand(weights, wide)
-    sums = tile_sums(target_tiles(tiles, tgt.shape[0]), count[0], src, tgt, wide, peaks, totals)
+    fetch.wait()
+    sums = tile_sums(target_tiles(tiles, tgt.shape[0]), tiles[0, 0], src, tgt, wide, peaks, totals)
     copies, blocks = out.shape[0], out.shape[1]
     if blocks == sums.shape[0]:
         out[...] = jnp.broadcast_to(sums[None], out.shape)
@@ -173,19 +200,21 @@
     src_pot[:, 1, :] = jnp.where(p == 0, other[...], mine[...])
 
 
-def half_step(kernel, outs, near_blocks, slots, scalars, *args):
+def half_step(kernel, outs, near_blocks, slots, picked, *args):
     return pl.pallas_call(
         kernel,
         out_shape=[s if isinstance(s, jax.ShapeDtypeStruct) else jax.ShapeDtypeStruct(s, F32) for s in outs],
-        in_specs=[SMEM] * len(scalars) + [VMEM] * len(args),
+        in_specs=[ANY] + [VMEM] * len(args),
         out_specs=[VMEM] * len(outs),
         scratch_shapes=[
             pltpu.VMEM((near_blocks, TILE, TILE), F32),
             pltpu.VMEM((slots + 1, 8, TILE), F32),
             pltpu.VMEM((slots + 1, 8, TILE), F32),
+            pltpu.SMEM(picked.shape, picked.dtype),
+            pltpu.SemaphoreType.DMA,
         ],
         compiler_params=PARAMS,
-    )(*scalars, *args)
+    )(picked, *args)
 
 
 def exchange(copies, peers):
@@ -209,12 +238,19 @@
     src, tgt = pl.pallas_call(
         pack_kernel,
         out_shape=[group] * 2,
-        in_specs=[pl.BlockSpec(memory_space=pl.ANY)] + [VMEM] * len(blocks),
+        in_specs=[ANY] + [VMEM] * len(blocks),
         out_specs=[VMEM] * 2,
         compiler_params=PARAMS,
     )(lists, *blocks)
-    tgt_pieces = [piece for side in shifts(tgt, "p") for piece in shifts(side, "core")]
-    return shifts(src, "x"), tgt_pieces
+    src_pieces, tgt_pieces = shifts(src, "x"), shifts(tgt, "p")
+    both = pl.pallas_call(
+        join_kernel,
+        out_shape=jax.ShapeDtypeStruct((len(tgt_pieces) * tgt.shape[0],) + tgt.shape[1:], tgt.dtype),
+        in_specs=[VMEM] * len(tgt_pieces),
+        out_specs=VMEM,
+        compiler_params=PARAMS,
+    )(*tgt_pieces)
+    return src_pieces, shifts(both, "core")
 
 
 def local(src_embed, tgt_embed, tiles, counts):
@@ -226,19 +262,18 @@
     lists = jnp.concatenate([tiles[0, 0], jnp.broadcast_to(counts[0, 0], (1, TILE))], axis=0)
     other_lists = partner(lists)
     src_pieces, tgt_pieces = bands(src_embed, tgt_embed, other_lists)
-    picked, count = pl.pallas_call(
+    place = jnp.stack([lax.axis_index(a) for a in ("x", "s", "y", "p", "core")]).astype(jnp.int32)
+    picked = pl.pallas_call(
         pick_kernel,
-        out_shape=[jax.ShapeDtypeStruct((2 * TILE + UNROLL,), jnp.int32), jax.ShapeDtypeStruct((1,), jnp.int32)],
+        out_shape=jax.ShapeDtypeStruct((8, TILE), jnp.int32),
         in_specs=[SMEM] * 3,
-        out_specs=[SMEM] * 2,
-        compiler_params=PARAMS,
-    )(lists, other_lists, parity)
+        out_specs=SMEM,
+        compiler_params=PARAMS,
+    )(lists, other_lists, place)
 
     srcs, tgts = (len(pieces) * pieces[0].shape[0] for pieces in (src_pieces, tgt_pieces))
     src_shape = jax.ShapeDtypeStruct((srcs,) + src_embed.shape, src_embed.dtype)
     tgt_shape = jax.ShapeDtypeStruct((tgts,) + tgt_embed.shape, tgt_embed.dtype)
-    scalars = (picked, count)
-    place = jnp.stack([lax.axis_index(a) for a in ("x", "s", "y", "p", "core")]).astype(jnp.int32)
     slots = srcs * tgts
     src_out, tgt_out = (srcs, srcs, TILE), (tgts, tgts, TILE)
     for sweep in range(ITERS):
@@ -248,13 +283,13 @@
                 [src_out, src_shape, tgt_shape, (srcs, TILE), (tgts, TILE)],
                 tgts,
                 slots,
-                scalars + (place,),
+                picked,
                 *src_pieces,
                 *tgt_pieces,
             )
         else:
             (parts,) = half_step(
-                functools.partial(source_kernel, log_cells), [src_out], tgts, slots, scalars, src, tgt, parts
+                functools.partial(source_kernel, log_cells), [src_out], tgts, slots, picked, src, tgt, parts
             )
         parts = exchange(parts, SRC_PEERS)
         last = sweep == ITERS - 1
@@ -263,7 +298,7 @@
             [(tgts, rows, TILE) if last else tgt_out, (srcs, TILE)],
             srcs,
             slots,
-            scalars,
+            picked,
             src,
             tgt,
             parts,

time: 115 us -> 116 us (level)
  Pallas kernels: 20.7 us -> 25.4 us
  waiting for transfers between devices: 14.7 us -> 19.2 us
  blocking collectives: 39.7 us -> 35.3 us
  starting transfers between devices: 37.6 us -> 33.6 us
    ppermute x12 -> x11, waiting for transfers between devices: 10.3 us -> 14.7 us  [shifts(): lax.ppermute(block, axis, [(i, (i + d) % n) for i in range(n)])]
    all_to_all x3, blocking collectives: 39.7 us -> 35.3 us  [exchange(): return lax.all_to_all(copies, peers, 0, 0, tiled=True)]
    all_to_all x1, starting transfers between devices: 10.1 us -> 6.9 us  [exchange(): return lax.all_to_all(copies, peers, 0, 0, tiled=True)]
    pallas_call x4, Pallas kernels: 16.1 us -> 19 us  [half_step(): pl.pallas_call(kernel, out_shape=[s if isinstance(s, jax.ShapeDtypeStruct...]
    pallas_call x2 -> x3, Pallas kernels: 3.93 us -> 5.74 us  [the longest x1 5.67 us: local(): pl.pallas_call(pick_kernel, out_shape=jax.ShapeDtypeStruct((8, TILE), jnp...]
    ppermute x12 -> x11, starting transfers between devices: 24.5 us -> 23.7 us  [shifts(): lax.ppermute(block, axis, [(i, (i + d) % n) for i in range(n)])]
  transfers between devices with their start and end apart: 15 -> 14, of which waited for: 5 -> 6; matrix products, arithmetic and copies ran while one was open for 0% -> 0% of each run, Pallas kernels for 3% -> 5%
where the time goes in v7:
time: 116 us; the launch traced here: 117 us
  blocking collectives  35.3 us (30%)
  starting transfers between devices  33.6 us (29%)
  Pallas kernels  25.4 us (22%)
  waiting for transfers between devices  19.2 us (17%)
  local copies, waits for them, and re-layouts  2.44 us (2%)
  between operations  1.39 us (1%)
    all_to_all x3, blocking collectives, exchange(): return lax.all_to_all(copies, peers, 0, 0, tiled=True)  35.3 us
    ppermute x11, starting transfers between devices, shifts(): lax.ppermute(block, axis, [(i, (i + d) % n) for i in range(n)])  23.7 us
    pallas_call x4, Pallas kernels, half_step(): pl.pallas_call(kernel, out_shape=[s if isinstance(s, jax.ShapeDtypeStruct...  19 us
    ppermute x11, waiting for transfers between devices, shifts(): lax.ppermute(block, axis, [(i, (i + d) % n) for i in range(n)])  14.7 us
    all_to_all x1, starting transfers between devices, exchange(): return lax.all_to_all(copies, peers, 0, 0, tiled=True)  6.9 us
    pallas_call x1, Pallas kernels, local(): pl.pallas_call(pick_kernel, out_shape=jax.ShapeDtypeStruct((8, TILE), jnp...  5.67 us
    ppermute x2, starting transfers between devices, local(): partner = lambda v: lax.ppermute(v, 'p', [(0, 1), (1, 0)])  3.07 us
    all_to_all x1, waiting for transfers between devices, exchange(): return lax.all_to_all(copies, peers, 0, 0, tiled=True)  2.79 us
  transfers between devices with their start and end apart: 14, of which 6 were waited for; matrix products, arithmetic and copies ran while one was open for 0% of the time, Pallas kernels for 5%

profile of v7, /device:TPU:1, one launch (start us, length us, event | category | flops | bytes accessed | tf_op | source)
XLA Modules:
  0.0 117.3 jit_solution(15836255164579880553)
XLA Ops:
  0.6 3.9 %collective-permute-start.1 = (bf16[128,256]{1,0:T(8,128)(2,1)}, bf16[128,256]{1,0:T(8,128)(2,1)S(1)}, u32[]{:S(2)}, u32[]{:S(2)}) collective-permute-start(bf16[128,256]{1,0:T(8,128)(2,1)} %src_mine.1), channel_id=1, source_target_pairs={{0,2},{2,4},{4,6},{6,0},{1,3},{3,5},{5,7},{7,1},{8,10},{10,12},{12... | collective-permute-start | bytes 196616 | tf_op jit(solution)/shard_map/ppermute | solution.py:226
  5.2 0.0 copy-start.2
  5.2 0.7 copy-done.2
  5.9 1.6 %collective-permute-start = (s32[3,128]{1,0:T(4,128)S(1)}, s32[3,128]{1,0:T(4,128)S(1)}, u32[]{:S(2)}, u32[]{:S(2)}) collective-permute-start(s32[3,128]{1,0:T(4,128)S(1)} %concatenate.3.mine), channel_id=1, source_target_pairs={{0,1},{1,0},{2,3},{3,2},{4,5},{5,4},{6,7},{7,6},{8,9},{9,8},{10,11... | collective-permute-start | bytes 4616 | tf_op jit(solution)/shard_map/ppermute | solution.py:260
  7.5 2.1 %collective-permute-start.3 = (bf16[128,256]{1,0:T(8,128)(2,1)}, bf16[128,256]{1,0:T(8,128)(2,1)S(1)}, u32[]{:S(2)}, u32[]{:S(2)}) collective-permute-start(bf16[128,256]{1,0:T(8,128)(2,1)} %src_mine.1), channel_id=1, source_target_pairs={{0,6},{2,0},{4,2},{6,4},{1,7},{3,1},{5,3},{7,5},{8,14},{10,8},{12,... | collective-permute-start | bytes 196616 | tf_op jit(solution)/shard_map/ppermute | solution.py:226
  9.6 4.5 %collective-permute-start.2 = (bf16[128,256]{1,0:T(8,128)(2,1)}, bf16[128,256]{1,0:T(8,128)(2,1)S(1)}, u32[]{:S(2)}, u32[]{:S(2)}) collective-permute-start(bf16[128,256]{1,0:T(8,128)(2,1)} %src_mine.1), channel_id=1, source_target_pairs={{0,4},{2,6},{4,0},{6,2},{1,5},{3,7},{5,1},{7,3},{8,12},{10,14},{12... | collective-permute-start | bytes 196616 | tf_op jit(solution)/shard_map/ppermute | solution.py:226
  14.1 1.3 %collective-permute-start.4 = (bf16[128,256]{1,0:T(8,128)(2,1)}, bf16[128,256]{1,0:T(8,128)(2,1)S(1)}, u32[]{:S(2)}, u32[]{:S(2)}) collective-permute-start(bf16[128,256]{1,0:T(8,128)(2,1)} %tgt_mine.1), channel_id=1, source_target_pairs={{0,64},{64,128},{128,192},{192,0},{1,65},{65,129},{129,193},{193,1... | collective-permute-start | bytes 196616 | tf_op jit(solution)/shard_map/ppermute | solution.py:226
  15.4 0.0 collective-permute-done.other.lists
  15.4 1.4 %collective-permute-start.6 = (bf16[128,256]{1,0:T(8,128)(2,1)}, bf16[128,256]{1,0:T(8,128)(2,1)S(1)}, u32[]{:S(2)}, u32[]{:S(2)}) collective-permute-start(bf16[128,256]{1,0:T(8,128)(2,1)} %tgt_mine.1), channel_id=1, source_target_pairs={{0,192},{64,0},{128,64},{192,128},{1,193},{65,1},{129,65},{193,129... | collective-permute-start | bytes 196616 | tf_op jit(solution)/shard_map/ppermute | solution.py:226
  16.8 0.0 collective-permute-done.1.refs_1_
  16.8 1.6 %collective-permute-start.5 = (bf16[128,256]{1,0:T(8,128)(2,1)}, bf16[128,256]{1,0:T(8,128)(2,1)S(1)}, u32[]{:S(2)}, u32[]{:S(2)}) collective-permute-start(bf16[128,256]{1,0:T(8,128)(2,1)} %tgt_mine.1), channel_id=1, source_target_pairs={{0,128},{64,192},{128,0},{192,64},{1,129},{65,193},{129,1},{193,65... | collective-permute-start | bytes 196616 | tf_op jit(solution)/shard_map/ppermute | solution.py:226
  18.5 0.0 copy-start
  18.5 0.8 copy-done
  19.3 0.0 copy-start.1
  19.3 0.8 copy-done.1
  20.2 0.0 collective-permute-done.3.refs_3_
  20.2 0.0 collective-permute-done.2.refs_2_
  20.2 0.0 collective-permute-done.4.refs_5_
  20.2 0.0 collective-permute-done.6.refs_7_
  20.2 1.8 %collective-permute-done.5.refs_6_ = bf16[128,256]{1,0:T(8,128)(2,1)S(1)} collective-permute-done((bf16[128,256]{1,0:T(8,128)(2,1)}, bf16[128,256]{1,0:T(8,128)(2,1)S(1)}, u32[]{:S(2)}, u32[]{:S(2)}) %collective-permute-start.5) | collective-permute-done | bytes 65568 | tf_op jit(solution)/shard_map/ppermute | solution.py:226
  22.0 0.8 collective-permute-start.10
  22.8 4.5 %collective-permute-done.10.refs_1_ = bf16[4,128,256]{2,1,0:T(8,128)(2,1)S(1)} collective-permute-done((bf16[4,128,256]{2,1,0:T(8,128)(2,1)S(1)}, bf16[4,128,256]{2,1,0:T(8,128)(2,1)S(1)}, u32[]{:S(2)}, u32[]{:S(2)}) %collective-permute-start.10) | collective-permute-done | bytes 262176 | tf_op jit(solution)/shard_map/ppermute | solution.py:226
  27.4 4.4 %collective-permute-start.11 = (bf16[8,128,256]{2,1,0:T(8,128)(2,1)S(1)}, bf16[8,128,256]{2,1,0:T(8,128)(2,1)S(1)}, u32[]{:S(2)}, u32[]{:S(2)}) collective-permute-start(bf16[8,128,256]{2,1,0:T(8,128)(2,1)S(1)} %shard_map.62.refs_4_), channel_id=1, source_target_pairs={{0,32},{32,0},{1,33},{33,1},{2,34},{34,2},{3,35},{35,3},{4,36},{36... | collective-permute-start | bytes 1572872 | tf_op jit(solution)/shard_map/ppermute | solution.py:226
  31.7 2.5 %collective-permute-start.9 = (bf16[4,128,256]{2,1,0:T(8,128)(2,1)S(1)}, bf16[4,128,256]{2,1,0:T(8,128)(2,1)S(1)}, u32[]{:S(2)}, u32[]{:S(2)}) collective-permute-start(bf16[4,128,256]{2,1,0:T(8,128)(2,1)S(1)} %get-tuple-element.18.refs_0_), channel_id=1, source_target_pairs={{0,24},{8,0},{16,8},{24,16},{1,25},{9,1},{17,9},{25,17},{2,26},{10... | collective-permute-start | bytes 786440 | tf_op jit(solution)/shard_map/ppermute | solution.py:226
  34.2 0.5 collective-permute-start.8
  34.8 0.6 collective-permute-start.7
  35.4 0.1 stack.20.place
  35.4 5.7 %shard_map.59.picked = s32[8,128]{1,0:T(8,128)S(1)} custom-call(s32[3,128]{1,0:T(4,128)S(1)} %concatenate.3.mine, s32[3,128]{1,0:T(4,128)S(1)} %collective-permute-done.other.lists, s32[5]{0:T(128)S(1)} %stack.20.place), custom_call_target="tpu_custom_call" | custom-call | tf_op jit(solution)/shard_map/pallas_call | solution.py:266
  41.1 4.2 %collective-permute-done.9.refs_3_ = bf16[4,128,256]{2,1,0:T(8,128)(2,1)S(1)} collective-permute-done((bf16[4,128,256]{2,1,0:T(8,128)(2,1)S(1)}, bf16[4,128,256]{2,1,0:T(8,128)(2,1)S(1)}, u32[]{:S(2)}, u32[]{:S(2)}) %collective-permute-start.9) | collective-permute-done | bytes 262176 | tf_op jit(solution)/shard_map/ppermute | solution.py:226
  45.4 0.0 collective-permute-done.8.refs_2_
  45.4 4.2 %collective-permute-done.7.refs_1_ = bf16[4,128,256]{2,1,0:T(8,128)(2,1)S(1)} collective-permute-done((bf16[4,128,256]{2,1,0:T(8,128)(2,1)S(1)}, bf16[4,128,256]{2,1,0:T(8,128)(2,1)S(1)}, u32[]{:S(2)}, u32[]{:S(2)}) %collective-permute-start.7) | collective-permute-done | bytes 262176 | tf_op jit(solution)/shard_map/ppermute | solution.py:226
  49.6 0.0 collective-permute-done.11.refs_5_
  49.6 5.4 %shard_map.63 = (f32[16,16,128]{2,1,0:T(8,128)S(1)}, bf16[16,128,256]{2,1,0:T(8,128)(2,1)S(1)}, bf16[16,128,256]{2,1,0:T(8,128)(2,1)S(1)}, f32[16,128]{1,0:T(8,128)S(1)}, f32[16,128]{1,0:T(8,128)S(1)}) custom-call(s32[8,128]{1,0:T(8,128)S(1)} %shard_map.59.picked, bf16[4,128,256]{2,1,0:T(8,128)(2,1)S(1)} %get-tuple-element.18.refs_0_, ...), custom_call_target="tpu_custom_call" | custom-call | tf_op jit(solution)/shard_map/pallas_call | solution.py:204
  55.0 12.9 %all_to_all.20.parts = f32[16,16,128]{2,1,0:T(8,128)S(1)} all-to-all(f32[16,16,128]{2,1,0:T(8,128)S(1)} %get-tuple-element.22), channel_id=1, replica_groups=mesh['y'=4,'core'=2,'x'=4,'s'=4,'p'=2] {'x','s'}, dimensions={0} | all-to-all | bytes 262144 | tf_op jit(solution)/shard_map/all_to_all | solution.py:221
  68.0 4.5 %shard_map.64 = (f32[16,16,128]{2,1,0:T(8,128)S(1)}, f32[16,128]{1,0:T(8,128)}) custom-call(s32[8,128]{1,0:T(8,128)S(1)} %shard_map.59.picked, bf16[16,128,256]{2,1,0:T(8,128)(2,1)S(1)} %get-tuple-element.20.src, bf16[16,128,256]{2,1,0:T(8,128)(2,1)S(1)} %get-tuple-element.21.tgt, f32[16,16,128]{2,1,0:T(8,128)S(1)} %all_to_all.20.parts, ...), custom_call_target="tpu_custom_call" | custom-call | tf_op jit(solution)/shard_map/pallas_call | solution.py:204
  72.5 10.2 %all_to_all.21.parts = f32[16,16,128]{2,1,0:T(8,128)S(1)} all-to-all(f32[16,16,128]{2,1,0:T(8,128)S(1)} %get-tuple-element.24), channel_id=1, replica_groups=mesh['y'=4,'core'=2,'x'=4,'s'=4,'p'=2] {'p','y','core'}, dimensions={0} | all-to-all | bytes 262144 | tf_op jit(solution)/shard_map/all_to_all | solution.py:221
  82.7 4.2 %shard_map.65 = f32[16,16,128]{2,1,0:T(8,128)S(1)} custom-call(s32[8,128]{1,0:T(8,128)S(1)} %shard_map.59.picked, bf16[16,128,256]{2,1,0:T(8,128)(2,1)S(1)} %get-tuple-element.20.src, bf16[16,128,256]{2,1,0:T(8,128)(2,1)S(1)} %get-tuple-element.21.tgt, f32[16,16,128]{2,1,0:T(8,128)S(1)} %all_to_all.21.parts), custom_call_target="tpu_custom_call" | custom-call | tf_op jit(solution)/shard_map/pallas_call | solution.py:204
  86.9 12.2 %all_to_all.22.parts = f32[16,16,128]{2,1,0:T(8,128)S(1)} all-to-all(f32[16,16,128]{2,1,0:T(8,128)S(1)} %shard_map.65), channel_id=1, replica_groups=mesh['y'=4,'core'=2,'x'=4,'s'=4,'p'=2] {'x','s'}, dimensions={0} | all-to-all | bytes 262144 | tf_op jit(solution)/shard_map/all_to_all | solution.py:221
  99.1 4.8 %shard_map.66 = (f32[16,8,128]{2,1,0:T(8,128)}, f32[16,128]{1,0:T(8,128)S(1)}) custom-call(s32[8,128]{1,0:T(8,128)S(1)} %shard_map.59.picked, bf16[16,128,256]{2,1,0:T(8,128)(2,1)S(1)} %get-tuple-element.20.src, bf16[16,128,256]{2,1,0:T(8,128)(2,1)S(1)} %get-tuple-element.21.tgt, f32[16,16,128]{2,1,0:T(8,128)S(1)} %all_to_all.22.parts, ...), custom_call_target="tpu_custom_call" | custom-call | tf_op jit(solution)/shard_map/pallas_call | solution.py:204
  103.9 6.9 %all-to-all-start.3 = ((f32[16,8,128]{2,1,0:T(8,128)}), f32[16,8,128]{2,1,0:T(8,128)S(1)}, u32[]{:S(2)}, u32[]{:S(2)}) async-start(f32[16,8,128]{2,1,0:T(8,128)} %get-tuple-element.25), calls=%async_computation.3 | async-start | bytes 131072 | tf_op jit(solution)/shard_map/all_to_all | solution.py:221
  110.8 1.4 %collective-permute-start.12 = (f32[16,128]{1,0:T(8,128)S(1)}, f32[16,128]{1,0:T(8,128)S(1)}, u32[]{:S(2)}, u32[]{:S(2)}) collective-permute-start(f32[16,128]{1,0:T(8,128)S(1)} %get-tuple-element.27.mine), channel_id=1, source_target_pairs={{0,1},{1,0},{2,3},{3,2},{4,5},{5,4},{6,7},{7,6},{8,9},{9,8},{10,11... | collective-permute-start | bytes 24584 | tf_op jit(solution)/shard_map/ppermute | solution.py:260
  112.2 1.7 %collective-permute-done.12.other = f32[16,128]{1,0:T(8,128)S(1)} collective-permute-done((f32[16,128]{1,0:T(8,128)S(1)}, f32[16,128]{1,0:T(8,128)S(1)}, u32[]{:S(2)}, u32[]{:S(2)}) %collective-permute-start.12) | collective-permute-done | bytes 8224 | tf_op jit(solution)/shard_map/ppermute | solution.py:260
  113.9 2.8 %all-to-all-done.3.parts = f32[16,8,128]{2,1,0:T(8,128)S(1)} async-done(((f32[16,8,128]{2,1,0:T(8,128)}), f32[16,8,128]{2,1,0:T(8,128)S(1)}, u32[]{:S(2)}, u32[]{:S(2)}) %all-to-all-start.3) | async-done | bytes 65568 | tf_op jit(solution)/shard_map/all_to_all | solution.py:221
  116.7 0.6 shard_map.67
  (4 shorter events, 0.1 us)
Async XLA Ops:
  0.6 16.2 %collective-permute-start.1 = (bf16[128,256]{1,0:T(8,128)(2,1)}, bf16[128,256]{1,0:T(8,128)(2,1)S(1)}, u32[]{:S(2)}, u32[]{:S(2)}) collective-permute-start(bf16[128,256]{1,0:T(8,128)(2,1)} %src_mine.1), channel_id=1, source_target_pairs={{0,2},{2,4},{4,6},{6,0},{1,3},{3,5},{5,7},{7,1},{8,10},{10,12},{12... | collective-permute-start | bytes 196616 | tf_op jit(solution)/shard_map/ppermute | solution.py:226
  5.2 0.7 copy-start.2
  5.9 9.5 %collective-permute-start = (s32[3,128]{1,0:T(4,128)S(1)}, s32[3,128]{1,0:T(4,128)S(1)}, u32[]{:S(2)}, u32[]{:S(2)}) collective-permute-start(s32[3,128]{1,0:T(4,128)S(1)} %concatenate.3.mine), channel_id=1, source_target_pairs={{0,1},{1,0},{2,3},{3,2},{4,5},{5,4},{6,7},{7,6},{8,9},{9,8},{10,11... | collective-permute-start | bytes 4616 | tf_op jit(solution)/shard_map/ppermute | solution.py:260
  7.5 12.7 %collective-permute-start.3 = (bf16[128,256]{1,0:T(8,128)(2,1)}, bf16[128,256]{1,0:T(8,128)(2,1)S(1)}, u32[]{:S(2)}, u32[]{:S(2)}) collective-permute-start(bf16[128,256]{1,0:T(8,128)(2,1)} %src_mine.1), channel_id=1, source_target_pairs={{0,6},{2,0},{4,2},{6,4},{1,7},{3,1},{5,3},{7,5},{8,14},{10,8},{12,... | collective-permute-start | bytes 196616 | tf_op jit(solution)/shard_map/ppermute | solution.py:226
  9.6 10.6 %collective-permute-start.2 = (bf16[128,256]{1,0:T(8,128)(2,1)}, bf16[128,256]{1,0:T(8,128)(2,1)S(1)}, u32[]{:S(2)}, u32[]{:S(2)}) collective-permute-start(bf16[128,256]{1,0:T(8,128)(2,1)} %src_mine.1), channel_id=1, source_target_pairs={{0,4},{2,6},{4,0},{6,2},{1,5},{3,7},{5,1},{7,3},{8,12},{10,14},{12... | collective-permute-start | bytes 196616 | tf_op jit(solution)/shard_map/ppermute | solution.py:226
  14.1 6.1 %collective-permute-start.4 = (bf16[128,256]{1,0:T(8,128)(2,1)}, bf16[128,256]{1,0:T(8,128)(2,1)S(1)}, u32[]{:S(2)}, u32[]{:S(2)}) collective-permute-start(bf16[128,256]{1,0:T(8,128)(2,1)} %tgt_mine.1), channel_id=1, source_target_pairs={{0,64},{64,128},{128,192},{192,0},{1,65},{65,129},{129,193},{193,1... | collective-permute-start | bytes 196616 | tf_op jit(solution)/shard_map/ppermute | solution.py:226
  15.4 4.8 %collective-permute-start.6 = (bf16[128,256]{1,0:T(8,128)(2,1)}, bf16[128,256]{1,0:T(8,128)(2,1)S(1)}, u32[]{:S(2)}, u32[]{:S(2)}) collective-permute-start(bf16[128,256]{1,0:T(8,128)(2,1)} %tgt_mine.1), channel_id=1, source_target_pairs={{0,192},{64,0},{128,64},{192,128},{1,193},{65,1},{129,65},{193,129... | collective-permute-start | bytes 196616 | tf_op jit(solution)/shard_map/ppermute | solution.py:226
  16.8 5.1 %collective-permute-start.5 = (bf16[128,256]{1,0:T(8,128)(2,1)}, bf16[128,256]{1,0:T(8,128)(2,1)S(1)}, u32[]{:S(2)}, u32[]{:S(2)}) collective-permute-start(bf16[128,256]{1,0:T(8,128)(2,1)} %tgt_mine.1), channel_id=1, source_target_pairs={{0,128},{64,192},{128,0},{192,64},{1,129},{65,193},{129,1},{193,65... | collective-permute-start | bytes 196616 | tf_op jit(solution)/shard_map/ppermute | solution.py:226
  18.5 0.8 copy-start
  19.3 0.8 copy-start.1
  22.0 5.3 %collective-permute-start.10 = (bf16[4,128,256]{2,1,0:T(8,128)(2,1)S(1)}, bf16[4,128,256]{2,1,0:T(8,128)(2,1)S(1)}, u32[]{:S(2)}, u32[]{:S(2)}) collective-permute-start(bf16[4,128,256]{2,1,0:T(8,128)(2,1)S(1)} %get-tuple-element.19.refs_0_), channel_id=1, source_target_pairs={{0,1},{1,0},{2,3},{3,2},{4,5},{5,4},{6,7},{7,6},{8,9},{9,8},{10,11... | collective-permute-start | bytes 786440 | tf_op jit(solution)/shard_map/ppermute | solution.py:226
  27.4 22.2 %collective-permute-start.11 = (bf16[8,128,256]{2,1,0:T(8,128)(2,1)S(1)}, bf16[8,128,256]{2,1,0:T(8,128)(2,1)S(1)}, u32[]{:S(2)}, u32[]{:S(2)}) collective-permute-start(bf16[8,128,256]{2,1,0:T(8,128)(2,1)S(1)} %shard_map.62.refs_4_), channel_id=1, source_target_pairs={{0,32},{32,0},{1,33},{33,1},{2,34},{34,2},{3,35},{35,3},{4,36},{36... | collective-permute-start | bytes 1572872 | tf_op jit(solution)/shard_map/ppermute | solution.py:226
  31.7 13.6 %collective-permute-start.9 = (bf16[4,128,256]{2,1,0:T(8,128)(2,1)S(1)}, bf16[4,128,256]{2,1,0:T(8,128)(2,1)S(1)}, u32[]{:S(2)}, u32[]{:S(2)}) collective-permute-start(bf16[4,128,256]{2,1,0:T(8,128)(2,1)S(1)} %get-tuple-element.18.refs_0_), channel_id=1, source_target_pairs={{0,24},{8,0},{16,8},{24,16},{1,25},{9,1},{17,9},{25,17},{2,26},{10... | collective-permute-start | bytes 786440 | tf_op jit(solution)/shard_map/ppermute | solution.py:226
  34.2 11.1 %collective-permute-start.8 = (bf16[4,128,256]{2,1,0:T(8,128)(2,1)S(1)}, bf16[4,128,256]{2,1,0:T(8,128)(2,1)S(1)}, u32[]{:S(2)}, u32[]{:S(2)}) collective-permute-start(bf16[4,128,256]{2,1,0:T(8,128)(2,1)S(1)} %get-tuple-element.18.refs_0_), channel_id=1, source_target_pairs={{0,16},{8,24},{16,0},{24,8},{1,17},{9,25},{17,1},{25,9},{2,18},{10... | collective-permute-start | bytes 786440 | tf_op jit(solution)/shard_map/ppermute | solution.py:226
  34.8 14.8 %collective-permute-start.7 = (bf16[4,128,256]{2,1,0:T(8,128)(2,1)S(1)}, bf16[4,128,256]{2,1,0:T(8,128)(2,1)S(1)}, u32[]{:S(2)}, u32[]{:S(2)}) collective-permute-start(bf16[4,128,256]{2,1,0:T(8,128)(2,1)S(1)} %get-tuple-element.18.refs_0_), channel_id=1, source_target_pairs={{0,8},{8,16},{16,24},{24,0},{1,9},{9,17},{17,25},{25,1},{2,10},{10... | collective-permute-start | bytes 786440 | tf_op jit(solution)/shard_map/ppermute | solution.py:226
  103.9 12.8 %all-to-all-start.3 = ((f32[16,8,128]{2,1,0:T(8,128)}), f32[16,8,128]{2,1,0:T(8,128)S(1)}, u32[]{:S(2)}, u32[]{:S(2)}) async-start(f32[16,8,128]{2,1,0:T(8,128)} %get-tuple-element.25), calls=%async_computation.3 | async-start | bytes 131072 | tf_op jit(solution)/shard_map/all_to_all | solution.py:221
  110.8 3.1 %collective-permute-start.12 = (f32[16,128]{1,0:T(8,128)S(1)}, f32[16,128]{1,0:T(8,128)S(1)}, u32[]{:S(2)}, u32[]{:S(2)}) collective-permute-start(f32[16,128]{1,0:T(8,128)S(1)} %get-tuple-element.27.mine), channel_id=1, source_target_pairs={{0,1},{1,0},{2,3},{3,2},{4,5},{5,4},{6,7},{7,6},{8,9},{9,8},{10,11... | collective-permute-start | bytes 24584 | tf_op jit(solution)/shard_map/ppermute | solution.py:260

commit v8 on v7

--- a/solution.py
+++ b/solution.py
@@ -10,6 +10,7 @@
 from jax.sharding import PartitionSpec as P
 
 TILE = 128
+LOG_TILE = 7
 ITERS = 2
 ENTROPY = 0.05
 KAPPA = math.log2(math.e) / ENTROPY
@@ -84,10 +85,12 @@
     targets = 8
 
     def scan(lists, col, start):
+        count = lists[2, 0]
+
         def step(k, at):
             a, b = lists[0, k], lists[1, k]
-            picked[1 + at // TILE, at % TILE] = (a // 2) * (2 * targets) + col * targets + b
-            return at + jnp.where((k < lists[2, 0]) & (a % 2 == p), 1, 0)
+            picked[1 + (at >> LOG_TILE), at & (TILE - 1)] = (a >> 1) * (2 * targets) + col * targets + b
+            return at + jnp.where((k < count) & ((a & 1) == p), 1, 0)
 
         return lax.fori_loop(0, TILE, step, start, unroll=8)
 
@@ -97,13 +100,13 @@
 
 
 def tile_code(tiles, k):
-    return tiles[1 + k // TILE, k % TILE]
+    return tiles[1 + (k >> LOG_TILE), k & (TILE - 1)]
 
 
 def source_tiles(tiles, tgt_blocks):
     def tile(k):
         code = tile_code(tiles, k)
-        return code % tgt_blocks, code // tgt_blocks
+        return lax.rem(code, tgt_blocks), lax.div(code, tgt_blocks)
 
     return tile
 
@@ -111,7 +114,7 @@
 def target_tiles(tiles, tgt_blocks):
     def tile(k):
         code = tile_code(tiles, k)
-        return code // tgt_blocks, code % tgt_blocks
+        return lax.div(code, tgt_blocks), lax.rem(code, tgt_blocks)
 
     return tile
 
@@ -130,7 +133,7 @@
         tgt[n] = refs[sides + n][...]
 
 
-def join_kernel(*refs):
+def join_kernel(after, *refs):
     blocks = refs[0].shape[0]
     for n, piece in enumerate(refs[:-1]):
         refs[-1][n * blocks : (n + 1) * blocks] = piece[...]
@@ -246,10 +249,10 @@
     both = pl.pallas_call(
         join_kernel,
         out_shape=jax.ShapeDtypeStruct((len(tgt_pieces) * tgt.shape[0],) + tgt.shape[1:], tgt.dtype),
-        in_specs=[VMEM] * len(tgt_pieces),
+        in_specs=[ANY] + [VMEM] * len(tgt_pieces),
         out_specs=VMEM,
         compiler_params=PARAMS,
-    )(*tgt_pieces)
+    )(src_pieces[-1], *tgt_pieces)
     return src_pieces, shifts(both, "core")
 
 

time: 116 us -> 115 us (level); the launches traced: 117 us -> 114 us
  Pallas kernels: 25.4 us -> 12.2 us
  blocking collectives: 35.3 us -> 44.9 us
  starting transfers between devices: 33.6 us -> 36 us
  waiting for transfers between devices: 19.2 us -> 17.5 us
    pallas_call x4, Pallas kernels: 19 us -> 8.15 us  [half_step(): pl.pallas_call(kernel, out_shape=[s if isinstance(s, jax.ShapeDtypeStruct...]
    all_to_all x3, blocking collectives: 35.3 us -> 44.9 us  [exchange(): return lax.all_to_all(copies, peers, 0, 0, tiled=True)]
    ppermute x11, starting transfers between devices: 23.7 us -> 26.5 us  [shifts(): lax.ppermute(block, axis, [(i, (i + d) % n) for i in range(n)])]
    pallas_call x1, Pallas kernels: 5.67 us -> 3.31 us  [local(): pl.pallas_call(pick_kernel, out_shape=jax.ShapeDtypeStruct((8, TILE), jnp...]
    ppermute x11, waiting for transfers between devices: 14.7 us -> 13.1 us  [shifts(): lax.ppermute(block, axis, [(i, (i + d) % n) for i in range(n)])]
  transfers between devices with their start and end apart: 14 -> 14, of which waited for: 6 -> 7; matrix products, arithmetic and copies ran while one was open for 0% -> 0% of each run, Pallas kernels for 5% -> 3%
where the time goes in v8:
time: 115 us; the launch traced here: 114 us
  blocking collectives  44.9 us (39%)
  starting transfers between devices  36 us (31%)
  waiting for transfers between devices  17.5 us (15%)
  Pallas kernels  12.2 us (11%)
  local copies, waits for them, and re-layouts  2.44 us (2%)
  between operations  1.39 us (1%)
    all_to_all x3, blocking collectives, exchange(): return lax.all_to_all(copies, peers, 0, 0, tiled=True)  44.9 us
    ppermute x11, starting transfers between devices, shifts(): lax.ppermute(block, axis, [(i, (i + d) % n) for i in range(n)])  26.5 us
    ppermute x11, waiting for transfers between devices, shifts(): lax.ppermute(block, axis, [(i, (i + d) % n) for i in range(n)])  13.1 us
    pallas_call x4, Pallas kernels, half_step(): pl.pallas_call(kernel, out_shape=[s if isinstance(s, jax.ShapeDtypeStruct...  8.15 us
    all_to_all x1, starting transfers between devices, exchange(): return lax.all_to_all(copies, peers, 0, 0, tiled=True)  6.45 us
    pallas_call x1, Pallas kernels, local(): pl.pallas_call(pick_kernel, out_shape=jax.ShapeDtypeStruct((8, TILE), jnp...  3.31 us
    ppermute x2, starting transfers between devices, local(): partner = lambda v: lax.ppermute(v, 'p', [(0, 1), (1, 0)])  3.03 us
    all_to_all x1, waiting for transfers between devices, exchange(): return lax.all_to_all(copies, peers, 0, 0, tiled=True)  2.77 us
  transfers between devices with their start and end apart: 14, of which 7 were waited for; matrix products, arithmetic and copies ran while one was open for 0% of the time, Pallas kernels for 3%

profile of v8, /device:TPU:1, one launch (start us, length us, event | category | flops | bytes accessed | tf_op | source)
XLA Modules:
  0.0 114.4 jit_solution(13949895067761288207)
XLA Ops:
  0.6 3.9 %collective-permute-start.1 = (bf16[128,256]{1,0:T(8,128)(2,1)}, bf16[128,256]{1,0:T(8,128)(2,1)S(1)}, u32[]{:S(2)}, u32[]{:S(2)}) collective-permute-start(bf16[128,256]{1,0:T(8,128)(2,1)} %src_mine.1), channel_id=1, source_target_pairs={{0,2},{2,4},{4,6},{6,0},{1,3},{3,5},{5,7},{7,1},{8,10},{10,12},{12... | collective-permute-start | bytes 196616 | tf_op jit(solution)/shard_map/ppermute | solution.py:229
  5.2 0.0 copy-start.2
  5.2 0.7 copy-done.2
  5.9 1.6 %collective-permute-start = (s32[3,128]{1,0:T(4,128)S(1)}, s32[3,128]{1,0:T(4,128)S(1)}, u32[]{:S(2)}, u32[]{:S(2)}) collective-permute-start(s32[3,128]{1,0:T(4,128)S(1)} %concatenate.3.mine), channel_id=1, source_target_pairs={{0,1},{1,0},{2,3},{3,2},{4,5},{5,4},{6,7},{7,6},{8,9},{9,8},{10,11... | collective-permute-start | bytes 4616 | tf_op jit(solution)/shard_map/ppermute | solution.py:263
  7.5 2.1 %collective-permute-start.3 = (bf16[128,256]{1,0:T(8,128)(2,1)}, bf16[128,256]{1,0:T(8,128)(2,1)S(1)}, u32[]{:S(2)}, u32[]{:S(2)}) collective-permute-start(bf16[128,256]{1,0:T(8,128)(2,1)} %src_mine.1), channel_id=1, source_target_pairs={{0,6},{2,0},{4,2},{6,4},{1,7},{3,1},{5,3},{7,5},{8,14},{10,8},{12,... | collective-permute-start | bytes 196616 | tf_op jit(solution)/shard_map/ppermute | solution.py:229
  9.6 4.5 %collective-permute-start.2 = (bf16[128,256]{1,0:T(8,128)(2,1)}, bf16[128,256]{1,0:T(8,128)(2,1)S(1)}, u32[]{:S(2)}, u32[]{:S(2)}) collective-permute-start(bf16[128,256]{1,0:T(8,128)(2,1)} %src_mine.1), channel_id=1, source_target_pairs={{0,4},{2,6},{4,0},{6,2},{1,5},{3,7},{5,1},{7,3},{8,12},{10,14},{12... | collective-permute-start | bytes 196616 | tf_op jit(solution)/shard_map/ppermute | solution.py:229
  14.1 1.3 %collective-permute-start.4 = (bf16[128,256]{1,0:T(8,128)(2,1)}, bf16[128,256]{1,0:T(8,128)(2,1)S(1)}, u32[]{:S(2)}, u32[]{:S(2)}) collective-permute-start(bf16[128,256]{1,0:T(8,128)(2,1)} %tgt_mine.1), channel_id=1, source_target_pairs={{0,64},{64,128},{128,192},{192,0},{1,65},{65,129},{129,193},{193,1... | collective-permute-start | bytes 196616 | tf_op jit(solution)/shard_map/ppermute | solution.py:229
  15.4 0.0 collective-permute-done.other.lists
  15.4 1.4 %collective-permute-start.6 = (bf16[128,256]{1,0:T(8,128)(2,1)}, bf16[128,256]{1,0:T(8,128)(2,1)S(1)}, u32[]{:S(2)}, u32[]{:S(2)}) collective-permute-start(bf16[128,256]{1,0:T(8,128)(2,1)} %tgt_mine.1), channel_id=1, source_target_pairs={{0,192},{64,0},{128,64},{192,128},{1,193},{65,1},{129,65},{193,129... | collective-permute-start | bytes 196616 | tf_op jit(solution)/shard_map/ppermute | solution.py:229
  16.8 0.0 collective-permute-done.1.refs_1_
  16.8 1.6 %collective-permute-start.5 = (bf16[128,256]{1,0:T(8,128)(2,1)}, bf16[128,256]{1,0:T(8,128)(2,1)S(1)}, u32[]{:S(2)}, u32[]{:S(2)}) collective-permute-start(bf16[128,256]{1,0:T(8,128)(2,1)} %tgt_mine.1), channel_id=1, source_target_pairs={{0,128},{64,192},{128,0},{192,64},{1,129},{65,193},{129,1},{193,65... | collective-permute-start | bytes 196616 | tf_op jit(solution)/shard_map/ppermute | solution.py:229
  18.5 0.0 copy-start
  18.5 0.8 copy-done
  19.3 0.0 copy-start.1
  19.3 0.8 copy-done.1
  20.2 0.0 collective-permute-done.3.refs_3_
  20.2 0.0 collective-permute-done.2.refs_2_
  20.2 0.0 collective-permute-done.4.refs_5_
  20.2 0.0 collective-permute-done.6.refs_7_
  20.2 1.8 %collective-permute-done.5.refs_6_ = bf16[128,256]{1,0:T(8,128)(2,1)S(1)} collective-permute-done((bf16[128,256]{1,0:T(8,128)(2,1)}, bf16[128,256]{1,0:T(8,128)(2,1)S(1)}, u32[]{:S(2)}, u32[]{:S(2)}) %collective-permute-start.5) | collective-permute-done | bytes 65568 | tf_op jit(solution)/shard_map/ppermute | solution.py:229
  22.0 0.8 collective-permute-start.10
  22.8 2.5 %collective-permute-start.9 = (bf16[4,128,256]{2,1,0:T(8,128)(2,1)S(1)}, bf16[4,128,256]{2,1,0:T(8,128)(2,1)S(1)}, u32[]{:S(2)}, u32[]{:S(2)}) collective-permute-start(bf16[4,128,256]{2,1,0:T(8,128)(2,1)S(1)} %get-tuple-element.18.refs_0_), channel_id=1, source_target_pairs={{0,24},{8,0},{16,8},{24,16},{1,25},{9,1},{17,9},{25,17},{2,26},{10... | collective-permute-start | bytes 786440 | tf_op jit(solution)/shard_map/ppermute | solution.py:229
  25.3 2.0 %collective-permute-done.10.refs_1_ = bf16[4,128,256]{2,1,0:T(8,128)(2,1)S(1)} collective-permute-done((bf16[4,128,256]{2,1,0:T(8,128)(2,1)S(1)}, bf16[4,128,256]{2,1,0:T(8,128)(2,1)S(1)}, u32[]{:S(2)}, u32[]{:S(2)}) %collective-permute-start.10) | collective-permute-done | bytes 262176 | tf_op jit(solution)/shard_map/ppermute | solution.py:229
  27.3 1.3 %collective-permute-done.9.after.refs_3_ = bf16[4,128,256]{2,1,0:T(8,128)(2,1)S(1)} collective-permute-done((bf16[4,128,256]{2,1,0:T(8,128)(2,1)S(1)}, bf16[4,128,256]{2,1,0:T(8,128)(2,1)S(1)}, u32[]{:S(2)}, u32[]{:S(2)}) %collective-permute-start.9) | collective-permute-done | bytes 262176 | tf_op jit(solution)/shard_map/ppermute | solution.py:229
  28.7 4.3 %collective-permute-start.11 = (bf16[8,128,256]{2,1,0:T(8,128)(2,1)S(1)}, bf16[8,128,256]{2,1,0:T(8,128)(2,1)S(1)}, u32[]{:S(2)}, u32[]{:S(2)}) collective-permute-start(bf16[8,128,256]{2,1,0:T(8,128)(2,1)S(1)} %shard_map.62.refs_4_), channel_id=1, source_target_pairs={{0,32},{32,0},{1,33},{33,1},{2,34},{34,2},{3,35},{35,3},{4,36},{36... | collective-permute-start | bytes 1572872 | tf_op jit(solution)/shard_map/ppermute | solution.py:229
  33.0 2.5 %collective-permute-start.8 = (bf16[4,128,256]{2,1,0:T(8,128)(2,1)S(1)}, bf16[4,128,256]{2,1,0:T(8,128)(2,1)S(1)}, u32[]{:S(2)}, u32[]{:S(2)}) collective-permute-start(bf16[4,128,256]{2,1,0:T(8,128)(2,1)S(1)} %get-tuple-element.18.refs_0_), channel_id=1, source_target_pairs={{0,16},{8,24},{16,0},{24,8},{1,17},{9,25},{17,1},{25,9},{2,18},{10... | collective-permute-start | bytes 786440 | tf_op jit(solution)/shard_map/ppermute | solution.py:229
  35.5 1.5 %collective-permute-start.7 = (bf16[4,128,256]{2,1,0:T(8,128)(2,1)S(1)}, bf16[4,128,256]{2,1,0:T(8,128)(2,1)S(1)}, u32[]{:S(2)}, u32[]{:S(2)}) collective-permute-start(bf16[4,128,256]{2,1,0:T(8,128)(2,1)S(1)} %get-tuple-element.18.refs_0_), channel_id=1, source_target_pairs={{0,8},{8,16},{16,24},{24,0},{1,9},{9,17},{17,25},{25,1},{2,10},{10... | collective-permute-start | bytes 786440 | tf_op jit(solution)/shard_map/ppermute | solution.py:229
  37.0 0.1 stack.20.place
  37.1 3.3 %shard_map.59.picked = s32[8,128]{1,0:T(8,128)S(1)} custom-call(s32[3,128]{1,0:T(4,128)S(1)} %concatenate.3.mine, s32[3,128]{1,0:T(4,128)S(1)} %collective-permute-done.other.lists, s32[5]{0:T(128)S(1)} %stack.20.place), custom_call_target="tpu_custom_call" | custom-call | tf_op jit(solution)/shard_map/pallas_call | solution.py:269
  40.4 2.0 %collective-permute-done.8.refs_2_ = bf16[4,128,256]{2,1,0:T(8,128)(2,1)S(1)} collective-permute-done((bf16[4,128,256]{2,1,0:T(8,128)(2,1)S(1)}, bf16[4,128,256]{2,1,0:T(8,128)(2,1)S(1)}, u32[]{:S(2)}, u32[]{:S(2)}) %collective-permute-start.8) | collective-permute-done | bytes 262176 | tf_op jit(solution)/shard_map/ppermute | solution.py:229
  42.4 6.0 %collective-permute-done.7.refs_1_ = bf16[4,128,256]{2,1,0:T(8,128)(2,1)S(1)} collective-permute-done((bf16[4,128,256]{2,1,0:T(8,128)(2,1)S(1)}, bf16[4,128,256]{2,1,0:T(8,128)(2,1)S(1)}, u32[]{:S(2)}, u32[]{:S(2)}) %collective-permute-start.7) | collective-permute-done | bytes 262176 | tf_op jit(solution)/shard_map/ppermute | solution.py:229
  48.4 0.0 collective-permute-done.11.refs_5_
  48.4 2.7 %shard_map.63 = (f32[16,16,128]{2,1,0:T(8,128)S(1)}, bf16[16,128,256]{2,1,0:T(8,128)(2,1)S(1)}, bf16[16,128,256]{2,1,0:T(8,128)(2,1)S(1)}, f32[16,128]{1,0:T(8,128)S(1)}, f32[16,128]{1,0:T(8,128)S(1)}) custom-call(s32[8,128]{1,0:T(8,128)S(1)} %shard_map.59.picked, bf16[4,128,256]{2,1,0:T(8,128)(2,1)S(1)} %get-tuple-element.18.refs_0_, ...), custom_call_target="tpu_custom_call" | custom-call | tf_op jit(solution)/shard_map/pallas_call | solution.py:207
  51.1 17.0 %all_to_all.20.parts = f32[16,16,128]{2,1,0:T(8,128)S(1)} all-to-all(f32[16,16,128]{2,1,0:T(8,128)S(1)} %get-tuple-element.22), channel_id=1, replica_groups=mesh['y'=4,'core'=2,'x'=4,'s'=4,'p'=2] {'x','s'}, dimensions={0} | all-to-all | bytes 262144 | tf_op jit(solution)/shard_map/all_to_all | solution.py:224
  68.1 1.9 %shard_map.64 = (f32[16,16,128]{2,1,0:T(8,128)S(1)}, f32[16,128]{1,0:T(8,128)}) custom-call(s32[8,128]{1,0:T(8,128)S(1)} %shard_map.59.picked, bf16[16,128,256]{2,1,0:T(8,128)(2,1)S(1)} %get-tuple-element.20.src, bf16[16,128,256]{2,1,0:T(8,128)(2,1)S(1)} %get-tuple-element.21.tgt, f32[16,16,128]{2,1,0:T(8,128)S(1)} %all_to_all.20.parts, ...), custom_call_target="tpu_custom_call" | custom-call | tf_op jit(solution)/shard_map/pallas_call | solution.py:207
  70.0 12.6 %all_to_all.21.parts = f32[16,16,128]{2,1,0:T(8,128)S(1)} all-to-all(f32[16,16,128]{2,1,0:T(8,128)S(1)} %get-tuple-element.24), channel_id=1, replica_groups=mesh['y'=4,'core'=2,'x'=4,'s'=4,'p'=2] {'p','y','core'}, dimensions={0} | all-to-all | bytes 262144 | tf_op jit(solution)/shard_map/all_to_all | solution.py:224
  82.6 1.5 %shard_map.65 = f32[16,16,128]{2,1,0:T(8,128)S(1)} custom-call(s32[8,128]{1,0:T(8,128)S(1)} %shard_map.59.picked, bf16[16,128,256]{2,1,0:T(8,128)(2,1)S(1)} %get-tuple-element.20.src, bf16[16,128,256]{2,1,0:T(8,128)(2,1)S(1)} %get-tuple-element.21.tgt, f32[16,16,128]{2,1,0:T(8,128)S(1)} %all_to_all.21.parts), custom_call_target="tpu_custom_call" | custom-call | tf_op jit(solution)/shard_map/pallas_call | solution.py:207
  84.1 15.4 %all_to_all.22.parts = f32[16,16,128]{2,1,0:T(8,128)S(1)} all-to-all(f32[16,16,128]{2,1,0:T(8,128)S(1)} %shard_map.65), channel_id=1, replica_groups=mesh['y'=4,'core'=2,'x'=4,'s'=4,'p'=2] {'x','s'}, dimensions={0} | all-to-all | bytes 262144 | tf_op jit(solution)/shard_map/all_to_all | solution.py:224
  99.4 2.1 %shard_map.66 = (f32[16,8,128]{2,1,0:T(8,128)}, f32[16,128]{1,0:T(8,128)S(1)}) custom-call(s32[8,128]{1,0:T(8,128)S(1)} %shard_map.59.picked, bf16[16,128,256]{2,1,0:T(8,128)(2,1)S(1)} %get-tuple-element.20.src, bf16[16,128,256]{2,1,0:T(8,128)(2,1)S(1)} %get-tuple-element.21.tgt, f32[16,16,128]{2,1,0:T(8,128)S(1)} %all_to_all.22.parts, ...), custom_call_target="tpu_custom_call" | custom-call | tf_op jit(solution)/shard_map/pallas_call | solution.py:207
  101.5 6.4 %all-to-all-start.3 = ((f32[16,8,128]{2,1,0:T(8,128)}), f32[16,8,128]{2,1,0:T(8,128)S(1)}, u32[]{:S(2)}, u32[]{:S(2)}) async-start(f32[16,8,128]{2,1,0:T(8,128)} %get-tuple-element.25), calls=%async_computation.3 | async-start | bytes 131072 | tf_op jit(solution)/shard_map/all_to_all | solution.py:224
  108.0 1.4 %collective-permute-start.12 = (f32[16,128]{1,0:T(8,128)S(1)}, f32[16,128]{1,0:T(8,128)S(1)}, u32[]{:S(2)}, u32[]{:S(2)}) collective-permute-start(f32[16,128]{1,0:T(8,128)S(1)} %get-tuple-element.27.mine), channel_id=1, source_target_pairs={{0,1},{1,0},{2,3},{3,2},{4,5},{5,4},{6,7},{7,6},{8,9},{9,8},{10,11... | collective-permute-start | bytes 24584 | tf_op jit(solution)/shard_map/ppermute | solution.py:263
  109.4 1.7 %collective-permute-done.12.other = f32[16,128]{1,0:T(8,128)S(1)} collective-permute-done((f32[16,128]{1,0:T(8,128)S(1)}, f32[16,128]{1,0:T(8,128)S(1)}, u32[]{:S(2)}, u32[]{:S(2)}) %collective-permute-start.12) | collective-permute-done | bytes 8224 | tf_op jit(solution)/shard_map/ppermute | solution.py:263
  111.0 2.8 %all-to-all-done.3.parts = f32[16,8,128]{2,1,0:T(8,128)S(1)} async-done(((f32[16,8,128]{2,1,0:T(8,128)}), f32[16,8,128]{2,1,0:T(8,128)S(1)}, u32[]{:S(2)}, u32[]{:S(2)}) %all-to-all-start.3) | async-done | bytes 65568 | tf_op jit(solution)/shard_map/all_to_all | solution.py:224
  113.8 0.6 shard_map.67
  (4 shorter events, 0.1 us)
Async XLA Ops:
  0.6 16.2 %collective-permute-start.1 = (bf16[128,256]{1,0:T(8,128)(2,1)}, bf16[128,256]{1,0:T(8,128)(2,1)S(1)}, u32[]{:S(2)}, u32[]{:S(2)}) collective-permute-start(bf16[128,256]{1,0:T(8,128)(2,1)} %src_mine.1), channel_id=1, source_target_pairs={{0,2},{2,4},{4,6},{6,0},{1,3},{3,5},{5,7},{7,1},{8,10},{10,12},{12... | collective-permute-start | bytes 196616 | tf_op jit(solution)/shard_map/ppermute | solution.py:229
  5.2 0.7 copy-start.2
  5.9 9.5 %collective-permute-start = (s32[3,128]{1,0:T(4,128)S(1)}, s32[3,128]{1,0:T(4,128)S(1)}, u32[]{:S(2)}, u32[]{:S(2)}) collective-permute-start(s32[3,128]{1,0:T(4,128)S(1)} %concatenate.3.mine), channel_id=1, source_target_pairs={{0,1},{1,0},{2,3},{3,2},{4,5},{5,4},{6,7},{7,6},{8,9},{9,8},{10,11... | collective-permute-start | bytes 4616 | tf_op jit(solution)/shard_map/ppermute | solution.py:263
  7.5 12.7 %collective-permute-start.3 = (bf16[128,256]{1,0:T(8,128)(2,1)}, bf16[128,256]{1,0:T(8,128)(2,1)S(1)}, u32[]{:S(2)}, u32[]{:S(2)}) collective-permute-start(bf16[128,256]{1,0:T(8,128)(2,1)} %src_mine.1), channel_id=1, source_target_pairs={{0,6},{2,0},{4,2},{6,4},{1,7},{3,1},{5,3},{7,5},{8,14},{10,8},{12,... | collective-permute-start | bytes 196616 | tf_op jit(solution)/shard_map/ppermute | solution.py:229
  9.6 10.6 %collective-permute-start.2 = (bf16[128,256]{1,0:T(8,128)(2,1)}, bf16[128,256]{1,0:T(8,128)(2,1)S(1)}, u32[]{:S(2)}, u32[]{:S(2)}) collective-permute-start(bf16[128,256]{1,0:T(8,128)(2,1)} %src_mine.1), channel_id=1, source_target_pairs={{0,4},{2,6},{4,0},{6,2},{1,5},{3,7},{5,1},{7,3},{8,12},{10,14},{12... | collective-permute-start | bytes 196616 | tf_op jit(solution)/shard_map/ppermute | solution.py:229
  14.1 6.1 %collective-permute-start.4 = (bf16[128,256]{1,0:T(8,128)(2,1)}, bf16[128,256]{1,0:T(8,128)(2,1)S(1)}, u32[]{:S(2)}, u32[]{:S(2)}) collective-permute-start(bf16[128,256]{1,0:T(8,128)(2,1)} %tgt_mine.1), channel_id=1, source_target_pairs={{0,64},{64,128},{128,192},{192,0},{1,65},{65,129},{129,193},{193,1... | collective-permute-start | bytes 196616 | tf_op jit(solution)/shard_map/ppermute | solution.py:229
  15.4 4.8 %collective-permute-start.6 = (bf16[128,256]{1,0:T(8,128)(2,1)}, bf16[128,256]{1,0:T(8,128)(2,1)S(1)}, u32[]{:S(2)}, u32[]{:S(2)}) collective-permute-start(bf16[128,256]{1,0:T(8,128)(2,1)} %tgt_mine.1), channel_id=1, source_target_pairs={{0,192},{64,0},{128,64},{192,128},{1,193},{65,1},{129,65},{193,129... | collective-permute-start | bytes 196616 | tf_op jit(solution)/shard_map/ppermute | solution.py:229
  16.8 5.1 %collective-permute-start.5 = (bf16[128,256]{1,0:T(8,128)(2,1)}, bf16[128,256]{1,0:T(8,128)(2,1)S(1)}, u32[]{:S(2)}, u32[]{:S(2)}) collective-permute-start(bf16[128,256]{1,0:T(8,128)(2,1)} %tgt_mine.1), channel_id=1, source_target_pairs={{0,128},{64,192},{128,0},{192,64},{1,129},{65,193},{129,1},{193,65... | collective-permute-start | bytes 196616 | tf_op jit(solution)/shard_map/ppermute | solution.py:229
  18.5 0.8 copy-start
  19.3 0.8 copy-start.1
  22.0 5.3 %collective-permute-start.10 = (bf16[4,128,256]{2,1,0:T(8,128)(2,1)S(1)}, bf16[4,128,256]{2,1,0:T(8,128)(2,1)S(1)}, u32[]{:S(2)}, u32[]{:S(2)}) collective-permute-start(bf16[4,128,256]{2,1,0:T(8,128)(2,1)S(1)} %get-tuple-element.19.refs_0_), channel_id=1, source_target_pairs={{0,1},{1,0},{2,3},{3,2},{4,5},{5,4},{6,7},{7,6},{8,9},{9,8},{10,11... | collective-permute-start | bytes 786440 | tf_op jit(solution)/shard_map/ppermute | solution.py:229
  22.8 5.8 %collective-permute-start.9 = (bf16[4,128,256]{2,1,0:T(8,128)(2,1)S(1)}, bf16[4,128,256]{2,1,0:T(8,128)(2,1)S(1)}, u32[]{:S(2)}, u32[]{:S(2)}) collective-permute-start(bf16[4,128,256]{2,1,0:T(8,128)(2,1)S(1)} %get-tuple-element.18.refs_0_), channel_id=1, source_target_pairs={{0,24},{8,0},{16,8},{24,16},{1,25},{9,1},{17,9},{25,17},{2,26},{10... | collective-permute-start | bytes 786440 | tf_op jit(solution)/shard_map/ppermute | solution.py:229
  28.7 19.7 %collective-permute-start.11 = (bf16[8,128,256]{2,1,0:T(8,128)(2,1)S(1)}, bf16[8,128,256]{2,1,0:T(8,128)(2,1)S(1)}, u32[]{:S(2)}, u32[]{:S(2)}) collective-permute-start(bf16[8,128,256]{2,1,0:T(8,128)(2,1)S(1)} %shard_map.62.refs_4_), channel_id=1, source_target_pairs={{0,32},{32,0},{1,33},{33,1},{2,34},{34,2},{3,35},{35,3},{4,36},{36... | collective-permute-start | bytes 1572872 | tf_op jit(solution)/shard_map/ppermute | solution.py:229
  33.0 9.4 %collective-permute-start.8 = (bf16[4,128,256]{2,1,0:T(8,128)(2,1)S(1)}, bf16[4,128,256]{2,1,0:T(8,128)(2,1)S(1)}, u32[]{:S(2)}, u32[]{:S(2)}) collective-permute-start(bf16[4,128,256]{2,1,0:T(8,128)(2,1)S(1)} %get-tuple-element.18.refs_0_), channel_id=1, source_target_pairs={{0,16},{8,24},{16,0},{24,8},{1,17},{9,25},{17,1},{25,9},{2,18},{10... | collective-permute-start | bytes 786440 | tf_op jit(solution)/shard_map/ppermute | solution.py:229
  35.5 12.9 %collective-permute-start.7 = (bf16[4,128,256]{2,1,0:T(8,128)(2,1)S(1)}, bf16[4,128,256]{2,1,0:T(8,128)(2,1)S(1)}, u32[]{:S(2)}, u32[]{:S(2)}) collective-permute-start(bf16[4,128,256]{2,1,0:T(8,128)(2,1)S(1)} %get-tuple-element.18.refs_0_), channel_id=1, source_target_pairs={{0,8},{8,16},{16,24},{24,0},{1,9},{9,17},{17,25},{25,1},{2,10},{10... | collective-permute-start | bytes 786440 | tf_op jit(solution)/shard_map/ppermute | solution.py:229
  101.5 12.3 %all-to-all-start.3 = ((f32[16,8,128]{2,1,0:T(8,128)}), f32[16,8,128]{2,1,0:T(8,128)S(1)}, u32[]{:S(2)}, u32[]{:S(2)}) async-start(f32[16,8,128]{2,1,0:T(8,128)} %get-tuple-element.25), calls=%async_computation.3 | async-start | bytes 131072 | tf_op jit(solution)/shard_map/all_to_all | solution.py:224
  108.0 3.1 %collective-permute-start.12 = (f32[16,128]{1,0:T(8,128)S(1)}, f32[16,128]{1,0:T(8,128)S(1)}, u32[]{:S(2)}, u32[]{:S(2)}) collective-permute-start(f32[16,128]{1,0:T(8,128)S(1)} %get-tuple-element.27.mine), channel_id=1, source_target_pairs={{0,1},{1,0},{2,3},{3,2},{4,5},{5,4},{6,7},{7,6},{8,9},{9,8},{10,11... | collective-permute-start | bytes 24584 | tf_op jit(solution)/shard_map/ppermute | solution.py:263

commit v9 on v8

--- a/solution.py
+++ b/solution.py
@@ -133,30 +133,24 @@
         tgt[n] = refs[sides + n][...]
 
 
-def join_kernel(after, *refs):
-    blocks = refs[0].shape[0]
-    for n, piece in enumerate(refs[:-1]):
-        refs[-1][n * blocks : (n + 1) * blocks] = piece[...]
+def after_kernel(first, block, out):
+    out[...] = block[...]
 
 
 def first_kernel(picked, *refs):
     pieces, (out, src, tgt, sq_src, sq_tgt, wide, peaks, totals, tiles, sem) = refs[:-10], refs[-10:]
     fetch = pltpu.make_async_copy(picked, tiles, sem)
     fetch.start()
-    tgt_pieces = pieces[4:]
-    sides, cores = len(pieces) - len(tgt_pieces), len(tgt_pieces)
+    sides = len(pieces) // 2
     fetch.wait()
     place = [tiles[0, 1 + n] for n in range(5)]
     for d in range(sides):
         x = lax.rem(place[0] + (sides - d), sides)
-        for n in range(pieces[d].shape[0]):
-            s = lax.rem(place[1] + (sides - n), sides)
+        p, core = place[3] ^ (d // 2), place[4] ^ (d % 2)
+        for n in range(sides):
+            s, y = (lax.rem(place[axis] + (sides - n), sides) for axis in (1, 2))
             src[x * sides + s] = pieces[d][n]
-    for d, piece in enumerate(tgt_pieces):
-        core = place[4] ^ d
-        for n in range(piece.shape[0]):
-            p, y = place[3] ^ (n // sides), lax.rem(place[2] + (sides - n % sides), sides)
-            tgt[p * (cores * sides) + cores * y + core] = piece[n]
+            tgt[p * (2 * sides) + 2 * y + core] = pieces[sides + d][n]
     for b in range(tgt.shape[0]):
         sq_tgt[b : b + 1, :] = square_rows(tgt[b])
     for a in range(src.shape[0]):
@@ -245,15 +239,11 @@
         out_specs=[VMEM] * 2,
         compiler_params=PARAMS,
     )(lists, *blocks)
-    src_pieces, tgt_pieces = shifts(src, "x"), shifts(tgt, "p")
-    both = pl.pallas_call(
-        join_kernel,
-        out_shape=jax.ShapeDtypeStruct((len(tgt_pieces) * tgt.shape[0],) + tgt.shape[1:], tgt.dtype),
-        in_specs=[ANY] + [VMEM] * len(tgt_pieces),
-        out_specs=VMEM,
-        compiler_params=PARAMS,
-    )(src_pieces[-1], *tgt_pieces)
-    return src_pieces, shifts(both, "core")
+    mine, partner = shifts(tgt, "p")
+    mine = pl.pallas_call(
+        after_kernel, out_shape=group, in_specs=[ANY, VMEM], out_specs=VMEM, compiler_params=PARAMS
+    )(partner, mine)
+    return shifts(src, "x"), [piece for side in (mine, partner) for piece in shifts(side, "core")]
 
 
 def local(src_embed, tgt_embed, tiles, counts):

time: 115 us -> 108 us (0.939); the launches traced: 114 us -> 106 us
  waiting for transfers between devices: 17.5 us -> 11 us
  Pallas kernels: 12.2 us -> 16.3 us
  blocking collectives: 44.9 us -> 41.2 us
  starting transfers between devices: 36 us -> 33.6 us
    ppermute x11 -> x12, waiting for transfers between devices: 13.1 us -> 6.52 us  [shifts(): lax.ppermute(block, axis, [(i, (i + d) % n) for i in range(n)])]
    pallas_call x4, Pallas kernels: 8.15 us -> 12.3 us  [half_step(): pl.pallas_call(kernel, out_shape=[s if isinstance(s, jax.ShapeDtypeStruct...]
    all_to_all x3, blocking collectives: 44.9 us -> 41.2 us  [exchange(): return lax.all_to_all(copies, peers, 0, 0, tiled=True)]
    ppermute x11 -> x12, starting transfers between devices: 26.5 us -> 23.8 us  [shifts(): lax.ppermute(block, axis, [(i, (i + d) % n) for i in range(n)])]
  transfers between devices with their start and end apart: 14 -> 15, of which waited for: 7 -> 5; matrix products, arithmetic and copies ran while one was open for 0% -> 0% of each run, Pallas kernels for 3% -> 3%
where the time goes in v9:
time: 108 us; the launch traced here: 106 us
  blocking collectives  41.2 us (38%)
  starting transfers between devices  33.6 us (31%)
  Pallas kernels  16.3 us (15%)
  waiting for transfers between devices  11 us (10%)
  local copies, waits for them, and re-layouts  2.44 us (2%)
  between operations  1.4 us (1%)
    all_to_all x3, blocking collectives, exchange(): return lax.all_to_all(copies, peers, 0, 0, tiled=True)  41.2 us
    ppermute x12, starting transfers between devices, shifts(): lax.ppermute(block, axis, [(i, (i + d) % n) for i in range(n)])  23.8 us
    pallas_call x4, Pallas kernels, half_step(): pl.pallas_call(kernel, out_shape=[s if isinstance(s, jax.ShapeDtypeStruct...  12.3 us
    all_to_all x1, starting transfers between devices, exchange(): return lax.all_to_all(copies, peers, 0, 0, tiled=True)  6.83 us
    ppermute x12, waiting for transfers between devices, shifts(): lax.ppermute(block, axis, [(i, (i + d) % n) for i in range(n)])  6.52 us
    pallas_call x1, Pallas kernels, local(): pl.pallas_call(pick_kernel, out_shape=jax.ShapeDtypeStruct((8, TILE), jnp...  3.31 us
    ppermute x2, starting transfers between devices, local(): partner = lambda v: lax.ppermute(v, 'p', [(0, 1), (1, 0)])  3.03 us
    all_to_all x1, waiting for transfers between devices, exchange(): return lax.all_to_all(copies, peers, 0, 0, tiled=True)  2.77 us
  transfers between devices with their start and end apart: 15, of which 5 were waited for; matrix products, arithmetic and copies ran while one was open for 0% of the time, Pallas kernels for 3%

profile of v9, /device:TPU:1, one launch (start us, length us, event | category | flops | bytes accessed | tf_op | source)
XLA Modules:
  0.0 105.9 jit_solution(6525961781361427833)
XLA Ops:
  0.6 3.9 %collective-permute-start.1 = (bf16[128,256]{1,0:T(8,128)(2,1)}, bf16[128,256]{1,0:T(8,128)(2,1)S(1)}, u32[]{:S(2)}, u32[]{:S(2)}) collective-permute-start(bf16[128,256]{1,0:T(8,128)(2,1)} %src_mine.1), channel_id=1, source_target_pairs={{0,2},{2,4},{4,6},{6,0},{1,3},{3,5},{5,7},{7,1},{8,10},{10,12},{12... | collective-permute-start | bytes 196616 | tf_op jit(solution)/shard_map/ppermute | solution.py:223
  5.2 0.0 copy-start.2
  5.2 0.7 copy-done.2
  5.9 1.6 %collective-permute-start = (s32[3,128]{1,0:T(4,128)S(1)}, s32[3,128]{1,0:T(4,128)S(1)}, u32[]{:S(2)}, u32[]{:S(2)}) collective-permute-start(s32[3,128]{1,0:T(4,128)S(1)} %concatenate.3.mine), channel_id=1, source_target_pairs={{0,1},{1,0},{2,3},{3,2},{4,5},{5,4},{6,7},{7,6},{8,9},{9,8},{10,11... | collective-permute-start | bytes 4616 | tf_op jit(solution)/shard_map/ppermute | solution.py:253
  7.5 2.1 %collective-permute-start.3 = (bf16[128,256]{1,0:T(8,128)(2,1)}, bf16[128,256]{1,0:T(8,128)(2,1)S(1)}, u32[]{:S(2)}, u32[]{:S(2)}) collective-permute-start(bf16[128,256]{1,0:T(8,128)(2,1)} %src_mine.1), channel_id=1, source_target_pairs={{0,6},{2,0},{4,2},{6,4},{1,7},{3,1},{5,3},{7,5},{8,14},{10,8},{12,... | collective-permute-start | bytes 196616 | tf_op jit(solution)/shard_map/ppermute | solution.py:223
  9.6 4.5 %collective-permute-start.2 = (bf16[128,256]{1,0:T(8,128)(2,1)}, bf16[128,256]{1,0:T(8,128)(2,1)S(1)}, u32[]{:S(2)}, u32[]{:S(2)}) collective-permute-start(bf16[128,256]{1,0:T(8,128)(2,1)} %src_mine.1), channel_id=1, source_target_pairs={{0,4},{2,6},{4,0},{6,2},{1,5},{3,7},{5,1},{7,3},{8,12},{10,14},{12... | collective-permute-start | bytes 196616 | tf_op jit(solution)/shard_map/ppermute | solution.py:223
  14.1 1.3 %collective-permute-start.4 = (bf16[128,256]{1,0:T(8,128)(2,1)}, bf16[128,256]{1,0:T(8,128)(2,1)S(1)}, u32[]{:S(2)}, u32[]{:S(2)}) collective-permute-start(bf16[128,256]{1,0:T(8,128)(2,1)} %tgt_mine.1), channel_id=1, source_target_pairs={{0,64},{64,128},{128,192},{192,0},{1,65},{65,129},{129,193},{193,1... | collective-permute-start | bytes 196616 | tf_op jit(solution)/shard_map/ppermute | solution.py:223
  15.4 0.0 collective-permute-done.other.lists
  15.4 1.4 %collective-permute-start.6 = (bf16[128,256]{1,0:T(8,128)(2,1)}, bf16[128,256]{1,0:T(8,128)(2,1)S(1)}, u32[]{:S(2)}, u32[]{:S(2)}) collective-permute-start(bf16[128,256]{1,0:T(8,128)(2,1)} %tgt_mine.1), channel_id=1, source_target_pairs={{0,192},{64,0},{128,64},{192,128},{1,193},{65,1},{129,65},{193,129... | collective-permute-start | bytes 196616 | tf_op jit(solution)/shard_map/ppermute | solution.py:223
  16.8 0.0 collective-permute-done.1.refs_1_
  16.8 1.6 %collective-permute-start.5 = (bf16[128,256]{1,0:T(8,128)(2,1)}, bf16[128,256]{1,0:T(8,128)(2,1)S(1)}, u32[]{:S(2)}, u32[]{:S(2)}) collective-permute-start(bf16[128,256]{1,0:T(8,128)(2,1)} %tgt_mine.1), channel_id=1, source_target_pairs={{0,128},{64,192},{128,0},{192,64},{1,129},{65,193},{129,1},{193,65... | collective-permute-start | bytes 196616 | tf_op jit(solution)/shard_map/ppermute | solution.py:223
  18.5 0.0 copy-start
  18.5 0.8 copy-done
  19.3 0.0 copy-start.1
  19.3 0.8 copy-done.1
  20.2 0.0 collective-permute-done.3.refs_3_
  20.2 0.0 collective-permute-done.2.refs_2_
  20.2 0.0 collective-permute-done.4.refs_5_
  20.2 0.0 collective-permute-done.6.refs_7_
  20.2 1.8 %collective-permute-done.5.refs_6_ = bf16[128,256]{1,0:T(8,128)(2,1)S(1)} collective-permute-done((bf16[128,256]{1,0:T(8,128)(2,1)}, bf16[128,256]{1,0:T(8,128)(2,1)S(1)}, u32[]{:S(2)}, u32[]{:S(2)}) %collective-permute-start.5) | collective-permute-done | bytes 65568 | tf_op jit(solution)/shard_map/ppermute | solution.py:223
  22.0 0.8 collective-permute-start.10
  22.8 2.5 %collective-permute-start.9 = (bf16[4,128,256]{2,1,0:T(8,128)(2,1)S(1)}, bf16[4,128,256]{2,1,0:T(8,128)(2,1)S(1)}, u32[]{:S(2)}, u32[]{:S(2)}) collective-permute-start(bf16[4,128,256]{2,1,0:T(8,128)(2,1)S(1)} %get-tuple-element.18.refs_0_), channel_id=1, source_target_pairs={{0,24},{8,0},{16,8},{24,16},{1,25},{9,1},{17,9},{25,17},{2,26},{10... | collective-permute-start | bytes 786440 | tf_op jit(solution)/shard_map/ppermute | solution.py:223
  25.3 0.5 collective-permute-start.8
  25.8 0.6 collective-permute-start.7
  26.5 0.9 collective-permute-done.10.first.refs_6_
  27.4 4.4 %collective-permute-start.11 = (bf16[4,128,256]{2,1,0:T(8,128)(2,1)S(1)}, bf16[4,128,256]{2,1,0:T(8,128)(2,1)S(1)}, u32[]{:S(2)}, u32[]{:S(2)}) collective-permute-start(bf16[4,128,256]{2,1,0:T(8,128)(2,1)S(1)} %shard_map.62.refs_4_), channel_id=1, source_target_pairs={{0,32},{32,0},{1,33},{33,1},{2,34},{34,2},{3,35},{35,3},{4,36},{36... | collective-permute-start | bytes 786440 | tf_op jit(solution)/shard_map/ppermute | solution.py:223
  31.7 0.1 collective-permute-start.12
  31.8 0.1 stack.20.place
  31.9 3.3 %shard_map.59.picked = s32[8,128]{1,0:T(8,128)S(1)} custom-call(s32[3,128]{1,0:T(4,128)S(1)} %concatenate.3.mine, s32[3,128]{1,0:T(4,128)S(1)} %collective-permute-done.other.lists, s32[5]{0:T(128)S(1)} %stack.20.place), custom_call_target="tpu_custom_call" | custom-call | tf_op jit(solution)/shard_map/pallas_call | solution.py:259
  35.2 0.0 collective-permute-done.9.refs_3_
  35.2 0.0 collective-permute-done.8.refs_2_
  35.2 3.8 %collective-permute-done.7.refs_1_ = bf16[4,128,256]{2,1,0:T(8,128)(2,1)S(1)} collective-permute-done((bf16[4,128,256]{2,1,0:T(8,128)(2,1)S(1)}, bf16[4,128,256]{2,1,0:T(8,128)(2,1)S(1)}, u32[]{:S(2)}, u32[]{:S(2)}) %collective-permute-start.7) | collective-permute-done | bytes 262176 | tf_op jit(solution)/shard_map/ppermute | solution.py:223
  39.1 0.0 collective-permute-done.11.refs_5_
  39.1 0.0 collective-permute-done.12.refs_7_
  39.1 3.7 %shard_map.63 = (f32[16,16,128]{2,1,0:T(8,128)S(1)}, bf16[16,128,256]{2,1,0:T(8,128)(2,1)S(1)}, bf16[16,128,256]{2,1,0:T(8,128)(2,1)S(1)}, f32[16,128]{1,0:T(8,128)S(1)}, f32[16,128]{1,0:T(8,128)S(1)}) custom-call(s32[8,128]{1,0:T(8,128)S(1)} %shard_map.59.picked, bf16[4,128,256]{2,1,0:T(8,128)(2,1)S(1)} %get-tuple-element.18.refs_0_, ...), custom_call_target="tpu_custom_call" | custom-call | tf_op jit(solution)/shard_map/pallas_call | solution.py:201
  42.8 14.0 %all_to_all.20.parts = f32[16,16,128]{2,1,0:T(8,128)S(1)} all-to-all(f32[16,16,128]{2,1,0:T(8,128)S(1)} %get-tuple-element.22), channel_id=1, replica_groups=mesh['y'=4,'core'=2,'x'=4,'s'=4,'p'=2] {'x','s'}, dimensions={0} | all-to-all | bytes 262144 | tf_op jit(solution)/shard_map/all_to_all | solution.py:218
  56.8 3.0 %shard_map.64 = (f32[16,16,128]{2,1,0:T(8,128)S(1)}, f32[16,128]{1,0:T(8,128)}) custom-call(s32[8,128]{1,0:T(8,128)S(1)} %shard_map.59.picked, bf16[16,128,256]{2,1,0:T(8,128)(2,1)S(1)} %get-tuple-element.20.src, bf16[16,128,256]{2,1,0:T(8,128)(2,1)S(1)} %get-tuple-element.21.tgt, f32[16,16,128]{2,1,0:T(8,128)S(1)} %all_to_all.20.parts, ...), custom_call_target="tpu_custom_call" | custom-call | tf_op jit(solution)/shard_map/pallas_call | solution.py:201
  59.9 13.3 %all_to_all.21.parts = f32[16,16,128]{2,1,0:T(8,128)S(1)} all-to-all(f32[16,16,128]{2,1,0:T(8,128)S(1)} %get-tuple-element.24), channel_id=1, replica_groups=mesh['y'=4,'core'=2,'x'=4,'s'=4,'p'=2] {'p','y','core'}, dimensions={0} | all-to-all | bytes 262144 | tf_op jit(solution)/shard_map/all_to_all | solution.py:218
  73.2 2.5 %shard_map.65 = f32[16,16,128]{2,1,0:T(8,128)S(1)} custom-call(s32[8,128]{1,0:T(8,128)S(1)} %shard_map.59.picked, bf16[16,128,256]{2,1,0:T(8,128)(2,1)S(1)} %get-tuple-element.20.src, bf16[16,128,256]{2,1,0:T(8,128)(2,1)S(1)} %get-tuple-element.21.tgt, f32[16,16,128]{2,1,0:T(8,128)S(1)} %all_to_all.21.parts), custom_call_target="tpu_custom_call" | custom-call | tf_op jit(solution)/shard_map/pallas_call | solution.py:201
  75.7 13.9 %all_to_all.22.parts = f32[16,16,128]{2,1,0:T(8,128)S(1)} all-to-all(f32[16,16,128]{2,1,0:T(8,128)S(1)} %shard_map.65), channel_id=1, replica_groups=mesh['y'=4,'core'=2,'x'=4,'s'=4,'p'=2] {'x','s'}, dimensions={0} | all-to-all | bytes 262144 | tf_op jit(solution)/shard_map/all_to_all | solution.py:218
  89.5 3.1 %shard_map.66 = (f32[16,8,128]{2,1,0:T(8,128)}, f32[16,128]{1,0:T(8,128)S(1)}) custom-call(s32[8,128]{1,0:T(8,128)S(1)} %shard_map.59.picked, bf16[16,128,256]{2,1,0:T(8,128)(2,1)S(1)} %get-tuple-element.20.src, bf16[16,128,256]{2,1,0:T(8,128)(2,1)S(1)} %get-tuple-element.21.tgt, f32[16,16,128]{2,1,0:T(8,128)S(1)} %all_to_all.22.parts, ...), custom_call_target="tpu_custom_call" | custom-call | tf_op jit(solution)/shard_map/pallas_call | solution.py:201
  92.7 6.8 %all-to-all-start.3 = ((f32[16,8,128]{2,1,0:T(8,128)}), f32[16,8,128]{2,1,0:T(8,128)S(1)}, u32[]{:S(2)}, u32[]{:S(2)}) async-start(f32[16,8,128]{2,1,0:T(8,128)} %get-tuple-element.25), calls=%async_computation.3 | async-start | bytes 131072 | tf_op jit(solution)/shard_map/all_to_all | solution.py:218
  99.5 1.4 %collective-permute-start.13 = (f32[16,128]{1,0:T(8,128)S(1)}, f32[16,128]{1,0:T(8,128)S(1)}, u32[]{:S(2)}, u32[]{:S(2)}) collective-permute-start(f32[16,128]{1,0:T(8,128)S(1)} %get-tuple-element.27.mine), channel_id=1, source_target_pairs={{0,1},{1,0},{2,3},{3,2},{4,5},{5,4},{6,7},{7,6},{8,9},{9,8},{10,11... | collective-permute-start | bytes 24584 | tf_op jit(solution)/shard_map/ppermute | solution.py:253
  100.9 1.7 %collective-permute-done.13.other = f32[16,128]{1,0:T(8,128)S(1)} collective-permute-done((f32[16,128]{1,0:T(8,128)S(1)}, f32[16,128]{1,0:T(8,128)S(1)}, u32[]{:S(2)}, u32[]{:S(2)}) %collective-permute-start.13) | collective-permute-done | bytes 8224 | tf_op jit(solution)/shard_map/ppermute | solution.py:253
  102.5 2.8 %all-to-all-done.3.parts = f32[16,8,128]{2,1,0:T(8,128)S(1)} async-done(((f32[16,8,128]{2,1,0:T(8,128)}), f32[16,8,128]{2,1,0:T(8,128)S(1)}, u32[]{:S(2)}, u32[]{:S(2)}) %all-to-all-start.3) | async-done | bytes 65568 | tf_op jit(solution)/shard_map/all_to_all | solution.py:218
  105.3 0.6 shard_map.67
  (4 shorter events, 0.1 us)
Async XLA Ops:
  0.6 16.2 %collective-permute-start.1 = (bf16[128,256]{1,0:T(8,128)(2,1)}, bf16[128,256]{1,0:T(8,128)(2,1)S(1)}, u32[]{:S(2)}, u32[]{:S(2)}) collective-permute-start(bf16[128,256]{1,0:T(8,128)(2,1)} %src_mine.1), channel_id=1, source_target_pairs={{0,2},{2,4},{4,6},{6,0},{1,3},{3,5},{5,7},{7,1},{8,10},{10,12},{12... | collective-permute-start | bytes 196616 | tf_op jit(solution)/shard_map/ppermute | solution.py:223
  5.2 0.7 copy-start.2
  5.9 9.5 %collective-permute-start = (s32[3,128]{1,0:T(4,128)S(1)}, s32[3,128]{1,0:T(4,128)S(1)}, u32[]{:S(2)}, u32[]{:S(2)}) collective-permute-start(s32[3,128]{1,0:T(4,128)S(1)} %concatenate.3.mine), channel_id=1, source_target_pairs={{0,1},{1,0},{2,3},{3,2},{4,5},{5,4},{6,7},{7,6},{8,9},{9,8},{10,11... | collective-permute-start | bytes 4616 | tf_op jit(solution)/shard_map/ppermute | solution.py:253
  7.5 12.7 %collective-permute-start.3 = (bf16[128,256]{1,0:T(8,128)(2,1)}, bf16[128,256]{1,0:T(8,128)(2,1)S(1)}, u32[]{:S(2)}, u32[]{:S(2)}) collective-permute-start(bf16[128,256]{1,0:T(8,128)(2,1)} %src_mine.1), channel_id=1, source_target_pairs={{0,6},{2,0},{4,2},{6,4},{1,7},{3,1},{5,3},{7,5},{8,14},{10,8},{12,... | collective-permute-start | bytes 196616 | tf_op jit(solution)/shard_map/ppermute | solution.py:223
  9.6 10.6 %collective-permute-start.2 = (bf16[128,256]{1,0:T(8,128)(2,1)}, bf16[128,256]{1,0:T(8,128)(2,1)S(1)}, u32[]{:S(2)}, u32[]{:S(2)}) collective-permute-start(bf16[128,256]{1,0:T(8,128)(2,1)} %src_mine.1), channel_id=1, source_target_pairs={{0,4},{2,6},{4,0},{6,2},{1,5},{3,7},{5,1},{7,3},{8,12},{10,14},{12... | collective-permute-start | bytes 196616 | tf_op jit(solution)/shard_map/ppermute | solution.py:223
  14.1 6.1 %collective-permute-start.4 = (bf16[128,256]{1,0:T(8,128)(2,1)}, bf16[128,256]{1,0:T(8,128)(2,1)S(1)}, u32[]{:S(2)}, u32[]{:S(2)}) collective-permute-start(bf16[128,256]{1,0:T(8,128)(2,1)} %tgt_mine.1), channel_id=1, source_target_pairs={{0,64},{64,128},{128,192},{192,0},{1,65},{65,129},{129,193},{193,1... | collective-permute-start | bytes 196616 | tf_op jit(solution)/shard_map/ppermute | solution.py:223
  15.4 4.8 %collective-permute-start.6 = (bf16[128,256]{1,0:T(8,128)(2,1)}, bf16[128,256]{1,0:T(8,128)(2,1)S(1)}, u32[]{:S(2)}, u32[]{:S(2)}) collective-permute-start(bf16[128,256]{1,0:T(8,128)(2,1)} %tgt_mine.1), channel_id=1, source_target_pairs={{0,192},{64,0},{128,64},{192,128},{1,193},{65,1},{129,65},{193,129... | collective-permute-start | bytes 196616 | tf_op jit(solution)/shard_map/ppermute | solution.py:223
  16.8 5.1 %collective-permute-start.5 = (bf16[128,256]{1,0:T(8,128)(2,1)}, bf16[128,256]{1,0:T(8,128)(2,1)S(1)}, u32[]{:S(2)}, u32[]{:S(2)}) collective-permute-start(bf16[128,256]{1,0:T(8,128)(2,1)} %tgt_mine.1), channel_id=1, source_target_pairs={{0,128},{64,192},{128,0},{192,64},{1,129},{65,193},{129,1},{193,65... | collective-permute-start | bytes 196616 | tf_op jit(solution)/shard_map/ppermute | solution.py:223
  18.5 0.8 copy-start
  19.3 0.8 copy-start.1
  22.0 5.3 %collective-permute-start.10 = (bf16[4,128,256]{2,1,0:T(8,128)(2,1)S(1)}, bf16[4,128,256]{2,1,0:T(8,128)(2,1)S(1)}, u32[]{:S(2)}, u32[]{:S(2)}) collective-permute-start(bf16[4,128,256]{2,1,0:T(8,128)(2,1)S(1)} %get-tuple-element.19.block), channel_id=1, source_target_pairs={{0,1},{1,0},{2,3},{3,2},{4,5},{5,4},{6,7},{7,6},{8,9},{9,8},{10,11... | collective-permute-start | bytes 786440 | tf_op jit(solution)/shard_map/ppermute | solution.py:223
  22.8 12.4 %collective-permute-start.9 = (bf16[4,128,256]{2,1,0:T(8,128)(2,1)S(1)}, bf16[4,128,256]{2,1,0:T(8,128)(2,1)S(1)}, u32[]{:S(2)}, u32[]{:S(2)}) collective-permute-start(bf16[4,128,256]{2,1,0:T(8,128)(2,1)S(1)} %get-tuple-element.18.refs_0_), channel_id=1, source_target_pairs={{0,24},{8,0},{16,8},{24,16},{1,25},{9,1},{17,9},{25,17},{2,26},{10... | collective-permute-start | bytes 786440 | tf_op jit(solution)/shard_map/ppermute | solution.py:223
  25.3 9.9 %collective-permute-start.8 = (bf16[4,128,256]{2,1,0:T(8,128)(2,1)S(1)}, bf16[4,128,256]{2,1,0:T(8,128)(2,1)S(1)}, u32[]{:S(2)}, u32[]{:S(2)}) collective-permute-start(bf16[4,128,256]{2,1,0:T(8,128)(2,1)S(1)} %get-tuple-element.18.refs_0_), channel_id=1, source_target_pairs={{0,16},{8,24},{16,0},{24,8},{1,17},{9,25},{17,1},{25,9},{2,18},{10... | collective-permute-start | bytes 786440 | tf_op jit(solution)/shard_map/ppermute | solution.py:223
  25.8 13.2 %collective-permute-start.7 = (bf16[4,128,256]{2,1,0:T(8,128)(2,1)S(1)}, bf16[4,128,256]{2,1,0:T(8,128)(2,1)S(1)}, u32[]{:S(2)}, u32[]{:S(2)}) collective-permute-start(bf16[4,128,256]{2,1,0:T(8,128)(2,1)S(1)} %get-tuple-element.18.refs_0_), channel_id=1, source_target_pairs={{0,8},{8,16},{16,24},{24,0},{1,9},{9,17},{17,25},{25,1},{2,10},{10... | collective-permute-start | bytes 786440 | tf_op jit(solution)/shard_map/ppermute | solution.py:223
  27.4 11.7 %collective-permute-start.11 = (bf16[4,128,256]{2,1,0:T(8,128)(2,1)S(1)}, bf16[4,128,256]{2,1,0:T(8,128)(2,1)S(1)}, u32[]{:S(2)}, u32[]{:S(2)}) collective-permute-start(bf16[4,128,256]{2,1,0:T(8,128)(2,1)S(1)} %shard_map.62.refs_4_), channel_id=1, source_target_pairs={{0,32},{32,0},{1,33},{33,1},{2,34},{34,2},{3,35},{35,3},{4,36},{36... | collective-permute-start | bytes 786440 | tf_op jit(solution)/shard_map/ppermute | solution.py:223
  31.7 7.4 %collective-permute-start.12 = (bf16[4,128,256]{2,1,0:T(8,128)(2,1)S(1)}, bf16[4,128,256]{2,1,0:T(8,128)(2,1)S(1)}, u32[]{:S(2)}, u32[]{:S(2)}) collective-permute-start(bf16[4,128,256]{2,1,0:T(8,128)(2,1)S(1)} %collective-permute-done.10.first.refs_6_), channel_id=1, source_target_pairs={{0,32},{32,0},{1,33},{33,1},{2,34},{34,2},{3,35},{35,3},{4,36},{36... | collective-permute-start | bytes 786440 | tf_op jit(solution)/shard_map/ppermute | solution.py:223
  92.7 12.7 %all-to-all-start.3 = ((f32[16,8,128]{2,1,0:T(8,128)}), f32[16,8,128]{2,1,0:T(8,128)S(1)}, u32[]{:S(2)}, u32[]{:S(2)}) async-start(f32[16,8,128]{2,1,0:T(8,128)} %get-tuple-element.25), calls=%async_computation.3 | async-start | bytes 131072 | tf_op jit(solution)/shard_map/all_to_all | solution.py:218
  99.5 3.1 %collective-permute-start.13 = (f32[16,128]{1,0:T(8,128)S(1)}, f32[16,128]{1,0:T(8,128)S(1)}, u32[]{:S(2)}, u32[]{:S(2)}) collective-permute-start(f32[16,128]{1,0:T(8,128)S(1)} %get-tuple-element.27.mine), channel_id=1, source_target_pairs={{0,1},{1,0},{2,3},{3,2},{4,5},{5,4},{6,7},{7,6},{8,9},{9,8},{10,11... | collective-permute-start | bytes 24584 | tf_op jit(solution)/shard_map/ppermute | solution.py:253

commit v10 on v9

--- a/solution.py
+++ b/solution.py
@@ -83,24 +83,29 @@
 def pick_kernel(mine, other, place, picked):
     p = place[3]
     targets = 8
-
-    def scan(lists, col, start):
-        count = lists[2, 0]
-
-        def step(k, at):
-            a, b = lists[0, k], lists[1, k]
-            picked[1 + (at >> LOG_TILE), at & (TILE - 1)] = (a >> 1) * (2 * targets) + col * targets + b
-            return at + jnp.where((k < count) & ((a & 1) == p), 1, 0)
-
-        return lax.fori_loop(0, TILE, step, start, unroll=8)
-
-    picked[0, 0] = scan(other, 1 - p, scan(mine, p, 0))
+    slots = 2 * TILE
+
+    def put(lists, k, col, at):
+        a, b = lists[0, k], lists[1, k]
+        picked[1 + (at >> LOG_TILE), at & (TILE - 1)] = (a >> 1) * (2 * targets) + col * targets + b
+        return jnp.where((k < lists[2, 0]) & ((a & 1) == p), 1, 0)
+
+    def step(k, ends):
+        front, back = ends
+        front = front + put(mine, k, p, front)
+        return front, back - put(other, k, 1 - p, back)
+
+    front, back = lax.fori_loop(0, TILE, step, (jnp.int32(0), jnp.int32(slots - 1)), unroll=8)
+    picked[0, 0] = front
+    picked[0, 1] = front + (slots - 1) - back
     for n in range(place.shape[0]):
-        picked[0, 1 + n] = place[n]
+        picked[0, 2 + n] = place[n]
 
 
 def tile_code(tiles, k):
-    return tiles[1 + (k >> LOG_TILE), k & (TILE - 1)]
+    first = tiles[0, 0]
+    at = jnp.where(k < first, k, 2 * TILE - 1 + first - k)
+    return tiles[1 + (at >> LOG_TILE), at & (TILE - 1)]
 
 
 def source_tiles(tiles, tgt_blocks):
@@ -119,22 +124,23 @@
     return tile
 
 
-def own_kernel(src_mine, tgt_mine, src, tgt):
-    src[...] = src_mine[...]
-    tgt[...] = tgt_mine[...]
-
-
-def pack_kernel(lists, *refs):
+def pack_kernel(lists, own, *refs):
     src, tgt = refs[-2:]
     sides = src.shape[0]
-    for n in range(sides):
-        src[n] = refs[n][...]
-    for n in range(tgt.shape[0]):
-        tgt[n] = refs[sides + n][...]
+    src[0] = own[0]
+    tgt[0] = own[1]
+    for n in range(1, sides):
+        src[n] = refs[n - 1][...]
+        tgt[n] = refs[sides - 1 + n - 1][...]
 
 
 def after_kernel(first, block, out):
     out[...] = block[...]
+
+
+def square_kernel(src, sq_src):
+    for a in range(src.shape[0]):
+        sq_src[a : a + 1, :] = square_rows(src[a])
 
 
 def first_kernel(picked, *refs):
@@ -143,7 +149,7 @@
     fetch.start()
     sides = len(pieces) // 2
     fetch.wait()
-    place = [tiles[0, 1 + n] for n in range(5)]
+    place = [tiles[0, 2 + n] for n in range(5)]
     for d in range(sides):
         x = lax.rem(place[0] + (sides - d), sides)
         p, core = place[3] ^ (d // 2), place[4] ^ (d % 2)
@@ -156,7 +162,7 @@
     for a in range(src.shape[0]):
         sq_src[a : a + 1, :] = square_rows(src[a])
     expand(sq_tgt[...] * -KAPPA, wide)
-    sums = tile_sums(source_tiles(tiles, tgt.shape[0]), tiles[0, 0], tgt, src, wide, peaks, totals)
+    sums = tile_sums(source_tiles(tiles, tgt.shape[0]), tiles[0, 1], tgt, src, wide, peaks, totals)
     out[...] = jnp.broadcast_to(sums[None], out.shape)
 
 
@@ -165,22 +171,25 @@
     fetch.start()
     expand(-log_cells - log_sum(parts[...]), wide)
     fetch.wait()
-    sums = tile_sums(source_tiles(tiles, tgt.shape[0]), tiles[0, 0], tgt, src, wide, peaks, totals)
+    sums = tile_sums(source_tiles(tiles, tgt.shape[0]), tiles[0, 1], tgt, src, wide, peaks, totals)
     out[...] = jnp.broadcast_to(sums[None], out.shape)
 
 
-def target_kernel(log_cells, picked, src, tgt, parts, sq_src, out, pot, wide, peaks, totals, tiles, sem):
+def target_kernel(log_cells, picked, src, tgt, parts, *refs):
+    refs, (wide, peaks, totals, tiles, sem) = refs[:-5], refs[-5:]
     fetch = pltpu.make_async_copy(picked, tiles, sem)
     fetch.start()
     weights = -log_cells - log_sum(parts[...])
-    pot[...] = weights * (1.0 / KAPPA) + sq_src[...]
     expand(weights, wide)
     fetch.wait()
-    sums = tile_sums(target_tiles(tiles, tgt.shape[0]), tiles[0, 0], src, tgt, wide, peaks, totals)
-    copies, blocks = out.shape[0], out.shape[1]
-    if blocks == sums.shape[0]:
+    sums = tile_sums(target_tiles(tiles, tgt.shape[0]), tiles[0, 1], src, tgt, wide, peaks, totals)
+    if len(refs) == 1:
+        (out,) = refs
         out[...] = jnp.broadcast_to(sums[None], out.shape)
     else:
+        sq_src, out, pot = refs
+        pot[...] = weights * (1.0 / KAPPA) + sq_src[...]
+        copies, blocks = out.shape[0], out.shape[1]
         cols = sums.shape[0] // blocks
         each = copies // cols
         for col in range(cols):
@@ -225,25 +234,22 @@
 
 
 def bands(src_embed, tgt_embed, lists):
-    block = jax.ShapeDtypeStruct(src_embed.shape, src_embed.dtype)
-    own = pl.pallas_call(
-        own_kernel, out_shape=[block] * 2, in_specs=[VMEM] * 2, out_specs=[VMEM] * 2, compiler_params=PARAMS
-    )(src_embed, tgt_embed)
-    src_blocks, tgt_blocks = shifts(src_embed, "s")[1:], shifts(tgt_embed, "y")[1:]
-    blocks = [own[0]] + src_blocks + [own[1]] + tgt_blocks
-    group = jax.ShapeDtypeStruct((1 + len(src_blocks),) + src_embed.shape, src_embed.dtype)
+    own = jnp.stack([src_embed, tgt_embed])
+    far = shifts(src_embed, "s")[1:] + shifts(tgt_embed, "y")[1:]
+    group = jax.ShapeDtypeStruct((lax.axis_size("s"),) + src_embed.shape, src_embed.dtype)
     src, tgt = pl.pallas_call(
         pack_kernel,
         out_shape=[group] * 2,
-        in_specs=[ANY] + [VMEM] * len(blocks),
+        in_specs=[ANY] + [VMEM] * (1 + len(far)),
         out_specs=[VMEM] * 2,
         compiler_params=PARAMS,
-    )(lists, *blocks)
+    )(lists, own, *far)
+    src_pieces = shifts(src, "x")
     mine, partner = shifts(tgt, "p")
     mine = pl.pallas_call(
         after_kernel, out_shape=group, in_specs=[ANY, VMEM], out_specs=VMEM, compiler_params=PARAMS
     )(partner, mine)
-    return shifts(src, "x"), [piece for side in (mine, partner) for piece in shifts(side, "core")]
+    return src_pieces, [piece for side in (mine, partner) for piece in shifts(side, "core")]
 
 
 def local(src_embed, tgt_embed, tiles, counts):
@@ -254,8 +260,8 @@
 
     lists = jnp.concatenate([tiles[0, 0], jnp.broadcast_to(counts[0, 0], (1, TILE))], axis=0)
     other_lists = partner(lists)
+    place = jnp.stack([lax.axis_index(a) for a in ("x", "s", "y", "p", "core")]).astype(jnp.int32)
     src_pieces, tgt_pieces = bands(src_embed, tgt_embed, other_lists)
-    place = jnp.stack([lax.axis_index(a) for a in ("x", "s", "y", "p", "core")]).astype(jnp.int32)
     picked = pl.pallas_call(
         pick_kernel,
         out_shape=jax.ShapeDtypeStruct((8, TILE), jnp.int32),
@@ -265,39 +271,25 @@
     )(lists, other_lists, place)
 
     srcs, tgts = (len(pieces) * pieces[0].shape[0] for pieces in (src_pieces, tgt_pieces))
+    tgt_shape = jax.ShapeDtypeStruct((tgts,) + tgt_embed.shape, tgt_embed.dtype)
     src_shape = jax.ShapeDtypeStruct((srcs,) + src_embed.shape, src_embed.dtype)
-    tgt_shape = jax.ShapeDtypeStruct((tgts,) + tgt_embed.shape, tgt_embed.dtype)
     slots = srcs * tgts
     src_out, tgt_out = (srcs, srcs, TILE), (tgts, tgts, TILE)
     for sweep in range(ITERS):
         if sweep == 0:
-            parts, src, tgt, sq_src, sq_tgt = half_step(
-                first_kernel,
-                [src_out, src_shape, tgt_shape, (srcs, TILE), (tgts, TILE)],
-                tgts,
-                slots,
-                picked,
-                *src_pieces,
-                *tgt_pieces,
-            )
+            outs = [src_out, src_shape, tgt_shape, (srcs, TILE), (tgts, TILE)]
+            parts, src, tgt, sq_src, sq_tgt = half_step(first_kernel, outs, tgts, slots, picked, *src_pieces, *tgt_pieces)
         else:
             (parts,) = half_step(
                 functools.partial(source_kernel, log_cells), [src_out], tgts, slots, picked, src, tgt, parts
             )
         parts = exchange(parts, SRC_PEERS)
-        last = sweep == ITERS - 1
-        parts, src_pot = half_step(
-            functools.partial(target_kernel, log_cells),
-            [(tgts, rows, TILE) if last else tgt_out, (srcs, TILE)],
-            srcs,
-            slots,
-            picked,
-            src,
-            tgt,
-            parts,
-            sq_src,
-        )
-        if last:
+        step = functools.partial(target_kernel, log_cells)
+        if sweep < ITERS - 1:
+            (parts,) = half_step(step, [tgt_out], srcs, slots, picked, src, tgt, parts)
+        else:
+            outs = [(tgts, rows, TILE), (srcs, TILE)]
+            parts, src_pot = half_step(step, outs, srcs, slots, picked, src, tgt, parts, sq_src)
             other_pot = partner(src_pot)
         parts = exchange(parts, TGT_PEERS)
     tgt_pot, both = pl.pallas_call(

time: 108 us -> 105 us (0.972); the launches traced: 106 us -> 105 us
  Pallas kernels: 16.3 us -> 13.6 us
  local copies, waits for them, and re-layouts: 2.44 us -> 0.76 us
  blocking collectives: 41.2 us -> 42.6 us
    pallas_call x4, Pallas kernels: 12.3 us -> 9.89 us  [half_step(): pl.pallas_call(kernel, out_shape=[s if isinstance(s, jax.ShapeDtypeStruct...]
    unnamed x6 -> x2, local copies, waits for them, and re-layouts: 2.35 us -> 0.67 us
    all_to_all x3, blocking collectives: 41.2 us -> 42.6 us  [exchange(): return lax.all_to_all(copies, peers, 0, 0, tiled=True)]
    ppermute x12, waiting for transfers between devices: 6.52 us -> 7.6 us  [shifts(): lax.ppermute(block, axis, [(i, (i + d) % n) for i in range(n)])]
  transfers between devices with their start and end apart: 15 -> 15, of which waited for: 5 -> 5; matrix products, arithmetic and copies ran while one was open for 0% -> 1% of each run, Pallas kernels for 3% -> 3%
where the time goes in v10:
time: 105 us
  blocking collectives  42.6 us (41%)
  starting transfers between devices  34.2 us (33%)
  Pallas kernels  13.6 us (13%)
  waiting for transfers between devices  12 us (11%)
  between operations  1.4 us (1%)
    all_to_all x3, blocking collectives, exchange(): return lax.all_to_all(copies, peers, 0, 0, tiled=True)  42.6 us
    ppermute x12, starting transfers between devices, shifts(): lax.ppermute(block, axis, [(i, (i + d) % n) for i in range(n)])  23.8 us
    pallas_call x4, Pallas kernels, half_step(): pl.pallas_call(kernel, out_shape=[s if isinstance(s, jax.ShapeDtypeStruct...  9.89 us
    ppermute x12, waiting for transfers between devices, shifts(): lax.ppermute(block, axis, [(i, (i + d) % n) for i in range(n)])  7.6 us
    all_to_all x1, starting transfers between devices, exchange(): return lax.all_to_all(copies, peers, 0, 0, tiled=True)  7.37 us
    ppermute x2, starting transfers between devices, local(): partner = lambda v: lax.ppermute(v, 'p', [(0, 1), (1, 0)])  3.03 us
    pallas_call x1, Pallas kernels, local(): pl.pallas_call(pick_kernel, out_shape=jax.ShapeDtypeStruct((8, TILE), jnp...  3.02 us
    all_to_all x1, waiting for transfers between devices, exchange(): return lax.all_to_all(copies, peers, 0, 0, tiled=True)  2.77 us
  transfers between devices with their start and end apart: 15, of which 5 were waited for; matrix products, arithmetic and copies ran while one was open for 1% of the time, Pallas kernels for 3%

profile of v10, /device:TPU:1, one launch (start us, length us, event | category | flops | bytes accessed | tf_op | source)
XLA Modules:
  0.0 105.5 jit_solution(2823760995292702924)
XLA Ops:
  0.6 3.9 %collective-permute-start.1 = (bf16[128,256]{1,0:T(8,128)(2,1)}, bf16[128,256]{1,0:T(8,128)(2,1)S(1)}, u32[]{:S(2)}, u32[]{:S(2)}) collective-permute-start(bf16[128,256]{1,0:T(8,128)(2,1)} %param.4), channel_id=1, source_target_pairs={{0,2},{2,4},{4,6},{6,0},{1,3},{3,5},{5,7},{7,1},{8,10},{10,12},{12... | collective-permute-start | bytes 196616 | tf_op jit(solution)/shard_map/ppermute | solution.py:232
  5.2 0.0 copy-start
  5.2 0.7 copy-done
  5.9 1.6 %collective-permute-start = (s32[3,128]{1,0:T(4,128)S(1)}, s32[3,128]{1,0:T(4,128)S(1)}, u32[]{:S(2)}, u32[]{:S(2)}) collective-permute-start(s32[3,128]{1,0:T(4,128)S(1)} %concatenate.3.mine), channel_id=1, source_target_pairs={{0,1},{1,0},{2,3},{3,2},{4,5},{5,4},{6,7},{7,6},{8,9},{9,8},{10,11... | collective-permute-start | bytes 4616 | tf_op jit(solution)/shard_map/ppermute | solution.py:259
  7.5 2.1 %collective-permute-start.3 = (bf16[128,256]{1,0:T(8,128)(2,1)}, bf16[128,256]{1,0:T(8,128)(2,1)S(1)}, u32[]{:S(2)}, u32[]{:S(2)}) collective-permute-start(bf16[128,256]{1,0:T(8,128)(2,1)} %param.4), channel_id=1, source_target_pairs={{0,6},{2,0},{4,2},{6,4},{1,7},{3,1},{5,3},{7,5},{8,14},{10,8},{12,... | collective-permute-start | bytes 196616 | tf_op jit(solution)/shard_map/ppermute | solution.py:232
  9.6 4.5 %collective-permute-start.2 = (bf16[128,256]{1,0:T(8,128)(2,1)}, bf16[128,256]{1,0:T(8,128)(2,1)S(1)}, u32[]{:S(2)}, u32[]{:S(2)}) collective-permute-start(bf16[128,256]{1,0:T(8,128)(2,1)} %param.4), channel_id=1, source_target_pairs={{0,4},{2,6},{4,0},{6,2},{1,5},{3,7},{5,1},{7,3},{8,12},{10,14},{12... | collective-permute-start | bytes 196616 | tf_op jit(solution)/shard_map/ppermute | solution.py:232
  14.1 1.3 %collective-permute-start.4 = (bf16[128,256]{1,0:T(8,128)(2,1)}, bf16[128,256]{1,0:T(8,128)(2,1)S(1)}, u32[]{:S(2)}, u32[]{:S(2)}) collective-permute-start(bf16[128,256]{1,0:T(8,128)(2,1)} %param.5), channel_id=1, source_target_pairs={{0,64},{64,128},{128,192},{192,0},{1,65},{65,129},{129,193},{193,1... | collective-permute-start | bytes 196616 | tf_op jit(solution)/shard_map/ppermute | solution.py:232
  15.4 0.0 collective-permute-done.other.lists
  15.4 1.4 %collective-permute-start.6 = (bf16[128,256]{1,0:T(8,128)(2,1)}, bf16[128,256]{1,0:T(8,128)(2,1)S(1)}, u32[]{:S(2)}, u32[]{:S(2)}) collective-permute-start(bf16[128,256]{1,0:T(8,128)(2,1)} %param.5), channel_id=1, source_target_pairs={{0,192},{64,0},{128,64},{192,128},{1,193},{65,1},{129,65},{193,129... | collective-permute-start | bytes 196616 | tf_op jit(solution)/shard_map/ppermute | solution.py:232
  16.8 0.0 collective-permute-done.1.refs_0_
  16.8 1.6 %collective-permute-start.5 = (bf16[128,256]{1,0:T(8,128)(2,1)}, bf16[128,256]{1,0:T(8,128)(2,1)S(1)}, u32[]{:S(2)}, u32[]{:S(2)}) collective-permute-start(bf16[128,256]{1,0:T(8,128)(2,1)} %param.5), channel_id=1, source_target_pairs={{0,128},{64,192},{128,0},{192,64},{1,129},{65,193},{129,1},{193,65... | collective-permute-start | bytes 196616 | tf_op jit(solution)/shard_map/ppermute | solution.py:232
  18.5 0.9 pad_maximum_fusion.own
  19.4 0.0 collective-permute-done.3.refs_2_
  19.4 0.0 collective-permute-done.2.refs_1_
  19.4 0.0 collective-permute-done.4.refs_3_
  19.4 0.0 collective-permute-done.6.refs_5_
  19.4 2.6 %collective-permute-done.5.refs_4_ = bf16[128,256]{1,0:T(8,128)(2,1)S(1)} collective-permute-done((bf16[128,256]{1,0:T(8,128)(2,1)}, bf16[128,256]{1,0:T(8,128)(2,1)S(1)}, u32[]{:S(2)}, u32[]{:S(2)}) %collective-permute-start.5) | collective-permute-done | bytes 65568 | tf_op jit(solution)/shard_map/ppermute | solution.py:232
  22.0 0.8 collective-permute-start.10
  22.8 2.5 %collective-permute-start.9 = (bf16[4,128,256]{2,1,0:T(8,128)(2,1)S(1)}, bf16[4,128,256]{2,1,0:T(8,128)(2,1)S(1)}, u32[]{:S(2)}, u32[]{:S(2)}) collective-permute-start(bf16[4,128,256]{2,1,0:T(8,128)(2,1)S(1)} %get-tuple-element.13.refs_0_), channel_id=1, source_target_pairs={{0,24},{8,0},{16,8},{24,16},{1,25},{9,1},{17,9},{25,17},{2,26},{10... | collective-permute-start | bytes 786440 | tf_op jit(solution)/shard_map/ppermute | solution.py:232
  25.3 0.5 collective-permute-start.8
  25.8 0.6 collective-permute-start.7
  26.5 0.9 collective-permute-done.10.first.refs_6_
  27.4 4.4 %collective-permute-start.11 = (bf16[4,128,256]{2,1,0:T(8,128)(2,1)S(1)}, bf16[4,128,256]{2,1,0:T(8,128)(2,1)S(1)}, u32[]{:S(2)}, u32[]{:S(2)}) collective-permute-start(bf16[4,128,256]{2,1,0:T(8,128)(2,1)S(1)} %shard_map.61.refs_4_), channel_id=1, source_target_pairs={{0,32},{32,0},{1,33},{33,1},{2,34},{34,2},{3,35},{35,3},{4,36},{36... | collective-permute-start | bytes 786440 | tf_op jit(solution)/shard_map/ppermute | solution.py:232
  31.7 0.1 collective-permute-start.12
  31.8 0.1 stack.29.place
  31.9 3.0 %shard_map.59.picked = s32[8,128]{1,0:T(8,128)S(1)} custom-call(s32[3,128]{1,0:T(4,128)S(1)} %concatenate.3.mine, s32[3,128]{1,0:T(4,128)S(1)} %collective-permute-done.other.lists, s32[5]{0:T(128)S(1)} %stack.29.place), custom_call_target="tpu_custom_call" | custom-call | tf_op jit(solution)/shard_map/pallas_call | solution.py:265
  34.9 0.0 collective-permute-done.9.refs_3_
  35.0 0.0 collective-permute-done.8.refs_2_
  35.0 4.1 %collective-permute-done.7.refs_1_ = bf16[4,128,256]{2,1,0:T(8,128)(2,1)S(1)} collective-permute-done((bf16[4,128,256]{2,1,0:T(8,128)(2,1)S(1)}, bf16[4,128,256]{2,1,0:T(8,128)(2,1)S(1)}, u32[]{:S(2)}, u32[]{:S(2)}) %collective-permute-start.7) | collective-permute-done | bytes 262176 | tf_op jit(solution)/shard_map/ppermute | solution.py:232
  39.1 0.0 collective-permute-done.11.refs_5_
  39.1 0.0 collective-permute-done.12.refs_7_
  39.1 3.2 %shard_map.62 = (f32[16,16,128]{2,1,0:T(8,128)S(1)}, bf16[16,128,256]{2,1,0:T(8,128)(2,1)S(1)}, bf16[16,128,256]{2,1,0:T(8,128)(2,1)S(1)}, f32[16,128]{1,0:T(8,128)S(1)}, f32[16,128]{1,0:T(8,128)S(1)}) custom-call(s32[8,128]{1,0:T(8,128)S(1)} %shard_map.59.picked, bf16[4,128,256]{2,1,0:T(8,128)(2,1)S(1)} %get-tuple-element.13.refs_0_, ...), custom_call_target="tpu_custom_call" | custom-call | tf_op jit(solution)/shard_map/pallas_call | solution.py:210
  42.3 14.2 %all_to_all.20.parts = f32[16,16,128]{2,1,0:T(8,128)S(1)} all-to-all(f32[16,16,128]{2,1,0:T(8,128)S(1)} %get-tuple-element.17), channel_id=1, replica_groups=mesh['y'=4,'core'=2,'x'=4,'s'=4,'p'=2] {'x','s'}, dimensions={0} | all-to-all | bytes 262144 | tf_op jit(solution)/shard_map/all_to_all | solution.py:227
  56.5 2.1 %shard_map.63 = f32[16,16,128]{2,1,0:T(8,128)S(1)} custom-call(s32[8,128]{1,0:T(8,128)S(1)} %shard_map.59.picked, bf16[16,128,256]{2,1,0:T(8,128)(2,1)S(1)} %get-tuple-element.15.src, bf16[16,128,256]{2,1,0:T(8,128)(2,1)S(1)} %get-tuple-element.16.tgt, f32[16,16,128]{2,1,0:T(8,128)S(1)} %all_to_all.20.parts), custom_call_target="tpu_custom_call" | custom-call | tf_op jit(solution)/shard_map/pallas_call | solution.py:210
  58.7 13.7 %all_to_all.21.parts = f32[16,16,128]{2,1,0:T(8,128)S(1)} all-to-all(f32[16,16,128]{2,1,0:T(8,128)S(1)} %shard_map.63), channel_id=1, replica_groups=mesh['y'=4,'core'=2,'x'=4,'s'=4,'p'=2] {'p','y','core'}, dimensions={0} | all-to-all | bytes 262144 | tf_op jit(solution)/shard_map/all_to_all | solution.py:227
  72.4 2.0 %shard_map.64 = f32[16,16,128]{2,1,0:T(8,128)S(1)} custom-call(s32[8,128]{1,0:T(8,128)S(1)} %shard_map.59.picked, bf16[16,128,256]{2,1,0:T(8,128)(2,1)S(1)} %get-tuple-element.15.src, bf16[16,128,256]{2,1,0:T(8,128)(2,1)S(1)} %get-tuple-element.16.tgt, f32[16,16,128]{2,1,0:T(8,128)S(1)} %all_to_all.21.parts), custom_call_target="tpu_custom_call" | custom-call | tf_op jit(solution)/shard_map/pallas_call | solution.py:210
  74.4 14.7 %all_to_all.22.parts = f32[16,16,128]{2,1,0:T(8,128)S(1)} all-to-all(f32[16,16,128]{2,1,0:T(8,128)S(1)} %shard_map.64), channel_id=1, replica_groups=mesh['y'=4,'core'=2,'x'=4,'s'=4,'p'=2] {'x','s'}, dimensions={0} | all-to-all | bytes 262144 | tf_op jit(solution)/shard_map/all_to_all | solution.py:227
  89.0 2.6 %shard_map.65 = (f32[16,8,128]{2,1,0:T(8,128)}, f32[16,128]{1,0:T(8,128)S(1)}) custom-call(s32[8,128]{1,0:T(8,128)S(1)} %shard_map.59.picked, bf16[16,128,256]{2,1,0:T(8,128)(2,1)S(1)} %get-tuple-element.15.src, bf16[16,128,256]{2,1,0:T(8,128)(2,1)S(1)} %get-tuple-element.16.tgt, f32[16,16,128]{2,1,0:T(8,128)S(1)} %all_to_all.22.parts, ...), custom_call_target="tpu_custom_call" | custom-call | tf_op jit(solution)/shard_map/pallas_call | solution.py:210
  91.6 7.4 %all-to-all-start.3 = ((f32[16,8,128]{2,1,0:T(8,128)}), f32[16,8,128]{2,1,0:T(8,128)S(1)}, u32[]{:S(2)}, u32[]{:S(2)}) async-start(f32[16,8,128]{2,1,0:T(8,128)} %get-tuple-element.19), calls=%async_computation.3 | async-start | bytes 131072 | tf_op jit(solution)/shard_map/all_to_all | solution.py:227
  99.0 1.4 %collective-permute-start.13 = (f32[16,128]{1,0:T(8,128)S(1)}, f32[16,128]{1,0:T(8,128)S(1)}, u32[]{:S(2)}, u32[]{:S(2)}) collective-permute-start(f32[16,128]{1,0:T(8,128)S(1)} %get-tuple-element.21.mine), channel_id=1, source_target_pairs={{0,1},{1,0},{2,3},{3,2},{4,5},{5,4},{6,7},{7,6},{8,9},{9,8},{10,11... | collective-permute-start | bytes 24584 | tf_op jit(solution)/shard_map/ppermute | solution.py:259
  100.4 1.7 %collective-permute-done.13.other = f32[16,128]{1,0:T(8,128)S(1)} collective-permute-done((f32[16,128]{1,0:T(8,128)S(1)}, f32[16,128]{1,0:T(8,128)S(1)}, u32[]{:S(2)}, u32[]{:S(2)}) %collective-permute-start.13) | collective-permute-done | bytes 8224 | tf_op jit(solution)/shard_map/ppermute | solution.py:259
  102.1 2.8 %all-to-all-done.3.parts = f32[16,8,128]{2,1,0:T(8,128)S(1)} async-done(((f32[16,8,128]{2,1,0:T(8,128)}), f32[16,8,128]{2,1,0:T(8,128)S(1)}, u32[]{:S(2)}, u32[]{:S(2)}) %all-to-all-start.3) | async-done | bytes 65568 | tf_op jit(solution)/shard_map/all_to_all | solution.py:227
  104.8 0.6 shard_map.66
  (3 shorter events, 0.1 us)
Async XLA Ops:
  0.6 16.2 %collective-permute-start.1 = (bf16[128,256]{1,0:T(8,128)(2,1)}, bf16[128,256]{1,0:T(8,128)(2,1)S(1)}, u32[]{:S(2)}, u32[]{:S(2)}) collective-permute-start(bf16[128,256]{1,0:T(8,128)(2,1)} %param.4), channel_id=1, source_target_pairs={{0,2},{2,4},{4,6},{6,0},{1,3},{3,5},{5,7},{7,1},{8,10},{10,12},{12... | collective-permute-start | bytes 196616 | tf_op jit(solution)/shard_map/ppermute | solution.py:232
  5.2 0.7 copy-start
  5.9 9.5 %collective-permute-start = (s32[3,128]{1,0:T(4,128)S(1)}, s32[3,128]{1,0:T(4,128)S(1)}, u32[]{:S(2)}, u32[]{:S(2)}) collective-permute-start(s32[3,128]{1,0:T(4,128)S(1)} %concatenate.3.mine), channel_id=1, source_target_pairs={{0,1},{1,0},{2,3},{3,2},{4,5},{5,4},{6,7},{7,6},{8,9},{9,8},{10,11... | collective-permute-start | bytes 4616 | tf_op jit(solution)/shard_map/ppermute | solution.py:259
  7.5 11.9 %collective-permute-start.3 = (bf16[128,256]{1,0:T(8,128)(2,1)}, bf16[128,256]{1,0:T(8,128)(2,1)S(1)}, u32[]{:S(2)}, u32[]{:S(2)}) collective-permute-start(bf16[128,256]{1,0:T(8,128)(2,1)} %param.4), channel_id=1, source_target_pairs={{0,6},{2,0},{4,2},{6,4},{1,7},{3,1},{5,3},{7,5},{8,14},{10,8},{12,... | collective-permute-start | bytes 196616 | tf_op jit(solution)/shard_map/ppermute | solution.py:232
  9.6 9.7 %collective-permute-start.2 = (bf16[128,256]{1,0:T(8,128)(2,1)}, bf16[128,256]{1,0:T(8,128)(2,1)S(1)}, u32[]{:S(2)}, u32[]{:S(2)}) collective-permute-start(bf16[128,256]{1,0:T(8,128)(2,1)} %param.4), channel_id=1, source_target_pairs={{0,4},{2,6},{4,0},{6,2},{1,5},{3,7},{5,1},{7,3},{8,12},{10,14},{12... | collective-permute-start | bytes 196616 | tf_op jit(solution)/shard_map/ppermute | solution.py:232
  14.1 5.3 %collective-permute-start.4 = (bf16[128,256]{1,0:T(8,128)(2,1)}, bf16[128,256]{1,0:T(8,128)(2,1)S(1)}, u32[]{:S(2)}, u32[]{:S(2)}) collective-permute-start(bf16[128,256]{1,0:T(8,128)(2,1)} %param.5), channel_id=1, source_target_pairs={{0,64},{64,128},{128,192},{192,0},{1,65},{65,129},{129,193},{193,1... | collective-permute-start | bytes 196616 | tf_op jit(solution)/shard_map/ppermute | solution.py:232
  15.4 4.0 %collective-permute-start.6 = (bf16[128,256]{1,0:T(8,128)(2,1)}, bf16[128,256]{1,0:T(8,128)(2,1)S(1)}, u32[]{:S(2)}, u32[]{:S(2)}) collective-permute-start(bf16[128,256]{1,0:T(8,128)(2,1)} %param.5), channel_id=1, source_target_pairs={{0,192},{64,0},{128,64},{192,128},{1,193},{65,1},{129,65},{193,129... | collective-permute-start | bytes 196616 | tf_op jit(solution)/shard_map/ppermute | solution.py:232
  16.8 5.1 %collective-permute-start.5 = (bf16[128,256]{1,0:T(8,128)(2,1)}, bf16[128,256]{1,0:T(8,128)(2,1)S(1)}, u32[]{:S(2)}, u32[]{:S(2)}) collective-permute-start(bf16[128,256]{1,0:T(8,128)(2,1)} %param.5), channel_id=1, source_target_pairs={{0,128},{64,192},{128,0},{192,64},{1,129},{65,193},{129,1},{193,65... | collective-permute-start | bytes 196616 | tf_op jit(solution)/shard_map/ppermute | solution.py:232
  22.0 5.3 %collective-permute-start.10 = (bf16[4,128,256]{2,1,0:T(8,128)(2,1)S(1)}, bf16[4,128,256]{2,1,0:T(8,128)(2,1)S(1)}, u32[]{:S(2)}, u32[]{:S(2)}) collective-permute-start(bf16[4,128,256]{2,1,0:T(8,128)(2,1)S(1)} %get-tuple-element.14.block), channel_id=1, source_target_pairs={{0,1},{1,0},{2,3},{3,2},{4,5},{5,4},{6,7},{7,6},{8,9},{9,8},{10,11... | collective-permute-start | bytes 786440 | tf_op jit(solution)/shard_map/ppermute | solution.py:232
  22.8 12.1 %collective-permute-start.9 = (bf16[4,128,256]{2,1,0:T(8,128)(2,1)S(1)}, bf16[4,128,256]{2,1,0:T(8,128)(2,1)S(1)}, u32[]{:S(2)}, u32[]{:S(2)}) collective-permute-start(bf16[4,128,256]{2,1,0:T(8,128)(2,1)S(1)} %get-tuple-element.13.refs_0_), channel_id=1, source_target_pairs={{0,24},{8,0},{16,8},{24,16},{1,25},{9,1},{17,9},{25,17},{2,26},{10... | collective-permute-start | bytes 786440 | tf_op jit(solution)/shard_map/ppermute | solution.py:232
  25.3 9.6 %collective-permute-start.8 = (bf16[4,128,256]{2,1,0:T(8,128)(2,1)S(1)}, bf16[4,128,256]{2,1,0:T(8,128)(2,1)S(1)}, u32[]{:S(2)}, u32[]{:S(2)}) collective-permute-start(bf16[4,128,256]{2,1,0:T(8,128)(2,1)S(1)} %get-tuple-element.13.refs_0_), channel_id=1, source_target_pairs={{0,16},{8,24},{16,0},{24,8},{1,17},{9,25},{17,1},{25,9},{2,18},{10... | collective-permute-start | bytes 786440 | tf_op jit(solution)/shard_map/ppermute | solution.py:232
  25.8 13.2 %collective-permute-start.7 = (bf16[4,128,256]{2,1,0:T(8,128)(2,1)S(1)}, bf16[4,128,256]{2,1,0:T(8,128)(2,1)S(1)}, u32[]{:S(2)}, u32[]{:S(2)}) collective-permute-start(bf16[4,128,256]{2,1,0:T(8,128)(2,1)S(1)} %get-tuple-element.13.refs_0_), channel_id=1, source_target_pairs={{0,8},{8,16},{16,24},{24,0},{1,9},{9,17},{17,25},{25,1},{2,10},{10... | collective-permute-start | bytes 786440 | tf_op jit(solution)/shard_map/ppermute | solution.py:232
  27.4 11.7 %collective-permute-start.11 = (bf16[4,128,256]{2,1,0:T(8,128)(2,1)S(1)}, bf16[4,128,256]{2,1,0:T(8,128)(2,1)S(1)}, u32[]{:S(2)}, u32[]{:S(2)}) collective-permute-start(bf16[4,128,256]{2,1,0:T(8,128)(2,1)S(1)} %shard_map.61.refs_4_), channel_id=1, source_target_pairs={{0,32},{32,0},{1,33},{33,1},{2,34},{34,2},{3,35},{35,3},{4,36},{36... | collective-permute-start | bytes 786440 | tf_op jit(solution)/shard_map/ppermute | solution.py:232
  31.7 7.4 %collective-permute-start.12 = (bf16[4,128,256]{2,1,0:T(8,128)(2,1)S(1)}, bf16[4,128,256]{2,1,0:T(8,128)(2,1)S(1)}, u32[]{:S(2)}, u32[]{:S(2)}) collective-permute-start(bf16[4,128,256]{2,1,0:T(8,128)(2,1)S(1)} %collective-permute-done.10.first.refs_6_), channel_id=1, source_target_pairs={{0,32},{32,0},{1,33},{33,1},{2,34},{34,2},{3,35},{35,3},{4,36},{36... | collective-permute-start | bytes 786440 | tf_op jit(solution)/shard_map/ppermute | solution.py:232
  91.6 13.2 %all-to-all-start.3 = ((f32[16,8,128]{2,1,0:T(8,128)}), f32[16,8,128]{2,1,0:T(8,128)S(1)}, u32[]{:S(2)}, u32[]{:S(2)}) async-start(f32[16,8,128]{2,1,0:T(8,128)} %get-tuple-element.19), calls=%async_computation.3 | async-start | bytes 131072 | tf_op jit(solution)/shard_map/all_to_all | solution.py:227
  99.0 3.1 %collective-permute-start.13 = (f32[16,128]{1,0:T(8,128)S(1)}, f32[16,128]{1,0:T(8,128)S(1)}, u32[]{:S(2)}, u32[]{:S(2)}) collective-permute-start(f32[16,128]{1,0:T(8,128)S(1)} %get-tuple-element.21.mine), channel_id=1, source_target_pairs={{0,1},{1,0},{2,3},{3,2},{4,5},{5,4},{6,7},{7,6},{8,9},{9,8},{10,11... | collective-permute-start | bytes 24584 | tf_op jit(solution)/shard_map/ppermute | solution.py:259

commit v11 on v10

--- a/solution.py
+++ b/solution.py
@@ -11,7 +11,6 @@
 
 TILE = 128
 LOG_TILE = 7
-ITERS = 2
 ENTROPY = 0.05
 KAPPA = math.log2(math.e) / ENTROPY
 EMPTY = -1e30
@@ -25,7 +24,7 @@
 VMEM = pl.BlockSpec(memory_space=pltpu.VMEM)
 SMEM = pl.BlockSpec(memory_space=pltpu.SMEM)
 ANY = pl.BlockSpec(memory_space=pl.ANY)
-PARAMS = pltpu.CompilerParams(vmem_limit_bytes=24 * 2**20)
+PARAMS = pltpu.CompilerParams(vmem_limit_bytes=48 * 2**20)
 
 
 def square_rows(cells):
@@ -51,24 +50,71 @@
         wide[n] = jnp.broadcast_to(columns[:, n : n + 1], (TILE, TILE))
 
 
-def tile_sums(tile, count, near, far, wide, peaks, totals):
-    near_blocks, far_blocks = near.shape[0], far.shape[0]
+def dot_tiles(near, far, saved, stage, sems):
+    def out(step):
+        half = step & 1
+        return pltpu.make_async_copy(stage.at[half], saved.at[pl.ds(step * UNROLL, UNROLL)], sems.at[half])
+
+    def before(step, steps):
+        pl.when(step >= 2)(lambda: out(step - 2).wait())
+
+    def tile(step, u, n, f):
+        inner = lax.dot_general(near[n], far[f], NT, preferred_element_type=F32) * (2.0 * KAPPA)
+        stage[step & 1, u] = inner
+        return inner
+
+    def after(step):
+        out(step).start()
+
+    def end(steps):
+        pl.when(steps >= 2)(lambda: out(steps - 2).wait())
+        pl.when(steps >= 1)(lambda: out(steps - 1).wait())
+
+    return before, tile, after, end
+
+
+def saved_tiles(saved, stage, sems):
+    def fetch(step):
+        half = step & 1
+        return pltpu.make_async_copy(saved.at[pl.ds(step * UNROLL, UNROLL)], stage.at[half], sems.at[half])
+
+    def before(step, steps):
+        pl.when(step + 1 < steps)(lambda: fetch(step + 1).start())
+        fetch(step).wait()
+
+    def tile(step, u, n, f):
+        return stage[step & 1, u]
+
+    def after(step):
+        pass
+
+    def end(steps):
+        pl.when(steps == 0)(lambda: fetch(0).wait())
+
+    return fetch, (before, tile, after, end)
+
+
+def tile_sums(place_of, count, source, near_blocks, far_blocks, wide, peaks, totals):
     spare = near_blocks * far_blocks
+    before, tile, after, end = source
     peaks[...] = jnp.full(peaks.shape, EMPTY, F32)
     totals[...] = jnp.zeros(totals.shape, F32)
-
-    @pl.loop(0, (count + UNROLL - 1) // UNROLL)
+    steps = (count + UNROLL - 1) // UNROLL
+
+    @pl.loop(0, steps)
     def _(step):
+        before(step, steps)
         for u in range(UNROLL):
             k = step * UNROLL + u
-            n, f = tile(jnp.where(k < count, k, 0))
-            inner = lax.dot_general(near[n], far[f], NT, preferred_element_type=F32)
-            score = (inner * (2.0 * KAPPA) + wide[n]).reshape(TILE // 8, 8, TILE)
+            n, f = place_of(jnp.where(k < count, k, 0))
+            score = (tile(step, u, n, f) + wide[n]).reshape(TILE // 8, 8, TILE)
             peak = jnp.max(score, axis=0)
             slot = jnp.where(k < count, f * near_blocks + n, spare)
             peaks[slot] = peak
             totals[slot] = jnp.sum(jnp.exp2(score - peak[None]), axis=0)
-
+        after(step)
+
+    end(steps)
     rows = []
     for f in range(far_blocks):
         at = pl.ds(f * near_blocks, near_blocks)
@@ -144,7 +190,8 @@
 
 
 def first_kernel(picked, *refs):
-    pieces, (out, src, tgt, sq_src, sq_tgt, wide, peaks, totals, tiles, sem) = refs[:-10], refs[-10:]
+    pieces, refs = refs[:-13], refs[-13:]
+    out, src, tgt, sq_src, sq_tgt, saved, wide, peaks, totals, tiles, sem, stage, sems = refs
     fetch = pltpu.make_async_copy(picked, tiles, sem)
     fetch.start()
     sides = len(pieces) // 2
@@ -157,44 +204,59 @@
             s, y = (lax.rem(place[axis] + (sides - n), sides) for axis in (1, 2))
             src[x * sides + s] = pieces[d][n]
             tgt[p * (2 * sides) + 2 * y + core] = pieces[sides + d][n]
-    for b in range(tgt.shape[0]):
+    srcs, tgts = src.shape[0], tgt.shape[0]
+    for b in range(tgts):
         sq_tgt[b : b + 1, :] = square_rows(tgt[b])
-    for a in range(src.shape[0]):
+    for a in range(srcs):
         sq_src[a : a + 1, :] = square_rows(src[a])
     expand(sq_tgt[...] * -KAPPA, wide)
-    sums = tile_sums(source_tiles(tiles, tgt.shape[0]), tiles[0, 1], tgt, src, wide, peaks, totals)
+    source = dot_tiles(tgt, src, saved, stage, sems)
+    sums = tile_sums(source_tiles(tiles, tgts), tiles[0, 1], source, tgts, srcs, wide, peaks, totals)
     out[...] = jnp.broadcast_to(sums[None], out.shape)
 
 
-def source_kernel(log_cells, picked, src, tgt, parts, out, wide, peaks, totals, tiles, sem):
+def target_kernel(log_cells, picked, src, tgt, parts, out, saved, wide, peaks, totals, tiles, sem, stage, sems):
     fetch = pltpu.make_async_copy(picked, tiles, sem)
     fetch.start()
     expand(-log_cells - log_sum(parts[...]), wide)
     fetch.wait()
-    sums = tile_sums(source_tiles(tiles, tgt.shape[0]), tiles[0, 1], tgt, src, wide, peaks, totals)
+    srcs, tgts = src.shape[0], tgt.shape[0]
+    source = dot_tiles(src, tgt, saved, stage, sems)
+    sums = tile_sums(target_tiles(tiles, tgts), tiles[0, 1], source, srcs, tgts, wide, peaks, totals)
     out[...] = jnp.broadcast_to(sums[None], out.shape)
 
 
-def target_kernel(log_cells, picked, src, tgt, parts, *refs):
-    refs, (wide, peaks, totals, tiles, sem) = refs[:-5], refs[-5:]
+def again_source_kernel(log_cells, picked, saved, parts, out, wide, peaks, totals, tiles, sem, stage, sems):
     fetch = pltpu.make_async_copy(picked, tiles, sem)
     fetch.start()
+    read, source = saved_tiles(saved, stage, sems)
+    read(0).start()
+    tgts, srcs = parts.shape[1], out.shape[1]
+    expand(-log_cells - log_sum(parts[...]), wide)
+    fetch.wait()
+    sums = tile_sums(source_tiles(tiles, tgts), tiles[0, 1], source, tgts, srcs, wide, peaks, totals)
+    out[...] = jnp.broadcast_to(sums[None], out.shape)
+
+
+def again_target_kernel(
+    log_cells, tgts, picked, saved, parts, sq_src, out, pot, wide, peaks, totals, tiles, sem, stage, sems
+):
+    fetch = pltpu.make_async_copy(picked, tiles, sem)
+    fetch.start()
+    read, source = saved_tiles(saved, stage, sems)
+    read(0).start()
+    srcs = parts.shape[1]
     weights = -log_cells - log_sum(parts[...])
+    pot[...] = weights * (1.0 / KAPPA) + sq_src[...]
     expand(weights, wide)
     fetch.wait()
-    sums = tile_sums(target_tiles(tiles, tgt.shape[0]), tiles[0, 1], src, tgt, wide, peaks, totals)
-    if len(refs) == 1:
-        (out,) = refs
-        out[...] = jnp.broadcast_to(sums[None], out.shape)
-    else:
-        sq_src, out, pot = refs
-        pot[...] = weights * (1.0 / KAPPA) + sq_src[...]
-        copies, blocks = out.shape[0], out.shape[1]
-        cols = sums.shape[0] // blocks
-        each = copies // cols
-        for col in range(cols):
-            piece = sums[col * blocks : (col + 1) * blocks]
-            out[col * each : (col + 1) * each] = jnp.broadcast_to(piece[None], (each,) + piece.shape)
+    sums = tile_sums(target_tiles(tiles, tgts), tiles[0, 1], source, srcs, tgts, wide, peaks, totals)
+    copies, blocks = out.shape[0], out.shape[1]
+    cols = tgts // blocks
+    each = copies // cols
+    for col in range(cols):
+        piece = sums[col * blocks : (col + 1) * blocks]
+        out[col * each : (col + 1) * each] = jnp.broadcast_to(piece[None], (each,) + piece.shape)
 
 
 def last_kernel(log_cells, parity, parts, sq_tgt, mine, other, tgt_pot, src_pot):
@@ -206,18 +268,20 @@
     src_pot[:, 1, :] = jnp.where(p == 0, other[...], mine[...])
 
 
-def half_step(kernel, outs, near_blocks, slots, picked, *args):
+def half_step(kernel, outs, near_blocks, slots, picked, *args, reads=0, writes=0):
     return pl.pallas_call(
         kernel,
         out_shape=[s if isinstance(s, jax.ShapeDtypeStruct) else jax.ShapeDtypeStruct(s, F32) for s in outs],
-        in_specs=[ANY] + [VMEM] * len(args),
-        out_specs=[VMEM] * len(outs),
+        in_specs=[ANY] * (1 + reads) + [VMEM] * (len(args) - reads),
+        out_specs=[VMEM] * (len(outs) - writes) + [ANY] * writes,
         scratch_shapes=[
             pltpu.VMEM((near_blocks, TILE, TILE), F32),
             pltpu.VMEM((slots + 1, 8, TILE), F32),
             pltpu.VMEM((slots + 1, 8, TILE), F32),
             pltpu.SMEM(picked.shape, picked.dtype),
             pltpu.SemaphoreType.DMA,
+            pltpu.VMEM((2, UNROLL, TILE, TILE), F32),
+            pltpu.SemaphoreType.DMA((2,)),
         ],
         compiler_params=PARAMS,
     )(picked, *args)
@@ -274,24 +338,23 @@
     tgt_shape = jax.ShapeDtypeStruct((tgts,) + tgt_embed.shape, tgt_embed.dtype)
     src_shape = jax.ShapeDtypeStruct((srcs,) + src_embed.shape, src_embed.dtype)
     slots = srcs * tgts
-    src_out, tgt_out = (srcs, srcs, TILE), (tgts, tgts, TILE)
-    for sweep in range(ITERS):
-        if sweep == 0:
-            outs = [src_out, src_shape, tgt_shape, (srcs, TILE), (tgts, TILE)]
-            parts, src, tgt, sq_src, sq_tgt = half_step(first_kernel, outs, tgts, slots, picked, *src_pieces, *tgt_pieces)
-        else:
-            (parts,) = half_step(
-                functools.partial(source_kernel, log_cells), [src_out], tgts, slots, picked, src, tgt, parts
-            )
-        parts = exchange(parts, SRC_PEERS)
-        step = functools.partial(target_kernel, log_cells)
-        if sweep < ITERS - 1:
-            (parts,) = half_step(step, [tgt_out], srcs, slots, picked, src, tgt, parts)
-        else:
-            outs = [(tgts, rows, TILE), (srcs, TILE)]
-            parts, src_pot = half_step(step, outs, srcs, slots, picked, src, tgt, parts, sq_src)
-            other_pot = partner(src_pot)
-        parts = exchange(parts, TGT_PEERS)
+    src_out, tgt_out, all_tiles = (srcs, srcs, TILE), (tgts, tgts, TILE), (slots, TILE, TILE)
+    outs = [src_out, src_shape, tgt_shape, (srcs, TILE), (tgts, TILE), all_tiles]
+    parts, src, tgt, sq_src, sq_tgt, src_saved = half_step(
+        first_kernel, outs, tgts, slots, picked, *src_pieces, *tgt_pieces, writes=1
+    )
+    parts = exchange(parts, SRC_PEERS)
+    step = functools.partial(target_kernel, log_cells)
+    parts, tgt_saved = half_step(step, [tgt_out, all_tiles], srcs, slots, picked, src, tgt, parts, writes=1)
+    parts = exchange(parts, TGT_PEERS)
+    step = functools.partial(again_source_kernel, log_cells)
+    (parts,) = half_step(step, [src_out], tgts, slots, picked, src_saved, parts, reads=1)
+    parts = exchange(parts, SRC_PEERS)
+    step = functools.partial(again_target_kernel, log_cells, tgts)
+    outs = [(tgts, rows, TILE), (srcs, TILE)]
+    parts, src_pot = half_step(step, outs, srcs, slots, picked, tgt_saved, parts, sq_src, reads=1)
+    other_pot = partner(src_pot)
+    parts = exchange(parts, TGT_PEERS)
     tgt_pot, both = pl.pallas_call(
         functools.partial(last_kernel, log_cells),
         out_shape=[jax.ShapeDtypeStruct((rows, TILE), F32), jax.ShapeDtypeStruct((srcs, 2, TILE), F32)],

time: 105 us -> 113 us (1.076)
  Pallas kernels: 13.6 us -> 25.5 us
  blocking collectives: 42.6 us -> 40.4 us
    pallas_call x4, Pallas kernels: 9.89 us -> 21.8 us  [half_step(): pl.pallas_call(kernel, out_shape=[s if isinstance(s, jax.ShapeDtypeStruct...]
    all_to_all x3, blocking collectives: 42.6 us -> 40.4 us  [exchange(): return lax.all_to_all(copies, peers, 0, 0, tiled=True)]
where the time goes in v11:
time: 113 us; the launch traced here: 114 us
  blocking collectives  40.4 us (36%)
  starting transfers between devices  33.3 us (29%)
  Pallas kernels  25.5 us (23%)
  waiting for transfers between devices  12 us (11%)
  between operations  1.39 us (1%)
    all_to_all x3, blocking collectives, exchange(): return lax.all_to_all(copies, peers, 0, 0, tiled=True)  40.4 us
    ppermute x12, starting transfers between devices, shifts(): lax.ppermute(block, axis, [(i, (i + d) % n) for i in range(n)])  23.8 us
    pallas_call x4, Pallas kernels, half_step(): pl.pallas_call(kernel, out_shape=[s if isinstance(s, jax.ShapeDtypeStruct...  21.8 us
    ppermute x12, waiting for transfers between devices, shifts(): lax.ppermute(block, axis, [(i, (i + d) % n) for i in range(n)])  7.6 us
    all_to_all x1, starting transfers between devices, exchange(): return lax.all_to_all(copies, peers, 0, 0, tiled=True)  6.57 us
    ppermute x2, starting transfers between devices, local(): partner = lambda v: lax.ppermute(v, 'p', [(0, 1), (1, 0)])  3.03 us
    pallas_call x1, Pallas kernels, local(): pl.pallas_call(pick_kernel, out_shape=jax.ShapeDtypeStruct((8, TILE), jnp...  3.02 us
    all_to_all x1, waiting for transfers between devices, exchange(): return lax.all_to_all(copies, peers, 0, 0, tiled=True)  2.77 us
  transfers between devices with their start and end apart: 15, of which 5 were waited for; matrix products, arithmetic and copies ran while one was open for 1% of the time, Pallas kernels for 3%

profile of v11, /device:TPU:1, one launch (start us, length us, event | category | flops | bytes accessed | tf_op | source)
XLA Modules:
  0.0 114.3 jit_solution(10473389934315678143)
XLA Ops:
  0.6 3.9 %collective-permute-start.1 = (bf16[128,256]{1,0:T(8,128)(2,1)}, bf16[128,256]{1,0:T(8,128)(2,1)S(1)}, u32[]{:S(2)}, u32[]{:S(2)}) collective-permute-start(bf16[128,256]{1,0:T(8,128)(2,1)} %param.4), channel_id=1, source_target_pairs={{0,2},{2,4},{4,6},{6,0},{1,3},{3,5},{5,7},{7,1},{8,10},{10,12},{12... | collective-permute-start | bytes 196616 | tf_op jit(solution)/shard_map/ppermute | solution.py:296
  5.2 0.7 concatenate.3.mine
  5.9 1.6 %collective-permute-start = (s32[3,128]{1,0:T(4,128)S(1)}, s32[3,128]{1,0:T(4,128)S(1)}, u32[]{:S(2)}, u32[]{:S(2)}) collective-permute-start(s32[3,128]{1,0:T(4,128)S(1)} %concatenate.3.mine), channel_id=1, source_target_pairs={{0,1},{1,0},{2,3},{3,2},{4,5},{5,4},{6,7},{7,6},{8,9},{9,8},{10,11... | collective-permute-start | bytes 4616 | tf_op jit(solution)/shard_map/ppermute | solution.py:323
  7.5 2.1 %collective-permute-start.3 = (bf16[128,256]{1,0:T(8,128)(2,1)}, bf16[128,256]{1,0:T(8,128)(2,1)S(1)}, u32[]{:S(2)}, u32[]{:S(2)}) collective-permute-start(bf16[128,256]{1,0:T(8,128)(2,1)} %param.4), channel_id=1, source_target_pairs={{0,6},{2,0},{4,2},{6,4},{1,7},{3,1},{5,3},{7,5},{8,14},{10,8},{12,... | collective-permute-start | bytes 196616 | tf_op jit(solution)/shard_map/ppermute | solution.py:296
  9.6 4.5 %collective-permute-start.2 = (bf16[128,256]{1,0:T(8,128)(2,1)}, bf16[128,256]{1,0:T(8,128)(2,1)S(1)}, u32[]{:S(2)}, u32[]{:S(2)}) collective-permute-start(bf16[128,256]{1,0:T(8,128)(2,1)} %param.4), channel_id=1, source_target_pairs={{0,4},{2,6},{4,0},{6,2},{1,5},{3,7},{5,1},{7,3},{8,12},{10,14},{12... | collective-permute-start | bytes 196616 | tf_op jit(solution)/shard_map/ppermute | solution.py:296
  14.1 1.3 %collective-permute-start.4 = (bf16[128,256]{1,0:T(8,128)(2,1)}, bf16[128,256]{1,0:T(8,128)(2,1)S(1)}, u32[]{:S(2)}, u32[]{:S(2)}) collective-permute-start(bf16[128,256]{1,0:T(8,128)(2,1)} %param.5), channel_id=1, source_target_pairs={{0,64},{64,128},{128,192},{192,0},{1,65},{65,129},{129,193},{193,1... | collective-permute-start | bytes 196616 | tf_op jit(solution)/shard_map/ppermute | solution.py:296
  15.4 0.0 collective-permute-done.other.lists
  15.4 1.4 %collective-permute-start.6 = (bf16[128,256]{1,0:T(8,128)(2,1)}, bf16[128,256]{1,0:T(8,128)(2,1)S(1)}, u32[]{:S(2)}, u32[]{:S(2)}) collective-permute-start(bf16[128,256]{1,0:T(8,128)(2,1)} %param.5), channel_id=1, source_target_pairs={{0,192},{64,0},{128,64},{192,128},{1,193},{65,1},{129,65},{193,129... | collective-permute-start | bytes 196616 | tf_op jit(solution)/shard_map/ppermute | solution.py:296
  16.8 0.0 collective-permute-done.1.refs_0_
  16.8 1.6 %collective-permute-start.5 = (bf16[128,256]{1,0:T(8,128)(2,1)}, bf16[128,256]{1,0:T(8,128)(2,1)S(1)}, u32[]{:S(2)}, u32[]{:S(2)}) collective-permute-start(bf16[128,256]{1,0:T(8,128)(2,1)} %param.5), channel_id=1, source_target_pairs={{0,128},{64,192},{128,0},{192,64},{1,129},{65,193},{129,1},{193,65... | collective-permute-start | bytes 196616 | tf_op jit(solution)/shard_map/ppermute | solution.py:296
  18.5 0.9 pad_maximum_fusion.own
  19.4 0.0 collective-permute-done.3.refs_2_
  19.4 0.0 collective-permute-done.2.refs_1_
  19.4 0.0 collective-permute-done.4.refs_3_
  19.4 0.0 collective-permute-done.6.refs_5_
  19.4 2.6 %collective-permute-done.5.refs_4_ = bf16[128,256]{1,0:T(8,128)(2,1)S(1)} collective-permute-done((bf16[128,256]{1,0:T(8,128)(2,1)}, bf16[128,256]{1,0:T(8,128)(2,1)S(1)}, u32[]{:S(2)}, u32[]{:S(2)}) %collective-permute-start.5) | collective-permute-done | bytes 65568 | tf_op jit(solution)/shard_map/ppermute | solution.py:296
  22.0 0.8 collective-permute-start.10
  22.8 2.5 %collective-permute-start.9 = (bf16[4,128,256]{2,1,0:T(8,128)(2,1)S(1)}, bf16[4,128,256]{2,1,0:T(8,128)(2,1)S(1)}, u32[]{:S(2)}, u32[]{:S(2)}) collective-permute-start(bf16[4,128,256]{2,1,0:T(8,128)(2,1)S(1)} %get-tuple-element.16.refs_0_), channel_id=1, source_target_pairs={{0,24},{8,0},{16,8},{24,16},{1,25},{9,1},{17,9},{25,17},{2,26},{10... | collective-permute-start | bytes 786440 | tf_op jit(solution)/shard_map/ppermute | solution.py:296
  25.3 0.5 collective-permute-start.8
  25.8 0.6 collective-permute-start.7
  26.5 0.9 collective-permute-done.10.first.refs_6_
  27.4 4.4 %collective-permute-start.11 = (bf16[4,128,256]{2,1,0:T(8,128)(2,1)S(1)}, bf16[4,128,256]{2,1,0:T(8,128)(2,1)S(1)}, u32[]{:S(2)}, u32[]{:S(2)}) collective-permute-start(bf16[4,128,256]{2,1,0:T(8,128)(2,1)S(1)} %shard_map.61.refs_4_), channel_id=1, source_target_pairs={{0,32},{32,0},{1,33},{33,1},{2,34},{34,2},{3,35},{35,3},{4,36},{36... | collective-permute-start | bytes 786440 | tf_op jit(solution)/shard_map/ppermute | solution.py:296
  31.7 0.1 collective-permute-start.12
  31.8 0.1 stack.29.place
  31.9 3.0 %shard_map.59.picked = s32[8,128]{1,0:T(8,128)S(1)} custom-call(s32[3,128]{1,0:T(4,128)S(1)} %concatenate.3.mine, s32[3,128]{1,0:T(4,128)S(1)} %collective-permute-done.other.lists, s32[5]{0:T(128)S(1)} %stack.29.place), custom_call_target="tpu_custom_call" | custom-call | tf_op jit(solution)/shard_map/pallas_call | solution.py:329
  34.9 0.0 collective-permute-done.9.refs_3_
  35.0 0.0 collective-permute-done.8.refs_2_
  35.0 4.1 %collective-permute-done.7.refs_1_ = bf16[4,128,256]{2,1,0:T(8,128)(2,1)S(1)} collective-permute-done((bf16[4,128,256]{2,1,0:T(8,128)(2,1)S(1)}, bf16[4,128,256]{2,1,0:T(8,128)(2,1)S(1)}, u32[]{:S(2)}, u32[]{:S(2)}) %collective-permute-start.7) | collective-permute-done | bytes 262176 | tf_op jit(solution)/shard_map/ppermute | solution.py:296
  39.1 0.0 collective-permute-done.11.refs_5_
  39.1 0.0 collective-permute-done.12.refs_7_
  39.1 6.6 %shard_map.62 = (f32[16,16,128]{2,1,0:T(8,128)S(1)}, bf16[16,128,256]{2,1,0:T(8,128)(2,1)S(1)}, bf16[16,128,256]{2,1,0:T(8,128)(2,1)S(1)}, f32[16,128]{1,0:T(8,1...) custom-call(s32[8,128]{1,0:T(8,128)S(1)} %shard_map.59.picked, ...), custom_call_target="tpu_custom_call" | custom-call | tf_op jit(solution)/shard_map/pallas_call | solution.py:272
  45.6 12.9 %all_to_all.20.parts = f32[16,16,128]{2,1,0:T(8,128)S(1)} all-to-all(f32[16,16,128]{2,1,0:T(8,128)S(1)} %get-tuple-element.20), channel_id=1, replica_groups=mesh['y'=4,'core'=2,'x'=4,'s'=4,'p'=2] {'x','s'}, dimensions={0} | all-to-all | bytes 262144 | tf_op jit(solution)/shard_map/all_to_all | solution.py:291
  58.5 5.3 %shard_map.63 = (f32[16,16,128]{2,1,0:T(8,128)S(1)}, f32[256,128,128]{2,1,0:T(8,128)}) custom-call(s32[8,128]{1,0:T(8,128)S(1)} %shard_map.59.picked, bf16[16,128,256]{2,1,0:T(8,128)(2,1)S(1)} %get-tuple-element.18.src, bf16[16,128,256]{2,1,0:T(8,128)(2,1)S(1)} %get-tuple-element.19.tgt, f32[16,16,128]{2,1,0:T(8,128)S(1)} %all_to_all.20.parts), custom_call_target="tpu_custom_call" | custom-call | tf_op jit(solution)/shard_map/pallas_call | solution.py:272
  63.8 14.5 %all_to_all.21.parts = f32[16,16,128]{2,1,0:T(8,128)S(1)} all-to-all(f32[16,16,128]{2,1,0:T(8,128)S(1)} %get-tuple-element.23), channel_id=1, replica_groups=mesh['y'=4,'core'=2,'x'=4,'s'=4,'p'=2] {'p','y','core'}, dimensions={0} | all-to-all | bytes 262144 | tf_op jit(solution)/shard_map/all_to_all | solution.py:291
  78.4 4.6 %shard_map.64 = f32[16,16,128]{2,1,0:T(8,128)S(1)} custom-call(s32[8,128]{1,0:T(8,128)S(1)} %shard_map.59.picked, f32[256,128,128]{2,1,0:T(8,128)} %get-tuple-element.22.saved, f32[16,16,128]{2,1,0:T(8,128)S(1)} %all_to_all.21.parts), custom_call_target="tpu_custom_call" | custom-call | tf_op jit(solution)/shard_map/pallas_call | solution.py:272
  83.0 13.0 %all_to_all.22.parts = f32[16,16,128]{2,1,0:T(8,128)S(1)} all-to-all(f32[16,16,128]{2,1,0:T(8,128)S(1)} %shard_map.64), channel_id=1, replica_groups=mesh['y'=4,'core'=2,'x'=4,'s'=4,'p'=2] {'x','s'}, dimensions={0} | all-to-all | bytes 262144 | tf_op jit(solution)/shard_map/all_to_all | solution.py:291
  96.0 5.3 %shard_map.65 = (f32[16,8,128]{2,1,0:T(8,128)}, f32[16,128]{1,0:T(8,128)S(1)}) custom-call(s32[8,128]{1,0:T(8,128)S(1)} %shard_map.59.picked, f32[256,128,128]{2,1,0:T(8,128)} %get-tuple-element.21.saved, f32[16,16,128]{2,1,0:T(8,128)S(1)} %all_to_all.22.parts, f32[16,128]{1,0:T(8,128)S(1)} %get-tuple-element.24.sq_src), custom_call_target="tpu_custom_call" | custom-call | tf_op jit(solution)/shard_map/pallas_call | solution.py:272
  101.3 6.6 %all-to-all-start.3 = ((f32[16,8,128]{2,1,0:T(8,128)}), f32[16,8,128]{2,1,0:T(8,128)S(1)}, u32[]{:S(2)}, u32[]{:S(2)}) async-start(f32[16,8,128]{2,1,0:T(8,128)} %get-tuple-element.25), calls=%async_computation.3 | async-start | bytes 131072 | tf_op jit(solution)/shard_map/all_to_all | solution.py:291
  107.9 1.4 %collective-permute-start.13 = (f32[16,128]{1,0:T(8,128)S(1)}, f32[16,128]{1,0:T(8,128)S(1)}, u32[]{:S(2)}, u32[]{:S(2)}) collective-permute-start(f32[16,128]{1,0:T(8,128)S(1)} %get-tuple-element.27.mine), channel_id=1, source_target_pairs={{0,1},{1,0},{2,3},{3,2},{4,5},{5,4},{6,7},{7,6},{8,9},{9,8},{10,11... | collective-permute-start | bytes 24584 | tf_op jit(solution)/shard_map/ppermute | solution.py:323
  109.3 1.7 %collective-permute-done.13.other = f32[16,128]{1,0:T(8,128)S(1)} collective-permute-done((f32[16,128]{1,0:T(8,128)S(1)}, f32[16,128]{1,0:T(8,128)S(1)}, u32[]{:S(2)}, u32[]{:S(2)}) %collective-permute-start.13) | collective-permute-done | bytes 8224 | tf_op jit(solution)/shard_map/ppermute | solution.py:323
  110.9 2.8 %all-to-all-done.3.parts = f32[16,8,128]{2,1,0:T(8,128)S(1)} async-done(((f32[16,8,128]{2,1,0:T(8,128)}), f32[16,8,128]{2,1,0:T(8,128)S(1)}, u32[]{:S(2)}, u32[]{:S(2)}) %all-to-all-start.3) | async-done | bytes 65568 | tf_op jit(solution)/shard_map/all_to_all | solution.py:291
  113.7 0.6 shard_map.66
  (2 shorter events, 0.1 us)
Async XLA Ops:
  0.6 16.2 %collective-permute-start.1 = (bf16[128,256]{1,0:T(8,128)(2,1)}, bf16[128,256]{1,0:T(8,128)(2,1)S(1)}, u32[]{:S(2)}, u32[]{:S(2)}) collective-permute-start(bf16[128,256]{1,0:T(8,128)(2,1)} %param.4), channel_id=1, source_target_pairs={{0,2},{2,4},{4,6},{6,0},{1,3},{3,5},{5,7},{7,1},{8,10},{10,12},{12... | collective-permute-start | bytes 196616 | tf_op jit(solution)/shard_map/ppermute | solution.py:296
  5.9 9.5 %collective-permute-start = (s32[3,128]{1,0:T(4,128)S(1)}, s32[3,128]{1,0:T(4,128)S(1)}, u32[]{:S(2)}, u32[]{:S(2)}) collective-permute-start(s32[3,128]{1,0:T(4,128)S(1)} %concatenate.3.mine), channel_id=1, source_target_pairs={{0,1},{1,0},{2,3},{3,2},{4,5},{5,4},{6,7},{7,6},{8,9},{9,8},{10,11... | collective-permute-start | bytes 4616 | tf_op jit(solution)/shard_map/ppermute | solution.py:323
  7.5 11.9 %collective-permute-start.3 = (bf16[128,256]{1,0:T(8,128)(2,1)}, bf16[128,256]{1,0:T(8,128)(2,1)S(1)}, u32[]{:S(2)}, u32[]{:S(2)}) collective-permute-start(bf16[128,256]{1,0:T(8,128)(2,1)} %param.4), channel_id=1, source_target_pairs={{0,6},{2,0},{4,2},{6,4},{1,7},{3,1},{5,3},{7,5},{8,14},{10,8},{12,... | collective-permute-start | bytes 196616 | tf_op jit(solution)/shard_map/ppermute | solution.py:296
  9.6 9.7 %collective-permute-start.2 = (bf16[128,256]{1,0:T(8,128)(2,1)}, bf16[128,256]{1,0:T(8,128)(2,1)S(1)}, u32[]{:S(2)}, u32[]{:S(2)}) collective-permute-start(bf16[128,256]{1,0:T(8,128)(2,1)} %param.4), channel_id=1, source_target_pairs={{0,4},{2,6},{4,0},{6,2},{1,5},{3,7},{5,1},{7,3},{8,12},{10,14},{12... | collective-permute-start | bytes 196616 | tf_op jit(solution)/shard_map/ppermute | solution.py:296
  14.1 5.3 %collective-permute-start.4 = (bf16[128,256]{1,0:T(8,128)(2,1)}, bf16[128,256]{1,0:T(8,128)(2,1)S(1)}, u32[]{:S(2)}, u32[]{:S(2)}) collective-permute-start(bf16[128,256]{1,0:T(8,128)(2,1)} %param.5), channel_id=1, source_target_pairs={{0,64},{64,128},{128,192},{192,0},{1,65},{65,129},{129,193},{193,1... | collective-permute-start | bytes 196616 | tf_op jit(solution)/shard_map/ppermute | solution.py:296
  15.4 4.0 %collective-permute-start.6 = (bf16[128,256]{1,0:T(8,128)(2,1)}, bf16[128,256]{1,0:T(8,128)(2,1)S(1)}, u32[]{:S(2)}, u32[]{:S(2)}) collective-permute-start(bf16[128,256]{1,0:T(8,128)(2,1)} %param.5), channel_id=1, source_target_pairs={{0,192},{64,0},{128,64},{192,128},{1,193},{65,1},{129,65},{193,129... | collective-permute-start | bytes 196616 | tf_op jit(solution)/shard_map/ppermute | solution.py:296
  16.8 5.1 %collective-permute-start.5 = (bf16[128,256]{1,0:T(8,128)(2,1)}, bf16[128,256]{1,0:T(8,128)(2,1)S(1)}, u32[]{:S(2)}, u32[]{:S(2)}) collective-permute-start(bf16[128,256]{1,0:T(8,128)(2,1)} %param.5), channel_id=1, source_target_pairs={{0,128},{64,192},{128,0},{192,64},{1,129},{65,193},{129,1},{193,65... | collective-permute-start | bytes 196616 | tf_op jit(solution)/shard_map/ppermute | solution.py:296
  22.0 5.3 %collective-permute-start.10 = (bf16[4,128,256]{2,1,0:T(8,128)(2,1)S(1)}, bf16[4,128,256]{2,1,0:T(8,128)(2,1)S(1)}, u32[]{:S(2)}, u32[]{:S(2)}) collective-permute-start(bf16[4,128,256]{2,1,0:T(8,128)(2,1)S(1)} %get-tuple-element.17.block), channel_id=1, source_target_pairs={{0,1},{1,0},{2,3},{3,2},{4,5},{5,4},{6,7},{7,6},{8,9},{9,8},{10,11... | collective-permute-start | bytes 786440 | tf_op jit(solution)/shard_map/ppermute | solution.py:296
  22.8 12.1 %collective-permute-start.9 = (bf16[4,128,256]{2,1,0:T(8,128)(2,1)S(1)}, bf16[4,128,256]{2,1,0:T(8,128)(2,1)S(1)}, u32[]{:S(2)}, u32[]{:S(2)}) collective-permute-start(bf16[4,128,256]{2,1,0:T(8,128)(2,1)S(1)} %get-tuple-element.16.refs_0_), channel_id=1, source_target_pairs={{0,24},{8,0},{16,8},{24,16},{1,25},{9,1},{17,9},{25,17},{2,26},{10... | collective-permute-start | bytes 786440 | tf_op jit(solution)/shard_map/ppermute | solution.py:296
  25.3 9.6 %collective-permute-start.8 = (bf16[4,128,256]{2,1,0:T(8,128)(2,1)S(1)}, bf16[4,128,256]{2,1,0:T(8,128)(2,1)S(1)}, u32[]{:S(2)}, u32[]{:S(2)}) collective-permute-start(bf16[4,128,256]{2,1,0:T(8,128)(2,1)S(1)} %get-tuple-element.16.refs_0_), channel_id=1, source_target_pairs={{0,16},{8,24},{16,0},{24,8},{1,17},{9,25},{17,1},{25,9},{2,18},{10... | collective-permute-start | bytes 786440 | tf_op jit(solution)/shard_map/ppermute | solution.py:296
  25.8 13.2 %collective-permute-start.7 = (bf16[4,128,256]{2,1,0:T(8,128)(2,1)S(1)}, bf16[4,128,256]{2,1,0:T(8,128)(2,1)S(1)}, u32[]{:S(2)}, u32[]{:S(2)}) collective-permute-start(bf16[4,128,256]{2,1,0:T(8,128)(2,1)S(1)} %get-tuple-element.16.refs_0_), channel_id=1, source_target_pairs={{0,8},{8,16},{16,24},{24,0},{1,9},{9,17},{17,25},{25,1},{2,10},{10... | collective-permute-start | bytes 786440 | tf_op jit(solution)/shard_map/ppermute | solution.py:296
  27.4 11.7 %collective-permute-start.11 = (bf16[4,128,256]{2,1,0:T(8,128)(2,1)S(1)}, bf16[4,128,256]{2,1,0:T(8,128)(2,1)S(1)}, u32[]{:S(2)}, u32[]{:S(2)}) collective-permute-start(bf16[4,128,256]{2,1,0:T(8,128)(2,1)S(1)} %shard_map.61.refs_4_), channel_id=1, source_target_pairs={{0,32},{32,0},{1,33},{33,1},{2,34},{34,2},{3,35},{35,3},{4,36},{36... | collective-permute-start | bytes 786440 | tf_op jit(solution)/shard_map/ppermute | solution.py:296
  31.7 7.4 %collective-permute-start.12 = (bf16[4,128,256]{2,1,0:T(8,128)(2,1)S(1)}, bf16[4,128,256]{2,1,0:T(8,128)(2,1)S(1)}, u32[]{:S(2)}, u32[]{:S(2)}) collective-permute-start(bf16[4,128,256]{2,1,0:T(8,128)(2,1)S(1)} %collective-permute-done.10.first.refs_6_), channel_id=1, source_target_pairs={{0,32},{32,0},{1,33},{33,1},{2,34},{34,2},{3,35},{35,3},{4,36},{36... | collective-permute-start | bytes 786440 | tf_op jit(solution)/shard_map/ppermute | solution.py:296
  101.3 12.4 %all-to-all-start.3 = ((f32[16,8,128]{2,1,0:T(8,128)}), f32[16,8,128]{2,1,0:T(8,128)S(1)}, u32[]{:S(2)}, u32[]{:S(2)}) async-start(f32[16,8,128]{2,1,0:T(8,128)} %get-tuple-element.25), calls=%async_computation.3 | async-start | bytes 131072 | tf_op jit(solution)/shard_map/all_to_all | solution.py:291
  107.9 3.1 %collective-permute-start.13 = (f32[16,128]{1,0:T(8,128)S(1)}, f32[16,128]{1,0:T(8,128)S(1)}, u32[]{:S(2)}, u32[]{:S(2)}) collective-permute-start(f32[16,128]{1,0:T(8,128)S(1)} %get-tuple-element.27.mine), channel_id=1, source_target_pairs={{0,1},{1,0},{2,3},{3,2},{4,5},{5,4},{6,7},{7,6},{8,9},{9,8},{10,11... | collective-permute-start | bytes 24584 | tf_op jit(solution)/shard_map/ppermute | solution.py:323

commit v12 on v11

--- a/solution.py
+++ b/solution.py
@@ -24,7 +24,7 @@
 VMEM = pl.BlockSpec(memory_space=pltpu.VMEM)
 SMEM = pl.BlockSpec(memory_space=pltpu.SMEM)
 ANY = pl.BlockSpec(memory_space=pl.ANY)
-PARAMS = pltpu.CompilerParams(vmem_limit_bytes=48 * 2**20)
+PARAMS = pltpu.CompilerParams(vmem_limit_bytes=10 * 2**20)
 
 
 def square_rows(cells):
@@ -50,71 +50,32 @@
         wide[n] = jnp.broadcast_to(columns[:, n : n + 1], (TILE, TILE))
 
 
-def dot_tiles(near, far, saved, stage, sems):
-    def out(step):
-        half = step & 1
-        return pltpu.make_async_copy(stage.at[half], saved.at[pl.ds(step * UNROLL, UNROLL)], sems.at[half])
-
-    def before(step, steps):
-        pl.when(step >= 2)(lambda: out(step - 2).wait())
-
-    def tile(step, u, n, f):
+def dot_tiles(near, far, saved):
+    def tile(at, n, f):
         inner = lax.dot_general(near[n], far[f], NT, preferred_element_type=F32) * (2.0 * KAPPA)
-        stage[step & 1, u] = inner
+        saved[at] = inner
         return inner
 
-    def after(step):
-        out(step).start()
-
-    def end(steps):
-        pl.when(steps >= 2)(lambda: out(steps - 2).wait())
-        pl.when(steps >= 1)(lambda: out(steps - 1).wait())
-
-    return before, tile, after, end
-
-
-def saved_tiles(saved, stage, sems):
-    def fetch(step):
-        half = step & 1
-        return pltpu.make_async_copy(saved.at[pl.ds(step * UNROLL, UNROLL)], stage.at[half], sems.at[half])
-
-    def before(step, steps):
-        pl.when(step + 1 < steps)(lambda: fetch(step + 1).start())
-        fetch(step).wait()
-
-    def tile(step, u, n, f):
-        return stage[step & 1, u]
-
-    def after(step):
-        pass
-
-    def end(steps):
-        pl.when(steps == 0)(lambda: fetch(0).wait())
-
-    return fetch, (before, tile, after, end)
+    return tile
 
 
 def tile_sums(place_of, count, source, near_blocks, far_blocks, wide, peaks, totals):
     spare = near_blocks * far_blocks
-    before, tile, after, end = source
     peaks[...] = jnp.full(peaks.shape, EMPTY, F32)
     totals[...] = jnp.zeros(totals.shape, F32)
     steps = (count + UNROLL - 1) // UNROLL
 
     @pl.loop(0, steps)
     def _(step):
-        before(step, steps)
         for u in range(UNROLL):
             k = step * UNROLL + u
             n, f = place_of(jnp.where(k < count, k, 0))
-            score = (tile(step, u, n, f) + wide[n]).reshape(TILE // 8, 8, TILE)
+            score = (source(k, n, f) + wide[n]).reshape(TILE // 8, 8, TILE)
             peak = jnp.max(score, axis=0)
             slot = jnp.where(k < count, f * near_blocks + n, spare)
             peaks[slot] = peak
             totals[slot] = jnp.sum(jnp.exp2(score - peak[None]), axis=0)
-        after(step)
-
-    end(steps)
+
     rows = []
     for f in range(far_blocks):
         at = pl.ds(f * near_blocks, near_blocks)
@@ -190,8 +151,8 @@
 
 
 def first_kernel(picked, *refs):
-    pieces, refs = refs[:-13], refs[-13:]
-    out, src, tgt, sq_src, sq_tgt, saved, wide, peaks, totals, tiles, sem, stage, sems = refs
+    pieces, refs = refs[:-11], refs[-11:]
+    out, src, tgt, sq_src, sq_tgt, saved, wide, peaks, totals, tiles, sem = refs
     fetch = pltpu.make_async_copy(picked, tiles, sem)
     fetch.start()
     sides = len(pieces) // 2
@@ -210,27 +171,26 @@
     for a in range(srcs):
         sq_src[a : a + 1, :] = square_rows(src[a])
     expand(sq_tgt[...] * -KAPPA, wide)
-    source = dot_tiles(tgt, src, saved, stage, sems)
+    source = dot_tiles(tgt, src, saved)
     sums = tile_sums(source_tiles(tiles, tgts), tiles[0, 1], source, tgts, srcs, wide, peaks, totals)
     out[...] = jnp.broadcast_to(sums[None], out.shape)
 
 
-def target_kernel(log_cells, picked, src, tgt, parts, out, saved, wide, peaks, totals, tiles, sem, stage, sems):
+def target_kernel(log_cells, picked, src, tgt, parts, out, saved, wide, peaks, totals, tiles, sem):
     fetch = pltpu.make_async_copy(picked, tiles, sem)
     fetch.start()
     expand(-log_cells - log_sum(parts[...]), wide)
     fetch.wait()
     srcs, tgts = src.shape[0], tgt.shape[0]
-    source = dot_tiles(src, tgt, saved, stage, sems)
+    source = dot_tiles(src, tgt, saved)
     sums = tile_sums(target_tiles(tiles, tgts), tiles[0, 1], source, srcs, tgts, wide, peaks, totals)
     out[...] = jnp.broadcast_to(sums[None], out.shape)
 
 
-def again_source_kernel(log_cells, picked, saved, parts, out, wide, peaks, totals, tiles, sem, stage, sems):
+def again_source_kernel(log_cells, picked, saved, parts, out, wide, peaks, totals, tiles, sem):
     fetch = pltpu.make_async_copy(picked, tiles, sem)
     fetch.start()
-    read, source = saved_tiles(saved, stage, sems)
-    read(0).start()
+    source = lambda at, n, f: saved[at]
     tgts, srcs = parts.shape[1], out.shape[1]
     expand(-log_cells - log_sum(parts[...]), wide)
     fetch.wait()
@@ -239,12 +199,11 @@
 
 
 def again_target_kernel(
-    log_cells, tgts, picked, saved, parts, sq_src, out, pot, wide, peaks, totals, tiles, sem, stage, sems
+    log_cells, tgts, picked, saved, parts, sq_src, out, pot, wide, peaks, totals, tiles, sem
 ):
     fetch = pltpu.make_async_copy(picked, tiles, sem)
     fetch.start()
-    read, source = saved_tiles(saved, stage, sems)
-    read(0).start()
+    source = lambda at, n, f: saved[at]
     srcs = parts.shape[1]
     weights = -log_cells - log_sum(parts[...])
     pot[...] = weights * (1.0 / KAPPA) + sq_src[...]
@@ -268,20 +227,18 @@
     src_pot[:, 1, :] = jnp.where(p == 0, other[...], mine[...])
 
 
-def half_step(kernel, outs, near_blocks, slots, picked, *args, reads=0, writes=0):
+def half_step(kernel, outs, near_blocks, slots, picked, *args):
     return pl.pallas_call(
         kernel,
         out_shape=[s if isinstance(s, jax.ShapeDtypeStruct) else jax.ShapeDtypeStruct(s, F32) for s in outs],
-        in_specs=[ANY] * (1 + reads) + [VMEM] * (len(args) - reads),
-        out_specs=[VMEM] * (len(outs) - writes) + [ANY] * writes,
+        in_specs=[ANY] + [VMEM] * len(args),
+        out_specs=[VMEM] * len(outs),
         scratch_shapes=[
             pltpu.VMEM((near_blocks, TILE, TILE), F32),
             pltpu.VMEM((slots + 1, 8, TILE), F32),
             pltpu.VMEM((slots + 1, 8, TILE), F32),
             pltpu.SMEM(picked.shape, picked.dtype),
             pltpu.SemaphoreType.DMA,
-            pltpu.VMEM((2, UNROLL, TILE, TILE), F32),
-            pltpu.SemaphoreType.DMA((2,)),
         ],
         compiler_params=PARAMS,
     )(picked, *args)
@@ -341,18 +298,18 @@
     src_out, tgt_out, all_tiles = (srcs, srcs, TILE), (tgts, tgts, TILE), (slots, TILE, TILE)
     outs = [src_out, src_shape, tgt_shape, (srcs, TILE), (tgts, TILE), all_tiles]
     parts, src, tgt, sq_src, sq_tgt, src_saved = half_step(
-        first_kernel, outs, tgts, slots, picked, *src_pieces, *tgt_pieces, writes=1
+        first_kernel, outs, tgts, slots, picked, *src_pieces, *tgt_pieces
     )
     parts = exchange(parts, SRC_PEERS)
     step = functools.partial(target_kernel, log_cells)
-    parts, tgt_saved = half_step(step, [tgt_out, all_tiles], srcs, slots, picked, src, tgt, parts, writes=1)
+    parts, tgt_saved = half_step(step, [tgt_out, all_tiles], srcs, slots, picked, src, tgt, parts)
     parts = exchange(parts, TGT_PEERS)
     step = functools.partial(again_source_kernel, log_cells)
-    (parts,) = half_step(step, [src_out], tgts, slots, picked, src_saved, parts, reads=1)
+    (parts,) = half_step(step, [src_out], tgts, slots, picked, src_saved, parts)
     parts = exchange(parts, SRC_PEERS)
     step = functools.partial(again_target_kernel, log_cells, tgts)
     outs = [(tgts, rows, TILE), (srcs, TILE)]
-    parts, src_pot = half_step(step, outs, srcs, slots, picked, tgt_saved, parts, sq_src, reads=1)
+    parts, src_pot = half_step(step, outs, srcs, slots, picked, tgt_saved, parts, sq_src)
     other_pot = partner(src_pot)
     parts = exchange(parts, TGT_PEERS)
     tgt_pot, both = pl.pallas_call(

time: 113 us -> 103 us (0.912)
  Pallas kernels: 25.5 us -> 12.5 us
  blocking collectives: 40.4 us -> 43.2 us
    pallas_call x4, Pallas kernels: 21.8 us -> 8.81 us  [half_step(): pl.pallas_call(kernel, out_shape=[s if isinstance(s, jax.ShapeDtypeStruct...]
    all_to_all x3, blocking collectives: 40.4 us -> 43.2 us  [exchange(): return lax.all_to_all(copies, peers, 0, 0, tiled=True)]
  transfers between devices with their start and end apart: 15 -> 15, of which waited for: 5 -> 5; matrix products, arithmetic and copies ran while one was open for 1% -> 2% of each run, Pallas kernels for 3% -> 3%
where the time goes in v12:
time: 103 us; the launch traced here: 104 us
  blocking collectives  43.2 us (42%)
  starting transfers between devices  33.4 us (32%)
  Pallas kernels  12.5 us (12%)
  waiting for transfers between devices  12 us (12%)
  between operations  1.39 us (1%)
    all_to_all x3, blocking collectives, exchange(): return lax.all_to_all(copies, peers, 0, 0, tiled=True)  43.2 us
    ppermute x12, starting transfers between devices, shifts(): lax.ppermute(block, axis, [(i, (i + d) % n) for i in range(n)])  23.8 us
    pallas_call x4, Pallas kernels, half_step(): pl.pallas_call(kernel, out_shape=[s if isinstance(s, jax.ShapeDtypeStruct...  8.81 us
    ppermute x12, waiting for transfers between devices, shifts(): lax.ppermute(block, axis, [(i, (i + d) % n) for i in range(n)])  7.6 us
    all_to_all x1, starting transfers between devices, exchange(): return lax.all_to_all(copies, peers, 0, 0, tiled=True)  6.59 us
    ppermute x2, starting transfers between devices, local(): partner = lambda v: lax.ppermute(v, 'p', [(0, 1), (1, 0)])  3.03 us
    pallas_call x1, Pallas kernels, local(): pl.pallas_call(pick_kernel, out_shape=jax.ShapeDtypeStruct((8, TILE), jnp...  3.02 us
    all_to_all x1, waiting for transfers between devices, exchange(): return lax.all_to_all(copies, peers, 0, 0, tiled=True)  2.77 us
  transfers between devices with their start and end apart: 15, of which 5 were waited for; matrix products, arithmetic and copies ran while one was open for 2% of the time, Pallas kernels for 3%

profile of v12, /device:TPU:1, one launch (start us, length us, event | category | flops | bytes accessed | tf_op | source)
XLA Modules:
  0.0 104.2 jit_solution(14197597243166555440)
XLA Ops:
  0.6 3.9 %collective-permute-start.1 = (bf16[128,256]{1,0:T(8,128)(2,1)}, bf16[128,256]{1,0:T(8,128)(2,1)S(1)}, u32[]{:S(2)}, u32[]{:S(2)}) collective-permute-start(bf16[128,256]{1,0:T(8,128)(2,1)} %param.4), channel_id=1, source_target_pairs={{0,2},{2,4},{4,6},{6,0},{1,3},{3,5},{5,7},{7,1},{8,10},{10,12},{12... | collective-permute-start | bytes 196616 | tf_op jit(solution)/shard_map/ppermute | solution.py:253
  5.2 0.7 concatenate.3.mine
  5.9 1.6 %collective-permute-start = (s32[3,128]{1,0:T(4,128)S(1)}, s32[3,128]{1,0:T(4,128)S(1)}, u32[]{:S(2)}, u32[]{:S(2)}) collective-permute-start(s32[3,128]{1,0:T(4,128)S(1)} %concatenate.3.mine), channel_id=1, source_target_pairs={{0,1},{1,0},{2,3},{3,2},{4,5},{5,4},{6,7},{7,6},{8,9},{9,8},{10,11... | collective-permute-start | bytes 4616 | tf_op jit(solution)/shard_map/ppermute | solution.py:280
  7.5 2.1 %collective-permute-start.3 = (bf16[128,256]{1,0:T(8,128)(2,1)}, bf16[128,256]{1,0:T(8,128)(2,1)S(1)}, u32[]{:S(2)}, u32[]{:S(2)}) collective-permute-start(bf16[128,256]{1,0:T(8,128)(2,1)} %param.4), channel_id=1, source_target_pairs={{0,6},{2,0},{4,2},{6,4},{1,7},{3,1},{5,3},{7,5},{8,14},{10,8},{12,... | collective-permute-start | bytes 196616 | tf_op jit(solution)/shard_map/ppermute | solution.py:253
  9.6 4.5 %collective-permute-start.2 = (bf16[128,256]{1,0:T(8,128)(2,1)}, bf16[128,256]{1,0:T(8,128)(2,1)S(1)}, u32[]{:S(2)}, u32[]{:S(2)}) collective-permute-start(bf16[128,256]{1,0:T(8,128)(2,1)} %param.4), channel_id=1, source_target_pairs={{0,4},{2,6},{4,0},{6,2},{1,5},{3,7},{5,1},{7,3},{8,12},{10,14},{12... | collective-permute-start | bytes 196616 | tf_op jit(solution)/shard_map/ppermute | solution.py:253
  14.1 1.3 %collective-permute-start.4 = (bf16[128,256]{1,0:T(8,128)(2,1)}, bf16[128,256]{1,0:T(8,128)(2,1)S(1)}, u32[]{:S(2)}, u32[]{:S(2)}) collective-permute-start(bf16[128,256]{1,0:T(8,128)(2,1)} %param.5), channel_id=1, source_target_pairs={{0,64},{64,128},{128,192},{192,0},{1,65},{65,129},{129,193},{193,1... | collective-permute-start | bytes 196616 | tf_op jit(solution)/shard_map/ppermute | solution.py:253
  15.4 0.0 collective-permute-done.other.lists
  15.4 1.4 %collective-permute-start.6 = (bf16[128,256]{1,0:T(8,128)(2,1)}, bf16[128,256]{1,0:T(8,128)(2,1)S(1)}, u32[]{:S(2)}, u32[]{:S(2)}) collective-permute-start(bf16[128,256]{1,0:T(8,128)(2,1)} %param.5), channel_id=1, source_target_pairs={{0,192},{64,0},{128,64},{192,128},{1,193},{65,1},{129,65},{193,129... | collective-permute-start | bytes 196616 | tf_op jit(solution)/shard_map/ppermute | solution.py:253
  16.8 0.0 collective-permute-done.1.refs_0_
  16.8 1.6 %collective-permute-start.5 = (bf16[128,256]{1,0:T(8,128)(2,1)}, bf16[128,256]{1,0:T(8,128)(2,1)S(1)}, u32[]{:S(2)}, u32[]{:S(2)}) collective-permute-start(bf16[128,256]{1,0:T(8,128)(2,1)} %param.5), channel_id=1, source_target_pairs={{0,128},{64,192},{128,0},{192,64},{1,129},{65,193},{129,1},{193,65... | collective-permute-start | bytes 196616 | tf_op jit(solution)/shard_map/ppermute | solution.py:253
  18.5 0.9 pad_maximum_fusion.own
  19.4 0.0 collective-permute-done.3.refs_2_
  19.4 0.0 collective-permute-done.2.refs_1_
  19.4 0.0 collective-permute-done.4.refs_3_
  19.4 0.0 collective-permute-done.6.refs_5_
  19.4 2.6 %collective-permute-done.5.refs_4_ = bf16[128,256]{1,0:T(8,128)(2,1)S(1)} collective-permute-done((bf16[128,256]{1,0:T(8,128)(2,1)}, bf16[128,256]{1,0:T(8,128)(2,1)S(1)}, u32[]{:S(2)}, u32[]{:S(2)}) %collective-permute-start.5) | collective-permute-done | bytes 65568 | tf_op jit(solution)/shard_map/ppermute | solution.py:253
  22.0 0.8 collective-permute-start.10
  22.8 2.5 %collective-permute-start.9 = (bf16[4,128,256]{2,1,0:T(8,128)(2,1)S(1)}, bf16[4,128,256]{2,1,0:T(8,128)(2,1)S(1)}, u32[]{:S(2)}, u32[]{:S(2)}) collective-permute-start(bf16[4,128,256]{2,1,0:T(8,128)(2,1)S(1)} %get-tuple-element.16.refs_0_), channel_id=1, source_target_pairs={{0,24},{8,0},{16,8},{24,16},{1,25},{9,1},{17,9},{25,17},{2,26},{10... | collective-permute-start | bytes 786440 | tf_op jit(solution)/shard_map/ppermute | solution.py:253
  25.3 0.5 collective-permute-start.8
  25.8 0.6 collective-permute-start.7
  26.5 0.9 collective-permute-done.10.first.refs_6_
  27.4 4.4 %collective-permute-start.11 = (bf16[4,128,256]{2,1,0:T(8,128)(2,1)S(1)}, bf16[4,128,256]{2,1,0:T(8,128)(2,1)S(1)}, u32[]{:S(2)}, u32[]{:S(2)}) collective-permute-start(bf16[4,128,256]{2,1,0:T(8,128)(2,1)S(1)} %shard_map.61.refs_4_), channel_id=1, source_target_pairs={{0,32},{32,0},{1,33},{33,1},{2,34},{34,2},{3,35},{35,3},{4,36},{36... | collective-permute-start | bytes 786440 | tf_op jit(solution)/shard_map/ppermute | solution.py:253
  31.7 0.1 collective-permute-start.12
  31.8 0.1 stack.29.place
  31.9 3.0 %shard_map.59.picked = s32[8,128]{1,0:T(8,128)S(1)} custom-call(s32[3,128]{1,0:T(4,128)S(1)} %concatenate.3.mine, s32[3,128]{1,0:T(4,128)S(1)} %collective-permute-done.other.lists, s32[5]{0:T(128)S(1)} %stack.29.place), custom_call_target="tpu_custom_call" | custom-call | tf_op jit(solution)/shard_map/pallas_call | solution.py:286
  34.9 0.0 collective-permute-done.9.refs_3_
  35.0 0.0 collective-permute-done.8.refs_2_
  35.0 4.1 %collective-permute-done.7.refs_1_ = bf16[4,128,256]{2,1,0:T(8,128)(2,1)S(1)} collective-permute-done((bf16[4,128,256]{2,1,0:T(8,128)(2,1)S(1)}, bf16[4,128,256]{2,1,0:T(8,128)(2,1)S(1)}, u32[]{:S(2)}, u32[]{:S(2)}) %collective-permute-start.7) | collective-permute-done | bytes 262176 | tf_op jit(solution)/shard_map/ppermute | solution.py:253
  39.1 0.0 collective-permute-done.11.refs_5_
  39.1 0.0 collective-permute-done.12.refs_7_
  39.1 3.2 %shard_map.62 = (f32[16,16,128]{2,1,0:T(8,128)S(1)}, bf16[16,128,256]{2,1,0:T(8,128)(2,1)S(1)}, bf16[16,128,256]{2,1,0:T(8,128)(2,1)S(1)}, f32[16,128]{1,0:T(8,1...) custom-call(s32[8,128]{1,0:T(8,128)S(1)} %shard_map.59.picked, ...), custom_call_target="tpu_custom_call" | custom-call | tf_op jit(solution)/shard_map/pallas_call | solution.py:231
  42.3 14.2 %all_to_all.20.parts = f32[16,16,128]{2,1,0:T(8,128)S(1)} all-to-all(f32[16,16,128]{2,1,0:T(8,128)S(1)} %get-tuple-element.20), channel_id=1, replica_groups=mesh['y'=4,'core'=2,'x'=4,'s'=4,'p'=2] {'x','s'}, dimensions={0} | all-to-all | bytes 262144 | tf_op jit(solution)/shard_map/all_to_all | solution.py:248
  56.5 2.1 %shard_map.63 = (f32[16,16,128]{2,1,0:T(8,128)S(1)}, f32[256,128,128]{2,1,0:T(8,128)S(1)}) custom-call(s32[8,128]{1,0:T(8,128)S(1)} %shard_map.59.picked, bf16[16,128,256]{2,1,0:T(8,128)(2,1)S(1)} %get-tuple-element.18.src, bf16[16,128,256]{2,1,0:T(8,128)(2,1)S(1)} %get-tuple-element.19.tgt, f32[16,16,128]{2,1,0:T(8,128)S(1)} %all_to_all.20.parts), custom_call_target="tpu_custom_call" | custom-call | tf_op jit(solution)/shard_map/pallas_call | solution.py:231
  58.7 16.4 %all_to_all.21.parts = f32[16,16,128]{2,1,0:T(8,128)S(1)} all-to-all(f32[16,16,128]{2,1,0:T(8,128)S(1)} %get-tuple-element.23), channel_id=1, replica_groups=mesh['y'=4,'core'=2,'x'=4,'s'=4,'p'=2] {'p','y','core'}, dimensions={0} | all-to-all | bytes 262144 | tf_op jit(solution)/shard_map/all_to_all | solution.py:248
  75.1 1.4 %shard_map.64 = f32[16,16,128]{2,1,0:T(8,128)S(1)} custom-call(s32[8,128]{1,0:T(8,128)S(1)} %shard_map.59.picked, f32[256,128,128]{2,1,0:T(8,128)S(1)} %get-tuple-element.22.saved, f32[16,16,128]{2,1,0:T(8,128)S(1)} %all_to_all.21.parts), custom_call_target="tpu_custom_call" | custom-call | tf_op jit(solution)/shard_map/pallas_call | solution.py:231
  76.6 12.5 %all_to_all.22.parts = f32[16,16,128]{2,1,0:T(8,128)S(1)} all-to-all(f32[16,16,128]{2,1,0:T(8,128)S(1)} %shard_map.64), channel_id=1, replica_groups=mesh['y'=4,'core'=2,'x'=4,'s'=4,'p'=2] {'x','s'}, dimensions={0} | all-to-all | bytes 262144 | tf_op jit(solution)/shard_map/all_to_all | solution.py:248
  89.1 2.0 %shard_map.65 = (f32[16,8,128]{2,1,0:T(8,128)}, f32[16,128]{1,0:T(8,128)S(1)}) custom-call(s32[8,128]{1,0:T(8,128)S(1)} %shard_map.59.picked, f32[256,128,128]{2,1,0:T(8,128)S(1)} %get-tuple-element.21.saved, f32[16,16,128]{2,1,0:T(8,128)S(1)} %all_to_all.22.parts, f32[16,128]{1,0:T(8,128)S(1)} %get-tuple-element.24.sq_src), custom_call_target="tpu_custom_call" | custom-call | tf_op jit(solution)/shard_map/pallas_call | solution.py:231
  91.1 6.6 %all-to-all-start.3 = ((f32[16,8,128]{2,1,0:T(8,128)}), f32[16,8,128]{2,1,0:T(8,128)S(1)}, u32[]{:S(2)}, u32[]{:S(2)}) async-start(f32[16,8,128]{2,1,0:T(8,128)} %get-tuple-element.25), calls=%async_computation.3 | async-start | bytes 131072 | tf_op jit(solution)/shard_map/all_to_all | solution.py:248
  97.7 1.4 %collective-permute-start.13 = (f32[16,128]{1,0:T(8,128)S(1)}, f32[16,128]{1,0:T(8,128)S(1)}, u32[]{:S(2)}, u32[]{:S(2)}) collective-permute-start(f32[16,128]{1,0:T(8,128)S(1)} %get-tuple-element.27.mine), channel_id=1, source_target_pairs={{0,1},{1,0},{2,3},{3,2},{4,5},{5,4},{6,7},{7,6},{8,9},{9,8},{10,11... | collective-permute-start | bytes 24584 | tf_op jit(solution)/shard_map/ppermute | solution.py:280
  99.1 1.7 %collective-permute-done.13.other = f32[16,128]{1,0:T(8,128)S(1)} collective-permute-done((f32[16,128]{1,0:T(8,128)S(1)}, f32[16,128]{1,0:T(8,128)S(1)}, u32[]{:S(2)}, u32[]{:S(2)}) %collective-permute-start.13) | collective-permute-done | bytes 8224 | tf_op jit(solution)/shard_map/ppermute | solution.py:280
  100.8 2.8 %all-to-all-done.3.parts = f32[16,8,128]{2,1,0:T(8,128)S(1)} async-done(((f32[16,8,128]{2,1,0:T(8,128)}), f32[16,8,128]{2,1,0:T(8,128)S(1)}, u32[]{:S(2)}, u32[]{:S(2)}) %all-to-all-start.3) | async-done | bytes 65568 | tf_op jit(solution)/shard_map/all_to_all | solution.py:248
  103.5 0.6 shard_map.66
  (2 shorter events, 0.1 us)
Async XLA Ops:
  0.6 16.2 %collective-permute-start.1 = (bf16[128,256]{1,0:T(8,128)(2,1)}, bf16[128,256]{1,0:T(8,128)(2,1)S(1)}, u32[]{:S(2)}, u32[]{:S(2)}) collective-permute-start(bf16[128,256]{1,0:T(8,128)(2,1)} %param.4), channel_id=1, source_target_pairs={{0,2},{2,4},{4,6},{6,0},{1,3},{3,5},{5,7},{7,1},{8,10},{10,12},{12... | collective-permute-start | bytes 196616 | tf_op jit(solution)/shard_map/ppermute | solution.py:253
  5.9 9.5 %collective-permute-start = (s32[3,128]{1,0:T(4,128)S(1)}, s32[3,128]{1,0:T(4,128)S(1)}, u32[]{:S(2)}, u32[]{:S(2)}) collective-permute-start(s32[3,128]{1,0:T(4,128)S(1)} %concatenate.3.mine), channel_id=1, source_target_pairs={{0,1},{1,0},{2,3},{3,2},{4,5},{5,4},{6,7},{7,6},{8,9},{9,8},{10,11... | collective-permute-start | bytes 4616 | tf_op jit(solution)/shard_map/ppermute | solution.py:280
  7.5 11.9 %collective-permute-start.3 = (bf16[128,256]{1,0:T(8,128)(2,1)}, bf16[128,256]{1,0:T(8,128)(2,1)S(1)}, u32[]{:S(2)}, u32[]{:S(2)}) collective-permute-start(bf16[128,256]{1,0:T(8,128)(2,1)} %param.4), channel_id=1, source_target_pairs={{0,6},{2,0},{4,2},{6,4},{1,7},{3,1},{5,3},{7,5},{8,14},{10,8},{12,... | collective-permute-start | bytes 196616 | tf_op jit(solution)/shard_map/ppermute | solution.py:253
  9.6 9.7 %collective-permute-start.2 = (bf16[128,256]{1,0:T(8,128)(2,1)}, bf16[128,256]{1,0:T(8,128)(2,1)S(1)}, u32[]{:S(2)}, u32[]{:S(2)}) collective-permute-start(bf16[128,256]{1,0:T(8,128)(2,1)} %param.4), channel_id=1, source_target_pairs={{0,4},{2,6},{4,0},{6,2},{1,5},{3,7},{5,1},{7,3},{8,12},{10,14},{12... | collective-permute-start | bytes 196616 | tf_op jit(solution)/shard_map/ppermute | solution.py:253
  14.1 5.3 %collective-permute-start.4 = (bf16[128,256]{1,0:T(8,128)(2,1)}, bf16[128,256]{1,0:T(8,128)(2,1)S(1)}, u32[]{:S(2)}, u32[]{:S(2)}) collective-permute-start(bf16[128,256]{1,0:T(8,128)(2,1)} %param.5), channel_id=1, source_target_pairs={{0,64},{64,128},{128,192},{192,0},{1,65},{65,129},{129,193},{193,1... | collective-permute-start | bytes 196616 | tf_op jit(solution)/shard_map/ppermute | solution.py:253
  15.4 4.0 %collective-permute-start.6 = (bf16[128,256]{1,0:T(8,128)(2,1)}, bf16[128,256]{1,0:T(8,128)(2,1)S(1)}, u32[]{:S(2)}, u32[]{:S(2)}) collective-permute-start(bf16[128,256]{1,0:T(8,128)(2,1)} %param.5), channel_id=1, source_target_pairs={{0,192},{64,0},{128,64},{192,128},{1,193},{65,1},{129,65},{193,129... | collective-permute-start | bytes 196616 | tf_op jit(solution)/shard_map/ppermute | solution.py:253
  16.8 5.1 %collective-permute-start.5 = (bf16[128,256]{1,0:T(8,128)(2,1)}, bf16[128,256]{1,0:T(8,128)(2,1)S(1)}, u32[]{:S(2)}, u32[]{:S(2)}) collective-permute-start(bf16[128,256]{1,0:T(8,128)(2,1)} %param.5), channel_id=1, source_target_pairs={{0,128},{64,192},{128,0},{192,64},{1,129},{65,193},{129,1},{193,65... | collective-permute-start | bytes 196616 | tf_op jit(solution)/shard_map/ppermute | solution.py:253
  22.0 5.3 %collective-permute-start.10 = (bf16[4,128,256]{2,1,0:T(8,128)(2,1)S(1)}, bf16[4,128,256]{2,1,0:T(8,128)(2,1)S(1)}, u32[]{:S(2)}, u32[]{:S(2)}) collective-permute-start(bf16[4,128,256]{2,1,0:T(8,128)(2,1)S(1)} %get-tuple-element.17.block), channel_id=1, source_target_pairs={{0,1},{1,0},{2,3},{3,2},{4,5},{5,4},{6,7},{7,6},{8,9},{9,8},{10,11... | collective-permute-start | bytes 786440 | tf_op jit(solution)/shard_map/ppermute | solution.py:253
  22.8 12.1 %collective-permute-start.9 = (bf16[4,128,256]{2,1,0:T(8,128)(2,1)S(1)}, bf16[4,128,256]{2,1,0:T(8,128)(2,1)S(1)}, u32[]{:S(2)}, u32[]{:S(2)}) collective-permute-start(bf16[4,128,256]{2,1,0:T(8,128)(2,1)S(1)} %get-tuple-element.16.refs_0_), channel_id=1, source_target_pairs={{0,24},{8,0},{16,8},{24,16},{1,25},{9,1},{17,9},{25,17},{2,26},{10... | collective-permute-start | bytes 786440 | tf_op jit(solution)/shard_map/ppermute | solution.py:253
  25.3 9.6 %collective-permute-start.8 = (bf16[4,128,256]{2,1,0:T(8,128)(2,1)S(1)}, bf16[4,128,256]{2,1,0:T(8,128)(2,1)S(1)}, u32[]{:S(2)}, u32[]{:S(2)}) collective-permute-start(bf16[4,128,256]{2,1,0:T(8,128)(2,1)S(1)} %get-tuple-element.16.refs_0_), channel_id=1, source_target_pairs={{0,16},{8,24},{16,0},{24,8},{1,17},{9,25},{17,1},{25,9},{2,18},{10... | collective-permute-start | bytes 786440 | tf_op jit(solution)/shard_map/ppermute | solution.py:253
  25.8 13.2 %collective-permute-start.7 = (bf16[4,128,256]{2,1,0:T(8,128)(2,1)S(1)}, bf16[4,128,256]{2,1,0:T(8,128)(2,1)S(1)}, u32[]{:S(2)}, u32[]{:S(2)}) collective-permute-start(bf16[4,128,256]{2,1,0:T(8,128)(2,1)S(1)} %get-tuple-element.16.refs_0_), channel_id=1, source_target_pairs={{0,8},{8,16},{16,24},{24,0},{1,9},{9,17},{17,25},{25,1},{2,10},{10... | collective-permute-start | bytes 786440 | tf_op jit(solution)/shard_map/ppermute | solution.py:253
  27.4 11.7 %collective-permute-start.11 = (bf16[4,128,256]{2,1,0:T(8,128)(2,1)S(1)}, bf16[4,128,256]{2,1,0:T(8,128)(2,1)S(1)}, u32[]{:S(2)}, u32[]{:S(2)}) collective-permute-start(bf16[4,128,256]{2,1,0:T(8,128)(2,1)S(1)} %shard_map.61.refs_4_), channel_id=1, source_target_pairs={{0,32},{32,0},{1,33},{33,1},{2,34},{34,2},{3,35},{35,3},{4,36},{36... | collective-permute-start | bytes 786440 | tf_op jit(solution)/shard_map/ppermute | solution.py:253
  31.7 7.4 %collective-permute-start.12 = (bf16[4,128,256]{2,1,0:T(8,128)(2,1)S(1)}, bf16[4,128,256]{2,1,0:T(8,128)(2,1)S(1)}, u32[]{:S(2)}, u32[]{:S(2)}) collective-permute-start(bf16[4,128,256]{2,1,0:T(8,128)(2,1)S(1)} %collective-permute-done.10.first.refs_6_), channel_id=1, source_target_pairs={{0,32},{32,0},{1,33},{33,1},{2,34},{34,2},{3,35},{35,3},{4,36},{36... | collective-permute-start | bytes 786440 | tf_op jit(solution)/shard_map/ppermute | solution.py:253
  91.1 12.4 %all-to-all-start.3 = ((f32[16,8,128]{2,1,0:T(8,128)}), f32[16,8,128]{2,1,0:T(8,128)S(1)}, u32[]{:S(2)}, u32[]{:S(2)}) async-start(f32[16,8,128]{2,1,0:T(8,128)} %get-tuple-element.25), calls=%async_computation.3 | async-start | bytes 131072 | tf_op jit(solution)/shard_map/all_to_all | solution.py:248
  97.7 3.1 %collective-permute-start.13 = (f32[16,128]{1,0:T(8,128)S(1)}, f32[16,128]{1,0:T(8,128)S(1)}, u32[]{:S(2)}, u32[]{:S(2)}) collective-permute-start(f32[16,128]{1,0:T(8,128)S(1)} %get-tuple-element.27.mine), channel_id=1, source_target_pairs={{0,1},{1,0},{2,3},{3,2},{4,5},{5,4},{6,7},{7,6},{8,9},{9,8},{10,11... | collective-permute-start | bytes 24584 | tf_op jit(solution)/shard_map/ppermute | solution.py:280

commit v13 on v12

--- a/solution.py
+++ b/solution.py
@@ -135,19 +135,20 @@
     src, tgt = refs[-2:]
     sides = src.shape[0]
     src[0] = own[0]
-    tgt[0] = own[1]
+    tgt[0:TILE] = own[1]
     for n in range(1, sides):
         src[n] = refs[n - 1][...]
-        tgt[n] = refs[sides - 1 + n - 1][...]
-
-
-def after_kernel(first, block, out):
-    out[...] = block[...]
-
-
-def square_kernel(src, sq_src):
-    for a in range(src.shape[0]):
-        sq_src[a : a + 1, :] = square_rows(src[a])
+        tgt[n * TILE : (n + 1) * TILE] = refs[sides - 1 + n - 1][...]
+    rows = lists[...].astype(F32).astype(tgt.dtype)
+    tgt[sides * TILE :, 0:TILE] = rows
+    tgt[sides * TILE :, TILE:] = jnp.zeros_like(rows)
+
+
+def after_kernel(theirs, ours, mine, partner, lists):
+    for n in range(mine.shape[0]):
+        mine[n] = ours[n * TILE : (n + 1) * TILE]
+        partner[n] = theirs[n * TILE : (n + 1) * TILE]
+    lists[...] = theirs[mine.shape[0] * TILE :, 0:TILE].astype(F32).astype(jnp.int32)
 
 
 def first_kernel(picked, *refs):
@@ -258,19 +259,24 @@
     own = jnp.stack([src_embed, tgt_embed])
     far = shifts(src_embed, "s")[1:] + shifts(tgt_embed, "y")[1:]
     group = jax.ShapeDtypeStruct((lax.axis_size("s"),) + src_embed.shape, src_embed.dtype)
+    rows, width = group.shape[0] * TILE + lists.shape[0], src_embed.shape[1]
     src, tgt = pl.pallas_call(
         pack_kernel,
-        out_shape=[group] * 2,
-        in_specs=[ANY] + [VMEM] * (1 + len(far)),
+        out_shape=[group, jax.ShapeDtypeStruct((rows, width), tgt_embed.dtype)],
+        in_specs=[VMEM] * (2 + len(far)),
         out_specs=[VMEM] * 2,
         compiler_params=PARAMS,
     )(lists, own, *far)
     src_pieces = shifts(src, "x")
-    mine, partner = shifts(tgt, "p")
-    mine = pl.pallas_call(
-        after_kernel, out_shape=group, in_specs=[ANY, VMEM], out_specs=VMEM, compiler_params=PARAMS
-    )(partner, mine)
-    return src_pieces, [piece for side in (mine, partner) for piece in shifts(side, "core")]
+    ours, theirs = shifts(tgt, "p")
+    mine, partner, other_lists = pl.pallas_call(
+        after_kernel,
+        out_shape=[group, group, jax.ShapeDtypeStruct(lists.shape, lists.dtype)],
+        in_specs=[VMEM] * 2,
+        out_specs=[VMEM] * 3,
+        compiler_params=PARAMS,
+    )(theirs, ours)
+    return src_pieces, [piece for side in (mine, partner) for piece in shifts(side, "core")], other_lists
 
 
 def local(src_embed, tgt_embed, tiles, counts):
@@ -279,10 +285,9 @@
     parity = lax.axis_index("p").astype(jnp.int32).reshape(1)
     partner = lambda v: lax.ppermute(v, "p", [(0, 1), (1, 0)])
 
-    lists = jnp.concatenate([tiles[0, 0], jnp.broadcast_to(counts[0, 0], (1, TILE))], axis=0)
-    other_lists = partner(lists)
+    lists = jnp.concatenate([tiles[0, 0], jnp.broadcast_to(counts[0, 0], (14, TILE))], axis=0)
     place = jnp.stack([lax.axis_index(a) for a in ("x", "s", "y", "p", "core")]).astype(jnp.int32)
-    src_pieces, tgt_pieces = bands(src_embed, tgt_embed, other_lists)
+    src_pieces, tgt_pieces, other_lists = bands(src_embed, tgt_embed, lists)
     picked = pl.pallas_call(
         pick_kernel,
         out_shape=jax.ShapeDtypeStruct((8, TILE), jnp.int32),

time: 103 us -> 102 us (level); the launches traced: 104 us -> 101 us
  starting transfers between devices: 33.4 us -> 31.6 us
    ppermute x2 -> x1, starting transfers between devices: 3.03 us -> 1.43 us  [local(): partner = lambda v: lax.ppermute(v, 'p', [(0, 1), (1, 0)])]
    all_to_all x1, starting transfers between devices: 6.59 us -> 5.47 us  [exchange(): return lax.all_to_all(copies, peers, 0, 0, tiled=True)]
  transfers between devices with their start and end apart: 15 -> 14, of which waited for: 5 -> 5; matrix products, arithmetic and copies ran while one was open for 2% -> 2% of each run, Pallas kernels for 3% -> 3%
where the time goes in v13:
time: 102 us; the launch traced here: 101 us
  blocking collectives  42.3 us (41%)
  starting transfers between devices  31.6 us (31%)
  Pallas kernels  12.6 us (12%)
  waiting for transfers between devices  11.4 us (11%)
  between operations  1.39 us (1%)
    all_to_all x3, blocking collectives, exchange(): return lax.all_to_all(copies, peers, 0, 0, tiled=True)  42.3 us
    ppermute x12, starting transfers between devices, shifts(): lax.ppermute(block, axis, [(i, (i + d) % n) for i in range(n)])  24.7 us
    pallas_call x4, Pallas kernels, half_step(): pl.pallas_call(kernel, out_shape=[s if isinstance(s, jax.ShapeDtypeStruct...  8.64 us
    ppermute x12, waiting for transfers between devices, shifts(): lax.ppermute(block, axis, [(i, (i + d) % n) for i in range(n)])  6.99 us
    all_to_all x1, starting transfers between devices, exchange(): return lax.all_to_all(copies, peers, 0, 0, tiled=True)  5.47 us
    pallas_call x1, Pallas kernels, local(): pl.pallas_call(pick_kernel, out_shape=jax.ShapeDtypeStruct((8, TILE), jnp...  3.23 us
    all_to_all x1, waiting for transfers between devices, exchange(): return lax.all_to_all(copies, peers, 0, 0, tiled=True)  2.79 us
  transfers between devices with their start and end apart: 14, of which 5 were waited for; matrix products, arithmetic and copies ran while one was open for 2% of the time, Pallas kernels for 3%

profile of v13, /device:TPU:1, one launch (start us, length us, event | category | flops | bytes accessed | tf_op | source)
XLA Modules:
  0.0 100.9 jit_solution(16849423378183437046)
XLA Ops:
  0.6 3.9 %collective-permute-start = (bf16[128,256]{1,0:T(8,128)(2,1)}, bf16[128,256]{1,0:T(8,128)(2,1)S(1)}, u32[]{:S(2)}, u32[]{:S(2)}) collective-permute-start(bf16[128,256]{1,0:T(8,128)(2,1)} %param.4), channel_id=1, source_target_pairs={{0,2},{2,4},{4,6},{6,0},{1,3},{3,5},{5,7},{7,1},{8,10},{10,12},{12... | collective-permute-start | bytes 196616 | tf_op jit(solution)/shard_map/ppermute | solution.py:254
  4.5 3.1 %collective-permute-start.2 = (bf16[128,256]{1,0:T(8,128)(2,1)}, bf16[128,256]{1,0:T(8,128)(2,1)S(1)}, u32[]{:S(2)}, u32[]{:S(2)}) collective-permute-start(bf16[128,256]{1,0:T(8,128)(2,1)} %param.4), channel_id=1, source_target_pairs={{0,6},{2,0},{4,2},{6,4},{1,7},{3,1},{5,3},{7,5},{8,14},{10,8},{12,... | collective-permute-start | bytes 196616 | tf_op jit(solution)/shard_map/ppermute | solution.py:254
  7.6 4.4 %collective-permute-start.1 = (bf16[128,256]{1,0:T(8,128)(2,1)}, bf16[128,256]{1,0:T(8,128)(2,1)S(1)}, u32[]{:S(2)}, u32[]{:S(2)}) collective-permute-start(bf16[128,256]{1,0:T(8,128)(2,1)} %param.4), channel_id=1, source_target_pairs={{0,4},{2,6},{4,0},{6,2},{1,5},{3,7},{5,1},{7,3},{8,12},{10,14},{12... | collective-permute-start | bytes 196616 | tf_op jit(solution)/shard_map/ppermute | solution.py:254
  12.0 1.3 %collective-permute-start.3 = (bf16[128,256]{1,0:T(8,128)(2,1)}, bf16[128,256]{1,0:T(8,128)(2,1)S(1)}, u32[]{:S(2)}, u32[]{:S(2)}) collective-permute-start(bf16[128,256]{1,0:T(8,128)(2,1)} %param.5), channel_id=1, source_target_pairs={{0,64},{64,128},{128,192},{192,0},{1,65},{65,129},{129,193},{193,1... | collective-permute-start | bytes 196616 | tf_op jit(solution)/shard_map/ppermute | solution.py:254
  13.3 1.4 %collective-permute-start.5 = (bf16[128,256]{1,0:T(8,128)(2,1)}, bf16[128,256]{1,0:T(8,128)(2,1)S(1)}, u32[]{:S(2)}, u32[]{:S(2)}) collective-permute-start(bf16[128,256]{1,0:T(8,128)(2,1)} %param.5), channel_id=1, source_target_pairs={{0,192},{64,0},{128,64},{192,128},{1,193},{65,1},{129,65},{193,129... | collective-permute-start | bytes 196616 | tf_op jit(solution)/shard_map/ppermute | solution.py:254
  15.4 0.7 concatenate.3.lists.mine
  16.1 0.0 collective-permute-done.refs_0_
  16.1 1.6 %collective-permute-start.4 = (bf16[128,256]{1,0:T(8,128)(2,1)}, bf16[128,256]{1,0:T(8,128)(2,1)S(1)}, u32[]{:S(2)}, u32[]{:S(2)}) collective-permute-start(bf16[128,256]{1,0:T(8,128)(2,1)} %param.5), channel_id=1, source_target_pairs={{0,128},{64,192},{128,0},{192,64},{1,129},{65,193},{129,1},{193,65... | collective-permute-start | bytes 196616 | tf_op jit(solution)/shard_map/ppermute | solution.py:254
  17.7 0.9 pad_maximum_fusion.own
  18.6 0.0 collective-permute-done.2.refs_2_
  18.6 0.0 collective-permute-done.1.refs_1_
  18.7 0.0 collective-permute-done.3.refs_3_
  18.7 0.0 collective-permute-done.5.refs_5_
  18.7 2.3 %collective-permute-done.4.refs_4_ = bf16[128,256]{1,0:T(8,128)(2,1)S(1)} collective-permute-done((bf16[128,256]{1,0:T(8,128)(2,1)}, bf16[128,256]{1,0:T(8,128)(2,1)S(1)}, u32[]{:S(2)}, u32[]{:S(2)}) %collective-permute-start.4) | collective-permute-done | bytes 65568 | tf_op jit(solution)/shard_map/ppermute | solution.py:254
  21.0 0.8 collective-permute-start.6
  21.8 2.5 %collective-permute-start.9 = (bf16[4,128,256]{2,1,0:T(8,128)(2,1)S(1)}, bf16[4,128,256]{2,1,0:T(8,128)(2,1)S(1)}, u32[]{:S(2)}, u32[]{:S(2)}) collective-permute-start(bf16[4,128,256]{2,1,0:T(8,128)(2,1)S(1)} %get-tuple-element.21.refs_0_), channel_id=1, source_target_pairs={{0,24},{8,0},{16,8},{24,16},{1,25},{9,1},{17,9},{25,17},{2,26},{10... | collective-permute-start | bytes 786440 | tf_op jit(solution)/shard_map/ppermute | solution.py:254
  24.3 0.5 collective-permute-start.8
  24.8 0.6 collective-permute-start.7
  25.4 1.0 collective-permute-done.6.theirs
  26.4 4.4 %collective-permute-start.10 = (bf16[4,128,256]{2,1,0:T(8,128)(2,1)S(1)}, bf16[4,128,256]{2,1,0:T(8,128)(2,1)S(1)}, u32[]{:S(2)}, u32[]{:S(2)}) collective-permute-start(bf16[4,128,256]{2,1,0:T(8,128)(2,1)S(1)} %get-tuple-element.22.refs_4_), channel_id=1, source_target_pairs={{0,32},{32,0},{1,33},{33,1},{2,34},{34,2},{3,35},{35,3},{4,36},{36... | collective-permute-start | bytes 786440 | tf_op jit(solution)/shard_map/ppermute | solution.py:254
  30.8 0.1 collective-permute-start.11
  30.9 0.1 stack.32.place
  31.0 3.2 %shard_map.61.picked = s32[8,128]{1,0:T(8,128)S(1)} custom-call(s32[16,128]{1,0:T(8,128)S(1)} %concatenate.3.lists.mine, s32[16,128]{1,0:T(8,128)S(1)} %get-tuple-element.20.other, s32[5]{0:T(128)S(1)} %stack.32.place), custom_call_target="tpu_custom_call" | custom-call | tf_op jit(solution)/shard_map/pallas_call | solution.py:291
  34.2 0.0 collective-permute-done.9.refs_3_
  34.2 0.0 collective-permute-done.8.refs_2_
  34.3 3.7 %collective-permute-done.7.refs_1_ = bf16[4,128,256]{2,1,0:T(8,128)(2,1)S(1)} collective-permute-done((bf16[4,128,256]{2,1,0:T(8,128)(2,1)S(1)}, bf16[4,128,256]{2,1,0:T(8,128)(2,1)S(1)}, u32[]{:S(2)}, u32[]{:S(2)}) %collective-permute-start.7) | collective-permute-done | bytes 262176 | tf_op jit(solution)/shard_map/ppermute | solution.py:254
  38.0 0.0 collective-permute-done.10.refs_5_
  38.0 0.0 collective-permute-done.11.refs_7_
  38.0 3.2 %shard_map.62 = (f32[16,16,128]{2,1,0:T(8,128)S(1)}, bf16[16,128,256]{2,1,0:T(8,128)(2,1)S(1)}, bf16[16,128,256]{2,1,0:T(8,128)(2,1)S(1)}, f32[16,128]{1,0:T(8,1...) custom-call(s32[8,128]{1,0:T(8,128)S(1)} %shard_map.61.picked, ...), custom_call_target="tpu_custom_call" | custom-call | tf_op jit(solution)/shard_map/pallas_call | solution.py:232
  41.2 12.8 %all_to_all.20.parts = f32[16,16,128]{2,1,0:T(8,128)S(1)} all-to-all(f32[16,16,128]{2,1,0:T(8,128)S(1)} %get-tuple-element.26), channel_id=1, replica_groups=mesh['y'=4,'core'=2,'x'=4,'s'=4,'p'=2] {'x','s'}, dimensions={0} | all-to-all | bytes 262144 | tf_op jit(solution)/shard_map/all_to_all | solution.py:249
  54.0 2.0 %shard_map.63 = (f32[16,16,128]{2,1,0:T(8,128)S(1)}, f32[256,128,128]{2,1,0:T(8,128)S(1)}) custom-call(s32[8,128]{1,0:T(8,128)S(1)} %shard_map.61.picked, bf16[16,128,256]{2,1,0:T(8,128)(2,1)S(1)} %get-tuple-element.24.src, bf16[16,128,256]{2,1,0:T(8,128)(2,1)S(1)} %get-tuple-element.25.tgt, f32[16,16,128]{2,1,0:T(8,128)S(1)} %all_to_all.20.parts), custom_call_target="tpu_custom_call" | custom-call | tf_op jit(solution)/shard_map/pallas_call | solution.py:232
  56.0 14.2 %all_to_all.21.parts = f32[16,16,128]{2,1,0:T(8,128)S(1)} all-to-all(f32[16,16,128]{2,1,0:T(8,128)S(1)} %get-tuple-element.29), channel_id=1, replica_groups=mesh['y'=4,'core'=2,'x'=4,'s'=4,'p'=2] {'p','y','core'}, dimensions={0} | all-to-all | bytes 262144 | tf_op jit(solution)/shard_map/all_to_all | solution.py:249
  70.2 1.4 %shard_map.64 = f32[16,16,128]{2,1,0:T(8,128)S(1)} custom-call(s32[8,128]{1,0:T(8,128)S(1)} %shard_map.61.picked, f32[256,128,128]{2,1,0:T(8,128)S(1)} %get-tuple-element.28.saved, f32[16,16,128]{2,1,0:T(8,128)S(1)} %all_to_all.21.parts), custom_call_target="tpu_custom_call" | custom-call | tf_op jit(solution)/shard_map/pallas_call | solution.py:232
  71.6 15.3 %all_to_all.22.parts = f32[16,16,128]{2,1,0:T(8,128)S(1)} all-to-all(f32[16,16,128]{2,1,0:T(8,128)S(1)} %shard_map.64), channel_id=1, replica_groups=mesh['y'=4,'core'=2,'x'=4,'s'=4,'p'=2] {'x','s'}, dimensions={0} | all-to-all | bytes 262144 | tf_op jit(solution)/shard_map/all_to_all | solution.py:249
  86.9 2.0 %shard_map.65 = (f32[16,8,128]{2,1,0:T(8,128)}, f32[16,128]{1,0:T(8,128)S(1)}) custom-call(s32[8,128]{1,0:T(8,128)S(1)} %shard_map.61.picked, f32[256,128,128]{2,1,0:T(8,128)S(1)} %get-tuple-element.27.saved, f32[16,16,128]{2,1,0:T(8,128)S(1)} %all_to_all.22.parts, f32[16,128]{1,0:T(8,128)S(1)} %get-tuple-element.30.sq_src), custom_call_target="tpu_custom_call" | custom-call | tf_op jit(solution)/shard_map/pallas_call | solution.py:232
  88.9 5.5 %all-to-all-start.3 = ((f32[16,8,128]{2,1,0:T(8,128)}), f32[16,8,128]{2,1,0:T(8,128)S(1)}, u32[]{:S(2)}, u32[]{:S(2)}) async-start(f32[16,8,128]{2,1,0:T(8,128)} %get-tuple-element.31), calls=%async_computation.3 | async-start | bytes 131072 | tf_op jit(solution)/shard_map/all_to_all | solution.py:249
  94.4 1.4 %collective-permute-start.12 = (f32[16,128]{1,0:T(8,128)S(1)}, f32[16,128]{1,0:T(8,128)S(1)}, u32[]{:S(2)}, u32[]{:S(2)}) collective-permute-start(f32[16,128]{1,0:T(8,128)S(1)} %get-tuple-element.33.mine), channel_id=1, source_target_pairs={{0,1},{1,0},{2,3},{3,2},{4,5},{5,4},{6,7},{7,6},{8,9},{9,8},{10,11... | collective-permute-start | bytes 24584 | tf_op jit(solution)/shard_map/ppermute | solution.py:286
  95.8 1.7 %collective-permute-done.12.other = f32[16,128]{1,0:T(8,128)S(1)} collective-permute-done((f32[16,128]{1,0:T(8,128)S(1)}, f32[16,128]{1,0:T(8,128)S(1)}, u32[]{:S(2)}, u32[]{:S(2)}) %collective-permute-start.12) | collective-permute-done | bytes 8224 | tf_op jit(solution)/shard_map/ppermute | solution.py:286
  97.5 2.8 %all-to-all-done.3.parts = f32[16,8,128]{2,1,0:T(8,128)S(1)} async-done(((f32[16,8,128]{2,1,0:T(8,128)}), f32[16,8,128]{2,1,0:T(8,128)S(1)}, u32[]{:S(2)}, u32[]{:S(2)}) %all-to-all-start.3) | async-done | bytes 65568 | tf_op jit(solution)/shard_map/all_to_all | solution.py:249
  100.3 0.6 shard_map.66
  (2 shorter events, 0.1 us)
Async XLA Ops:
  0.6 15.5 %collective-permute-start = (bf16[128,256]{1,0:T(8,128)(2,1)}, bf16[128,256]{1,0:T(8,128)(2,1)S(1)}, u32[]{:S(2)}, u32[]{:S(2)}) collective-permute-start(bf16[128,256]{1,0:T(8,128)(2,1)} %param.4), channel_id=1, source_target_pairs={{0,2},{2,4},{4,6},{6,0},{1,3},{3,5},{5,7},{7,1},{8,10},{10,12},{12... | collective-permute-start | bytes 196616 | tf_op jit(solution)/shard_map/ppermute | solution.py:254
  4.5 14.1 %collective-permute-start.2 = (bf16[128,256]{1,0:T(8,128)(2,1)}, bf16[128,256]{1,0:T(8,128)(2,1)S(1)}, u32[]{:S(2)}, u32[]{:S(2)}) collective-permute-start(bf16[128,256]{1,0:T(8,128)(2,1)} %param.4), channel_id=1, source_target_pairs={{0,6},{2,0},{4,2},{6,4},{1,7},{3,1},{5,3},{7,5},{8,14},{10,8},{12,... | collective-permute-start | bytes 196616 | tf_op jit(solution)/shard_map/ppermute | solution.py:254
  7.6 11.0 %collective-permute-start.1 = (bf16[128,256]{1,0:T(8,128)(2,1)}, bf16[128,256]{1,0:T(8,128)(2,1)S(1)}, u32[]{:S(2)}, u32[]{:S(2)}) collective-permute-start(bf16[128,256]{1,0:T(8,128)(2,1)} %param.4), channel_id=1, source_target_pairs={{0,4},{2,6},{4,0},{6,2},{1,5},{3,7},{5,1},{7,3},{8,12},{10,14},{12... | collective-permute-start | bytes 196616 | tf_op jit(solution)/shard_map/ppermute | solution.py:254
  12.0 6.6 %collective-permute-start.3 = (bf16[128,256]{1,0:T(8,128)(2,1)}, bf16[128,256]{1,0:T(8,128)(2,1)S(1)}, u32[]{:S(2)}, u32[]{:S(2)}) collective-permute-start(bf16[128,256]{1,0:T(8,128)(2,1)} %param.5), channel_id=1, source_target_pairs={{0,64},{64,128},{128,192},{192,0},{1,65},{65,129},{129,193},{193,1... | collective-permute-start | bytes 196616 | tf_op jit(solution)/shard_map/ppermute | solution.py:254
  13.3 5.3 %collective-permute-start.5 = (bf16[128,256]{1,0:T(8,128)(2,1)}, bf16[128,256]{1,0:T(8,128)(2,1)S(1)}, u32[]{:S(2)}, u32[]{:S(2)}) collective-permute-start(bf16[128,256]{1,0:T(8,128)(2,1)} %param.5), channel_id=1, source_target_pairs={{0,192},{64,0},{128,64},{192,128},{1,193},{65,1},{129,65},{193,129... | collective-permute-start | bytes 196616 | tf_op jit(solution)/shard_map/ppermute | solution.py:254
  16.1 4.8 %collective-permute-start.4 = (bf16[128,256]{1,0:T(8,128)(2,1)}, bf16[128,256]{1,0:T(8,128)(2,1)S(1)}, u32[]{:S(2)}, u32[]{:S(2)}) collective-permute-start(bf16[128,256]{1,0:T(8,128)(2,1)} %param.5), channel_id=1, source_target_pairs={{0,128},{64,192},{128,0},{192,64},{1,129},{65,193},{129,1},{193,65... | collective-permute-start | bytes 196616 | tf_op jit(solution)/shard_map/ppermute | solution.py:254
  21.0 5.4 %collective-permute-start.6 = (bf16[528,256]{1,0:T(8,128)(2,1)S(1)}, bf16[528,256]{1,0:T(8,128)(2,1)S(1)}, u32[]{:S(2)}, u32[]{:S(2)}) collective-permute-start(bf16[528,256]{1,0:T(8,128)(2,1)S(1)} %get-tuple-element.19.ours), channel_id=1, source_target_pairs={{0,1},{1,0},{2,3},{3,2},{4,5},{5,4},{6,7},{7,6},{8,9},{9,8},{10,11... | collective-permute-start | bytes 811016 | tf_op jit(solution)/shard_map/ppermute | solution.py:254
  21.8 12.4 %collective-permute-start.9 = (bf16[4,128,256]{2,1,0:T(8,128)(2,1)S(1)}, bf16[4,128,256]{2,1,0:T(8,128)(2,1)S(1)}, u32[]{:S(2)}, u32[]{:S(2)}) collective-permute-start(bf16[4,128,256]{2,1,0:T(8,128)(2,1)S(1)} %get-tuple-element.21.refs_0_), channel_id=1, source_target_pairs={{0,24},{8,0},{16,8},{24,16},{1,25},{9,1},{17,9},{25,17},{2,26},{10... | collective-permute-start | bytes 786440 | tf_op jit(solution)/shard_map/ppermute | solution.py:254
  24.3 10.0 %collective-permute-start.8 = (bf16[4,128,256]{2,1,0:T(8,128)(2,1)S(1)}, bf16[4,128,256]{2,1,0:T(8,128)(2,1)S(1)}, u32[]{:S(2)}, u32[]{:S(2)}) collective-permute-start(bf16[4,128,256]{2,1,0:T(8,128)(2,1)S(1)} %get-tuple-element.21.refs_0_), channel_id=1, source_target_pairs={{0,16},{8,24},{16,0},{24,8},{1,17},{9,25},{17,1},{25,9},{2,18},{10... | collective-permute-start | bytes 786440 | tf_op jit(solution)/shard_map/ppermute | solution.py:254
  24.8 13.2 %collective-permute-start.7 = (bf16[4,128,256]{2,1,0:T(8,128)(2,1)S(1)}, bf16[4,128,256]{2,1,0:T(8,128)(2,1)S(1)}, u32[]{:S(2)}, u32[]{:S(2)}) collective-permute-start(bf16[4,128,256]{2,1,0:T(8,128)(2,1)S(1)} %get-tuple-element.21.refs_0_), channel_id=1, source_target_pairs={{0,8},{8,16},{16,24},{24,0},{1,9},{9,17},{17,25},{25,1},{2,10},{10... | collective-permute-start | bytes 786440 | tf_op jit(solution)/shard_map/ppermute | solution.py:254
  26.4 11.6 %collective-permute-start.10 = (bf16[4,128,256]{2,1,0:T(8,128)(2,1)S(1)}, bf16[4,128,256]{2,1,0:T(8,128)(2,1)S(1)}, u32[]{:S(2)}, u32[]{:S(2)}) collective-permute-start(bf16[4,128,256]{2,1,0:T(8,128)(2,1)S(1)} %get-tuple-element.22.refs_4_), channel_id=1, source_target_pairs={{0,32},{32,0},{1,33},{33,1},{2,34},{34,2},{3,35},{35,3},{4,36},{36... | collective-permute-start | bytes 786440 | tf_op jit(solution)/shard_map/ppermute | solution.py:254
  30.8 7.2 %collective-permute-start.11 = (bf16[4,128,256]{2,1,0:T(8,128)(2,1)S(1)}, bf16[4,128,256]{2,1,0:T(8,128)(2,1)S(1)}, u32[]{:S(2)}, u32[]{:S(2)}) collective-permute-start(bf16[4,128,256]{2,1,0:T(8,128)(2,1)S(1)} %get-tuple-element.23.refs_6_), channel_id=1, source_target_pairs={{0,32},{32,0},{1,33},{33,1},{2,34},{34,2},{3,35},{35,3},{4,36},{36... | collective-permute-start | bytes 786440 | tf_op jit(solution)/shard_map/ppermute | solution.py:254
  88.9 11.4 %all-to-all-start.3 = ((f32[16,8,128]{2,1,0:T(8,128)}), f32[16,8,128]{2,1,0:T(8,128)S(1)}, u32[]{:S(2)}, u32[]{:S(2)}) async-start(f32[16,8,128]{2,1,0:T(8,128)} %get-tuple-element.31), calls=%async_computation.3 | async-start | bytes 131072 | tf_op jit(solution)/shard_map/all_to_all | solution.py:249
  94.4 3.1 %collective-permute-start.12 = (f32[16,128]{1,0:T(8,128)S(1)}, f32[16,128]{1,0:T(8,128)S(1)}, u32[]{:S(2)}, u32[]{:S(2)}) collective-permute-start(f32[16,128]{1,0:T(8,128)S(1)} %get-tuple-element.33.mine), channel_id=1, source_target_pairs={{0,1},{1,0},{2,3},{3,2},{4,5},{5,4},{6,7},{7,6},{8,9},{9,8},{10,11... | collective-permute-start | bytes 24584 | tf_op jit(solution)/shard_map/ppermute | solution.py:286

commit v14 on v13

--- a/solution.py
+++ b/solution.py
@@ -14,7 +14,8 @@
 ENTROPY = 0.05
 KAPPA = math.log2(math.e) / ENTROPY
 EMPTY = -1e30
-UNROLL = 16
+SUM_STEP = 16
+DOT_STEP = 32
 ROW = ("y", "core")
 COL = ("x", "s", "p")
 SRC_PEERS = ("x", "s")
@@ -59,16 +60,16 @@
     return tile
 
 
-def tile_sums(place_of, count, source, near_blocks, far_blocks, wide, peaks, totals):
+def tile_sums(place_of, count, source, near_blocks, far_blocks, wide, peaks, totals, group=SUM_STEP):
     spare = near_blocks * far_blocks
     peaks[...] = jnp.full(peaks.shape, EMPTY, F32)
     totals[...] = jnp.zeros(totals.shape, F32)
-    steps = (count + UNROLL - 1) // UNROLL
+    steps = (count + group - 1) // group
 
     @pl.loop(0, steps)
     def _(step):
-        for u in range(UNROLL):
-            k = step * UNROLL + u
+        for u in range(group):
+            k = step * group + u
             n, f = place_of(jnp.where(k < count, k, 0))
             score = (source(k, n, f) + wide[n]).reshape(TILE // 8, 8, TILE)
             peak = jnp.max(score, axis=0)
@@ -173,7 +174,7 @@
         sq_src[a : a + 1, :] = square_rows(src[a])
     expand(sq_tgt[...] * -KAPPA, wide)
     source = dot_tiles(tgt, src, saved)
-    sums = tile_sums(source_tiles(tiles, tgts), tiles[0, 1], source, tgts, srcs, wide, peaks, totals)
+    sums = tile_sums(source_tiles(tiles, tgts), tiles[0, 1], source, tgts, srcs, wide, peaks, totals, DOT_STEP)
     out[...] = jnp.broadcast_to(sums[None], out.shape)
 
 
@@ -184,7 +185,7 @@
     fetch.wait()
     srcs, tgts = src.shape[0], tgt.shape[0]
     source = dot_tiles(src, tgt, saved)
-    sums = tile_sums(target_tiles(tiles, tgts), tiles[0, 1], source, srcs, tgts, wide, peaks, totals)
+    sums = tile_sums(target_tiles(tiles, tgts), tiles[0, 1], source, srcs, tgts, wide, peaks, totals, DOT_STEP)
     out[...] = jnp.broadcast_to(sums[None], out.shape)
 
 

time: 102 us -> 100 us (0.980)
  blocking collectives: 42.3 us -> 39.7 us
  Pallas kernels: 12.6 us -> 14.8 us
    all_to_all x3, blocking collectives: 42.3 us -> 39.7 us  [exchange(): return lax.all_to_all(copies, peers, 0, 0, tiled=True)]
    pallas_call x4, Pallas kernels: 8.64 us -> 10.9 us  [half_step(): pl.pallas_call(kernel, out_shape=[s if isinstance(s, jax.ShapeDtypeStruct...]
where the time goes in v14:
time: 100 us; the launch traced here: 99.8 us
  blocking collectives  39.7 us (40%)
  starting transfers between devices  30.8 us (31%)
  Pallas kernels  14.8 us (15%)
  waiting for transfers between devices  11.4 us (11%)
  between operations  1.39 us (1%)
    all_to_all x3, blocking collectives, exchange(): return lax.all_to_all(copies, peers, 0, 0, tiled=True)  39.7 us
    ppermute x12, starting transfers between devices, shifts(): lax.ppermute(block, axis, [(i, (i + d) % n) for i in range(n)])  24.7 us
    pallas_call x4, Pallas kernels, half_step(): pl.pallas_call(kernel, out_shape=[s if isinstance(s, jax.ShapeDtypeStruct...  10.9 us
    ppermute x12, waiting for transfers between devices, shifts(): lax.ppermute(block, axis, [(i, (i + d) % n) for i in range(n)])  6.99 us
    all_to_all x1, starting transfers between devices, exchange(): return lax.all_to_all(copies, peers, 0, 0, tiled=True)  4.67 us
    pallas_call x1, Pallas kernels, local(): pl.pallas_call(pick_kernel, out_shape=jax.ShapeDtypeStruct((8, TILE), jnp...  3.23 us
    all_to_all x1, waiting for transfers between devices, exchange(): return lax.all_to_all(copies, peers, 0, 0, tiled=True)  2.77 us
  transfers between devices with their start and end apart: 14, of which 5 were waited for; matrix products, arithmetic and copies ran while one was open for 2% of the time, Pallas kernels for 3%

profile of v14, /device:TPU:1, one launch (start us, length us, event | category | flops | bytes accessed | tf_op | source)
XLA Modules:
  0.0 99.8 jit_solution(14938375081725238417)
XLA Ops:
  0.6 3.9 %collective-permute-start = (bf16[128,256]{1,0:T(8,128)(2,1)}, bf16[128,256]{1,0:T(8,128)(2,1)S(1)}, u32[]{:S(2)}, u32[]{:S(2)}) collective-permute-start(bf16[128,256]{1,0:T(8,128)(2,1)} %param.4), channel_id=1, source_target_pairs={{0,2},{2,4},{4,6},{6,0},{1,3},{3,5},{5,7},{7,1},{8,10},{10,12},{12... | collective-permute-start | bytes 196616 | tf_op jit(solution)/shard_map/ppermute | solution.py:255
  4.5 3.1 %collective-permute-start.2 = (bf16[128,256]{1,0:T(8,128)(2,1)}, bf16[128,256]{1,0:T(8,128)(2,1)S(1)}, u32[]{:S(2)}, u32[]{:S(2)}) collective-permute-start(bf16[128,256]{1,0:T(8,128)(2,1)} %param.4), channel_id=1, source_target_pairs={{0,6},{2,0},{4,2},{6,4},{1,7},{3,1},{5,3},{7,5},{8,14},{10,8},{12,... | collective-permute-start | bytes 196616 | tf_op jit(solution)/shard_map/ppermute | solution.py:255
  7.6 4.4 %collective-permute-start.1 = (bf16[128,256]{1,0:T(8,128)(2,1)}, bf16[128,256]{1,0:T(8,128)(2,1)S(1)}, u32[]{:S(2)}, u32[]{:S(2)}) collective-permute-start(bf16[128,256]{1,0:T(8,128)(2,1)} %param.4), channel_id=1, source_target_pairs={{0,4},{2,6},{4,0},{6,2},{1,5},{3,7},{5,1},{7,3},{8,12},{10,14},{12... | collective-permute-start | bytes 196616 | tf_op jit(solution)/shard_map/ppermute | solution.py:255
  12.0 1.3 %collective-permute-start.3 = (bf16[128,256]{1,0:T(8,128)(2,1)}, bf16[128,256]{1,0:T(8,128)(2,1)S(1)}, u32[]{:S(2)}, u32[]{:S(2)}) collective-permute-start(bf16[128,256]{1,0:T(8,128)(2,1)} %param.5), channel_id=1, source_target_pairs={{0,64},{64,128},{128,192},{192,0},{1,65},{65,129},{129,193},{193,1... | collective-permute-start | bytes 196616 | tf_op jit(solution)/shard_map/ppermute | solution.py:255
  13.3 1.4 %collective-permute-start.5 = (bf16[128,256]{1,0:T(8,128)(2,1)}, bf16[128,256]{1,0:T(8,128)(2,1)S(1)}, u32[]{:S(2)}, u32[]{:S(2)}) collective-permute-start(bf16[128,256]{1,0:T(8,128)(2,1)} %param.5), channel_id=1, source_target_pairs={{0,192},{64,0},{128,64},{192,128},{1,193},{65,1},{129,65},{193,129... | collective-permute-start | bytes 196616 | tf_op jit(solution)/shard_map/ppermute | solution.py:255
  15.4 0.7 concatenate.3.lists.mine
  16.1 0.0 collective-permute-done.refs_0_
  16.1 1.6 %collective-permute-start.4 = (bf16[128,256]{1,0:T(8,128)(2,1)}, bf16[128,256]{1,0:T(8,128)(2,1)S(1)}, u32[]{:S(2)}, u32[]{:S(2)}) collective-permute-start(bf16[128,256]{1,0:T(8,128)(2,1)} %param.5), channel_id=1, source_target_pairs={{0,128},{64,192},{128,0},{192,64},{1,129},{65,193},{129,1},{193,65... | collective-permute-start | bytes 196616 | tf_op jit(solution)/shard_map/ppermute | solution.py:255
  17.7 0.9 pad_maximum_fusion.own
  18.6 0.0 collective-permute-done.2.refs_2_
  18.6 0.0 collective-permute-done.1.refs_1_
  18.7 0.0 collective-permute-done.3.refs_3_
  18.7 0.0 collective-permute-done.5.refs_5_
  18.7 2.3 %collective-permute-done.4.refs_4_ = bf16[128,256]{1,0:T(8,128)(2,1)S(1)} collective-permute-done((bf16[128,256]{1,0:T(8,128)(2,1)}, bf16[128,256]{1,0:T(8,128)(2,1)S(1)}, u32[]{:S(2)}, u32[]{:S(2)}) %collective-permute-start.4) | collective-permute-done | bytes 65568 | tf_op jit(solution)/shard_map/ppermute | solution.py:255
  21.0 0.8 collective-permute-start.6
  21.8 2.5 %collective-permute-start.9 = (bf16[4,128,256]{2,1,0:T(8,128)(2,1)S(1)}, bf16[4,128,256]{2,1,0:T(8,128)(2,1)S(1)}, u32[]{:S(2)}, u32[]{:S(2)}) collective-permute-start(bf16[4,128,256]{2,1,0:T(8,128)(2,1)S(1)} %get-tuple-element.21.refs_0_), channel_id=1, source_target_pairs={{0,24},{8,0},{16,8},{24,16},{1,25},{9,1},{17,9},{25,17},{2,26},{10... | collective-permute-start | bytes 786440 | tf_op jit(solution)/shard_map/ppermute | solution.py:255
  24.3 0.5 collective-permute-start.8
  24.8 0.6 collective-permute-start.7
  25.4 1.0 collective-permute-done.6.theirs
  26.4 4.4 %collective-permute-start.10 = (bf16[4,128,256]{2,1,0:T(8,128)(2,1)S(1)}, bf16[4,128,256]{2,1,0:T(8,128)(2,1)S(1)}, u32[]{:S(2)}, u32[]{:S(2)}) collective-permute-start(bf16[4,128,256]{2,1,0:T(8,128)(2,1)S(1)} %get-tuple-element.22.refs_4_), channel_id=1, source_target_pairs={{0,32},{32,0},{1,33},{33,1},{2,34},{34,2},{3,35},{35,3},{4,36},{36... | collective-permute-start | bytes 786440 | tf_op jit(solution)/shard_map/ppermute | solution.py:255
  30.8 0.1 collective-permute-start.11
  30.9 0.1 stack.32.place
  31.0 3.2 %shard_map.61.picked = s32[8,128]{1,0:T(8,128)S(1)} custom-call(s32[16,128]{1,0:T(8,128)S(1)} %concatenate.3.lists.mine, s32[16,128]{1,0:T(8,128)S(1)} %get-tuple-element.20.other, s32[5]{0:T(128)S(1)} %stack.32.place), custom_call_target="tpu_custom_call" | custom-call | tf_op jit(solution)/shard_map/pallas_call | solution.py:292
  34.2 0.0 collective-permute-done.9.refs_3_
  34.2 0.0 collective-permute-done.8.refs_2_
  34.3 3.7 %collective-permute-done.7.refs_1_ = bf16[4,128,256]{2,1,0:T(8,128)(2,1)S(1)} collective-permute-done((bf16[4,128,256]{2,1,0:T(8,128)(2,1)S(1)}, bf16[4,128,256]{2,1,0:T(8,128)(2,1)S(1)}, u32[]{:S(2)}, u32[]{:S(2)}) %collective-permute-start.7) | collective-permute-done | bytes 262176 | tf_op jit(solution)/shard_map/ppermute | solution.py:255
  38.0 0.0 collective-permute-done.10.refs_5_
  38.0 0.0 collective-permute-done.11.refs_7_
  38.0 3.8 %shard_map.62 = (f32[16,16,128]{2,1,0:T(8,128)S(1)}, bf16[16,128,256]{2,1,0:T(8,128)(2,1)S(1)}, bf16[16,128,256]{2,1,0:T(8,128)(2,1)S(1)}, f32[16,128]{1,0:T(8,1...) custom-call(s32[8,128]{1,0:T(8,128)S(1)} %shard_map.61.picked, ...), custom_call_target="tpu_custom_call" | custom-call | tf_op jit(solution)/shard_map/pallas_call | solution.py:233
  41.8 12.2 %all_to_all.20.parts = f32[16,16,128]{2,1,0:T(8,128)S(1)} all-to-all(f32[16,16,128]{2,1,0:T(8,128)S(1)} %get-tuple-element.26), channel_id=1, replica_groups=mesh['y'=4,'core'=2,'x'=4,'s'=4,'p'=2] {'x','s'}, dimensions={0} | all-to-all | bytes 262144 | tf_op jit(solution)/shard_map/all_to_all | solution.py:250
  54.0 2.7 %shard_map.63 = (f32[16,16,128]{2,1,0:T(8,128)S(1)}, f32[256,128,128]{2,1,0:T(8,128)S(1)}) custom-call(s32[8,128]{1,0:T(8,128)S(1)} %shard_map.61.picked, bf16[16,128,256]{2,1,0:T(8,128)(2,1)S(1)} %get-tuple-element.24.src, bf16[16,128,256]{2,1,0:T(8,128)(2,1)S(1)} %get-tuple-element.25.tgt, f32[16,16,128]{2,1,0:T(8,128)S(1)} %all_to_all.20.parts), custom_call_target="tpu_custom_call" | custom-call | tf_op jit(solution)/shard_map/pallas_call | solution.py:233
  56.8 14.7 %all_to_all.21.parts = f32[16,16,128]{2,1,0:T(8,128)S(1)} all-to-all(f32[16,16,128]{2,1,0:T(8,128)S(1)} %get-tuple-element.29), channel_id=1, replica_groups=mesh['y'=4,'core'=2,'x'=4,'s'=4,'p'=2] {'p','y','core'}, dimensions={0} | all-to-all | bytes 262144 | tf_op jit(solution)/shard_map/all_to_all | solution.py:250
  71.4 1.9 %shard_map.64 = f32[16,16,128]{2,1,0:T(8,128)S(1)} custom-call(s32[8,128]{1,0:T(8,128)S(1)} %shard_map.61.picked, f32[256,128,128]{2,1,0:T(8,128)S(1)} %get-tuple-element.28.saved, f32[16,16,128]{2,1,0:T(8,128)S(1)} %all_to_all.21.parts), custom_call_target="tpu_custom_call" | custom-call | tf_op jit(solution)/shard_map/pallas_call | solution.py:233
  73.3 12.8 %all_to_all.22.parts = f32[16,16,128]{2,1,0:T(8,128)S(1)} all-to-all(f32[16,16,128]{2,1,0:T(8,128)S(1)} %shard_map.64), channel_id=1, replica_groups=mesh['y'=4,'core'=2,'x'=4,'s'=4,'p'=2] {'x','s'}, dimensions={0} | all-to-all | bytes 262144 | tf_op jit(solution)/shard_map/all_to_all | solution.py:250
  86.2 2.5 %shard_map.65 = (f32[16,8,128]{2,1,0:T(8,128)}, f32[16,128]{1,0:T(8,128)S(1)}) custom-call(s32[8,128]{1,0:T(8,128)S(1)} %shard_map.61.picked, f32[256,128,128]{2,1,0:T(8,128)S(1)} %get-tuple-element.27.saved, f32[16,16,128]{2,1,0:T(8,128)S(1)} %all_to_all.22.parts, f32[16,128]{1,0:T(8,128)S(1)} %get-tuple-element.30.sq_src), custom_call_target="tpu_custom_call" | custom-call | tf_op jit(solution)/shard_map/pallas_call | solution.py:233
  88.6 4.7 %all-to-all-start.3 = ((f32[16,8,128]{2,1,0:T(8,128)}), f32[16,8,128]{2,1,0:T(8,128)S(1)}, u32[]{:S(2)}, u32[]{:S(2)}) async-start(f32[16,8,128]{2,1,0:T(8,128)} %get-tuple-element.31), calls=%async_computation.3 | async-start | bytes 131072 | tf_op jit(solution)/shard_map/all_to_all | solution.py:250
  93.3 1.4 %collective-permute-start.12 = (f32[16,128]{1,0:T(8,128)S(1)}, f32[16,128]{1,0:T(8,128)S(1)}, u32[]{:S(2)}, u32[]{:S(2)}) collective-permute-start(f32[16,128]{1,0:T(8,128)S(1)} %get-tuple-element.33.mine), channel_id=1, source_target_pairs={{0,1},{1,0},{2,3},{3,2},{4,5},{5,4},{6,7},{7,6},{8,9},{9,8},{10,11... | collective-permute-start | bytes 24584 | tf_op jit(solution)/shard_map/ppermute | solution.py:287
  94.7 1.7 %collective-permute-done.12.other = f32[16,128]{1,0:T(8,128)S(1)} collective-permute-done((f32[16,128]{1,0:T(8,128)S(1)}, f32[16,128]{1,0:T(8,128)S(1)}, u32[]{:S(2)}, u32[]{:S(2)}) %collective-permute-start.12) | collective-permute-done | bytes 8224 | tf_op jit(solution)/shard_map/ppermute | solution.py:287
  96.4 2.8 %all-to-all-done.3.parts = f32[16,8,128]{2,1,0:T(8,128)S(1)} async-done(((f32[16,8,128]{2,1,0:T(8,128)}), f32[16,8,128]{2,1,0:T(8,128)S(1)}, u32[]{:S(2)}, u32[]{:S(2)}) %all-to-all-start.3) | async-done | bytes 65568 | tf_op jit(solution)/shard_map/all_to_all | solution.py:250
  99.1 0.6 shard_map.66
  (2 shorter events, 0.1 us)
Async XLA Ops:
  0.6 15.5 %collective-permute-start = (bf16[128,256]{1,0:T(8,128)(2,1)}, bf16[128,256]{1,0:T(8,128)(2,1)S(1)}, u32[]{:S(2)}, u32[]{:S(2)}) collective-permute-start(bf16[128,256]{1,0:T(8,128)(2,1)} %param.4), channel_id=1, source_target_pairs={{0,2},{2,4},{4,6},{6,0},{1,3},{3,5},{5,7},{7,1},{8,10},{10,12},{12... | collective-permute-start | bytes 196616 | tf_op jit(solution)/shard_map/ppermute | solution.py:255
  4.5 14.1 %collective-permute-start.2 = (bf16[128,256]{1,0:T(8,128)(2,1)}, bf16[128,256]{1,0:T(8,128)(2,1)S(1)}, u32[]{:S(2)}, u32[]{:S(2)}) collective-permute-start(bf16[128,256]{1,0:T(8,128)(2,1)} %param.4), channel_id=1, source_target_pairs={{0,6},{2,0},{4,2},{6,4},{1,7},{3,1},{5,3},{7,5},{8,14},{10,8},{12,... | collective-permute-start | bytes 196616 | tf_op jit(solution)/shard_map/ppermute | solution.py:255
  7.6 11.0 %collective-permute-start.1 = (bf16[128,256]{1,0:T(8,128)(2,1)}, bf16[128,256]{1,0:T(8,128)(2,1)S(1)}, u32[]{:S(2)}, u32[]{:S(2)}) collective-permute-start(bf16[128,256]{1,0:T(8,128)(2,1)} %param.4), channel_id=1, source_target_pairs={{0,4},{2,6},{4,0},{6,2},{1,5},{3,7},{5,1},{7,3},{8,12},{10,14},{12... | collective-permute-start | bytes 196616 | tf_op jit(solution)/shard_map/ppermute | solution.py:255
  12.0 6.6 %collective-permute-start.3 = (bf16[128,256]{1,0:T(8,128)(2,1)}, bf16[128,256]{1,0:T(8,128)(2,1)S(1)}, u32[]{:S(2)}, u32[]{:S(2)}) collective-permute-start(bf16[128,256]{1,0:T(8,128)(2,1)} %param.5), channel_id=1, source_target_pairs={{0,64},{64,128},{128,192},{192,0},{1,65},{65,129},{129,193},{193,1... | collective-permute-start | bytes 196616 | tf_op jit(solution)/shard_map/ppermute | solution.py:255
  13.3 5.3 %collective-permute-start.5 = (bf16[128,256]{1,0:T(8,128)(2,1)}, bf16[128,256]{1,0:T(8,128)(2,1)S(1)}, u32[]{:S(2)}, u32[]{:S(2)}) collective-permute-start(bf16[128,256]{1,0:T(8,128)(2,1)} %param.5), channel_id=1, source_target_pairs={{0,192},{64,0},{128,64},{192,128},{1,193},{65,1},{129,65},{193,129... | collective-permute-start | bytes 196616 | tf_op jit(solution)/shard_map/ppermute | solution.py:255
  16.1 4.8 %collective-permute-start.4 = (bf16[128,256]{1,0:T(8,128)(2,1)}, bf16[128,256]{1,0:T(8,128)(2,1)S(1)}, u32[]{:S(2)}, u32[]{:S(2)}) collective-permute-start(bf16[128,256]{1,0:T(8,128)(2,1)} %param.5), channel_id=1, source_target_pairs={{0,128},{64,192},{128,0},{192,64},{1,129},{65,193},{129,1},{193,65... | collective-permute-start | bytes 196616 | tf_op jit(solution)/shard_map/ppermute | solution.py:255
  21.0 5.4 %collective-permute-start.6 = (bf16[528,256]{1,0:T(8,128)(2,1)S(1)}, bf16[528,256]{1,0:T(8,128)(2,1)S(1)}, u32[]{:S(2)}, u32[]{:S(2)}) collective-permute-start(bf16[528,256]{1,0:T(8,128)(2,1)S(1)} %get-tuple-element.19.ours), channel_id=1, source_target_pairs={{0,1},{1,0},{2,3},{3,2},{4,5},{5,4},{6,7},{7,6},{8,9},{9,8},{10,11... | collective-permute-start | bytes 811016 | tf_op jit(solution)/shard_map/ppermute | solution.py:255
  21.8 12.4 %collective-permute-start.9 = (bf16[4,128,256]{2,1,0:T(8,128)(2,1)S(1)}, bf16[4,128,256]{2,1,0:T(8,128)(2,1)S(1)}, u32[]{:S(2)}, u32[]{:S(2)}) collective-permute-start(bf16[4,128,256]{2,1,0:T(8,128)(2,1)S(1)} %get-tuple-element.21.refs_0_), channel_id=1, source_target_pairs={{0,24},{8,0},{16,8},{24,16},{1,25},{9,1},{17,9},{25,17},{2,26},{10... | collective-permute-start | bytes 786440 | tf_op jit(solution)/shard_map/ppermute | solution.py:255
  24.3 10.0 %collective-permute-start.8 = (bf16[4,128,256]{2,1,0:T(8,128)(2,1)S(1)}, bf16[4,128,256]{2,1,0:T(8,128)(2,1)S(1)}, u32[]{:S(2)}, u32[]{:S(2)}) collective-permute-start(bf16[4,128,256]{2,1,0:T(8,128)(2,1)S(1)} %get-tuple-element.21.refs_0_), channel_id=1, source_target_pairs={{0,16},{8,24},{16,0},{24,8},{1,17},{9,25},{17,1},{25,9},{2,18},{10... | collective-permute-start | bytes 786440 | tf_op jit(solution)/shard_map/ppermute | solution.py:255
  24.8 13.2 %collective-permute-start.7 = (bf16[4,128,256]{2,1,0:T(8,128)(2,1)S(1)}, bf16[4,128,256]{2,1,0:T(8,128)(2,1)S(1)}, u32[]{:S(2)}, u32[]{:S(2)}) collective-permute-start(bf16[4,128,256]{2,1,0:T(8,128)(2,1)S(1)} %get-tuple-element.21.refs_0_), channel_id=1, source_target_pairs={{0,8},{8,16},{16,24},{24,0},{1,9},{9,17},{17,25},{25,1},{2,10},{10... | collective-permute-start | bytes 786440 | tf_op jit(solution)/shard_map/ppermute | solution.py:255
  26.4 11.6 %collective-permute-start.10 = (bf16[4,128,256]{2,1,0:T(8,128)(2,1)S(1)}, bf16[4,128,256]{2,1,0:T(8,128)(2,1)S(1)}, u32[]{:S(2)}, u32[]{:S(2)}) collective-permute-start(bf16[4,128,256]{2,1,0:T(8,128)(2,1)S(1)} %get-tuple-element.22.refs_4_), channel_id=1, source_target_pairs={{0,32},{32,0},{1,33},{33,1},{2,34},{34,2},{3,35},{35,3},{4,36},{36... | collective-permute-start | bytes 786440 | tf_op jit(solution)/shard_map/ppermute | solution.py:255
  30.8 7.2 %collective-permute-start.11 = (bf16[4,128,256]{2,1,0:T(8,128)(2,1)S(1)}, bf16[4,128,256]{2,1,0:T(8,128)(2,1)S(1)}, u32[]{:S(2)}, u32[]{:S(2)}) collective-permute-start(bf16[4,128,256]{2,1,0:T(8,128)(2,1)S(1)} %get-tuple-element.23.refs_6_), channel_id=1, source_target_pairs={{0,32},{32,0},{1,33},{33,1},{2,34},{34,2},{3,35},{35,3},{4,36},{36... | collective-permute-start | bytes 786440 | tf_op jit(solution)/shard_map/ppermute | solution.py:255
  88.6 10.5 %all-to-all-start.3 = ((f32[16,8,128]{2,1,0:T(8,128)}), f32[16,8,128]{2,1,0:T(8,128)S(1)}, u32[]{:S(2)}, u32[]{:S(2)}) async-start(f32[16,8,128]{2,1,0:T(8,128)} %get-tuple-element.31), calls=%async_computation.3 | async-start | bytes 131072 | tf_op jit(solution)/shard_map/all_to_all | solution.py:250
  93.3 3.1 %collective-permute-start.12 = (f32[16,128]{1,0:T(8,128)S(1)}, f32[16,128]{1,0:T(8,128)S(1)}, u32[]{:S(2)}, u32[]{:S(2)}) collective-permute-start(f32[16,128]{1,0:T(8,128)S(1)} %get-tuple-element.33.mine), channel_id=1, source_target_pairs={{0,1},{1,0},{2,3},{3,2},{4,5},{5,4},{6,7},{7,6},{8,9},{9,8},{10,11... | collective-permute-start | bytes 24584 | tf_op jit(solution)/shard_map/ppermute | solution.py:287
